TPU v7x, 32 devices: a whole 2x2x4 slice. The times are simulated.
32 devices in a mesh: dp: 8 (over z, y), tensor: 4 (over x, core).
Axes of the slice: x: 2, y: 2, z: 4, core: 2. Of those that a mesh axis runs over, the one named last changes fastest.
Arguments:
- tokens: bfloat16 [8, 1024, 768], P(None, 'dp'), may hold values from -6 to 6, as said below
- dealing_order: int32 [8], replicated, may hold values from 0 to 7, each once
- lengths: int32 [8], replicated, may hold values from 1 to 1024, 6144 in all
- project_weight: float32 [2, 768, 3, 768], P(None, 'dp', None, 'tensor'), may hold values from -0.14433757 to 0.14433757, as said below
- gate_up_weight: float32 [2, 768, 2, 3072], P(None, 'dp', None, 'tensor'), may hold values from -0.14433757 to 0.14433757, as said below
- output_weight: float32 [2, 768, 768], P(None, 'tensor', 'dp'), may hold values from -3 to 3
- down_weight: float32 [2, 3072, 768], P(None, 'tensor', 'dp'), may hold values from -0.109375 to 0.109375
- norm_gains: float32 [2, 2, 768], replicated, may hold values from 0.1 to 1.9
- norm_biases: float32 [2, 2, 768], replicated, may hold values from -1.75 to 1.75
- cotangent: bfloat16 [8, 1024, 768], P('dp', 'tensor'), may hold values from -6 to 6
Outputs:
- layer_outputs: float32 [8, 1024, 768], P('dp', 'tensor')
- tokens_gradient: float32 [8, 1024, 768], P(None, 'dp')
- project_gradient: float32 [2, 768, 3, 768], P(None, 'dp', None, 'tensor')
- gate_up_gradient: float32 [2, 768, 2, 3072], P(None, 'dp', None, 'tensor')
- output_gradient: float32 [2, 768, 768], P(None, 'tensor', 'dp')
- down_gradient: float32 [2, 3072, 768], P(None, 'tensor', 'dp')
- gains_gradient: float32 [2, 2, 768], replicated
- biases_gradient: float32 [2, 2, 768], replicated
Inputs may be any that keep to these rules, and one draw needn't show every extreme that they name: `dealing_order`: a permutation of the 8 sequences. The lengths sum to 6144 and the longest is exactly 1024. `tokens`: entries of mean 0 and deviation 1. `project_weight`: entries of mean 0 and deviation 768 ** -0.5. `gate_up_weight`: entries of mean 0 and deviation 768 ** -0.5.
All inputs are finite; a program needn't handle non-finite values.
Results may differ from a plain program's by a relative error of at most 0.024.
Values may be sent and summed in bfloat16 or wider, within the bound.
No kernel may reach another device: no remote copies, remote signals or barrier semaphores. Data moves between devices by JAX's collectives and lax.ppermute only.
A program may use at most 192 MiB of HBM per device.

v0:
```python
import math

import jax
import jax.numpy as jnp
from jax import lax
from jax.sharding import PartitionSpec as P

HD = 64
LAYERS = 2


epsilon = 1e-05
rotary_base = 1000.0


def rotary_tables(length, head_size):
    half_size = head_size // 2
    places = jnp.arange(length, dtype=jnp.float32)[:, None]
    freq_steps = jnp.arange(half_size, dtype=jnp.float32)[None, :]
    angles = places * jnp.exp(freq_steps * (-2.0 * math.log(rotary_base) / head_size))
    return (jnp.cos(angles)[:, None, :], jnp.sin(angles)[:, None, :])


def rotate(values, cosine_table, sine_table):
    half_size = values.shape[-1] // 2
    first_half = values[..., :half_size]
    second = values[..., half_size:]
    return jnp.concatenate(
        [
            first_half * cosine_table - second * sine_table,
            second * cosine_table + first_half * sine_table,
        ],
        axis=-1,
    )


def rotate_back(gradient, cosine_table, sine_table):
    half_size = gradient.shape[-1] // 2
    first_half = gradient[..., :half_size]
    second = gradient[..., half_size:]
    return jnp.concatenate(
        [
            first_half * cosine_table + second * sine_table,
            second * cosine_table - first_half * sine_table,
        ],
        axis=-1,
    )


def norm_forward(values, gain_vector, shift_vector):
    centred = values - jnp.mean(values, axis=-1, keepdims=True)
    scaled = lax.rsqrt(jnp.mean(centred * centred, axis=-1, keepdims=True) + epsilon)
    return centred * scaled * gain_vector + shift_vector


def norm_backward(values, gain_vector, incoming):
    centred = values - jnp.mean(values, axis=-1, keepdims=True)
    scaled = lax.rsqrt(jnp.mean(centred * centred, axis=-1, keepdims=True) + epsilon)
    normal = centred * scaled
    weighted = incoming * gain_vector
    inner_sum = (
        weighted
        - jnp.mean(weighted, axis=-1, keepdims=True)
        - normal * jnp.mean(weighted * normal, axis=-1, keepdims=True)
    )
    gain_grad = jnp.sum(incoming * normal, axis=(0, 1))
    shift_grad = jnp.sum(incoming, axis=(0, 1))
    return (inner_sum * scaled, gain_grad, shift_grad)


def spread_rows(values):
    return lax.all_gather(values, "tensor", axis=1, tiled=True)


def sum_rows(values):
    return lax.psum_scatter(values, "tensor", scatter_dimension=1, tiled=True)


def collect_rows(values):
    return lax.all_gather(values, "tensor", axis=1, tiled=True)


def gather_sums(values):
    return lax.psum_scatter(values, "tensor", scatter_dimension=1, tiled=True)


def masked_scores(queries, key_rows, length):
    score_scale = 1.0 / math.sqrt(queries.shape[-1])
    scores = (
        jnp.einsum("qhd,khd->hqk", queries, key_rows, preferred_element_type=jnp.float32)
        * score_scale
    )
    usable = jnp.arange(scores.shape[-1]) < length
    return (jnp.where(usable[None, None, :], scores, -1e30), score_scale)


def attend_forward(operands):
    queries, key_rows, values_in, length = operands
    scores, score_scale = masked_scores(queries, key_rows, length)
    row_top = jnp.max(scores, axis=-1, keepdims=True)
    exponent = jnp.exp(scores - row_top)
    row_total = jnp.sum(exponent, axis=-1, keepdims=True)
    weights = (exponent / row_total).astype(jnp.bfloat16)
    context = jnp.einsum("hqk,khd->qhd", weights, values_in, preferred_element_type=jnp.float32)
    return (context.astype(jnp.bfloat16), row_top + jnp.log(row_total))


def attend_backward(operands):
    queries, key_rows, values_in, length, logsum, context_grad = operands
    scores, score_scale = masked_scores(queries, key_rows, length)
    weights = jnp.exp(scores - logsum)
    rounded = weights.astype(jnp.bfloat16)
    weight_grad = jnp.einsum(
        "qhd,khd->hqk", context_grad, values_in, preferred_element_type=jnp.float32
    )
    inner_sum = jnp.sum(weights * weight_grad, axis=-1, keepdims=True)
    score_grad = (weights * (weight_grad - inner_sum)).astype(jnp.bfloat16)
    query_grad = (
        jnp.einsum("hqk,khd->qhd", score_grad, key_rows, preferred_element_type=jnp.float32)
        * score_scale
    )
    key_grad = (
        jnp.einsum("hqk,qhd->khd", score_grad, queries, preferred_element_type=jnp.float32)
        * score_scale
    )
    value_grad = jnp.einsum(
        "hqk,qhd->khd", rounded, context_grad, preferred_element_type=jnp.float32
    )
    return (query_grad, key_grad, value_grad)


def contract_rows(left, right):
    return lax.dot_general(
        left, right, (((0,), (0,)), ((), ())), preferred_element_type=jnp.float32
    )


def contract_cols(left, right):
    return lax.dot_general(
        left, right, (((1,), (1,)), ((), ())), preferred_element_type=jnp.float32
    )


def layer_forward(
    full_rows, residual, lengths_now, weights_now, gain_pair, shift_pair, cosine_table, sine_table
):
    project_now, gate_up_now, output_now, down_now = weights_now
    seq_count, length, model_width = full_rows.shape
    row_count = seq_count * length
    inner_width = project_now.shape[-1]
    heads_here = inner_width // HD
    flat_rows = full_rows.reshape(row_count, model_width)
    projected = jnp.dot(
        flat_rows,
        project_now.reshape(model_width, 3 * inner_width),
        preferred_element_type=jnp.float32,
    )
    projected = projected.reshape(seq_count, length, 3, heads_here, HD)
    queries = rotate(projected[:, :, 0], cosine_table, sine_table).astype(jnp.bfloat16)
    key_rows = rotate(projected[:, :, 1], cosine_table, sine_table).astype(jnp.bfloat16)
    values_in = projected[:, :, 2].astype(jnp.bfloat16)
    context, logsum = lax.map(attend_forward, (queries, key_rows, values_in, lengths_now))
    context_flat = context.reshape(row_count, inner_width)
    attended = jnp.dot(context_flat, output_now, preferred_element_type=jnp.float32).reshape(
        seq_count, length, model_width
    )
    first_sum = residual + sum_rows(attended)
    hidden = norm_forward(first_sum, gain_pair[0], shift_pair[0])
    hidden_rows = spread_rows(hidden.astype(jnp.bfloat16)).reshape(row_count, model_width)
    gate_up = jnp.dot(
        hidden_rows, gate_up_now.reshape(model_width, -1), preferred_element_type=jnp.float32
    )
    gate_up = gate_up.reshape(row_count, 2, gate_up_now.shape[-1])
    active = (jax.nn.silu(gate_up[:, 0]) * gate_up[:, 1]).astype(jnp.bfloat16)
    mixed_part = jnp.dot(active, down_now, preferred_element_type=jnp.float32).reshape(
        seq_count, length, model_width
    )
    second_sum = hidden + sum_rows(mixed_part)
    result = norm_forward(second_sum, gain_pair[1], shift_pair[1])
    saved_state = (
        flat_rows,
        queries,
        key_rows,
        values_in,
        context_flat,
        logsum,
        first_sum,
        hidden_rows,
        gate_up,
        active,
        second_sum,
    )
    return (result, saved_state)


def layer_backward(
    incoming, saved_state, lengths_now, weights_now, gain_pair, cosine_table, sine_table
):
    (
        flat_rows,
        queries,
        key_rows,
        values_in,
        context_flat,
        logsum,
        first_sum,
        hidden_rows,
        gate_up,
        active,
        second_sum,
    ) = saved_state
    project_now, gate_up_now, output_now, down_now = weights_now
    seq_count, length, heads_here, head_size = queries.shape
    row_count, model_width = flat_rows.shape
    inner_width = project_now.shape[-1]
    second_grad, gain_two, shift_two = norm_backward(second_sum, gain_pair[1], incoming)
    mixed_rows = collect_rows(second_grad.astype(jnp.bfloat16)).reshape(row_count, model_width)
    down_grad = contract_rows(active, mixed_rows)
    active_grad = contract_cols(mixed_rows, down_now)
    gate_values = gate_up[:, 0]
    up_values = gate_up[:, 1]
    sigmoid_gate = jax.nn.sigmoid(gate_values)
    gate_grad = active_grad * up_values * sigmoid_gate * (1.0 + gate_values * (1.0 - sigmoid_gate))
    up_grad = active_grad * gate_values * sigmoid_gate
    pair_grad = jnp.stack([gate_grad, up_grad], axis=1).astype(jnp.bfloat16).reshape(row_count, -1)
    gate_up_grad = contract_rows(hidden_rows, pair_grad)
    hidden_part = contract_cols(pair_grad, gate_up_now.reshape(model_width, -1))
    hidden_grad = second_grad + gather_sums(hidden_part.reshape(seq_count, length, model_width))
    first_grad, gain_one, shift_one = norm_backward(first_sum, gain_pair[0], hidden_grad)
    attended_rows = collect_rows(first_grad.astype(jnp.bfloat16)).reshape(row_count, model_width)
    output_grad = contract_rows(context_flat, attended_rows)
    context_grad = (
        contract_cols(attended_rows, output_now)
        .astype(jnp.bfloat16)
        .reshape(seq_count, length, heads_here, head_size)
    )
    query_grad, key_grad, value_grad = lax.map(
        attend_backward, (queries, key_rows, values_in, lengths_now, logsum, context_grad)
    )
    query_grad = rotate_back(query_grad, cosine_table, sine_table)
    key_grad = rotate_back(key_grad, cosine_table, sine_table)
    triple = (
        jnp.stack([query_grad, key_grad, value_grad], axis=2)
        .astype(jnp.bfloat16)
        .reshape(row_count, 3 * inner_width)
    )
    project_grad = contract_rows(flat_rows, triple)
    input_part = contract_cols(triple, project_now.reshape(model_width, -1))
    input_grad = first_grad + gather_sums(input_part.reshape(seq_count, length, model_width))
    weight_grads = (
        project_grad.reshape(model_width, 3, inner_width),
        gate_up_grad.reshape(model_width, 2, -1),
        output_grad,
        down_grad,
    )
    return (
        input_grad,
        weight_grads,
        jnp.stack([gain_one, gain_two]),
        jnp.stack([shift_one, shift_two]),
    )


def on_device(
    tokens,
    dealing_order,
    lengths,
    project_weight,
    gate_up_weight,
    output_weight,
    down_weight,
    norm_gains,
    norm_biases,
    cotangent,
):
    dp_index = lax.axis_index("dp")
    tensor_count = lax.axis_size("tensor")
    tensor_index = lax.axis_index("tensor")
    picked = jnp.take(tokens, dealing_order, axis=0)
    arrived = lax.all_to_all(picked, "dp", split_axis=0, concat_axis=1, tiled=True)
    local_count = arrived.shape[0]
    length = arrived.shape[1]
    quarter = length // tensor_count
    ordered_lengths = jnp.take(lengths, dealing_order)
    lengths_now = lax.dynamic_slice_in_dim(ordered_lengths, dp_index * local_count, local_count)
    cosine_table, sine_table = rotary_tables(length, HD)
    positions = tensor_index * quarter + jnp.arange(quarter)
    usable = (positions[None, :] < lengths_now[:, None])[:, :, None]
    full_rows = arrived
    current = lax.dynamic_slice_in_dim(arrived, tensor_index * quarter, quarter, 1).astype(
        jnp.float32
    )
    stored = []
    saved_all = []
    for depth_index in range(LAYERS):
        gathered = (
            lax.all_gather(
                project_weight[depth_index].astype(jnp.bfloat16), "dp", axis=0, tiled=True
            ),
            lax.all_gather(
                gate_up_weight[depth_index].astype(jnp.bfloat16), "dp", axis=0, tiled=True
            ),
            lax.all_gather(
                output_weight[depth_index].astype(jnp.bfloat16), "dp", axis=1, tiled=True
            ),
            lax.all_gather(down_weight[depth_index].astype(jnp.bfloat16), "dp", axis=1, tiled=True),
        )
        if depth_index > 0:
            full_rows = spread_rows(current.astype(jnp.bfloat16))
        current, saved_state = layer_forward(
            full_rows,
            current,
            lengths_now,
            gathered,
            norm_gains[depth_index],
            norm_biases[depth_index],
            cosine_table,
            sine_table,
        )
        stored.append(gathered)
        saved_all.append(saved_state)
    layer_outputs = jnp.where(usable, current, 0.0)
    incoming = jnp.where(usable, cotangent.astype(jnp.float32), 0.0)
    weight_sets = []
    gain_sets = []
    shift_sets = []
    for depth_index in reversed(range(LAYERS)):
        weights_now = stored[depth_index]
        incoming, layer_grads, gain_grads, shift_grads = layer_backward(
            incoming,
            saved_all[depth_index],
            lengths_now,
            weights_now,
            norm_gains[depth_index],
            cosine_table,
            sine_table,
        )
        weight_sets.insert(0, layer_grads)
        gain_sets.insert(0, gain_grads)
        shift_sets.insert(0, shift_grads)
    stacked = tuple(
        (jnp.stack([layer_set[member] for layer_set in weight_sets]) for member in range(4))
    )
    stacked = (
        lax.psum_scatter(stacked[0], "dp", scatter_dimension=1, tiled=True),
        lax.psum_scatter(stacked[1], "dp", scatter_dimension=1, tiled=True),
        lax.psum_scatter(stacked[2], "dp", scatter_dimension=2, tiled=True),
        lax.psum_scatter(stacked[3], "dp", scatter_dimension=2, tiled=True),
    )
    gains_total, biases_total = lax.psum(
        (jnp.stack(gain_sets), jnp.stack(shift_sets)), ("dp", "tensor")
    )
    final_rows = lax.all_gather(incoming, "tensor", axis=1, tiled=True)
    received = lax.all_to_all(final_rows, "dp", split_axis=1, concat_axis=0, tiled=True)
    returned = jnp.zeros_like(received).at[dealing_order].set(received)
    return (
        layer_outputs,
        returned,
        stacked[0],
        stacked[1],
        stacked[2],
        stacked[3],
        gains_total,
        biases_total,
    )


def solution(mesh):
    placed = (
        P(None, "dp", None),
        P(),
        P(),
        P(None, "dp", None, "tensor"),
        P(None, "dp", None, "tensor"),
        P(None, "tensor", "dp"),
        P(None, "tensor", "dp"),
        P(),
        P(),
        P("dp", "tensor", None),
    )
    return jax.shard_map(
        on_device,
        mesh=mesh,
        in_specs=placed,
        out_specs=(
            P("dp", "tensor", None),
            P(None, "dp", None),
            P(None, "dp", None, "tensor"),
            P(None, "dp", None, "tensor"),
            P(None, "tensor", "dp"),
            P(None, "tensor", "dp"),
            P(),
            P(),
        ),
        check_vma=False,
    )
```

profile of v0, /device:TPU:0, one launch (start us, length us, event | category | flops | bytes accessed | tf_op | source)
XLA Modules:
  0.0 1522.8 jit_solution(6889309907420662876)
XLA Ops:
  13.4 7.3 all-to-all-start
  21.5 58.6 %all-gather.1 = bf16[1,192,768]{1,0,2:T(2,128)(2,1)S(1)} all-gather(bf16[1,192,96]{1,0,2:T(2,128)(2,1)S(1)} %get-tuple-element.227), channel_id=3, replica_groups=mesh['dp'=8,'tensor'=4] {'dp'}, dimensions={2}, use_global_device_ids=true | all-gather | bytes 331776 | tf_op jit(solution)/shard_map/all_gather | solution.py:303
  82.4 35.8 %all-gather = bf16[1,768,3,192]{3,2,0,1:T(4,128)(2,1)S(1)} all-gather(bf16[1,96,3,192]{3,2,0,1:T(4,128)(2,1)S(1)} %get-tuple-element.214), channel_id=2, replica_groups=mesh['dp'=8,'tensor'=4] {'dp'}, dimensions={1}, use_global_device_ids=true | all-gather | bytes 995328 | tf_op jit(solution)/shard_map/all_gather | solution.py:297
  122.2 2.9 convolution_bitcast_fusion.9
  141.0 34.2 %reduce-scatter.16.cloned.1.call-done = f32[1,256,768]{2,1,0:T(8,128)} async-done(((f32[1,1024,768]{2,1,0:T(8,128)}), f32[1,256,768]{2,1,0:T(8,128)}) %reduce-scatter.16.cloned.1.call-update) | async-done | bytes 786448 | tf_op jit(solution)/shard_map/reduce_scatter | solution.py:76
  179.9 12.1 all-gather.37.cloned.1.call-done
  192.1 4.3 copy.83
  196.3 15.9 %all-gather.21.cloned.1.call-done = bf16[1,1024,768]{2,1,0:T(8,128)(2,1)} async-done(((bf16[1,256,768]{2,1,0:T(8,128)(2,1)}), bf16[1,1024,768]{2,1,0:T(8,128)(2,1)}) %all-gather.21.cloned.1.call-update) | async-done | bytes 1572880 | tf_op jit(solution)/shard_map/all_gather | solution.py:72
  212.2 7.5 fusion.38
  219.7 36.9 %all-gather.39.cloned.1.call-done = bf16[1,768,768]{1,2,0:T(8,128)(2,1)} async-done(((bf16[1,768,96]{1,2,0:T(8,128)(2,1)}), bf16[1,768,768]{1,2,0:T(8,128)(2,1)}) %all-gather.39.cloned.1.call-update) | async-done | bytes 1179664 | tf_op jit(solution)/shard_map/all_gather | solution.py:306
  256.6 6.9 convolution_bitcast_fusion.4
  263.6 36.5 %reduce-scatter.18.cloned.1.call-done = f32[1,256,768]{2,1,0:T(8,128)} async-done(((f32[1,1024,768]{2,1,0:T(8,128)}), f32[1,256,768]{2,1,0:T(8,128)}) %reduce-scatter.18.cloned.1.call-update) | async-done | bytes 786448 | tf_op jit(solution)/shard_map/reduce_scatter | solution.py:76
  302.8 32.1 %all-gather.5 = bf16[1,192,768]{1,0,2:T(2,128)(2,1)S(1)} all-gather(bf16[1,192,96]{1,0,2:T(2,128)(2,1)S(1)} %get-tuple-element.226), channel_id=7, replica_groups=mesh['dp'=8,'tensor'=4] {'dp'}, dimensions={2}, use_global_device_ids=true | all-gather | bytes 331776 | tf_op jit(solution)/shard_map/all_gather | solution.py:303
  336.5 38.2 %all-gather.4 = bf16[1,768,3,192]{3,2,0,1:T(4,128)(2,1)S(1)} all-gather(bf16[1,96,3,192]{3,2,0,1:T(4,128)(2,1)} %get-tuple-element.215), channel_id=6, replica_groups=mesh['dp'=8,'tensor'=4] {'dp'}, dimensions={1}, use_global_device_ids=true | all-gather | bytes 995328 | tf_op jit(solution)/shard_map/all_gather | solution.py:297
  384.4 2.9 copy-done.3
  393.4 34.8 %reduce-scatter.20.cloned.1.call-done = f32[1,256,768]{2,1,0:T(8,128)} async-done(((f32[1,1024,768]{2,1,0:T(8,128)}), f32[1,256,768]{2,1,0:T(8,128)}) %reduce-scatter.20.cloned.1.call-update) | async-done | bytes 786448 | tf_op jit(solution)/shard_map/reduce_scatter | solution.py:76
  431.5 8.8 reduce-scatter.22.cloned.1.call-start
  440.3 42.7 %all-gather.41.cloned.1.call-done = bf16[1,768,2,768]{3,1,2,0:T(8,128)(2,1)} async-done(((bf16[1,96,2,768]{3,1,2,0:T(8,128)(2,1)}), bf16[1,768,2,768]{3,1,2,0:T(8,128)(2,1)}) %all-gather.41.cloned.1.call-update) | async-done | bytes 2359312 | tf_op jit(solution)/shard_map/all_gather | solution.py:300
  483.1 4.3 copy.87
  487.3 15.9 %all-gather.25.cloned.1.call-done = bf16[1,1024,768]{2,1,0:T(8,128)(2,1)} async-done(((bf16[1,256,768]{2,1,0:T(8,128)(2,1)}), bf16[1,1024,768]{2,1,0:T(8,128)(2,1)}) %all-gather.25.cloned.1.call-update) | async-done | bytes 1572880 | tf_op jit(solution)/shard_map/all_gather | solution.py:72
  503.2 7.5 fusion.36
  510.7 36.3 %all-gather.43.cloned.1.call-done = bf16[1,768,768]{1,2,0:T(8,128)(2,1)} async-done(((bf16[1,768,96]{1,2,0:T(8,128)(2,1)}), bf16[1,768,768]{1,2,0:T(8,128)(2,1)}) %all-gather.43.cloned.1.call-update) | async-done | bytes 1179664 | tf_op jit(solution)/shard_map/all_gather | solution.py:306
  547.0 6.9 convolution_bitcast_fusion.2
  555.2 35.3 %reduce-scatter.22.cloned.1.call-done = f32[1,256,768]{2,1,0:T(8,128)} async-done(((f32[1,1024,768]{2,1,0:T(8,128)}), f32[1,256,768]{2,1,0:T(8,128)}) %reduce-scatter.22.cloned.1.call-update) | async-done | bytes 786448 | tf_op jit(solution)/shard_map/reduce_scatter | solution.py:76
  597.0 19.8 %all-gather.27.cloned.1.call-done = bf16[1,1024,768]{2,1,0:T(8,128)(2,1)} async-done(((bf16[1,256,768]{2,1,0:T(8,128)(2,1)}), bf16[1,1024,768]{2,1,0:T(8,128)(2,1)}) %all-gather.27.cloned.1.call-update) | async-done | bytes 1572880 | tf_op jit(solution)/shard_map/all_gather | solution.py:80
  616.8 6.2 fusion.19
  624.6 4.4 fusion.50
  629.1 38.1 %reduce-scatter.24.cloned.1.call-done = f32[1,256,768]{2,1,0:T(8,128)} async-done(((f32[1,1024,768]{2,1,0:T(8,128)}), f32[1,256,768]{2,1,0:T(8,128)}) %reduce-scatter.24.cloned.1.call-update) | async-done | bytes 786448 | tf_op jit(solution)/shard_map/reduce_scatter | solution.py:84
  667.2 3.3 multiply_reduce_fusion.3
  672.2 19.1 %all-gather.29.cloned.1.call-done = bf16[1,1024,768]{2,1,0:T(8,128)(2,1)} async-done(((bf16[1,256,768]{2,1,0:T(8,128)(2,1)}), bf16[1,1024,768]{2,1,0:T(8,128)(2,1)}) %all-gather.29.cloned.1.call-update) | async-done | bytes 1572880 | tf_op jit(solution)/shard_map/all_gather | solution.py:80
  693.4 6.8 fusion.88
  700.2 6.3 multiply_reduce_fusion.1
  707.5 5.2 multiply_convert_fusion.1
  712.7 5.0 fusion.86
  720.5 3.1 convolution_bitcast_fusion.1
  723.7 38.0 %reduce-scatter.26.cloned.1.call-done = f32[1,256,768]{2,1,0:T(8,128)} async-done(((f32[1,1024,768]{2,1,0:T(8,128)}), f32[1,256,768]{2,1,0:T(8,128)}) %reduce-scatter.26.cloned.1.call-update) | async-done | bytes 786448 | tf_op jit(solution)/shard_map/reduce_scatter | solution.py:84
  764.4 19.6 %all-gather.31.cloned.1.call-done = bf16[1,1024,768]{2,1,0:T(8,128)(2,1)} async-done(((bf16[1,256,768]{2,1,0:T(8,128)(2,1)}), bf16[1,1024,768]{2,1,0:T(8,128)(2,1)}) %all-gather.31.cloned.1.call-update) | async-done | bytes 1572880 | tf_op jit(solution)/shard_map/all_gather | solution.py:80
  784.0 6.2 fusion.29
  791.9 4.4 fusion.53
  796.4 37.9 %reduce-scatter.28.cloned.1.call-done = f32[1,256,768]{2,1,0:T(8,128)} async-done(((f32[1,1024,768]{2,1,0:T(8,128)}), f32[1,256,768]{2,1,0:T(8,128)}) %reduce-scatter.28.cloned.1.call-update) | async-done | bytes 786448 | tf_op jit(solution)/shard_map/reduce_scatter | solution.py:84
  837.2 19.6 %all-gather.33.cloned.1.call-done = bf16[1,1024,768]{2,1,0:T(8,128)(2,1)} async-done(((bf16[1,256,768]{2,1,0:T(8,128)(2,1)}), bf16[1,1024,768]{2,1,0:T(8,128)(2,1)}) %all-gather.33.cloned.1.call-update) | async-done | bytes 1572880 | tf_op jit(solution)/shard_map/all_gather | solution.py:80
  858.9 6.8 fusion.91
  865.6 6.2 multiply_reduce_fusion
  872.9 5.3 multiply_convert_fusion
  878.2 5.0 fusion.84
  886.0 3.1 convolution_bitcast_fusion
  889.2 38.1 %reduce-scatter.30.cloned.1.call-done = f32[1,256,768]{2,1,0:T(8,128)} async-done(((f32[1,1024,768]{2,1,0:T(8,128)}), f32[1,256,768]{2,1,0:T(8,128)}) %reduce-scatter.30.cloned.1.call-update) | async-done | bytes 786448 | tf_op jit(solution)/shard_map/reduce_scatter | solution.py:84
  929.6 4.8 convolution_bitcast_fusion.6
  934.4 5.2 convolution_bitcast_fusion.7
  942.1 8.3 copy.99
  963.5 7.1 copy.119
  970.5 8.0 reshape.701
  979.9 4.7 fusion.47
  987.3 4.3 pad_maximum_fusion
  991.6 6.9 copy.96
  998.6 5.5 all-to-all-start.1
  1005.4 178.8 %all-reduce.4.cloned.1.call-done = f32[2,768,768]{1,0,2:T(2,128)} async-done(((f32[2,768,768]{1,0,2:T(2,128)}), f32[2,768,768]{1,0,2:T(2,128)}) %all-reduce.4.cloned.1.call-update) | async-done | bytes 4718608
  1186.3 40.6 %all-reduce.1 = (f32[2,2,768]{2,1,0:T(2,128)}, f32[2,2,768]{2,1,0:T(2,128)}) all-reduce(f32[2,2,768]{2,1,0:T(2,128)S(1)} %pad_maximum_fusion.16, f32[2,2,768]{2,1,0:T(2,128)S(1)} %pad_maximum_fusion.17), channel_id=1, replica_groups=mesh['dp'=8,'tensor'=4] {'dp','tensor'}, use_global_device_ids=true, to_apply=%region_39.40 | all-reduce | flops 6144 | bytes 49152 | tf_op jit(solution)/shard_map/psum | solution.py:350
  1226.9 24.1 %reduce-scatter.36.cloned.1.call-done = f32[96,384]{1,0:T(8,128)} async-done(((f32[768,384]{1,0:T(8,128)}), f32[96,384]{1,0:T(8,128)}) %reduce-scatter.36.cloned.1.call-update) | async-done | bytes 147472
  1252.9 79.8 %reduce-scatter.34.cloned.1.call-done = f32[96,1152]{1,0:T(8,128)} async-done(((f32[768,1152]{1,0:T(8,128)}), f32[96,1152]{1,0:T(8,128)}) %reduce-scatter.34.cloned.1.call-update) | async-done | bytes 442384
  1335.3 163.7 %reduce-scatter.32.cloned.1.call-done = f32[2,96,2,768]{3,1,2,0:T(8,128)} async-done(((f32[2,768,2,768]{3,1,2,0:T(8,128)}), f32[2,96,2,768]{3,1,2,0:T(8,128)}) %reduce-scatter.32.cloned.1.call-update) | async-done | bytes 1179664 | tf_op jit(solution)/shard_map/reduce_scatter | solution.py:346
  1499.0 3.2 copy.101
  1502.2 3.7 copy.124
  1507.9 6.8 scatter_fusion
  (390 shorter events, 117.0 us)
Async XLA Ops:
  12.0 8.7 copy-start.49
  12.0 8.9 copy-start.48
  13.4 108.8 %all-to-all-start = ((bf16[8,128,768]{2,1,0:T(8,128)(2,1)}), bf16[8,128,768]{2,1,0:T(8,128)(2,1)S(1)}, u32[]{:S(2)}, u32[]{:S(2)}) async-start(bf16[8,128,768]{2,1,0:T(8,128)(2,1)} %broadcast_select_fusion), calls=%async_computation | async-start | bytes 3145728 | tf_op jit(solution)/shard_map/all_to_all | solution.py:280
  20.7 154.5 %reduce-scatter.16.cloned.1.call-start = ((), (), s32[]{:S(2)}) async-start(), calls=%async_computation.13 | async-start | bytes 3932160 | tf_op jit(solution)/shard_map/reduce_scatter | solution.py:76
  122.2 257.4 %copy-start.7 = (f32[1024,32]{0,1:T(8,128)}, f32[1024,32]{0,1:T(8,128)S(1)}, u32[]{:S(2)}) copy-start(f32[1024,32]{0,1:T(8,128)S(1)} %get-tuple-element.228) | copy-start | bytes 393220
  122.2 257.4 %copy-start.9 = (f32[1024,32]{0,1:T(8,128)}, f32[1024,32]{0,1:T(8,128)S(1)}, u32[]{:S(2)}) copy-start(f32[1024,32]{0,1:T(8,128)S(1)} %get-tuple-element.229) | copy-start | bytes 393220
  122.2 52.9 %copy-start.13 = (bf16[8,128,768]{2,1,0:T(8,128)(2,1)}, bf16[8,128,768]{2,1,0:T(8,128)(2,1)S(1)}, u32[]{:S(2)}) copy-start(bf16[8,128,768]{2,1,0:T(8,128)(2,1)S(1)} %all-to-all-done) | copy-start | bytes 4718596
  138.0 54.1 %all-gather.37.cloned.1.call-start = ((), (), s32[]{:S(2)}) async-start(), calls=%async_computation.30 | async-start | bytes 2654208 | tf_op jit(solution)/shard_map/all_gather | solution.py:300
  140.2 71.9 %all-gather.21.cloned.1.call-start = ((), (), s32[]{:S(2)}) async-start(), calls=%async_computation.14 | async-start | bytes 1966080 | tf_op jit(solution)/shard_map/all_gather | solution.py:72
  141.0 159.1 %copy-start.52 = (f32[768]{0:T(1024)}, f32[768]{0:T(1024)S(1)}, u32[]{:S(2)}) copy-start(f32[768]{0:T(1024)S(1)} %get-tuple-element.239) | copy-start | bytes 9220
  141.0 160.8 %copy-start.67 = (f32[768]{0:T(1024)}, f32[768]{0:T(1024)S(1)}, u32[]{:S(2)}) copy-start(f32[768]{0:T(1024)S(1)} %get-tuple-element.163) | copy-start | bytes 9220
  141.0 287.2 %copy-start.54 = (f32[768]{0:T(1024)}, f32[768]{0:T(1024)S(1)}, u32[]{:S(2)}) copy-start(f32[768]{0:T(1024)S(1)} %get-tuple-element.240) | copy-start | bytes 9220
  141.0 289.0 %copy-start.56 = (f32[768]{0:T(1024)}, f32[768]{0:T(1024)S(1)}, u32[]{:S(2)}) copy-start(f32[768]{0:T(1024)S(1)} %get-tuple-element.238) | copy-start | bytes 9220
  141.0 289.0 %copy-start.66 = (f32[768]{0:T(1024)}, f32[768]{0:T(1024)S(1)}, u32[]{:S(2)}) copy-start(f32[768]{0:T(1024)S(1)} %get-tuple-element.165) | copy-start | bytes 9220
  176.5 123.6 %copy-start.62 = (f32[256]{0:T(256)}, f32[256]{0:T(256)S(1)}, u32[]{:S(2)}) copy-start(f32[256]{0:T(256)S(1)} %broadcast_multiply_fusion.11) | copy-start | bytes 3076
  176.7 123.4 %copy-start.71 = (f32[256]{0:T(256)}, f32[256]{0:T(256)S(1)}, u32[]{:S(2)}) copy-start(f32[256]{0:T(256)S(1)} %add_rsqrt_fusion.3) | copy-start | bytes 3076
  177.7 78.9 %all-gather.39.cloned.1.call-start = ((), (), s32[]{:S(2)}) async-start(), calls=%async_computation.31 | async-start | bytes 1327104 | tf_op jit(solution)/shard_map/all_gather | solution.py:306
  179.6 120.5 %reduce-scatter.18.cloned.1.call-start = ((), (), s32[]{:S(2)}) async-start(), calls=%async_computation.15 | async-start | bytes 3932160 | tf_op jit(solution)/shard_map/reduce_scatter | solution.py:76
  263.5 113.2 %all-gather.23.cloned.1.call-start = ((), (), s32[]{:S(2)}) async-start(), calls=%async_computation.16 | async-start | bytes 1966080 | tf_op jit(solution)/shard_map/all_gather | solution.py:72
  301.5 126.7 %copy-start.64 = (f32[256]{0:T(256)}, f32[256]{0:T(256)S(1)}, u32[]{:S(2)}) copy-start(f32[256]{0:T(256)S(1)} %broadcast_multiply_fusion.10) | copy-start | bytes 3076
  301.8 75.0 %copy-start.73 = (f32[256]{0:T(256)}, f32[256]{0:T(256)S(1)}, u32[]{:S(2)}) copy-start(f32[256]{0:T(256)S(1)} %add_rsqrt_fusion.2) | copy-start | bytes 3076
  302.8 125.5 %reduce-scatter.20.cloned.1.call-start = ((), (), s32[]{:S(2)}) async-start(), calls=%async_computation.17 | async-start | bytes 3932160 | tf_op jit(solution)/shard_map/reduce_scatter | solution.py:76
  390.3 37.9 %copy-start.68 = (f32[768]{0:T(1024)S(1)}, f32[768]{0:T(1024)}, u32[]{:S(2)}) copy-start(f32[768]{0:T(1024)} %copy-done.67) | copy-start | bytes 9220
  390.3 37.9 %copy-start.74 = (f32[256]{0:T(256)S(1)}, f32[256]{0:T(256)}, u32[]{:S(2)}) copy-start(f32[256]{0:T(256)} %copy-done.73) | copy-start | bytes 3076
  392.6 90.4 %all-gather.41.cloned.1.call-start = ((), (), s32[]{:S(2)}) async-start(), calls=%async_computation.32 | async-start | bytes 2654208 | tf_op jit(solution)/shard_map/all_gather | solution.py:300
  393.4 109.8 %all-gather.25.cloned.1.call-start = ((), (), s32[]{:S(2)}) async-start(), calls=%async_computation.18 | async-start | bytes 1966080 | tf_op jit(solution)/shard_map/all_gather | solution.py:72
  429.7 57.6 %copy-start.69 = (f32[256]{0:T(256)}, f32[256]{0:T(256)S(1)}, u32[]{:S(2)}) copy-start(f32[256]{0:T(256)S(1)} %broadcast_multiply_fusion.9) | copy-start | bytes 3076
  429.9 57.4 %copy-start.76 = (f32[256]{0:T(256)}, f32[256]{0:T(256)S(1)}, u32[]{:S(2)}) copy-start(f32[256]{0:T(256)S(1)} %add_rsqrt_fusion.1) | copy-start | bytes 3076
  430.9 116.1 %all-gather.43.cloned.1.call-start = ((), (), s32[]{:S(2)}) async-start(), calls=%async_computation.33 | async-start | bytes 1327104 | tf_op jit(solution)/shard_map/all_gather | solution.py:306
  431.5 159.0 %reduce-scatter.22.cloned.1.call-start = ((), (), s32[]{:S(2)}) async-start(), calls=%async_computation.19 | async-start | bytes 3932160 | tf_op jit(solution)/shard_map/reduce_scatter | solution.py:76
  553.9 38.3 %copy-start.6 = (bf16[1,256,768]{2,1,0:T(8,128)(2,1)S(1)}, bf16[1,256,768]{2,1,0:T(8,128)(2,1)}, u32[]{:S(2)}) copy-start(bf16[1,256,768]{2,1,0:T(8,128)(2,1)} %param.19) | copy-start | bytes 1179652
  553.9 62.9 %all-gather.27.cloned.1.call-start = ((), (), s32[]{:S(2)}) async-start(), calls=%async_computation.20 | async-start | bytes 1966080 | tf_op jit(solution)/shard_map/all_gather | solution.py:80
  597.0 70.2 %reduce-scatter.24.cloned.1.call-start = ((), (), s32[]{:S(2)}) async-start(), calls=%async_computation.21 | async-start | bytes 3932160 | tf_op jit(solution)/shard_map/reduce_scatter | solution.py:84
  616.8 7.9 copy-start.16
  629.1 62.2 %all-gather.29.cloned.1.call-start = ((), (), s32[]{:S(2)}) async-start(), calls=%async_computation.22 | async-start | bytes 1966080 | tf_op jit(solution)/shard_map/all_gather | solution.py:80
  670.6 20.7 %copy-start.45 = (bf16[1,192,768]{2,1,0:T(8,128)(2,1)S(1)}, bf16[1,192,768]{2,1,0:T(8,128)(2,1)}, u32[]{:S(2)}) copy-start(bf16[1,192,768]{2,1,0:T(8,128)(2,1)} %copy.86) | copy-start | bytes 884740
  671.7 90.0 %reduce-scatter.26.cloned.1.call-start = ((), (), s32[]{:S(2)}) async-start(), calls=%async_computation.23 | async-start | bytes 3932160 | tf_op jit(solution)/shard_map/reduce_scatter | solution.py:84
  693.4 13.1 slice-start.3
  700.2 7.3 slice-start.5
  723.6 38.1 %copy-start.55 = (f32[768]{0:T(1024)S(1)}, f32[768]{0:T(1024)}, u32[]{:S(2)}) copy-start(f32[768]{0:T(1024)} %copy-done.54) | copy-start | bytes 9220
  723.6 38.1 %copy-start.65 = (f32[256]{0:T(256)S(1)}, f32[256]{0:T(256)}, u32[]{:S(2)}) copy-start(f32[256]{0:T(256)} %copy-done.64) | copy-start | bytes 3076
  723.6 38.1 %copy-start.75 = (f32[256]{0:T(256)S(1)}, f32[256]{0:T(256)}, u32[]{:S(2)}) copy-start(f32[256]{0:T(256)} %copy-done.73) | copy-start | bytes 3076
  723.6 60.4 %all-gather.31.cloned.1.call-start = ((), (), s32[]{:S(2)}) async-start(), calls=%async_computation.24 | async-start | bytes 1966080 | tf_op jit(solution)/shard_map/all_gather | solution.py:80
  764.4 69.9 %reduce-scatter.28.cloned.1.call-start = ((), (), s32[]{:S(2)}) async-start(), calls=%async_computation.25 | async-start | bytes 3932160 | tf_op jit(solution)/shard_map/reduce_scatter | solution.py:84
  784.0 7.9 copy-start.15
  796.3 38.0 %copy-start.53 = (f32[768]{0:T(1024)S(1)}, f32[768]{0:T(1024)}, u32[]{:S(2)}) copy-start(f32[768]{0:T(1024)} %copy-done.52) | copy-start | bytes 9220
  796.3 38.0 %copy-start.63 = (f32[256]{0:T(256)S(1)}, f32[256]{0:T(256)}, u32[]{:S(2)}) copy-start(f32[256]{0:T(256)} %copy-done.62) | copy-start | bytes 3076
  796.3 38.0 %copy-start.72 = (f32[256]{0:T(256)S(1)}, f32[256]{0:T(256)}, u32[]{:S(2)}) copy-start(f32[256]{0:T(256)} %copy-done.71) | copy-start | bytes 3076
  796.3 60.5 %all-gather.33.cloned.1.call-start = ((), (), s32[]{:S(2)}) async-start(), calls=%async_computation.26 | async-start | bytes 1966080 | tf_op jit(solution)/shard_map/all_gather | solution.py:80
  834.3 22.5 %copy-start.43 = (bf16[1,192,768]{2,1,0:T(8,128)(2,1)S(1)}, bf16[1,192,768]{2,1,0:T(8,128)(2,1)}, u32[]{:S(2)}) copy-start(bf16[1,192,768]{2,1,0:T(8,128)(2,1)} %copy.81) | copy-start | bytes 884740
  836.9 90.3 %reduce-scatter.30.cloned.1.call-start = ((), (), s32[]{:S(2)}) async-start(), calls=%async_computation.27 | async-start | bytes 3932160 | tf_op jit(solution)/shard_map/reduce_scatter | solution.py:84
  858.8 13.0 slice-start
  865.6 7.3 slice-start.2
  889.1 40.5 %copy-start.95 = (bf16[1,1024,768]{2,1,0:T(8,128)(2,1)S(1)}, bf16[1,1024,768]{2,1,0:T(8,128)(2,1)}, u32[]{:S(2)}) copy-start(bf16[1,1024,768]{2,1,0:T(8,128)(2,1)} %all-gather.27.cloned.1.call-done) | copy-start | bytes 4718596
  889.1 102.5 %all-gather.35.cloned.1.call-start = ((), (), s32[]{:S(2)}) async-start(), calls=%async_computation.28 | async-start | bytes 3932160 | tf_op jit(solution)/shard_map/all_gather | solution.py:353
  929.4 254.9 %all-reduce.4.cloned.1.call-start = ((), (), s32[]{:S(2)}) async-start(), calls=%async_computation.36 | async-start | bytes 9437184
  950.4 300.6 %reduce-scatter.36.cloned.1.call-start = ((), (), s32[]{:S(2)}) async-start(), calls=%async_computation.35 | async-start | bytes 1327104
  957.6 375.2 %reduce-scatter.34.cloned.1.call-start = ((), (), s32[]{:S(2)}) async-start(), calls=%async_computation.34 | async-start | bytes 3981312
  978.5 520.5 %reduce-scatter.32.cloned.1.call-start = ((), (), s32[]{:S(2)}) async-start(), calls=%async_computation.29 | async-start | bytes 10616832 | tf_op jit(solution)/shard_map/reduce_scatter | solution.py:346
  998.5 6.8 copy-start.79
  998.5 6.8 copy-start.82
  998.5 6.8 copy-start.81
  998.6 503.6 %all-to-all-start.1 = ((f32[1,1024,768]{2,0,1:T(1,128)}), f32[1,1024,768]{2,0,1:T(1,128)}, u32[]{:S(2)}, u32[]{:S(2)}) async-start(f32[1,1024,768]{2,0,1:T(1,128)} %copy.96), calls=%async_computation.9 | async-start | bytes 6291456 | tf_op jit(solution)/shard_map/all_to_all | solution.py:354
  1505.9 8.7 copy-start.1
  (72 other events, 217.7 us)
Sparse Core Ops, SparseCore 0:
  138.1 37.0 reduce-scatter.15
  263.6 36.3 reduce-scatter.17
  554.1 36.4 reduce-scatter.21
  597.1 19.6 all-gather.26
  629.2 37.9 reduce-scatter.23
  723.7 37.9 reduce-scatter.25
  837.1 19.6 all-gather.32
  889.2 37.9 reduce-scatter.29
Sparse Core Ops, SparseCore 1:
  141.2 50.8 all-gather.36
  194.1 18.0 all-gather.20
  215.1 41.5 all-gather.38
  302.8 19.5 all-gather.22
  392.7 35.5 reduce-scatter.19
  431.2 51.8 all-gather.40
  485.1 18.0 all-gather.24
  505.5 41.5 all-gather.42
  671.8 19.5 all-gather.28
  764.4 19.5 all-gather.30
  796.4 37.8 reduce-scatter.27
  929.4 28.3 all-gather.34
  961.3 222.9 all-reduce.3
  1187.7 63.3 reduce-scatter.35
  1254.7 78.0 reduce-scatter.33
  1336.3 162.6 reduce-scatter.31
where the time goes:
time: 1530 us; the launch traced here: 1520 us
  waiting for transfers between devices  979 us (64%)
  blocking collectives  205 us (13%)
  matrix products  142 us (9%)
  local copies, waits for them, and re-layouts  99.2 us (6%)
  other arithmetic  55.3 us (4%)
  starting transfers between devices  23.8 us (2%)
  between operations  18.7 us (1%)
    unnamed x27, waiting for transfers between devices  284 us
    reduce_scatter x1, waiting for transfers between devices, on_device(): lax.psum_scatter(stacked[1], 'dp', scatter_dimension=1, tiled=True)  164 us
    reduce_scatter x4, waiting for transfers between devices, gather_sums(): return lax.psum_scatter(values, 'tensor', scatter_dimension=1, tiled=True)  152 us
    reduce_scatter x4, waiting for transfers between devices, sum_rows(): return lax.psum_scatter(values, 'tensor', scatter_dimension=1, tiled=True)  141 us
    all_gather x2, blocking collectives, on_device(): lax.all_gather(output_weight[depth_index].astype(jnp.bfloat16), 'dp', axi...  90.7 us
    all_gather x4, waiting for transfers between devices, collect_rows(): return lax.all_gather(values, 'tensor', axis=1, tiled=True)  78 us
    all_gather x2, blocking collectives, on_device(): lax.all_gather(project_weight[depth_index].astype(jnp.bfloat16), 'dp', ax...  74 us
    all_gather x2, waiting for transfers between devices, on_device(): lax.all_gather(down_weight[depth_index].astype(jnp.bfloat16), 'dp', axis=...  73.3 us
  transfers between devices with their start and end apart: 26, of which 22 were waited for; matrix products, arithmetic and copies ran while one was open for 8% of the time, Pallas kernels for 0%

commit v1 on v0

v1 whole, which is shorter than its diff:
```python
import functools
import math

import jax
import jax.numpy as jnp
import numpy as np
from jax import lax
from jax.experimental import pallas as pl
from jax.experimental.pallas import tpu as pltpu
from jax.sharding import PartitionSpec as P

HD = 64
LAYERS = 2
epsilon = 1e-05
rotary_base = 1000.0
LOG2E = math.log2(math.e)
F32 = jnp.float32
BF16 = jnp.bfloat16
VMEM_LIMIT = 16 * 1024 * 1024
COST = 0.001


def sds(*shape, dtype=BF16):
    return jax.ShapeDtypeStruct(shape, dtype)


def call(kernel, outs, *operands, flops=0, trans=0, scalars=0, scratch=()):
    vmem = pl.BlockSpec(memory_space=pltpu.VMEM)
    smem = pl.BlockSpec(memory_space=pltpu.SMEM)
    moved = sum(a.size * a.dtype.itemsize for a in list(operands) + list(outs))
    return pl.pallas_call(
        kernel,
        in_specs=[smem] * scalars + [vmem] * (len(operands) - scalars),
        out_specs=[vmem] * len(outs),
        out_shape=list(outs),
        scratch_shapes=list(scratch),
        compiler_params=pltpu.CompilerParams(vmem_limit_bytes=VMEM_LIMIT),
        cost_estimate=pl.CostEstimate(
            flops=int(COST * flops),
            bytes_accessed=int(COST * moved),
            transcendentals=int(COST * trans),
        ),
    )(*operands)


def swap_core(value):
    return lax.ppermute(value, "tensor", [(i, i ^ 1) for i in range(lax.axis_size("tensor"))])


def swap_x(value):
    return lax.ppermute(value, "tensor", [(i, i ^ 2) for i in range(lax.axis_size("tensor"))])


def swap_dp(value, step):
    return lax.ppermute(value, "dp", [(i, i ^ step) for i in range(lax.axis_size("dp"))])


def place_kernel(index_ref, *refs):
    *pieces, whole_ref = refs
    rows = pieces[0].shape[0]
    for offset, piece in enumerate(pieces):
        start = pl.multiple_of((index_ref[0] ^ offset) * rows, rows)
        whole_ref[pl.ds(start, rows), :] = piece[...]


def gather_rows(shard):
    count = lax.axis_size("dp")
    rows, width = shard.shape
    if count != 8 or rows % 16:
        return lax.all_gather(shard, "dp", axis=0, tiled=True)
    index = lax.axis_index("dp").astype(jnp.int32).reshape(1)
    along = [swap_dp(shard, step) for step in (2, 4, 6)]
    near = swap_dp(shard, 1)
    across = [swap_dp(piece, 1) for piece in along]
    pieces = [shard, near, along[0], across[0], along[1], across[1], along[2], across[2]]
    return call(place_kernel, [sds(count * rows, width)], index, *pieces, scalars=1)[0]


def scatter_sum(kept, sent):
    count = lax.axis_size("dp")
    pair = (kept.astype(F32) + swap_dp(sent, 1).astype(F32)).astype(BF16)
    groups = [[i for i in range(count) if i % 2 == parity] for parity in (0, 1)]
    arrived = lax.all_to_all(pair, "dp", 0, 0, axis_index_groups=groups, tiled=True)
    return jnp.sum(arrived.astype(F32), axis=0)


def sum_everywhere(value):
    for step in (1, 2):
        value = value + lax.ppermute(value, "tensor", [(i, i ^ step) for i in range(4)])
    count = lax.axis_size("dp")
    step = 1
    while step < count:
        value = value + swap_dp(value, step)
        step *= 2
    return value


def dot_nt(left, right):
    return lax.dot_general(left, right, (((1,), (1,)), ((), ())), preferred_element_type=F32)


def dot_nn(left, right):
    return lax.dot_general(left, right, (((1,), (0,)), ((), ())), preferred_element_type=F32)


def dot_tn(left, right):
    return lax.dot_general(left, right, (((0,), (0,)), ((), ())), preferred_element_type=F32)


def swap_halves(values):
    width = values.shape[-1]
    lane = lax.broadcasted_iota(jnp.int32, values.shape, 1)
    return jnp.where(
        lane % HD < HD // 2,
        pltpu.roll(values, width - HD // 2, 1),
        pltpu.roll(values, HD // 2, 1),
    )


def widen(table, width):
    return jnp.concatenate([table] * (width // table.shape[1]), axis=1)


def qkv_kernel(*refs):
    *x_refs, w_ref, cos_ref, sin_ref, bias_ref, q_ref, k_ref, v_ref, kt_ref, vt_ref = refs
    inner = v_ref.shape[1]
    extra = q_ref.shape[1] - inner
    weight = w_ref[:, : 3 * inner]
    for step, x_ref in enumerate(x_refs):
        block = x_ref.shape[0]
        here = pl.ds(step * block, block)
        projected = dot_nn(x_ref[...], weight)
        pair = projected[:, : 2 * inner]
        turned = pair * widen(cos_ref[here, :], 2 * inner) + swap_halves(pair) * widen(
            sin_ref[here, :], 2 * inner
        )
        lane = lax.broadcasted_iota(jnp.int32, (block, extra), 1)
        queries = turned[:, :inner] * (1.0 / math.sqrt(HD))
        keys = turned[:, inner:]
        values = projected[:, 2 * inner :]
        one = jnp.where(lane == 0, 1.0, 0.0)
        mark = jnp.where(lane == 0, bias_ref[here, :extra], 0.0)
        q_ref[here, :] = jnp.concatenate([queries, one], axis=1).astype(BF16)
        k_ref[here, :] = jnp.concatenate([keys, mark], axis=1).astype(BF16)
        v_ref[here, :] = values.astype(BF16)
        kt_ref[:, here] = keys.T.astype(BF16)
        vt_ref[:, here] = values.T.astype(BF16)


def qkv_call(pieces, weight, tables, inner):
    rows = sum(p.shape[0] for p in pieces)
    width = weight.shape[0]
    return call(
        qkv_kernel,
        [sds(rows, inner + HD), sds(rows, inner + HD), sds(rows, inner)] + [sds(inner, rows)] * 2,
        *pieces, weight, *tables,
        flops=2 * rows * width * 3 * inner,
    )


def head_mask(shape, head, inner):
    lane = lax.broadcasted_iota(jnp.int32, shape, 1)
    return ((lane >= head * HD) & (lane < (head + 1) * HD)) | (lane >= inner)


def attend_kernel(chunk, q_ref, k_ref, vt_ref, w_ref, c_ref, lse_ref, theirs_ref, mine_ref):
    inner = c_ref.shape[1]
    weight = w_ref[:, 3 * inner :]
    half = c_ref.shape[0] // 2
    for part in (1, 0):
        queries = q_ref[pl.ds((2 * chunk + part) * half, half), :]
        columns, stats = [], []
        for head in range(inner // HD):
            masked = jnp.where(head_mask(queries.shape, head, inner), queries, 0)
            scores = dot_nt(k_ref[...], masked)
            shift = jnp.max(scores, axis=0, keepdims=True) * LOG2E
            exps = jnp.exp2(scores * LOG2E - shift)
            total = jnp.sum(exps, axis=0, keepdims=True)
            mixed = dot_nn(vt_ref[head * HD : (head + 1) * HD, :], exps.astype(BF16))
            columns.append(mixed * (1.0 / total))
            stats.append(shift + jnp.log2(total))
        context = jnp.concatenate(columns, axis=0).T.astype(BF16)
        here = pl.ds(part * half, half)
        c_ref[here, :] = context
        pad = lse_ref.shape[0] - len(stats)
        lse_ref[:, here] = jnp.concatenate(stats + [jnp.zeros((pad, half), F32)], axis=0)
        partial = dot_nt(context, weight)
        if part:
            theirs_ref[...] = partial.astype(BF16)
        else:
            mine_ref[...] = partial


def attend_call(chunk, chunks, queries, keys, values_t, weight):
    length, padded = queries.shape
    rows, inner, width = length // chunks, padded - HD, weight.shape[0]
    return call(
        functools.partial(attend_kernel, chunk),
        [
            sds(rows, inner), sds(8, rows, dtype=F32),
            sds(rows // 2, width), sds(rows // 2, width, dtype=F32),
        ],
        queries, keys, values_t, weight,
        flops=4 * rows * length * 256 * (inner // HD) + 2 * rows * inner * width,
        trans=rows * length * (inner // HD),
    )


def norm_kernel(base_ref, pair_ref, other_ref, gain_ref, shift_ref, sum_ref, out_ref, low_ref):
    values = base_ref[...].astype(F32) + (pair_ref[...] + other_ref[...].astype(F32))
    sum_ref[...] = values
    centred = values - jnp.mean(values, axis=-1, keepdims=True)
    scaled = lax.rsqrt(jnp.mean(centred * centred, axis=-1, keepdims=True) + epsilon)
    result = centred * scaled * gain_ref[...] + shift_ref[...]
    out_ref[...] = result
    low_ref[...] = result.astype(BF16)


def norm_call(base, pair, other, gain, shift):
    rows, width = pair.shape
    return call(
        norm_kernel,
        [sds(rows, width, dtype=F32), sds(rows, width, dtype=F32), sds(rows, width)],
        base, pair, other, gain, shift,
        flops=10 * rows * width,
    )


def norm_back_kernel(*refs):
    *in_refs, values_ref, gain_ref, out_ref, low_ref, vec_ref = refs
    incoming = in_refs[0][...].astype(F32)
    for ref in in_refs[1:]:
        incoming = incoming + ref[...].astype(F32)
    values = values_ref[...]
    centred = values - jnp.mean(values, axis=-1, keepdims=True)
    scaled = lax.rsqrt(jnp.mean(centred * centred, axis=-1, keepdims=True) + epsilon)
    normal = centred * scaled
    weighted = incoming * gain_ref[...]
    result = scaled * (
        weighted
        - jnp.mean(weighted, axis=-1, keepdims=True)
        - normal * jnp.mean(weighted * normal, axis=-1, keepdims=True)
    )
    out_ref[...] = result
    low_ref[...] = result.astype(BF16)
    vec_ref[0:1, :] = jnp.sum(incoming * normal, axis=0, keepdims=True)
    vec_ref[1:2, :] = jnp.sum(incoming, axis=0, keepdims=True)


def norm_back_call(incoming, values, gain):
    rows, width = values.shape
    return call(
        norm_back_kernel,
        [sds(rows, width, dtype=F32), sds(rows, width), sds(2, width, dtype=F32)],
        *incoming, values, gain,
        flops=16 * rows * width,
    )


def mlp_kernel(mine_in, theirs_in, w_ref, gu_ref, act_ref, theirs_ref, mine_ref):
    hidden = act_ref.shape[1]
    half = mine_in.shape[0]
    for part, x_ref in ((1, theirs_in), (0, mine_in)):
        here = pl.ds(part * half, half)
        rows = x_ref[...]
        gate = dot_nn(rows, w_ref[:, :hidden])
        up = dot_nn(rows, w_ref[:, hidden : 2 * hidden])
        active = (gate * jax.nn.sigmoid(gate) * up).astype(BF16)
        gu_ref[here, :hidden] = gate.astype(BF16)
        gu_ref[here, hidden:] = up.astype(BF16)
        act_ref[here, :] = active
        partial = dot_nt(active, w_ref[:, 2 * hidden :])
        if part:
            theirs_ref[...] = partial.astype(BF16)
        else:
            mine_ref[...] = partial


def mlp_call(mine, theirs, weight):
    half, width = mine.shape
    hidden = weight.shape[1] // 3
    return call(
        mlp_kernel,
        [
            sds(2 * half, 2 * hidden), sds(2 * half, hidden),
            sds(half, width), sds(half, width, dtype=F32),
        ],
        mine, theirs, weight,
        flops=4 * half * width * weight.shape[1],
        trans=2 * half * hidden,
    )


def mlp_back_kernel(mine_in, theirs_in, gu_ref, w_ref, dg_ref, theirs_ref, mine_ref):
    hidden = gu_ref.shape[1] // 2
    half = mine_in.shape[0]
    for part, x_ref in ((1, theirs_in), (0, mine_in)):
        here = pl.ds(part * half, half)
        active_grad = dot_nn(x_ref[...], w_ref[:, 2 * hidden :])
        gate = gu_ref[here, :hidden].astype(F32)
        up = gu_ref[here, hidden:].astype(F32)
        sigmoid = jax.nn.sigmoid(gate)
        gate_grad = (active_grad * up * sigmoid * (1.0 + gate * (1.0 - sigmoid))).astype(BF16)
        up_grad = (active_grad * gate * sigmoid).astype(BF16)
        dg_ref[here, :hidden] = gate_grad
        dg_ref[here, hidden:] = up_grad
        partial = dot_nt(gate_grad, w_ref[:, :hidden]) + dot_nt(
            up_grad, w_ref[:, hidden : 2 * hidden]
        )
        if part:
            theirs_ref[...] = partial.astype(BF16)
        else:
            mine_ref[...] = partial


def mlp_back_call(mine, theirs, gate_up, weight):
    half, width = mine.shape
    return call(
        mlp_back_kernel,
        [
            sds(*gate_up.shape), sds(half, width), sds(half, width, dtype=F32),
        ],
        mine, theirs, gate_up, weight,
        flops=4 * half * width * weight.shape[1],
        trans=2 * half * weight.shape[1] // 3,
    )


def context_back_kernel(mine_in, theirs_in, w_ref, dc_ref):
    inner = dc_ref.shape[1]
    half = mine_in.shape[0]
    weight = w_ref[:, 3 * inner :]
    dc_ref[:half, :] = dot_nn(mine_in[...], weight).astype(BF16)
    dc_ref[half:, :] = dot_nn(theirs_in[...], weight).astype(BF16)


def context_back_call(mine, theirs, weight):
    half, width = mine.shape
    inner = weight.shape[1] // 4
    return call(
        context_back_kernel, [sds(2 * half, inner)], mine, theirs, weight,
        flops=4 * half * width * inner,
    )[0]


def attend_back_kernel(
    q_ref, dc_ref, lse_ref, k_ref, v_ref, kt_ref, cosq_ref, sinq_ref, cos_ref, sin_ref,
    dp_ref, dk_ref, dv_ref,
):
    step = pl.program_id(0)
    inner = v_ref.shape[1]
    block, padded = q_ref.shape

    @pl.when(step == 0)
    def _():
        dk_ref[...] = jnp.zeros_like(dk_ref)
        dv_ref[...] = jnp.zeros_like(dv_ref)

    def turn_back(gradient, cosine, sine):
        cosine = widen(cosine, gradient.shape[1])
        sine = widen(sine, gradient.shape[1])
        return (gradient * cosine - swap_halves(gradient) * sine)[:, :inner]

    queries = q_ref[...]
    context_grad = dc_ref[...]
    columns = []
    for head in range(inner // HD):
        masked = jnp.where(head_mask(queries.shape, head, inner), queries, 0)
        masked_grad = jnp.where(head_mask(context_grad.shape, head, inner), context_grad, 0)
        scores = dot_nt(k_ref[...], masked)
        weights = jnp.exp2(scores * LOG2E - lse_ref[head : head + 1, :])
        weight_grad = dot_nt(v_ref[...], masked_grad)
        inner_sum = jnp.sum(weights * weight_grad, axis=0, keepdims=True)
        score_grad = (weights * (weight_grad - inner_sum)).astype(BF16)
        dk_ref[...] += dot_nn(score_grad, masked)
        dv_ref[...] += dot_nn(weights.astype(BF16), masked_grad)
        columns.append(dot_nn(kt_ref[head * HD : (head + 1) * HD, :], score_grad))
    columns.append(jnp.zeros((padded - inner, block), F32))
    query_grad = jnp.concatenate(columns, axis=0).T * (1.0 / math.sqrt(HD))
    here = pl.ds(pl.multiple_of(step * block, block), block)
    dp_ref[here, :inner] = turn_back(query_grad, cosq_ref[...], sinq_ref[...]).astype(BF16)

    @pl.when(step == pl.num_programs(0) - 1)
    def _():
        dp_ref[:, inner : 2 * inner] = turn_back(
            dk_ref[...], cos_ref[...], sin_ref[...]
        ).astype(BF16)
        dp_ref[:, 2 * inner :] = dv_ref[...].astype(BF16)


def attend_back_call(queries, context_grad, logsum, keys, values, keys_t, cosine, sine):
    rows, padded = queries.shape
    inner = padded - HD
    heads = inner // HD
    block = 256
    row_spec = lambda n: pl.BlockSpec((block, n), lambda i: (i, 0))
    whole = lambda a: pl.BlockSpec(a.shape, lambda i: (0, 0))
    return pl.pallas_call(
        attend_back_kernel,
        grid=(rows // block,),
        in_specs=[
            row_spec(padded), row_spec(inner), pl.BlockSpec((8, block), lambda i: (0, i)),
            whole(keys), whole(values), whole(keys_t), row_spec(128), row_spec(128),
            whole(cosine), whole(sine),
        ],
        out_specs=pl.BlockSpec((rows, 3 * inner), lambda i: (0, 0)),
        out_shape=sds(rows, 3 * inner),
        scratch_shapes=[pltpu.VMEM((rows, padded), F32), pltpu.VMEM((rows, inner), F32)],
        compiler_params=pltpu.CompilerParams(
            vmem_limit_bytes=VMEM_LIMIT, dimension_semantics=("arbitrary",)
        ),
        cost_estimate=pl.CostEstimate(
            flops=int(COST * 10 * rows * rows * 256 * heads),
            bytes_accessed=int(COST * 16 * rows * padded),
            transcendentals=int(COST * rows * rows * heads),
        ),
    )(queries, context_grad, logsum, keys, values, keys_t, cosine, sine, cosine, sine)


def input_back_kernel(chunk, dp_ref, w_ref, theirs_ref, mine_ref):
    half = mine_ref.shape[0]
    total = dp_ref.shape[1]
    weight = w_ref[:, :total]
    theirs_ref[...] = dot_nt(dp_ref[pl.ds((2 * chunk + 1) * half, half), :], weight).astype(BF16)
    mine_ref[...] = dot_nt(dp_ref[pl.ds(2 * chunk * half, half), :], weight)


def input_back_call(chunk, chunks, triple, weight):
    half, width = triple.shape[0] // (2 * chunks), weight.shape[0]
    return call(
        functools.partial(input_back_kernel, chunk),
        [sds(half, width), sds(half, width, dtype=F32)],
        triple, weight,
        flops=4 * half * triple.shape[1] * width,
    )


def input_last_kernel(index_ref, dp_ref, w_ref, *refs):
    *grad_refs, kept_ref, sent_ref = refs
    core, side = index_ref[0], index_ref[1]
    rows, total = dp_ref.shape
    quarter = rows // 4
    split = kept_ref.shape[1]
    weight = w_ref[:, :total]
    for step in range(4):
        chunk, part = step // 2, step % 2
        partial = dot_nt(dp_ref[pl.ds(step * quarter, quarter), :], weight)
        if not part:
            partial = partial + jnp.where(side == chunk, grad_refs[chunk][...], 0.0)
        start = pl.multiple_of((2 * chunk + (core ^ part)) * quarter, quarter)
        low, high = partial[:, :split], partial[:, split:]
        kept_ref[pl.ds(start, quarter), :] = jnp.where(core == 0, low, high)
        sent_ref[pl.ds(start, quarter), :] = jnp.where(core == 0, high, low).astype(BF16)


def input_last_call(index, triple, weight, grads):
    rows, width = triple.shape[0], weight.shape[0]
    return call(
        input_last_kernel,
        [sds(rows, width // 2, dtype=F32), sds(rows, width // 2)],
        index, triple, weight, *grads,
        flops=2 * rows * triple.shape[1] * width, scalars=1,
    )


def weight_kernel(counts, index_ref, *refs):
    *in_refs, kept_ref, sent_ref = refs
    parity = index_ref[0]
    blocks, rows, _ = kept_ref.shape
    wide = 4 * rows if blocks % 2 == 0 and (4 * rows) % 128 == 0 else 2 * blocks * rows
    column = 0
    lefts, rights = [], []
    for left_count, right_count in counts:
        lefts.append(in_refs[:left_count])
        rights.append(in_refs[left_count : left_count + right_count])
        in_refs = in_refs[left_count + right_count :]
    for left, right in zip(lefts, rights):
        width = right[0].shape[1]
        share = min(width, 768)
        ratio = len(left) // len(right)
        for first in range(0, 2 * blocks * rows, wide):
            for start in range(0, width, share):
                total = None
                for number, left_ref in enumerate(left):
                    size = left_ref.shape[0]
                    right_ref = right[number // ratio]
                    term = dot_tn(
                        left_ref[:, first : first + wide],
                        right_ref[
                            pl.ds((number % ratio) * size, size), start : start + share
                        ],
                    )
                    total = term if total is None else total + term
                for offset in range(0, wide, 2 * rows):
                    even = total[offset : offset + rows].astype(BF16)
                    odd = total[offset + rows : offset + 2 * rows].astype(BF16)
                    block = (first + offset) // (2 * rows)
                    where = pl.ds(column + start, share)
                    kept_ref[block, :, where] = jnp.where(parity == 0, even, odd)
                    sent_ref[block, :, where] = jnp.where(parity == 0, odd, even)
        column += width


def weight_call(parity, pairs, count):
    width = pairs[0][0][0].shape[1]
    total = sum(right[0].shape[1] for _, right in pairs)
    rows = sum(piece.shape[0] for piece in pairs[0][0])
    operands = [piece for left, right in pairs for piece in (*left, *right)]
    counts = tuple((len(left), len(right)) for left, right in pairs)
    shape = sds(count // 2, width // count, total)
    return call(
        functools.partial(weight_kernel, counts),
        [shape, shape],
        parity, *operands,
        flops=2 * rows * width * total, scalars=1,
    )


def finish_pair(mine, theirs):
    pair = mine + swap_core(theirs).astype(F32)
    return pair, swap_x(pair.astype(BF16))


def layer_forward(pieces, residual, first_weight, second_weight, gains, shifts, tables, inner):
    chunks = len(residual)
    queries, keys, values, keys_t, values_t = qkv_call(pieces, first_weight, tables, inner)
    context, logsum, first_sum, hidden, hidden_pieces = [], [], [], [], []
    partial = []
    for k in range(chunks):
        c, l, theirs, mine = attend_call(k, chunks, queries, keys, values_t, first_weight)
        context.append(c)
        logsum.append(l)
        partial.append((mine, theirs))
    for k in range(chunks):
        s, h, low = norm_call(
            residual[k], *finish_pair(*partial[k]), gains[0:1], shifts[0:1]
        )
        first_sum.append(s)
        hidden.append(h)
        hidden_pieces.append((low, swap_core(low)))
    gate_up, active, second_sum, result, result_pieces, partial = [], [], [], [], [], []
    for k in range(chunks):
        g, a, theirs, mine = mlp_call(*hidden_pieces[k], second_weight)
        gate_up.append(g)
        active.append(a)
        partial.append((mine, theirs))
    for k in range(chunks):
        s, y, low = norm_call(hidden[k], *finish_pair(*partial[k]), gains[1:2], shifts[1:2])
        second_sum.append(s)
        result.append(y)
        result_pieces.append(low)
    saved = (
        pieces, queries, keys, values, keys_t, context, jnp.concatenate(logsum, axis=1),
        first_sum, [p for pair in hidden_pieces for p in pair], gate_up, active, second_sum,
    )
    return result, result_pieces, saved


def layer_backward(incoming, saved, first_weight, second_weight, gains, tables, parity, count):
    (
        pieces, queries, keys, values, keys_t, context, logsum,
        first_sum, hidden_pieces, gate_up, active, second_sum,
    ) = saved
    chunks = len(incoming)
    second_grad, mixed, vectors_two = [], [], 0.0
    for k in range(chunks):
        grad, low, vector = norm_back_call(incoming[k], second_sum[k], gains[1:2])
        second_grad.append(grad)
        vectors_two = vectors_two + vector
        mixed.append((low, swap_core(low)))
    pair_grads, partial = [], []
    for k in range(chunks):
        dg, theirs, mine = mlp_back_call(*mixed[k], gate_up[k], second_weight)
        pair_grads.append(dg)
        partial.append((mine, theirs))
    first_grad, attended, context_grad, vectors_one = [], [], [], 0.0
    for k in range(chunks):
        incoming_k = (second_grad[k], *finish_pair(*partial[k]))
        grad, low, vector = norm_back_call(incoming_k, first_sum[k], gains[0:1])
        first_grad.append(grad)
        vectors_one = vectors_one + vector
        attended.append((low, swap_core(low)))
        context_grad.append(context_back_call(*attended[k], first_weight))
    flat = lambda pairs: [p for pair in pairs for p in pair]
    second_grads = weight_call(
        parity, [(hidden_pieces, pair_grads), (flat(mixed), active)], count
    )
    triple = attend_back_call(
        queries, jnp.concatenate(context_grad, axis=0), logsum, keys, values, keys_t, *tables[:2]
    )
    first_grads = weight_call(parity, [(pieces, [triple]), (flat(attended), context)], count)
    return first_grad, triple, first_grads, second_grads, (vectors_one, vectors_two)


def rotary_tables(length):
    half = HD // 2
    angles = np.arange(length, dtype=np.float64)[:, None] * np.exp(
        np.arange(half, dtype=np.float64)[None, :] * (-2.0 * math.log(rotary_base) / HD)
    )
    cosine, sine = np.cos(angles), np.sin(angles)
    return (
        np.concatenate([cosine] * 4, axis=1).astype(np.float32),
        np.concatenate([-sine, sine] * 2, axis=1).astype(np.float32),
    )


def deal(tokens, dealing_order, quarter_index):
    count, part, width = tokens.shape
    share = part // 4
    mine = lax.dynamic_slice_in_dim(tokens, quarter_index * share, share, 1)
    picked = jnp.take(mine, dealing_order, axis=0)
    arrived = lax.all_to_all(picked, "dp", split_axis=0, concat_axis=0, tiled=True)
    far = swap_x(arrived)
    pieces = jnp.stack([arrived, swap_core(arrived), far, swap_core(far)])
    blocks = [
        lax.dynamic_index_in_dim(pieces, quarter_index ^ slot, 0, keepdims=False)
        for slot in range(4)
    ]
    return jnp.stack(blocks, axis=1).reshape(count * part, width)


def on_device(
    tokens, dealing_order, lengths, project_weight, gate_up_weight, output_weight, down_weight,
    norm_gains, norm_biases, cotangent,
):
    dp_index = lax.axis_index("dp")
    tensor_index = lax.axis_index("tensor")
    core, side = tensor_index % 2, tensor_index // 2
    count, part, width = tokens.shape
    dp_count = lax.axis_size("dp")
    length = 4 * cotangent.shape[1]
    quarter = length // 4
    chunks = 2
    inner = output_weight.shape[1]
    hidden = down_weight.shape[1]
    rows_here = project_weight.shape[1]

    def shards(layer):
        first = jnp.concatenate(
            [project_weight[layer].reshape(rows_here, -1), output_weight[layer].T], axis=1
        ).astype(BF16)
        second = jnp.concatenate(
            [gate_up_weight[layer].reshape(rows_here, -1), down_weight[layer].T], axis=1
        ).astype(BF16)
        return first, second

    weights = [tuple(gather_rows(shard) for shard in shards(0))]
    for layer in range(1, LAYERS):
        weights.append(
            tuple(lax.all_gather(shard, "dp", axis=0, tiled=True) for shard in shards(layer))
        )

    length_now = jnp.take(lengths, jnp.take(dealing_order, dp_index))

    def local_order(rows):
        split = rows.reshape(chunks, 2, quarter, rows.shape[-1])
        return jnp.where(core == 0, split, split[:, ::-1])

    places = jnp.arange(length)[:, None]
    marks = jnp.where(places < length_now, 0.0, -1e30).astype(F32)
    tables = tuple(
        local_order(table).reshape(length, 128)
        for table in (*map(jnp.asarray, rotary_tables(length)), jnp.broadcast_to(marks, (length, 128)))
    )
    usable = [
        ((2 * k + core) * quarter + jnp.arange(quarter) < length_now)[:, None]
        for k in range(chunks)
    ]

    dealt = local_order(deal(tokens, dealing_order, tensor_index))
    pieces = [dealt[k, h] for k in range(chunks) for h in range(2)]
    current = pieces[::2]
    saved_all = []
    for layer in range(LAYERS):
        current, low, saved = layer_forward(
            pieces, current, *weights[layer], norm_gains[layer], norm_biases[layer], tables, inner
        )
        saved_all.append(saved)
        if layer < LAYERS - 1:
            pieces = [p for piece in low for p in (piece, swap_core(piece))]
    shown = jnp.where(side == 0, current[0], current[1])
    shown_usable = jnp.where(side == 0, usable[0], usable[1])
    layer_outputs = jnp.where(shown_usable, shown, 0.0)[None]

    own = cotangent[0]
    other = swap_x(own)
    seeds = [jnp.where(side == 0, own, other), jnp.where(side == 0, other, own)]
    incoming = [(jnp.where(usable[k], seeds[k], jnp.zeros_like(own)),) for k in range(chunks)]
    parity = (dp_index % 2).astype(jnp.int32).reshape(1)
    first_sets, second_sets, norm_sets = [], [], []
    for layer in reversed(range(LAYERS)):
        first_grad, triple, first_grads, second_grads, vectors = layer_backward(
            incoming, saved_all[layer], *weights[layer], norm_gains[layer], tables, parity, dp_count
        )
        if layer:
            partial = [input_back_call(k, chunks, triple, weights[layer][0]) for k in range(chunks)]
            incoming = [
                (first_grad[k], *finish_pair(partial[k][1], partial[k][0])) for k in range(chunks)
            ]
        first_sets.insert(0, scatter_sum(*first_grads))
        second_sets.insert(0, scatter_sum(*second_grads))
        norm_sets.insert(0, jnp.stack(vectors))
    norms_total = sum_everywhere(jnp.stack(norm_sets) * 0.5)

    where = jnp.stack([core, side]).astype(jnp.int32)
    kept, sent = input_last_call(where, triple, weights[0][0], first_grad)
    pair = (kept + swap_core(sent).astype(F32)).reshape(count, 2, part // 2, width // 2)
    mine = lax.dynamic_index_in_dim(pair, side, 1, keepdims=False)
    theirs = lax.dynamic_index_in_dim(pair, 1 - side, 1, keepdims=False).astype(BF16)
    total = (mine + swap_x(theirs).astype(F32)).astype(BF16)
    received = lax.all_to_all(total, "dp", split_axis=0, concat_axis=0, tiled=True)
    other = swap_x(received)
    half = jnp.where(
        side == 0,
        jnp.concatenate([received, other], axis=1),
        jnp.concatenate([other, received], axis=1),
    )
    other = swap_core(half)
    full = jnp.where(
        core == 0,
        jnp.concatenate([half, other], axis=2),
        jnp.concatenate([other, half], axis=2),
    )
    returned = jnp.take(full, jnp.argsort(dealing_order), axis=0).astype(F32)

    first_total, second_total = jnp.stack(first_sets), jnp.stack(second_sets)
    return (
        layer_outputs,
        returned,
        first_total[..., : 3 * inner].reshape(project_weight.shape),
        second_total[..., : 2 * hidden].reshape(gate_up_weight.shape),
        jnp.swapaxes(first_total[..., 3 * inner :], 1, 2),
        jnp.swapaxes(second_total[..., 2 * hidden :], 1, 2),
        norms_total[:, :, 0],
        norms_total[:, :, 1],
    )


def solution(mesh):
    placed = (
        P(None, "dp", None),
        P(),
        P(),
        P(None, "dp", None, "tensor"),
        P(None, "dp", None, "tensor"),
        P(None, "tensor", "dp"),
        P(None, "tensor", "dp"),
        P(),
        P(),
        P("dp", "tensor", None),
    )
    return jax.shard_map(
        on_device,
        mesh=mesh,
        in_specs=placed,
        out_specs=(
            P("dp", "tensor", None),
            P(None, "dp", None),
            P(None, "dp", None, "tensor"),
            P(None, "dp", None, "tensor"),
            P(None, "tensor", "dp"),
            P(None, "tensor", "dp"),
            P(),
            P(),
        ),
        check_vma=False,
    )
```

time: 1530 us -> 603 us (0.39)
  waiting for transfers between devices: 979 us -> 263 us
  blocking collectives: 205 us -> 0 us
  matrix products: 142 us -> 0 us
  Pallas kernels: 0 us -> 118 us
  starting transfers between devices: 23.8 us -> 87.5 us
  local copies, waits for them, and re-layouts: 99.2 us -> 64.7 us
    reduce_scatter x9 -> x0, waiting for transfers between devices: 457 us -> none  [the longest x1 164 us: on_device(): lax.psum_scatter(stacked[1], 'dp', scatter_dimension=1, tiled=True)]
    unnamed x27 -> x2, waiting for transfers between devices: 284 us -> 0.03 us
    ppermute x0 -> x73, waiting for transfers between devices: none -> 251 us  [the longest x21 144 us: swap_dp(): lax.ppermute(value, 'dp', [(i, i ^ step) for i in range(lax.axis_size('dp...]
    all_gather x12 -> x2, waiting for transfers between devices: 238 us -> 0.01 us  [on_device(): lax.all_gather(shard, 'dp', axis=0, tiled=True)]
    all_gather x4 -> x0, blocking collectives: 165 us -> none  [the longest x2 90.7 us: on_device(): lax.all_gather(output_weight[depth_index].astype(jnp.bfloat16), 'dp', axi...]
    dot_general x36 -> x0, matrix products: 142 us -> none  [the longest x8 31.6 us: contract_cols(): lax.dot_general(left, right, (((1,), (1,)), ((), ())), preferred_element_...]
    pallas_call x0 -> x45, Pallas kernels: none -> 118 us  [the longest x43 91.1 us: call(): pl.pallas_call(kernel, in_specs=[smem] * scalars + [vmem] * (len(operands...]
    ppermute x0 -> x73, starting transfers between devices: none -> 57 us  [the longest x21 30 us: swap_dp(): lax.ppermute(value, 'dp', [(i, i ^ step) for i in range(lax.axis_size('dp...]
  transfers between devices with their start and end apart: 26 -> 81, of which waited for: 22 -> 35; matrix products, arithmetic and copies ran while one was open for 8% -> 7% of each run, Pallas kernels for 0% -> 20%
where the time goes in v1:
time: 603 us; the launch traced here: 592 us
  waiting for transfers between devices  263 us (44%)
  Pallas kernels  118 us (20%)
  starting transfers between devices  87.5 us (15%)
  local copies, waits for them, and re-layouts  64.7 us (11%)
  other arithmetic  40 us (7%)
  between operations  18 us (3%)
    ppermute x21, waiting for transfers between devices, swap_dp(): lax.ppermute(value, 'dp', [(i, i ^ step) for i in range(lax.axis_size('dp...  144 us
    ppermute x18, waiting for transfers between devices, swap_x(): lax.ppermute(value, 'tensor', [(i, i ^ 2) for i in range(lax.axis_size('t...  101 us
    pallas_call x43, Pallas kernels, call(): pl.pallas_call(kernel, in_specs=[smem] * scalars + [vmem] * (len(operands...  91.1 us
    unnamed x347, local copies, waits for them, and re-layouts  55.5 us
    ppermute x21, starting transfers between devices, swap_dp(): lax.ppermute(value, 'dp', [(i, i ^ step) for i in range(lax.axis_size('dp...  30 us
    pallas_call x2, Pallas kernels, attend_back_call(): pl.pallas_call(attend_back_kernel, grid=(rows // block,), in_specs=[row_s...  27.3 us
    ppermute x18, starting transfers between devices, swap_x(): lax.ppermute(value, 'tensor', [(i, i ^ 2) for i in range(lax.axis_size('t...  21.2 us
    all_to_all x4, starting transfers between devices, scatter_sum(): lax.all_to_all(pair, 'dp', 0, 0, axis_index_groups=groups, tiled=True)  19.5 us
  transfers between devices with their start and end apart: 81, of which 35 were waited for; matrix products, arithmetic and copies ran while one was open for 7% of the time, Pallas kernels for 20%

profile of v1, /device:TPU:0, one launch (start us, length us, event | category | flops | bytes accessed | tf_op | source)
XLA Modules:
  0.0 591.8 jit_solution(5295365390485894099)
XLA Ops:
  12.2 7.3 %all-to-all-start = ((bf16[8,32,768]{2,1,0:T(8,128)(2,1)}), bf16[8,32,768]{2,1,0:T(8,128)(2,1)S(1)}, u32[]{:S(2)}, u32[]{:S(2)}) async-start(bf16[8,32,768]{2,1,0:T(8,128)(2,1)} %broadcast_select_fusion), calls=%async_computation | async-start | bytes 786432 | tf_op jit(solution)/shard_map/all_to_all | solution.py:612
  23.4 2.4 collective-permute-start.6
  28.4 10.1 %all-to-all-done = bf16[8,32,768]{2,1,0:T(8,128)(2,1)S(1)} async-done(((bf16[8,32,768]{2,1,0:T(8,128)(2,1)}), bf16[8,32,768]{2,1,0:T(8,128)(2,1)S(1)}, u32[]{:S(2)}, u32[]{:S(2)}) %all-to-all-start) | async-done | bytes 393248 | tf_op jit(solution)/shard_map/all_to_all | solution.py:612
  43.3 2.9 collective-permute-done.1
  50.3 7.3 %collective-permute-done.5.refs_3_ = bf16[96,768]{1,0:T(8,128)(2,1)S(1)} collective-permute-done((bf16[96,768]{1,0:T(8,128)(2,1)S(1)}, bf16[96,768]{1,0:T(8,128)(2,1)S(1)}, u32[]{:S(2)}, u32[]{:S(2)}) %collective-permute-start.5) | collective-permute-done | bytes 147488 | tf_op jit(solution)/shard_map/ppermute | solution.py:55
  57.6 4.5 collective-permute-done.7.refs_5_
  62.1 3.0 collective-permute-done.9.refs_7_
  67.7 2.2 shard_map.180
  69.9 4.7 shard_map.181
  74.8 5.0 shard_map.186
  81.0 3.3 collective-permute-start.16
  87.8 26.0 %collective-permute-done.14.refs_2_ = bf16[96,2304]{1,0:T(8,128)(2,1)S(1)} collective-permute-done((bf16[96,2304]{1,0:T(8,128)(2,1)S(1)}, bf16[96,2304]{1,0:T(8,128)(2,1)S(1)}, u32[]{:S(2)}, u32[]{:S(2)}) %collective-permute-start.14) | collective-permute-done | bytes 442400 | tf_op jit(solution)/shard_map/ppermute | solution.py:55
  115.9 14.3 %collective-permute-done.18.refs_6_ = bf16[96,2304]{1,0:T(8,128)(2,1)S(1)} collective-permute-done((bf16[96,2304]{1,0:T(8,128)(2,1)S(1)}, bf16[96,2304]{1,0:T(8,128)(2,1)S(1)}, u32[]{:S(2)}, u32[]{:S(2)}) %collective-permute-start.18) | collective-permute-done | bytes 442400 | tf_op jit(solution)/shard_map/ppermute | solution.py:55
  135.9 18.4 %collective-permute-done.15.refs_3_ = bf16[96,2304]{1,0:T(8,128)(2,1)S(1)} collective-permute-done((bf16[96,2304]{1,0:T(8,128)(2,1)S(1)}, bf16[96,2304]{1,0:T(8,128)(2,1)S(1)}, u32[]{:S(2)}, u32[]{:S(2)}) %collective-permute-start.15) | collective-permute-done | bytes 442400 | tf_op jit(solution)/shard_map/ppermute | solution.py:55
  154.3 10.5 %collective-permute-done.17.refs_5_ = bf16[96,2304]{1,0:T(8,128)(2,1)S(1)} collective-permute-done((bf16[96,2304]{1,0:T(8,128)(2,1)S(1)}, bf16[96,2304]{1,0:T(8,128)(2,1)S(1)}, u32[]{:S(2)}, u32[]{:S(2)}) %collective-permute-start.17) | collective-permute-done | bytes 442400 | tf_op jit(solution)/shard_map/ppermute | solution.py:55
  164.8 8.5 %collective-permute-done.19.refs_7_ = bf16[96,2304]{1,0:T(8,128)(2,1)S(1)} collective-permute-done((bf16[96,2304]{1,0:T(8,128)(2,1)S(1)}, bf16[96,2304]{1,0:T(8,128)(2,1)S(1)}, u32[]{:S(2)}, u32[]{:S(2)}) %collective-permute-start.19) | collective-permute-done | bytes 442400 | tf_op jit(solution)/shard_map/ppermute | solution.py:55
  173.5 2.1 shard_map.184
  176.6 2.1 shard_map.188
  182.3 9.1 %collective-permute-done.21.other_ref = bf16[256,768]{1,0:T(8,128)(2,1)S(1)} collective-permute-done((bf16[256,768]{1,0:T(8,128)(2,1)S(1)}, bf16[256,768]{1,0:T(8,128)(2,1)S(1)}, u32[]{:S(2)}, u32[]{:S(2)}) %collective-permute-start.21) | collective-permute-done | bytes 393248 | tf_op jit(solution)/shard_map/ppermute | solution.py:51
  194.3 4.7 collective-permute-done.27.other_ref
  208.3 3.6 shard_map.190
  211.9 4.9 shard_map.195
  217.5 4.7 shard_map.191
  225.7 9.2 %collective-permute-done.35.other_ref = bf16[256,768]{1,0:T(8,128)(2,1)S(1)} collective-permute-done((bf16[256,768]{1,0:T(8,128)(2,1)S(1)}, bf16[256,768]{1,0:T(8,128)(2,1)S(1)}, u32[]{:S(2)}, u32[]{:S(2)}) %collective-permute-start.35) | collective-permute-done | bytes 393248 | tf_op jit(solution)/shard_map/ppermute | solution.py:51
  236.1 6.6 %collective-permute-done.30.other_ref = bf16[256,768]{1,0:T(8,128)(2,1)S(1)} collective-permute-done((bf16[256,768]{1,0:T(8,128)(2,1)S(1)}, bf16[256,768]{1,0:T(8,128)(2,1)S(1)}, u32[]{:S(2)}, u32[]{:S(2)}) %collective-permute-start.30) | collective-permute-done | bytes 393248 | tf_op jit(solution)/shard_map/ppermute | solution.py:51
  250.4 2.6 shard_map.197
  259.9 3.3 shard_map.193
  269.0 8.0 %collective-permute-done.38.other_ref = bf16[256,768]{1,0:T(8,128)(2,1)S(1)} collective-permute-done((bf16[256,768]{1,0:T(8,128)(2,1)S(1)}, bf16[256,768]{1,0:T(8,128)(2,1)S(1)}, u32[]{:S(2)}, u32[]{:S(2)}) %collective-permute-start.38) | collective-permute-done | bytes 393248 | tf_op jit(solution)/shard_map/ppermute | solution.py:51
  279.6 5.4 collective-permute-done.33.other_ref
  286.7 2.5 shard_map.204
  291.0 2.6 shard_map.200
  296.6 9.2 %collective-permute-done.46.refs_2_ = bf16[256,768]{1,0:T(8,128)(2,1)S(1)} collective-permute-done((bf16[256,768]{1,0:T(8,128)(2,1)S(1)}, bf16[256,768]{1,0:T(8,128)(2,1)S(1)}, u32[]{:S(2)}, u32[]{:S(2)}) %collective-permute-start.46) | collective-permute-done | bytes 393248 | tf_op jit(solution)/shard_map/ppermute | solution.py:51
  307.8 6.0 %collective-permute-done.42.refs_2_ = bf16[256,768]{1,0:T(8,128)(2,1)S(1)} collective-permute-done((bf16[256,768]{1,0:T(8,128)(2,1)S(1)}, bf16[256,768]{1,0:T(8,128)(2,1)S(1)}, u32[]{:S(2)}, u32[]{:S(2)}) %collective-permute-start.42) | collective-permute-done | bytes 393248 | tf_op jit(solution)/shard_map/ppermute | solution.py:51
  328.5 6.3 %shard_map.223 = (bf16[4,96,2304]{2,1,0:T(8,128)(2,1)S(1)}, bf16[4,96,2304]{2,1,0:T(8,128)(2,1)}) custom-call(s32[1]{0:T(128)} %bitcast.46.index_ref, bf16[256,768]{1,0:T(8,128)(2,1)} %get-tuple-element.147.mine_in.refs_0_, bf16[256,768]{1,0:T(8,128)(2,1)} %collective-permute-done.31.theirs_in.refs_1_, bf16[256,768]{1,0:T(8,128)(2,1)S(1)} %copy-done.48, ...), custom_call_target="tpu_custom_call" | custom-call | flops 3623878 | bytes 11403 | tf_op jit(solution)/shard_map/pallas_call | solution.py:31
  339.9 13.7 %shard_map.207.dp_ref.refs_4_ = bf16[1024,576]{1,0:T(8,128)(2,1)S(1)} custom-call(bf16[1024,256]{1,0:T(8,128)(2,1)S(1)} %copy-done.27, bf16[1024,192]{1,0:T(8,128)(2,1)S(1)} %pad_maximum_fusion.3.dc_ref, f32[8,1024]{1,0:T(8,128)S(1)} %pad_maximum_fusion.10.lse_ref, bf16[1024,256]{1,0:T(8,128)(2,1)S(1)} %copy-done.29, bf16[1024,192]{1,0:T(8,128)(2,1)S(1)} %copy-done.128, ...), custom_call_target="tpu_custom_call" | custom-call | flops 8053063 | bytes 4194 | tf_op jit(solution)/shard_map/pallas_call | solution.py:398
  355.9 3.8 shard_map.221
  362.8 9.7 %collective-permute-done.55.refs_2_ = bf16[256,768]{1,0:T(8,128)(2,1)S(1)} collective-permute-done((bf16[256,768]{1,0:T(8,128)(2,1)S(1)}, bf16[256,768]{1,0:T(8,128)(2,1)S(1)}, u32[]{:S(2)}, u32[]{:S(2)}) %collective-permute-start.55) | collective-permute-done | bytes 393248 | tf_op jit(solution)/shard_map/ppermute | solution.py:51
  374.8 5.4 collective-permute-done.49.refs_2_
  383.1 5.6 collective-permute-done.65
  389.7 4.3 all-to-all-start.3
  395.4 4.4 shard_map.215
  401.0 4.5 shard_map.210
  407.9 3.1 add_convert_fusion
  411.1 5.2 all-to-all-start.5
  419.7 9.8 %collective-permute-done.58.refs_2_ = bf16[256,768]{1,0:T(8,128)(2,1)S(1)} collective-permute-done((bf16[256,768]{1,0:T(8,128)(2,1)S(1)}, bf16[256,768]{1,0:T(8,128)(2,1)S(1)}, u32[]{:S(2)}, u32[]{:S(2)}) %collective-permute-start.58) | collective-permute-done | bytes 393248 | tf_op jit(solution)/shard_map/ppermute | solution.py:51
  431.1 5.8 collective-permute-done.52.refs_2_
  441.9 13.6 %shard_map.218.dp_ref.refs_4_ = bf16[1024,576]{1,0:T(8,128)(2,1)S(1)} custom-call(bf16[1024,256]{1,0:T(8,128)(2,1)S(1)} %copy-done.23, bf16[1024,192]{1,0:T(8,128)(2,1)S(1)} %pad_maximum_fusion.4.dc_ref, f32[8,1024]{1,0:T(8,128)S(1)} %pad_maximum_fusion.11.lse_ref, bf16[1024,256]{1,0:T(8,128)(2,1)S(1)} %copy-done.25, bf16[1024,192]{1,0:T(8,128)(2,1)S(1)} %copy-done.126, ...), custom_call_target="tpu_custom_call" | custom-call | flops 8053063 | bytes 4194 | tf_op jit(solution)/shard_map/pallas_call | solution.py:398
  459.1 6.6 %shard_map.222 = (bf16[4,96,2304]{2,1,0:T(8,128)(2,1)S(1)}, bf16[4,96,2304]{2,1,0:T(8,128)(2,1)}) custom-call(s32[1]{0:T(128)} %bitcast.46.index_ref, bf16[256,768]{1,0:T(8,128)(2,1)S(1)} %copy-done.39, bf16[256,768]{1,0:T(8,128)(2,1)S(1)} %copy-done.41, bf16[256,768]{1,0:T(8,128)(2,1)S(1)} %copy-done.43, bf16[256,768]{1,0:T(8,128)(2,1)S(1)} %copy-done.45, ...), custom_call_target="tpu_custom_call" | custom-call | flops 3623878 | bytes 11403 | tf_op jit(solution)/shard_map/pallas_call | solution.py:31
  466.4 2.9 shard_map.219
  470.5 3.2 collective-permute-done.64
  474.6 4.8 all-to-all-start.2
  482.5 8.9 %collective-permute-done.61 = bf16[8,64,384]{2,1,0:T(8,128)(2,1)S(1)} collective-permute-done((bf16[8,64,384]{2,1,0:T(8,128)(2,1)S(1)}, bf16[8,64,384]{2,1,0:T(8,128)(2,1)S(1)}, u32[]{:S(2)}, u32[]{:S(2)}) %collective-permute-start.61) | collective-permute-done | bytes 393248 | tf_op jit(solution)/shard_map/ppermute | solution.py:51
  492.3 2.6 all-to-all-done.2
  494.9 3.6 all-to-all-start.1
  498.5 16.4 %collective-permute-done.66 = bf16[4,96,2304]{2,1,0:T(8,128)(2,1)} collective-permute-done((bf16[4,96,2304]{2,1,0:T(8,128)(2,1)}, bf16[4,96,2304]{2,1,0:T(8,128)(2,1)}, u32[]{:S(2)}, u32[]{:S(2)}) %collective-permute-start.66) | collective-permute-done | bytes 1769504 | tf_op jit(solution)/shard_map/ppermute | solution.py:55
  514.9 3.1 add_convert_fusion.1
  518.0 5.2 all-to-all-start.4
  524.4 2.8 collective-permute-done.69
  528.7 2.4 collective-permute-done.70
  535.2 16.6 %collective-permute-done.71 = f32[2,2,2,768]{3,2,1,0:T(2,128)S(1)} collective-permute-done((f32[2,2,2,768]{3,2,1,0:T(2,128)S(1)}, f32[2,2,2,768]{3,2,1,0:T(2,128)S(1)}, u32[]{:S(2)}, u32[]{:S(2)}) %collective-permute-start.71) | collective-permute-done | bytes 24608 | tf_op jit(solution)/shard_map/ppermute | solution.py:55
  551.9 4.7 collective-permute-start.72
  557.7 7.2 %collective-permute-done.72 = f32[2,2,2,768]{3,2,1,0:T(2,128)S(1)} collective-permute-done((f32[2,2,2,768]{3,2,1,0:T(2,128)S(1)}, f32[2,2,2,768]{3,2,1,0:T(2,128)S(1)}, u32[]{:S(2)}, u32[]{:S(2)}) %collective-permute-start.72) | collective-permute-done | bytes 24608 | tf_op jit(solution)/shard_map/ppermute | solution.py:55
  570.8 2.9 maximum_select_fusion
  581.6 3.0 reshape.110
  (587 shorter events, 164.9 us)
Async XLA Ops:
  7.2 194.6 %all-gather.3.cloned.1.call-start = ((), (), s32[]{:S(2)}) async-start(), calls=%async_computation.6 | async-start | bytes 1327104 | tf_op jit(solution)/shard_map/all_gather | solution.py:650
  12.2 26.3 %all-to-all-start = ((bf16[8,32,768]{2,1,0:T(8,128)(2,1)}), bf16[8,32,768]{2,1,0:T(8,128)(2,1)S(1)}, u32[]{:S(2)}, u32[]{:S(2)}) async-start(bf16[8,32,768]{2,1,0:T(8,128)(2,1)} %broadcast_select_fusion), calls=%async_computation | async-start | bytes 786432 | tf_op jit(solution)/shard_map/all_to_all | solution.py:612
  19.4 226.9 %all-gather.5.cloned.1.call-start = ((), (), s32[]{:S(2)}) async-start(), calls=%async_computation.7 | async-start | bytes 3981312 | tf_op jit(solution)/shard_map/all_gather | solution.py:650
  19.9 23.3 %collective-permute-start.3 = (bf16[96,768]{1,0:T(8,128)(2,1)S(1)}, bf16[96,768]{1,0:T(8,128)(2,1)S(1)}, u32[]{:S(2)}, u32[]{:S(2)}) collective-permute-start(bf16[96,768]{1,0:T(8,128)(2,1)S(1)} %pad_maximum_fusion.8.refs_0_), channel_id=1, source_target_pairs={{0,4},{4,0},{8,12},{12,8},{16,20},{20,16},{24,28},{28,24},{1,5},{5... | collective-permute-start | bytes 442376 | tf_op jit(solution)/shard_map/ppermute | solution.py:55
  22.0 25.7 %collective-permute-start.4 = (bf16[96,768]{1,0:T(8,128)(2,1)S(1)}, bf16[96,768]{1,0:T(8,128)(2,1)S(1)}, u32[]{:S(2)}, u32[]{:S(2)}) collective-permute-start(bf16[96,768]{1,0:T(8,128)(2,1)S(1)} %pad_maximum_fusion.8.refs_0_), channel_id=1, source_target_pairs={{0,8},{4,12},{8,0},{12,4},{16,24},{20,28},{24,16},{28,20},{1,9},{5... | collective-permute-start | bytes 442376 | tf_op jit(solution)/shard_map/ppermute | solution.py:55
  23.4 24.8 %collective-permute-start.6 = (bf16[96,768]{1,0:T(8,128)(2,1)S(1)}, bf16[96,768]{1,0:T(8,128)(2,1)S(1)}, u32[]{:S(2)}, u32[]{:S(2)}) collective-permute-start(bf16[96,768]{1,0:T(8,128)(2,1)S(1)} %pad_maximum_fusion.8.refs_0_), channel_id=1, source_target_pairs={{0,16},{4,20},{8,24},{12,28},{16,0},{20,4},{24,8},{28,12},{1,17},{... | collective-permute-start | bytes 442376 | tf_op jit(solution)/shard_map/ppermute | solution.py:55
  25.8 24.0 %collective-permute-start.8 = (bf16[96,768]{1,0:T(8,128)(2,1)S(1)}, bf16[96,768]{1,0:T(8,128)(2,1)S(1)}, u32[]{:S(2)}, u32[]{:S(2)}) collective-permute-start(bf16[96,768]{1,0:T(8,128)(2,1)S(1)} %pad_maximum_fusion.8.refs_0_), channel_id=1, source_target_pairs={{0,24},{4,28},{8,16},{12,20},{16,8},{20,12},{24,0},{28,4},{1,25},{... | collective-permute-start | bytes 442376 | tf_op jit(solution)/shard_map/ppermute | solution.py:55
  38.4 7.8 %collective-permute-start.1 = (bf16[8,32,768]{2,1,0:T(8,128)(2,1)S(1)}, bf16[8,32,768]{2,1,0:T(8,128)(2,1)S(1)}, u32[]{:S(2)}, u32[]{:S(2)}) collective-permute-start(bf16[8,32,768]{2,1,0:T(8,128)(2,1)S(1)} %all-to-all-done), channel_id=1, source_target_pairs={{0,2},{1,3},{2,0},{3,1},{4,6},{5,7},{6,4},{7,5},{8,10},{9,11},{10,... | collective-permute-start | bytes 1179656 | tf_op jit(solution)/shard_map/ppermute | solution.py:51
  43.2 21.9 %collective-permute-start = (bf16[8,32,768]{2,1,0:T(8,128)(2,1)S(1)}, bf16[8,32,768]{2,1,0:T(8,128)(2,1)}, u32[]{:S(2)}, u32[]{:S(2)}) collective-permute-start(bf16[8,32,768]{2,1,0:T(8,128)(2,1)S(1)} %all-to-all-done), channel_id=1, source_target_pairs={{0,1},{1,0},{2,3},{3,2},{4,5},{5,4},{6,7},{7,6},{8,9},{9,8},{10,11... | collective-permute-start | bytes 1179656 | tf_op jit(solution)/shard_map/ppermute | solution.py:47
  46.2 18.9 %collective-permute-start.2 = (bf16[8,32,768]{2,1,0:T(8,128)(2,1)S(1)}, bf16[8,32,768]{2,1,0:T(8,128)(2,1)}, u32[]{:S(2)}, u32[]{:S(2)}) collective-permute-start(bf16[8,32,768]{2,1,0:T(8,128)(2,1)S(1)} %collective-permute-done.1), channel_id=1, source_target_pairs={{0,1},{1,0},{2,3},{3,2},{4,5},{5,4},{6,7},{7,6},{8,9},{9,8},{10,11... | collective-permute-start | bytes 1179656 | tf_op jit(solution)/shard_map/ppermute | solution.py:47
  47.7 9.9 %collective-permute-start.5 = (bf16[96,768]{1,0:T(8,128)(2,1)S(1)}, bf16[96,768]{1,0:T(8,128)(2,1)S(1)}, u32[]{:S(2)}, u32[]{:S(2)}) collective-permute-start(bf16[96,768]{1,0:T(8,128)(2,1)S(1)} %collective-permute-done.4.refs_2_), channel_id=1, source_target_pairs={{0,4},{4,0},{8,12},{12,8},{16,20},{20,16},{24,28},{28,24},{1,5},{5... | collective-permute-start | bytes 442376 | tf_op jit(solution)/shard_map/ppermute | solution.py:55
  48.2 13.8 %collective-permute-start.7 = (bf16[96,768]{1,0:T(8,128)(2,1)S(1)}, bf16[96,768]{1,0:T(8,128)(2,1)S(1)}, u32[]{:S(2)}, u32[]{:S(2)}) collective-permute-start(bf16[96,768]{1,0:T(8,128)(2,1)S(1)} %collective-permute-done.6.refs_4_), channel_id=1, source_target_pairs={{0,4},{4,0},{8,12},{12,8},{16,20},{20,16},{24,28},{28,24},{1,5},{5... | collective-permute-start | bytes 442376 | tf_op jit(solution)/shard_map/ppermute | solution.py:55
  49.8 15.2 %collective-permute-start.9 = (bf16[96,768]{1,0:T(8,128)(2,1)S(1)}, bf16[96,768]{1,0:T(8,128)(2,1)S(1)}, u32[]{:S(2)}, u32[]{:S(2)}) collective-permute-start(bf16[96,768]{1,0:T(8,128)(2,1)S(1)} %collective-permute-done.8.refs_6_), channel_id=1, source_target_pairs={{0,4},{4,0},{8,12},{12,8},{16,20},{20,16},{24,28},{28,24},{1,5},{5... | collective-permute-start | bytes 442376 | tf_op jit(solution)/shard_map/ppermute | solution.py:55
  74.6 10.8 %collective-permute-start.10 = (bf16[256,768]{1,0:T(8,128)(2,1)S(1)}, bf16[256,768]{1,0:T(8,128)(2,1)S(1)}, u32[]{:S(2)}, u32[]{:S(2)}) collective-permute-start(bf16[256,768]{1,0:T(8,128)(2,1)S(1)} %get-tuple-element.127), channel_id=1, source_target_pairs={{0,1},{1,0},{2,3},{3,2},{4,5},{5,4},{6,7},{7,6},{8,9},{9,8},{10,11... | collective-permute-start | bytes 1179656 | tf_op jit(solution)/shard_map/ppermute | solution.py:47
  80.9 32.9 %collective-permute-start.14 = (bf16[96,2304]{1,0:T(8,128)(2,1)S(1)}, bf16[96,2304]{1,0:T(8,128)(2,1)S(1)}, u32[]{:S(2)}, u32[]{:S(2)}) collective-permute-start(bf16[96,2304]{1,0:T(8,128)(2,1)S(1)} %pad_maximum_fusion.5.refs_0_), channel_id=1, source_target_pairs={{0,8},{4,12},{8,0},{12,4},{16,24},{20,28},{24,16},{28,20},{1,9},{5... | collective-permute-start | bytes 1327112 | tf_op jit(solution)/shard_map/ppermute | solution.py:55
  81.0 34.3 %collective-permute-start.16 = (bf16[96,2304]{1,0:T(8,128)(2,1)S(1)}, bf16[96,2304]{1,0:T(8,128)(2,1)S(1)}, u32[]{:S(2)}, u32[]{:S(2)}) collective-permute-start(bf16[96,2304]{1,0:T(8,128)(2,1)S(1)} %pad_maximum_fusion.5.refs_0_), channel_id=1, source_target_pairs={{0,16},{4,20},{8,24},{12,28},{16,0},{20,4},{24,8},{28,12},{1,17},{... | collective-permute-start | bytes 1327112 | tf_op jit(solution)/shard_map/ppermute | solution.py:55
  84.4 45.9 %collective-permute-start.18 = (bf16[96,2304]{1,0:T(8,128)(2,1)S(1)}, bf16[96,2304]{1,0:T(8,128)(2,1)S(1)}, u32[]{:S(2)}, u32[]{:S(2)}) collective-permute-start(bf16[96,2304]{1,0:T(8,128)(2,1)S(1)} %pad_maximum_fusion.5.refs_0_), channel_id=1, source_target_pairs={{0,24},{4,28},{8,16},{12,20},{16,8},{20,12},{24,0},{28,4},{1,25},{... | collective-permute-start | bytes 1327112 | tf_op jit(solution)/shard_map/ppermute | solution.py:55
  85.5 46.2 %collective-permute-start.11 = (bf16[256,768]{1,0:T(8,128)(2,1)S(1)}, bf16[256,768]{1,0:T(8,128)(2,1)S(1)}, u32[]{:S(2)}, u32[]{:S(2)}) collective-permute-start(bf16[256,768]{1,0:T(8,128)(2,1)S(1)} %get-tuple-element.305), channel_id=1, source_target_pairs={{0,2},{1,3},{2,0},{3,1},{4,6},{5,7},{6,4},{7,5},{8,10},{9,11},{10,... | collective-permute-start | bytes 1179656 | tf_op jit(solution)/shard_map/ppermute | solution.py:51
  87.2 47.0 %collective-permute-start.24 = (bf16[256,768]{1,0:T(8,128)(2,1)S(1)}, bf16[256,768]{1,0:T(8,128)(2,1)S(1)}, u32[]{:S(2)}, u32[]{:S(2)}) collective-permute-start(bf16[256,768]{1,0:T(8,128)(2,1)S(1)} %get-tuple-element.301), channel_id=1, source_target_pairs={{0,2},{1,3},{2,0},{3,1},{4,6},{5,7},{6,4},{7,5},{8,10},{9,11},{10,... | collective-permute-start | bytes 1179656 | tf_op jit(solution)/shard_map/ppermute | solution.py:51
  113.8 21.6 %collective-permute-start.13 = (bf16[96,2304]{1,0:T(8,128)(2,1)S(1)}, bf16[96,2304]{1,0:T(8,128)(2,1)S(1)}, u32[]{:S(2)}, u32[]{:S(2)}) collective-permute-start(bf16[96,2304]{1,0:T(8,128)(2,1)S(1)} %pad_maximum_fusion.5.refs_0_), channel_id=1, source_target_pairs={{0,4},{4,0},{8,12},{12,8},{16,20},{20,16},{24,28},{28,24},{1,5},{5... | collective-permute-start | bytes 1327112 | tf_op jit(solution)/shard_map/ppermute | solution.py:55
  115.3 39.0 %collective-permute-start.15 = (bf16[96,2304]{1,0:T(8,128)(2,1)S(1)}, bf16[96,2304]{1,0:T(8,128)(2,1)S(1)}, u32[]{:S(2)}, u32[]{:S(2)}) collective-permute-start(bf16[96,2304]{1,0:T(8,128)(2,1)S(1)} %collective-permute-done.14.refs_2_), channel_id=1, source_target_pairs={{0,4},{4,0},{8,12},{12,8},{16,20},{20,16},{24,28},{28,24},{1,5},{5... | collective-permute-start | bytes 1327112 | tf_op jit(solution)/shard_map/ppermute | solution.py:55
  130.2 34.6 %collective-permute-start.17 = (bf16[96,2304]{1,0:T(8,128)(2,1)S(1)}, bf16[96,2304]{1,0:T(8,128)(2,1)S(1)}, u32[]{:S(2)}, u32[]{:S(2)}) collective-permute-start(bf16[96,2304]{1,0:T(8,128)(2,1)S(1)} %collective-permute-done.16.refs_4_), channel_id=1, source_target_pairs={{0,4},{4,0},{8,12},{12,8},{16,20},{20,16},{24,28},{28,24},{1,5},{5... | collective-permute-start | bytes 1327112 | tf_op jit(solution)/shard_map/ppermute | solution.py:55
  131.7 41.6 %collective-permute-start.19 = (bf16[96,2304]{1,0:T(8,128)(2,1)S(1)}, bf16[96,2304]{1,0:T(8,128)(2,1)S(1)}, u32[]{:S(2)}, u32[]{:S(2)}) collective-permute-start(bf16[96,2304]{1,0:T(8,128)(2,1)S(1)} %collective-permute-done.18.refs_6_), channel_id=1, source_target_pairs={{0,4},{4,0},{8,12},{12,8},{16,20},{20,16},{24,28},{28,24},{1,5},{5... | collective-permute-start | bytes 1327112 | tf_op jit(solution)/shard_map/ppermute | solution.py:55
  134.2 39.3 %collective-permute-start.12 = (bf16[256,768]{1,0:T(8,128)(2,1)S(1)}, bf16[256,768]{1,0:T(8,128)(2,1)S(1)}, u32[]{:S(2)}, u32[]{:S(2)}) collective-permute-start(bf16[256,768]{1,0:T(8,128)(2,1)S(1)} %get-tuple-element.129.mine_in.refs_0_), channel_id=1, source_target_pairs={{0,1},{1,0},{2,3},{3,2},{4,5},{5,4},{6,7},{7,6},{8,9},{9,8},{10,11... | collective-permute-start | bytes 1179656 | tf_op jit(solution)/shard_map/ppermute | solution.py:47
  135.4 41.1 %collective-permute-start.25 = (bf16[256,768]{1,0:T(8,128)(2,1)S(1)}, bf16[256,768]{1,0:T(8,128)(2,1)S(1)}, u32[]{:S(2)}, u32[]{:S(2)}) collective-permute-start(bf16[256,768]{1,0:T(8,128)(2,1)S(1)} %get-tuple-element.137.mine_in.refs_2_), channel_id=1, source_target_pairs={{0,1},{1,0},{2,3},{3,2},{4,5},{5,4},{6,7},{7,6},{8,9},{9,8},{10,11... | collective-permute-start | bytes 1179656 | tf_op jit(solution)/shard_map/ppermute | solution.py:47
  179.4 12.0 %collective-permute-start.21 = (bf16[256,768]{1,0:T(8,128)(2,1)S(1)}, bf16[256,768]{1,0:T(8,128)(2,1)S(1)}, u32[]{:S(2)}, u32[]{:S(2)}) collective-permute-start(bf16[256,768]{1,0:T(8,128)(2,1)S(1)} %get-tuple-element.303), channel_id=1, source_target_pairs={{0,2},{1,3},{2,0},{3,1},{4,6},{5,7},{6,4},{7,5},{8,10},{9,11},{10,... | collective-permute-start | bytes 1179656 | tf_op jit(solution)/shard_map/ppermute | solution.py:51
  181.1 17.9 %collective-permute-start.27 = (bf16[256,768]{1,0:T(8,128)(2,1)S(1)}, bf16[256,768]{1,0:T(8,128)(2,1)S(1)}, u32[]{:S(2)}, u32[]{:S(2)}) collective-permute-start(bf16[256,768]{1,0:T(8,128)(2,1)S(1)} %get-tuple-element.299), channel_id=1, source_target_pairs={{0,2},{1,3},{2,0},{3,1},{4,6},{5,7},{6,4},{7,5},{8,10},{9,11},{10,... | collective-permute-start | bytes 1179656 | tf_op jit(solution)/shard_map/ppermute | solution.py:51
  194.3 7.5 %collective-permute-start.22 = (bf16[256,768]{1,0:T(8,128)(2,1)}, bf16[256,768]{1,0:T(8,128)(2,1)}, u32[]{:S(2)}, u32[]{:S(2)}) collective-permute-start(bf16[256,768]{1,0:T(8,128)(2,1)} %get-tuple-element.133.refs_0_), channel_id=1, source_target_pairs={{0,1},{1,0},{2,3},{3,2},{4,5},{5,4},{6,7},{7,6},{8,9},{9,8},{10,11... | collective-permute-start | bytes 1179656 | tf_op jit(solution)/shard_map/ppermute | solution.py:47
  222.9 11.9 %collective-permute-start.35 = (bf16[256,768]{1,0:T(8,128)(2,1)S(1)}, bf16[256,768]{1,0:T(8,128)(2,1)S(1)}, u32[]{:S(2)}, u32[]{:S(2)}) collective-permute-start(bf16[256,768]{1,0:T(8,128)(2,1)S(1)} %get-tuple-element.293), channel_id=1, source_target_pairs={{0,2},{1,3},{2,0},{3,1},{4,6},{5,7},{6,4},{7,5},{8,10},{9,11},{10,... | collective-permute-start | bytes 1179656 | tf_op jit(solution)/shard_map/ppermute | solution.py:51
  224.6 18.2 %collective-permute-start.30 = (bf16[256,768]{1,0:T(8,128)(2,1)S(1)}, bf16[256,768]{1,0:T(8,128)(2,1)S(1)}, u32[]{:S(2)}, u32[]{:S(2)}) collective-permute-start(bf16[256,768]{1,0:T(8,128)(2,1)S(1)} %get-tuple-element.297), channel_id=1, source_target_pairs={{0,2},{1,3},{2,0},{3,1},{4,6},{5,7},{6,4},{7,5},{8,10},{9,11},{10,... | collective-permute-start | bytes 1179656 | tf_op jit(solution)/shard_map/ppermute | solution.py:51
  236.1 9.5 %collective-permute-start.36 = (bf16[256,768]{1,0:T(8,128)(2,1)S(1)}, bf16[256,768]{1,0:T(8,128)(2,1)S(1)}, u32[]{:S(2)}, u32[]{:S(2)}) collective-permute-start(bf16[256,768]{1,0:T(8,128)(2,1)S(1)} %get-tuple-element.155.mine_in.refs_2_), channel_id=1, source_target_pairs={{0,1},{1,0},{2,3},{3,2},{4,5},{5,4},{6,7},{7,6},{8,9},{9,8},{10,11... | collective-permute-start | bytes 1179656 | tf_op jit(solution)/shard_map/ppermute | solution.py:47
  245.6 12.3 %collective-permute-start.31 = (bf16[256,768]{1,0:T(8,128)(2,1)}, bf16[256,768]{1,0:T(8,128)(2,1)}, u32[]{:S(2)}, u32[]{:S(2)}) collective-permute-start(bf16[256,768]{1,0:T(8,128)(2,1)} %get-tuple-element.147.mine_in.refs_0_), channel_id=1, source_target_pairs={{0,1},{1,0},{2,3},{3,2},{4,5},{5,4},{6,7},{7,6},{8,9},{9,8},{10,11... | collective-permute-start | bytes 1179656 | tf_op jit(solution)/shard_map/ppermute | solution.py:47
  255.9 8.0 %collective-permute-start.37 = (bf16[256,768]{1,0:T(8,128)(2,1)}, bf16[256,768]{1,0:T(8,128)(2,1)}, u32[]{:S(2)}, u32[]{:S(2)}) collective-permute-start(bf16[256,768]{1,0:T(8,128)(2,1)} %get-tuple-element.157), channel_id=1, source_target_pairs={{0,1},{1,0},{2,3},{3,2},{4,5},{5,4},{6,7},{7,6},{8,9},{9,8},{10,11... | collective-permute-start | bytes 1179656 | tf_op jit(solution)/shard_map/ppermute | solution.py:47
  256.4 11.3 %collective-permute-start.39 = (bf16[256,768]{1,0:T(8,128)(2,1)}, bf16[256,768]{1,0:T(8,128)(2,1)}, u32[]{:S(2)}, u32[]{:S(2)}) collective-permute-start(bf16[256,768]{1,0:T(8,128)(2,1)} %bitcast.42), channel_id=1, source_target_pairs={{0,2},{1,3},{2,0},{3,1},{4,6},{5,7},{6,4},{7,5},{8,10},{9,11},{10,... | collective-permute-start | bytes 1179656 | tf_op jit(solution)/shard_map/ppermute | solution.py:51
  265.0 12.0 %collective-permute-start.38 = (bf16[256,768]{1,0:T(8,128)(2,1)S(1)}, bf16[256,768]{1,0:T(8,128)(2,1)S(1)}, u32[]{:S(2)}, u32[]{:S(2)}) collective-permute-start(bf16[256,768]{1,0:T(8,128)(2,1)S(1)} %get-tuple-element.291), channel_id=1, source_target_pairs={{0,2},{1,3},{2,0},{3,1},{4,6},{5,7},{6,4},{7,5},{8,10},{9,11},{10,... | collective-permute-start | bytes 1179656 | tf_op jit(solution)/shard_map/ppermute | solution.py:51
  265.8 19.2 %collective-permute-start.33 = (bf16[256,768]{1,0:T(8,128)(2,1)S(1)}, bf16[256,768]{1,0:T(8,128)(2,1)S(1)}, u32[]{:S(2)}, u32[]{:S(2)}) collective-permute-start(bf16[256,768]{1,0:T(8,128)(2,1)S(1)} %get-tuple-element.295), channel_id=1, source_target_pairs={{0,2},{1,3},{2,0},{3,1},{4,6},{5,7},{6,4},{7,5},{8,10},{9,11},{10,... | collective-permute-start | bytes 1179656 | tf_op jit(solution)/shard_map/ppermute | solution.py:51
  293.9 12.0 %collective-permute-start.46 = (bf16[256,768]{1,0:T(8,128)(2,1)S(1)}, bf16[256,768]{1,0:T(8,128)(2,1)S(1)}, u32[]{:S(2)}, u32[]{:S(2)}) collective-permute-start(bf16[256,768]{1,0:T(8,128)(2,1)S(1)} %get-tuple-element.286), channel_id=1, source_target_pairs={{0,2},{1,3},{2,0},{3,1},{4,6},{5,7},{6,4},{7,5},{8,10},{9,11},{10,... | collective-permute-start | bytes 1179656 | tf_op jit(solution)/shard_map/ppermute | solution.py:51
  295.6 18.3 %collective-permute-start.42 = (bf16[256,768]{1,0:T(8,128)(2,1)S(1)}, bf16[256,768]{1,0:T(8,128)(2,1)S(1)}, u32[]{:S(2)}, u32[]{:S(2)}) collective-permute-start(bf16[256,768]{1,0:T(8,128)(2,1)S(1)} %get-tuple-element.284), channel_id=1, source_target_pairs={{0,2},{1,3},{2,0},{3,1},{4,6},{5,7},{6,4},{7,5},{8,10},{9,11},{10,... | collective-permute-start | bytes 1179656 | tf_op jit(solution)/shard_map/ppermute | solution.py:51
  307.8 28.5 %collective-permute-start.47 = (bf16[256,768]{1,0:T(8,128)(2,1)}, bf16[256,768]{1,0:T(8,128)(2,1)}, u32[]{:S(2)}, u32[]{:S(2)}) collective-permute-start(bf16[256,768]{1,0:T(8,128)(2,1)} %get-tuple-element.176.mine_in.refs_7_), channel_id=1, source_target_pairs={{0,1},{1,0},{2,3},{3,2},{4,5},{5,4},{6,7},{7,6},{8,9},{9,8},{10,11... | collective-permute-start | bytes 1179656 | tf_op jit(solution)/shard_map/ppermute | solution.py:47
  316.7 21.2 %collective-permute-start.43 = (bf16[256,768]{1,0:T(8,128)(2,1)}, bf16[256,768]{1,0:T(8,128)(2,1)}, u32[]{:S(2)}, u32[]{:S(2)}) collective-permute-start(bf16[256,768]{1,0:T(8,128)(2,1)} %get-tuple-element.168.mine_in.refs_5_), channel_id=1, source_target_pairs={{0,1},{1,0},{2,3},{3,2},{4,5},{5,4},{6,7},{7,6},{8,9},{9,8},{10,11... | collective-permute-start | bytes 1179656 | tf_op jit(solution)/shard_map/ppermute | solution.py:47
  334.8 73.1 %collective-permute-start.67 = (bf16[4,96,2304]{2,1,0:T(8,128)(2,1)}, bf16[4,96,2304]{2,1,0:T(8,128)(2,1)}, u32[]{:S(2)}, u32[]{:S(2)}) collective-permute-start(bf16[4,96,2304]{2,1,0:T(8,128)(2,1)} %get-tuple-element.229), channel_id=1, source_target_pairs={{0,4},{4,0},{8,12},{12,8},{16,20},{20,16},{24,28},{28,24},{1,5},{5... | collective-permute-start | bytes 5308424 | tf_op jit(solution)/shard_map/ppermute | solution.py:55
  359.7 29.0 %collective-permute-start.65 = (bf16[4,96,768]{2,1,0:T(8,128)(2,1)S(1)}, bf16[4,96,768]{2,1,0:T(8,128)(2,1)S(1)}, u32[]{:S(2)}, u32[]{:S(2)}) collective-permute-start(bf16[4,96,768]{2,1,0:T(8,128)(2,1)S(1)} %get-tuple-element.217), channel_id=1, source_target_pairs={{0,4},{4,0},{8,12},{12,8},{16,20},{20,16},{24,28},{28,24},{1,5},{5... | collective-permute-start | bytes 1769480 | tf_op jit(solution)/shard_map/ppermute | solution.py:55
  360.5 12.0 %collective-permute-start.55 = (bf16[256,768]{1,0:T(8,128)(2,1)S(1)}, bf16[256,768]{1,0:T(8,128)(2,1)S(1)}, u32[]{:S(2)}, u32[]{:S(2)}) collective-permute-start(bf16[256,768]{1,0:T(8,128)(2,1)S(1)} %get-tuple-element.282), channel_id=1, source_target_pairs={{0,2},{1,3},{2,0},{3,1},{4,6},{5,7},{6,4},{7,5},{8,10},{9,11},{10,... | collective-permute-start | bytes 1179656 | tf_op jit(solution)/shard_map/ppermute | solution.py:51
  361.7 18.5 %collective-permute-start.49 = (bf16[256,768]{1,0:T(8,128)(2,1)S(1)}, bf16[256,768]{1,0:T(8,128)(2,1)S(1)}, u32[]{:S(2)}, u32[]{:S(2)}) collective-permute-start(bf16[256,768]{1,0:T(8,128)(2,1)S(1)} %get-tuple-element.278), channel_id=1, source_target_pairs={{0,2},{1,3},{2,0},{3,1},{4,6},{5,7},{6,4},{7,5},{8,10},{9,11},{10,... | collective-permute-start | bytes 1179656 | tf_op jit(solution)/shard_map/ppermute | solution.py:51
  374.8 19.2 %collective-permute-start.56 = (bf16[256,768]{1,0:T(8,128)(2,1)}, bf16[256,768]{1,0:T(8,128)(2,1)}, u32[]{:S(2)}, u32[]{:S(2)}) collective-permute-start(bf16[256,768]{1,0:T(8,128)(2,1)} %get-tuple-element.196.mine_in.refs_8_), channel_id=1, source_target_pairs={{0,1},{1,0},{2,3},{3,2},{4,5},{5,4},{6,7},{7,6},{8,9},{9,8},{10,11... | collective-permute-start | bytes 1179656 | tf_op jit(solution)/shard_map/ppermute | solution.py:47
  383.1 17.9 %collective-permute-start.50 = (bf16[256,768]{1,0:T(8,128)(2,1)}, bf16[256,768]{1,0:T(8,128)(2,1)}, u32[]{:S(2)}, u32[]{:S(2)}) collective-permute-start(bf16[256,768]{1,0:T(8,128)(2,1)} %get-tuple-element.185.mine_in.refs_6_), channel_id=1, source_target_pairs={{0,1},{1,0},{2,3},{3,2},{4,5},{5,4},{6,7},{7,6},{8,9},{9,8},{10,11... | collective-permute-start | bytes 1179656 | tf_op jit(solution)/shard_map/ppermute | solution.py:47
  389.7 21.4 %all-to-all-start.3 = ((bf16[4,96,768]{2,1,0:T(8,128)(2,1)}), bf16[4,96,768]{2,1,0:T(8,128)(2,1)}, u32[]{:S(2)}, u32[]{:S(2)}) async-start(bf16[4,96,768]{2,1,0:T(8,128)(2,1)} %add_convert_fusion.2), calls=%async_computation.3 | async-start | bytes 1179648 | tf_op jit(solution)/shard_map/all_to_all | solution.py:83
  401.0 15.3 %collective-permute-start.57 = (bf16[256,768]{1,0:T(8,128)(2,1)}, bf16[256,768]{1,0:T(8,128)(2,1)}, u32[]{:S(2)}, u32[]{:S(2)}) collective-permute-start(bf16[256,768]{1,0:T(8,128)(2,1)} %get-tuple-element.199), channel_id=1, source_target_pairs={{0,1},{1,0},{2,3},{3,2},{4,5},{5,4},{6,7},{7,6},{8,9},{9,8},{10,11... | collective-permute-start | bytes 1179656 | tf_op jit(solution)/shard_map/ppermute | solution.py:47
  407.6 10.9 %collective-permute-start.51 = (bf16[256,768]{1,0:T(8,128)(2,1)}, bf16[256,768]{1,0:T(8,128)(2,1)S(1)}, u32[]{:S(2)}, u32[]{:S(2)}) collective-permute-start(bf16[256,768]{1,0:T(8,128)(2,1)} %get-tuple-element.188), channel_id=1, source_target_pairs={{0,1},{1,0},{2,3},{3,2},{4,5},{5,4},{6,7},{7,6},{8,9},{9,8},{10,11... | collective-permute-start | bytes 1179656 | tf_op jit(solution)/shard_map/ppermute | solution.py:47
  411.1 63.6 %all-to-all-start.5 = ((bf16[4,96,2304]{2,1,0:T(8,128)(2,1)}), bf16[4,96,2304]{2,1,0:T(8,128)(2,1)}, u32[]{:S(2)}, u32[]{:S(2)}) async-start(bf16[4,96,2304]{2,1,0:T(8,128)(2,1)} %add_convert_fusion), calls=%async_computation.5 | async-start | bytes 3538944 | tf_op jit(solution)/shard_map/all_to_all | solution.py:83
  417.5 12.1 %collective-permute-start.58 = (bf16[256,768]{1,0:T(8,128)(2,1)S(1)}, bf16[256,768]{1,0:T(8,128)(2,1)S(1)}, u32[]{:S(2)}, u32[]{:S(2)}) collective-permute-start(bf16[256,768]{1,0:T(8,128)(2,1)S(1)} %get-tuple-element.280), channel_id=1, source_target_pairs={{0,2},{1,3},{2,0},{3,1},{4,6},{5,7},{6,4},{7,5},{8,10},{9,11},{10,... | collective-permute-start | bytes 1179656 | tf_op jit(solution)/shard_map/ppermute | solution.py:51
  418.7 18.2 %collective-permute-start.52 = (bf16[256,768]{1,0:T(8,128)(2,1)S(1)}, bf16[256,768]{1,0:T(8,128)(2,1)S(1)}, u32[]{:S(2)}, u32[]{:S(2)}) collective-permute-start(bf16[256,768]{1,0:T(8,128)(2,1)S(1)} %get-tuple-element.276), channel_id=1, source_target_pairs={{0,2},{1,3},{2,0},{3,1},{4,6},{5,7},{6,4},{7,5},{8,10},{9,11},{10,... | collective-permute-start | bytes 1179656 | tf_op jit(solution)/shard_map/ppermute | solution.py:51
  431.1 8.5 %collective-permute-start.59 = (bf16[256,768]{1,0:T(8,128)(2,1)S(1)}, bf16[256,768]{1,0:T(8,128)(2,1)S(1)}, u32[]{:S(2)}, u32[]{:S(2)}) collective-permute-start(bf16[256,768]{1,0:T(8,128)(2,1)S(1)} %get-tuple-element.201.mine_in.refs_7_), channel_id=1, source_target_pairs={{0,1},{1,0},{2,3},{3,2},{4,5},{5,4},{6,7},{7,6},{8,9},{9,8},{10,11... | collective-permute-start | bytes 1179656 | tf_op jit(solution)/shard_map/ppermute | solution.py:47
  457.5 16.2 %collective-permute-start.64 = (bf16[4,96,768]{2,1,0:T(8,128)(2,1)S(1)}, bf16[4,96,768]{2,1,0:T(8,128)(2,1)S(1)}, u32[]{:S(2)}, u32[]{:S(2)}) collective-permute-start(bf16[4,96,768]{2,1,0:T(8,128)(2,1)S(1)} %get-tuple-element.213), channel_id=1, source_target_pairs={{0,4},{4,0},{8,12},{12,8},{16,20},{20,16},{24,28},{28,24},{1,5},{5... | collective-permute-start | bytes 1769480 | tf_op jit(solution)/shard_map/ppermute | solution.py:55
  465.8 49.1 %collective-permute-start.66 = (bf16[4,96,2304]{2,1,0:T(8,128)(2,1)}, bf16[4,96,2304]{2,1,0:T(8,128)(2,1)}, u32[]{:S(2)}, u32[]{:S(2)}) collective-permute-start(bf16[4,96,2304]{2,1,0:T(8,128)(2,1)} %get-tuple-element.223), channel_id=1, source_target_pairs={{0,4},{4,0},{8,12},{12,8},{16,20},{20,16},{24,28},{28,24},{1,5},{5... | collective-permute-start | bytes 5308424 | tf_op jit(solution)/shard_map/ppermute | solution.py:55
  470.4 9.0 %collective-permute-start.60 = (bf16[1024,384]{1,0:T(8,128)(2,1)}, bf16[1024,384]{1,0:T(8,128)(2,1)}, u32[]{:S(2)}, u32[]{:S(2)}) collective-permute-start(bf16[1024,384]{1,0:T(8,128)(2,1)} %get-tuple-element.209), channel_id=1, source_target_pairs={{0,1},{1,0},{2,3},{3,2},{4,5},{5,4},{6,7},{7,6},{8,9},{9,8},{10,11... | collective-permute-start | bytes 2359304 | tf_op jit(solution)/shard_map/ppermute | solution.py:47
  474.6 20.2 %all-to-all-start.2 = ((bf16[4,96,768]{2,1,0:T(8,128)(2,1)}), bf16[4,96,768]{2,1,0:T(8,128)(2,1)S(1)}, u32[]{:S(2)}, u32[]{:S(2)}) async-start(bf16[4,96,768]{2,1,0:T(8,128)(2,1)} %add_convert_fusion.3), calls=%async_computation.2 | async-start | bytes 1179648 | tf_op jit(solution)/shard_map/all_to_all | solution.py:83
  481.3 10.2 %collective-permute-start.61 = (bf16[8,64,384]{2,1,0:T(8,128)(2,1)S(1)}, bf16[8,64,384]{2,1,0:T(8,128)(2,1)S(1)}, u32[]{:S(2)}, u32[]{:S(2)}) collective-permute-start(bf16[8,64,384]{2,1,0:T(8,128)(2,1)S(1)} %fusion.4), channel_id=1, source_target_pairs={{0,2},{1,3},{2,0},{3,1},{4,6},{5,7},{6,4},{7,5},{8,10},{9,11},{10,... | collective-permute-start | bytes 1179656 | tf_op jit(solution)/shard_map/ppermute | solution.py:51
  482.4 40.8 %collective-permute-start.68 = (f32[2,2,2,768]{3,2,1,0:T(2,128)S(1)}, f32[2,2,2,768]{3,2,1,0:T(2,128)S(1)}, u32[]{:S(2)}, u32[]{:S(2)}) collective-permute-start(f32[2,2,2,768]{3,2,1,0:T(2,128)S(1)} %maximum_multiply_fusion), channel_id=1, source_target_pairs={{0,1},{1,0},{2,3},{3,2},{4,5},{5,4},{6,7},{7,6},{8,9},{9,8},{10,11... | collective-permute-start | bytes 73736 | tf_op jit(solution)/shard_map/ppermute | solution.py:89
  494.9 23.1 %all-to-all-start.1 = ((bf16[8,64,384]{2,1,0:T(8,128)(2,1)}), bf16[8,64,384]{2,1,0:T(8,128)(2,1)S(1)}, u32[]{:S(2)}, u32[]{:S(2)}) async-start(bf16[8,64,384]{2,1,0:T(8,128)(2,1)} %fusion.1), calls=%async_computation.1 | async-start | bytes 786432 | tf_op jit(solution)/shard_map/all_to_all | solution.py:711
  518.0 59.7 %all-to-all-start.4 = ((bf16[4,96,2304]{2,1,0:T(8,128)(2,1)}), bf16[4,96,2304]{2,1,0:T(8,128)(2,1)}, u32[]{:S(2)}, u32[]{:S(2)}) async-start(bf16[4,96,2304]{2,1,0:T(8,128)(2,1)} %add_convert_fusion.1), calls=%async_computation.4 | async-start | bytes 3538944 | tf_op jit(solution)/shard_map/all_to_all | solution.py:83
  531.1 20.8 %collective-permute-start.71 = (f32[2,2,2,768]{3,2,1,0:T(2,128)S(1)}, f32[2,2,2,768]{3,2,1,0:T(2,128)S(1)}, u32[]{:S(2)}, u32[]{:S(2)}) collective-permute-start(f32[2,2,2,768]{3,2,1,0:T(2,128)S(1)} %add.209), channel_id=1, source_target_pairs={{0,8},{4,12},{8,0},{12,4},{16,24},{20,28},{24,16},{28,20},{1,9},{5... | collective-permute-start | bytes 73736 | tf_op jit(solution)/shard_map/ppermute | solution.py:55
  533.2 31.8 %collective-permute-start.62 = (bf16[8,64,384]{2,1,0:T(8,128)(2,1)S(1)}, bf16[8,64,384]{2,1,0:T(8,128)(2,1)S(1)}, u32[]{:S(2)}, u32[]{:S(2)}) collective-permute-start(bf16[8,64,384]{2,1,0:T(8,128)(2,1)S(1)} %all-to-all-done.1), channel_id=1, source_target_pairs={{0,2},{1,3},{2,0},{3,1},{4,6},{5,7},{6,4},{7,5},{8,10},{9,11},{10,... | collective-permute-start | bytes 1179656 | tf_op jit(solution)/shard_map/ppermute | solution.py:51
  551.9 13.1 %collective-permute-start.72 = (f32[2,2,2,768]{3,2,1,0:T(2,128)S(1)}, f32[2,2,2,768]{3,2,1,0:T(2,128)S(1)}, u32[]{:S(2)}, u32[]{:S(2)}) collective-permute-start(f32[2,2,2,768]{3,2,1,0:T(2,128)S(1)} %add.210), channel_id=1, source_target_pairs={{0,16},{4,20},{8,24},{12,28},{16,0},{20,4},{24,8},{28,12},{1,17},{... | collective-permute-start | bytes 73736 | tf_op jit(solution)/shard_map/ppermute | solution.py:55
  (187 other events, 1234.8 us)
Sparse Core Ops, SparseCore 0:
  10.8 57.9 all-gather.2
  71.0 95.8 all-gather.4

commit v2 on v1

v2 whole, which is shorter than its diff:
```python
import functools
import math

import jax
import jax.numpy as jnp
import numpy as np
from jax import lax
from jax.experimental import pallas as pl
from jax.experimental.pallas import tpu as pltpu
from jax.sharding import PartitionSpec as P

HD = 64
LAYERS = 2
epsilon = 1e-05
rotary_base = 1000.0
LOG2E = math.log2(math.e)
F32 = jnp.float32
BF16 = jnp.bfloat16
VMEM_LIMIT = 12 * 1024 * 1024
COST = 0.001
KEEP = True


def sds(*shape, dtype=BF16):
    return jax.ShapeDtypeStruct(shape, dtype)


class Order:
    last = ()
    waiting = ()
    kept = []


def keep(*arrays):
    Order.kept.extend(arrays)


def drop(*arrays):
    gone = {id(a) for a in arrays}
    Order.kept = [a for a in Order.kept if id(a) not in gone]


def call(kernel, outs, *operands, flops=0, trans=0, scalars=0, after=(), alias=None):
    after = (*after, *Order.waiting, *Order.last)
    Order.waiting = ()
    taken = {id(a) for a in operands}
    held = [a for a in Order.kept if id(a) not in taken] if KEEP else []
    vmem = pl.BlockSpec(memory_space=pltpu.VMEM)
    smem = pl.BlockSpec(memory_space=pltpu.SMEM)
    moved = sum(a.size * a.dtype.itemsize for a in list(operands) + list(outs))
    used = len(operands)

    def body(*refs):
        kernel(*refs[:used], *refs[used + len(held) + len(after) :])

    results = pl.pallas_call(
        body,
        in_specs=[smem] * scalars
        + [vmem] * (used - scalars + len(held))
        + [pl.BlockSpec(memory_space=pl.ANY)] * len(after),
        out_specs=[vmem] * len(outs),
        out_shape=list(outs),
        input_output_aliases=alias or {},
        compiler_params=pltpu.CompilerParams(vmem_limit_bytes=VMEM_LIMIT),
        cost_estimate=pl.CostEstimate(
            flops=int(COST * flops),
            bytes_accessed=int(COST * moved),
            transcendentals=int(COST * trans),
        ),
    )(*operands, *held, *after)
    Order.last = (min(results, key=lambda r: r.size * r.dtype.itemsize),)
    return results


def swap_core(value):
    return lax.ppermute(value, "tensor", [(i, i ^ 1) for i in range(lax.axis_size("tensor"))])


def swap_x(value):
    return lax.ppermute(value, "tensor", [(i, i ^ 2) for i in range(lax.axis_size("tensor"))])


def swap_dp(value, step):
    return lax.ppermute(value, "dp", [(i, i ^ step) for i in range(lax.axis_size("dp"))])


def stepwise(rows):
    return lax.axis_size("dp") == 8 and rows % 16 == 0


def place_kernel(spots, split, index_ref, *refs):
    *pieces, first_ref, second_ref = refs
    rows = pieces[0].shape[0]
    for (offset, column), piece in zip(spots, pieces):
        here = pl.ds(pl.multiple_of((index_ref[3] ^ offset) * rows, rows), rows)
        width = piece.shape[1]
        if column < split:
            first_ref[here, :] = piece[:, :split]
            second_ref[here, : width - split] = piece[:, split:]
        else:
            second_ref[here, column - split : column - split + width] = piece[...]


def copy_kernel(in_ref, out_ref):
    out_ref[...] = in_ref[...]


def gather_start(shard, halves):
    if not stepwise(shard.shape[0]):
        return {(0, 0): lax.all_gather(shard, "dp", axis=0, tiled=True)}
    pieces = {(0, 0): shard, (1, 0): swap_dp(shard, 1)}
    for step in (2, 4, 6):
        column = 0
        for part in halves if step > 2 else [shard]:
            along = swap_dp(part, step)
            pieces[step, column] = along
            pieces[step + 1, column] = swap_dp(along, 1)
            column += part.shape[1]
    return pieces


def first_gather(shard, meanwhile):
    if not stepwise(shard.shape[0]):
        for step in meanwhile:
            step()
        return {(0, 0): lax.all_gather(shard, "dp", axis=0, tiled=True)}
    pieces = {(0, 0): shard, (1, 0): swap_dp(shard, 1)}
    sent, across = shard, pieces[1, 0]
    for number, step in enumerate((4, 6, 2)):
        along = swap_dp(sent, step)
        pieces[step, 0] = along
        if step != 2:
            sent = call(copy_kernel, [sds(*shard.shape)], shard, after=[along, across])[0]
        across = pieces[step + 1, 0] = swap_dp(along, 1)
        if number < len(meanwhile):
            meanwhile[number]()
    return pieces


def gather_finish(where, pieces, split, after=()):
    if len(pieces) == 1:
        whole = pieces[0, 0]
        return whole[:, :split], whole[:, split:]
    rows, width = pieces[0, 0].shape
    outs = [sds(8 * rows, n) for n in (split, width - split)]
    return call(
        functools.partial(place_kernel, tuple(pieces), split),
        outs, where, *pieces.values(), scalars=1, after=after,
    )


def scatter_add_kernel(index_ref, kept_ref, *refs):
    steps = kept_ref.shape[0]
    other_refs, out_refs = refs[:-steps], refs[-steps:]
    own = index_ref[3] // 2
    for step, out_ref in enumerate(out_refs):
        start = 0
        for other_ref in other_refs:
            here = pl.ds(start, other_ref.shape[2])
            total = kept_ref[own ^ step, :, here].astype(F32) + other_ref[own ^ step].astype(F32)
            out_ref[:, here] = total.astype(BF16)
            start += other_ref.shape[2]


def scatter_start(sums):
    if isinstance(sums, (list, tuple)):
        return [sums[0]] + [swap_dp(part, 1) for part in sums[1:]]
    return [lax.psum_scatter(sums, "dp", scatter_dimension=0, tiled=True)]


def scatter_finish(where, started):
    if len(started) == 1:
        return started
    kept, *others = started
    count, rows, width = kept.shape
    outs = call(scatter_add_kernel, [sds(rows, width)] * count, where, kept, *others, scalars=1)
    return [outs[0]] + [swap_dp(out, 2 * step) for step, out in enumerate(outs) if step]


def total_kernel(*refs):
    *in_refs, out_ref = refs
    out_ref[...] = total_of(in_refs)


def total_call(parts):
    rows, width = parts[0].shape[-2:]
    return [call(total_kernel, [sds(rows, width, dtype=F32)], *parts)[0]]


def dot_nt(left, right):
    return lax.dot_general(left, right, (((1,), (1,)), ((), ())), preferred_element_type=F32)


def dot_nn(left, right):
    return lax.dot_general(left, right, (((1,), (0,)), ((), ())), preferred_element_type=F32)


def dot_tn(left, right):
    return lax.dot_general(left, right, (((0,), (0,)), ((), ())), preferred_element_type=F32)


def swap_halves(values):
    width = values.shape[-1]
    lane = lax.broadcasted_iota(jnp.int32, values.shape, 1)
    return jnp.where(
        lane % HD < HD // 2,
        pltpu.roll(values, width - HD // 2, 1),
        pltpu.roll(values, HD // 2, 1),
    )


def widen(table, width):
    return jnp.concatenate([table] * (width // table.shape[1]), axis=1)


def qkv_kernel(*refs):
    *x_refs, w_ref, cos_ref, sin_ref, bias_ref, q_ref, k_ref, v_ref, kt_ref, vt_ref = refs
    inner = v_ref.shape[1]
    extra = q_ref.shape[1] - inner
    weight = w_ref[:, : 3 * inner]
    block = 256
    parts = [
        x_ref.at[pl.ds(start, block), :]
        for x_ref in x_refs
        for start in range(0, x_ref.shape[0], block)
    ]
    for step, x_ref in enumerate(parts):
        here = pl.ds(step * block, block)
        projected = dot_nn(x_ref[...], weight)
        pair = projected[:, : 2 * inner]
        turned = pair * widen(cos_ref[here, :], 2 * inner) + swap_halves(pair) * widen(
            sin_ref[here, :], 2 * inner
        )
        lane = lax.broadcasted_iota(jnp.int32, (block, extra), 1)
        queries = turned[:, :inner] * (1.0 / math.sqrt(HD))
        keys = turned[:, inner:]
        values = projected[:, 2 * inner :]
        one = jnp.where(lane == 0, 1.0, 0.0)
        mark = jnp.where(lane == 0, bias_ref[here, :extra], 0.0)
        q_ref[here, :] = jnp.concatenate([queries, one], axis=1).astype(BF16)
        k_ref[here, :] = jnp.concatenate([keys, mark], axis=1).astype(BF16)
        v_ref[here, :] = values.astype(BF16)
        kt_ref[:, here] = keys.T.astype(BF16)
        vt_ref[:, here] = values.T.astype(BF16)


def qkv_call(pieces, weight, tables, inner, after):
    rows = sum(p.shape[0] for p in pieces)
    width = weight.shape[0]
    return call(
        qkv_kernel,
        [sds(rows, inner + HD), sds(rows, inner + HD), sds(rows, inner)] + [sds(inner, rows)] * 2,
        *pieces, weight, *tables,
        flops=2 * rows * width * 3 * inner,
        after=after,
    )


def head_mask(shape, head, inner):
    lane = lax.broadcasted_iota(jnp.int32, shape, 1)
    return ((lane >= head * HD) & (lane < (head + 1) * HD)) | (lane >= inner)


def attend_kernel(part, q_ref, k_ref, vt_ref, w_ref, c_ref, lse_ref, out_ref):
    rows, inner = c_ref.shape
    queries = q_ref[pl.ds(part * rows, rows), :]
    columns, stats = [], []
    for head in range(inner // HD):
        masked = jnp.where(head_mask(queries.shape, head, inner), queries, 0)
        scores = dot_nt(k_ref[...], masked)
        shift = jnp.max(scores, axis=0, keepdims=True) * LOG2E
        exps = jnp.exp2(scores * LOG2E - shift)
        total = jnp.sum(exps, axis=0, keepdims=True)
        mixed = dot_nn(vt_ref[head * HD : (head + 1) * HD, :], exps.astype(BF16))
        columns.append(mixed * (1.0 / total))
        stats.append(shift + jnp.log2(total))
    context = jnp.concatenate(columns, axis=0).T.astype(BF16)
    c_ref[...] = context
    pad = lse_ref.shape[0] - len(stats)
    lse_ref[...] = jnp.concatenate(stats + [jnp.zeros((pad, rows), F32)], axis=0)
    out_ref[...] = dot_nt(context, w_ref[:, 3 * inner :]).astype(out_ref.dtype)


def attend_call(part, queries, keys, values_t, weight, dtype, after=()):
    length, padded = queries.shape
    rows, inner, width = length // 4, padded - HD, weight.shape[0]
    return call(
        functools.partial(attend_kernel, part),
        [sds(rows, inner), sds(8, rows, dtype=F32), sds(rows, width, dtype=dtype)],
        queries, keys, values_t, weight,
        flops=4 * rows * length * 256 * (inner // HD) + 2 * rows * inner * width,
        trans=rows * length * (inner // HD),
        after=after,
    )


def norm_kernel(base_ref, pair_ref, other_ref, gain_ref, shift_ref, low_ref, normal_ref, scale_ref, *out):
    values = base_ref[...].astype(F32) + (pair_ref[...] + other_ref[...].astype(F32))
    centred = values - jnp.mean(values, axis=-1, keepdims=True)
    scaled = lax.rsqrt(jnp.mean(centred * centred, axis=-1, keepdims=True) + epsilon)
    normal = centred * scaled
    result = normal * gain_ref[...] + shift_ref[...]
    low_ref[...] = result.astype(BF16)
    normal_ref[...] = normal.astype(BF16)
    scale_ref[...] = jnp.broadcast_to(scaled, scale_ref.shape)
    for ref in out:
        ref[...] = result


def norm_call(base, pair, other, gain, shift, last, after=()):
    rows, width = pair.shape
    return call(
        norm_kernel,
        [sds(rows, width), sds(rows, width), sds(rows, 128, dtype=F32)]
        + [sds(rows, width, dtype=F32)] * last,
        base, pair, other, gain, shift,
        flops=10 * rows * width,
        after=after,
    )


def norm_back_kernel(*refs):
    *in_refs, normal_ref, scale_ref, gain_ref, low_ref, vec_ref = refs
    incoming = in_refs[0][...].astype(F32)
    for ref in in_refs[1:]:
        incoming = incoming + ref[...].astype(F32)
    normal = normal_ref[...].astype(F32)
    weighted = incoming * gain_ref[...]
    result = scale_ref[:, 0:1] * (
        weighted
        - jnp.mean(weighted, axis=-1, keepdims=True)
        - normal * jnp.mean(weighted * normal, axis=-1, keepdims=True)
    )
    low_ref[...] = result.astype(BF16)
    vec_ref[0:1, :] = jnp.sum(incoming * normal, axis=0, keepdims=True)
    vec_ref[1:2, :] = jnp.sum(incoming, axis=0, keepdims=True)


def norm_back_call(incoming, normal, scale, gain, after=()):
    rows, width = normal.shape
    return call(
        norm_back_kernel,
        [sds(rows, width), sds(2, width, dtype=F32)],
        *incoming, normal, scale, gain,
        flops=16 * rows * width,
        after=after,
    )


def mask_of(where_ref, chunk, rows):
    place = lax.broadcasted_iota(jnp.int32, (rows, 128), 0)
    usable = (2 * chunk + where_ref[0]) * rows + place < where_ref[4]
    return jnp.where(usable, 1.0, 0.0)[:, 0:1]


def seed_kernel(chunk, where_ref, own_ref, other_ref, out_ref):
    seed = jnp.where(where_ref[1] == chunk, own_ref[...].astype(F32), other_ref[...].astype(F32))
    out_ref[...] = (seed * mask_of(where_ref, chunk, out_ref.shape[0])).astype(BF16)


def show_kernel(where_ref, first_ref, second_ref, out_ref):
    rows = out_ref.shape[0]
    first = first_ref[...] * mask_of(where_ref, 0, rows)
    second = second_ref[...] * mask_of(where_ref, 1, rows)
    out_ref[...] = jnp.where(where_ref[1] == 0, first, second)


def gather_vectors_kernel(*refs):
    *in_refs, out_ref = refs
    for row in range(out_ref.shape[0] // 2):
        pair = in_refs[2 * row][...] + in_refs[2 * row + 1][...]
        out_ref[2 * row : 2 * row + 2, :] = pair * 0.5


def norms_kernel(left_ref, right_ref, gains_ref, biases_ref):
    for row in range(left_ref.shape[0] // 2):
        for member, out_ref in enumerate((gains_ref, biases_ref)):
            here = pl.ds(2 * row + member, 1)
            out_ref[row // 2, pl.ds(row % 2, 1), :] = left_ref[here, :] + right_ref[here, :]


def add_kernel(left_ref, right_ref, out_ref):
    total = left_ref[...].astype(F32) + right_ref[...].astype(F32)
    out_ref[...] = total.astype(out_ref.dtype)


def add_call(left, right, dtype, after=()):
    return call(add_kernel, [sds(*left.shape, dtype=dtype)], left, right, after=after)[0]


def mlp_parts(w_ref):
    hidden = w_ref.shape[1] // 3
    return [w_ref[:, part * hidden : (part + 1) * hidden] for part in range(3)]


def mlp_kernel(x_ref, w_ref, out_ref):
    gate_weight, up_weight, down_weight = mlp_parts(w_ref)
    rows = x_ref[...]
    gate = dot_nn(rows, gate_weight)
    up = dot_nn(rows, up_weight)
    active = (gate * jax.nn.sigmoid(gate) * up).astype(BF16)
    out_ref[...] = dot_nt(active, down_weight).astype(out_ref.dtype)


def mlp_call(piece, weight, dtype):
    rows, width = piece.shape
    return call(
        mlp_kernel, [sds(rows, width, dtype=dtype)], piece, weight,
        flops=2 * rows * width * weight.shape[1],
        trans=rows * weight.shape[1] // 3,
    )[0]


def mlp_back_kernel(x_ref, grad_ref, w_ref, act_ref, dg_ref, out_ref):
    gate_weight, up_weight, down_weight = mlp_parts(w_ref)
    hidden = act_ref.shape[1]
    rows = x_ref[...]
    gate = dot_nn(rows, gate_weight)
    up = dot_nn(rows, up_weight)
    active_grad = dot_nn(grad_ref[...], down_weight)
    sigmoid = jax.nn.sigmoid(gate)
    silu = gate * sigmoid
    act_ref[...] = (silu * up).astype(BF16)
    gate_grad = (active_grad * up * sigmoid * (1.0 + gate * (1.0 - sigmoid))).astype(BF16)
    up_grad = (active_grad * silu).astype(BF16)
    dg_ref[:, :hidden] = gate_grad
    dg_ref[:, hidden:] = up_grad
    partial = dot_nt(gate_grad, gate_weight) + dot_nt(up_grad, up_weight)
    out_ref[...] = partial.astype(out_ref.dtype)


def mlp_back_call(piece, grad, weight, dtype):
    rows, width = piece.shape
    hidden = weight.shape[1] // 3
    return call(
        mlp_back_kernel,
        [sds(rows, hidden), sds(rows, 2 * hidden), sds(rows, width, dtype=dtype)],
        piece, grad, weight,
        flops=10 * rows * width * hidden,
        trans=rows * hidden,
    )


def context_back_kernel(mine_in, theirs_in, w_ref, dc_ref):
    inner = dc_ref.shape[1]
    half = mine_in.shape[0]
    weight = w_ref[:, 3 * inner :]
    dc_ref[:half, :] = dot_nn(mine_in[...], weight).astype(BF16)
    dc_ref[half:, :] = dot_nn(theirs_in[...], weight).astype(BF16)


def context_back_call(mine, theirs, weight):
    half, width = mine.shape
    inner = weight.shape[1] // 4
    return call(
        context_back_kernel, [sds(2 * half, inner)], mine, theirs, weight,
        flops=4 * half * width * inner,
    )[0]


def attend_back_kernel(
    first, last, q_ref, dc_ref, lse_ref, k_ref, v_ref, kt_ref, cos_ref, sin_ref, *refs
):
    if first:
        dk_in, dv_in, *refs = refs
    if last and first:
        dq_in, *refs = refs
    dq_ref, dk_ref, dv_ref = refs
    rows, inner = dc_ref.shape
    length, padded = k_ref.shape
    block = min(256, rows)

    def turn_back(gradient, cosine, sine):
        cosine = widen(cosine, gradient.shape[1])
        sine = widen(sine, gradient.shape[1])
        return (gradient * cosine - swap_halves(gradient) * sine)[:, :inner]

    if first:
        dk_ref[...] = dk_in[...]
        dv_ref[...] = dv_in[...]
    else:
        dk_ref[...] = jnp.zeros_like(dk_ref)
        dv_ref[...] = jnp.zeros_like(dv_ref)

    def step_of(step, carry):
        start = pl.multiple_of(step * block, block)
        here = pl.ds(start, block)
        there = pl.ds(pl.multiple_of(first + step * block, block), block)
        queries = q_ref[there, :]
        context_grad = dc_ref[here, :]
        columns = []
        for head in range(inner // HD):
            masked = jnp.where(head_mask(queries.shape, head, inner), queries, 0)
            masked_grad = jnp.where(head_mask(context_grad.shape, head, inner), context_grad, 0)
            scores = dot_nt(k_ref[...], masked)
            weights = jnp.exp2(scores * LOG2E - lse_ref[head : head + 1, there])
            weight_grad = dot_nt(v_ref[...], masked_grad)
            inner_sum = jnp.sum(weights * weight_grad, axis=0, keepdims=True)
            score_grad = (weights * (weight_grad - inner_sum)).astype(BF16)
            dk_ref[...] += dot_nn(score_grad, masked)
            dv_ref[...] += dot_nn(weights.astype(BF16), masked_grad)
            columns.append(dot_nn(kt_ref[head * HD : (head + 1) * HD, :], score_grad))
        columns.append(jnp.zeros((padded - inner, block), F32))
        query_grad = jnp.concatenate(columns, axis=0).T * (1.0 / math.sqrt(HD))
        turned = turn_back(query_grad, cos_ref[there, :], sin_ref[there, :]).astype(BF16)
        dq_ref[there if last else here, :inner] = turned
        return carry

    lax.fori_loop(0, rows // block, step_of, 0)
    if last:
        if first:
            dq_ref[:first, :inner] = dq_in[...]
        dq_ref[:, inner : 2 * inner] = turn_back(dk_ref[...], cos_ref[...], sin_ref[...]).astype(
            BF16
        )
        dq_ref[:, 2 * inner :] = dv_ref[...].astype(BF16)


def attend_back_call(first, last, operands, carried, after):
    length, padded = operands[0].shape
    rows, inner = operands[1].shape
    out = sds(length, 3 * inner) if last else sds(rows, inner)
    return call(
        functools.partial(attend_back_kernel, first, last),
        [out, sds(length, padded, dtype=F32), sds(length, inner, dtype=F32)],
        *operands, *carried,
        flops=10 * rows * length * 256 * (inner // HD),
        trans=rows * length * (inner // HD),
        after=after,
    )


def input_back_kernel(part, dp_ref, w_ref, out_ref):
    rows = out_ref.shape[0]
    here = pl.ds(part * rows, rows)
    out_ref[...] = dot_nt(dp_ref[here, :], w_ref[:, : dp_ref.shape[1]]).astype(out_ref.dtype)


def input_back_call(part, triple, weight, dtype, after=()):
    rows, width = triple.shape[0] // 4, weight.shape[0]
    return call(
        functools.partial(input_back_kernel, part),
        [sds(rows, width, dtype=dtype)],
        triple, weight,
        flops=2 * rows * triple.shape[1] * width,
        after=after,
    )[0]


def input_last_kernel(index_ref, dp_ref, w_ref, *refs):
    *grad_refs, kept_ref, sent_ref = refs
    core, side = index_ref[0], index_ref[1]
    rows, total = dp_ref.shape
    quarter = rows // 4
    split = kept_ref.shape[1]
    weight = w_ref[:, :total]
    for step in range(4):
        chunk, part = step // 2, step % 2
        partial = dot_nt(dp_ref[pl.ds(step * quarter, quarter), :], weight)
        if not part:
            partial = partial + jnp.where(side == chunk, grad_refs[chunk][...].astype(F32), 0.0)
        start = pl.multiple_of((2 * chunk + (core ^ part)) * quarter, quarter)
        low, high = partial[:, :split], partial[:, split:]
        kept_ref[pl.ds(start, quarter), :] = jnp.where(core == 0, low, high)
        sent_ref[pl.ds(start, quarter), :] = jnp.where(core == 0, high, low).astype(BF16)


def input_last_call(index, triple, weight, grads, after):
    rows, width = triple.shape[0], weight.shape[0]
    return call(
        input_last_kernel,
        [sds(rows, width // 2, dtype=F32), sds(rows, width // 2)],
        index, triple, weight, *grads,
        flops=2 * rows * triple.shape[1] * width, scalars=1, after=after,
    )


def side_kernel(index_ref, kept_ref, other_ref, mine_ref, theirs_ref):
    side = index_ref[1]
    count, half, _ = mine_ref.shape
    for block in range(count):
        halves = []
        for part in range(2):
            here = pl.ds((2 * block + part) * half, half)
            halves.append(kept_ref[here, :] + other_ref[here, :].astype(F32))
        mine_ref[block] = jnp.where(side == 0, halves[0], halves[1])
        theirs_ref[block] = jnp.where(side == 0, halves[1], halves[0]).astype(BF16)


SHARE = 768


def weight_kernel(counts, index_ref, *refs):
    in_count = sum(left + right for left, right in counts)
    in_refs, (kept_ref, *sent_refs) = refs[:in_count], refs[in_count:]
    blocks, rows, _ = kept_ref.shape
    width = blocks * rows * (2 if sent_refs else 1)
    wide = 4 * rows if width % (4 * rows) == 0 and (4 * rows) % 128 == 0 else width
    column = 0
    lefts, rights = [], []
    for left_count, right_count in counts:
        lefts.append(in_refs[:left_count])
        rights.append(in_refs[left_count : left_count + right_count])
        in_refs = in_refs[left_count + right_count :]
    for left, right in zip(lefts, rights):
        columns = right[0].shape[1]
        share = min(columns, SHARE)
        ratio = len(left) // len(right)
        for start in range(0, columns, share):
            for first in range(0, width, wide):
                total = None
                for number, left_ref in enumerate(left):
                    size = left_ref.shape[0]
                    right_ref = right[number // ratio]
                    term = dot_tn(
                        left_ref[:, first : first + wide],
                        right_ref[
                            pl.ds((number % ratio) * size, size), start : start + share
                        ],
                    )
                    total = term if total is None else total + term
                where = pl.ds(column + start, share)
                there = pl.ds((column + start) % SHARE, share)
                for offset in range(0, wide, 2 * rows):
                    even = total[offset : offset + rows].astype(BF16)
                    odd = total[offset + rows : offset + 2 * rows].astype(BF16)
                    block = (first + offset) // (2 * rows)
                    if not sent_refs:
                        kept_ref[2 * block, :, where] = even
                        kept_ref[2 * block + 1, :, where] = odd
                    else:
                        sent_ref = sent_refs[(column + start) // SHARE]
                        kept_ref[block, :, where] = jnp.where(index_ref[5] == 0, even, odd)
                        sent_ref[block, :, there] = jnp.where(index_ref[5] == 0, odd, even)
        column += columns


def weight_call(parity, pairs, count, after=()):
    width = pairs[0][0][0].shape[1]
    total = sum(right[0].shape[1] for _, right in pairs)
    rows = sum(piece.shape[0] for piece in pairs[0][0])
    operands = [piece for left, right in pairs for piece in (*left, *right)]
    counts = tuple((len(left), len(right)) for left, right in pairs)
    flops = 2 * rows * width * total
    if parity is None:
        return call(
            functools.partial(weight_kernel, counts, None),
            [sds(count, width // count, total)],
            *operands, flops=flops, after=after,
        )[0]
    shape = (count // 2, width // count)
    return call(
        functools.partial(weight_kernel, counts),
        [sds(*shape, total)] + [sds(*shape, SHARE)] * (total // SHARE),
        parity, *operands, flops=flops, scalars=1, after=after,
    )


def total_of(refs):
    parts = [
        part
        for ref in refs
        for part in ([ref[i] for i in range(ref.shape[0])] if len(ref.shape) == 3 else [ref[...]])
    ]
    total = parts[0].astype(F32)
    for part in parts[1:]:
        total = total + part.astype(F32)
    return total


def grads_kernel(counts, *refs):
    out_refs = refs[-4:]
    position = 0
    for layer, groups in enumerate(counts):
        parts = []
        for count in groups:
            parts.append(total_of(refs[position : position + count]))
            position += count
        whole = jnp.concatenate(parts, axis=1)
        project_ref, gate_up_ref, output_ref, down_ref = out_refs
        inner, hidden = output_ref.shape[1], down_ref.shape[2]
        for part in range(3):
            project_ref[layer, part] = whole[:, part * inner : (part + 1) * inner]
        output_ref[layer] = whole[:, 3 * inner : 4 * inner].T
        for part in range(2):
            start = 4 * inner + part * hidden
            gate_up_ref[layer, :, part, :] = whole[:, start : start + hidden]
        down_ref[layer] = whole[:, 4 * inner + 2 * hidden :]


def last_kernel(
    turned, order_ref, where_ref, near_ref, far_ref, near_other_ref, far_other_ref, out_ref
):
    core, side = where_ref[0], where_ref[1]
    count, half, split = near_ref.shape
    for source in range(count):
        target = order_ref[where_ref[3] ^ source if turned else source]
        for ref, flip in ((near_ref, 0), (far_ref, 1)):
            here = pl.ds(pl.multiple_of((side ^ flip) * half, half), half)
            other = near_other_ref if ref is near_ref else far_other_ref
            own, swapped = ref[source].astype(F32), other[source].astype(F32)
            out_ref[target, here, :split] = jnp.where(core == 0, own, swapped)
            out_ref[target, here, split:] = jnp.where(core == 0, swapped, own)


def pair_kernel(mine_ref, other_ref, pair_ref, low_ref):
    pair = mine_ref[...] + other_ref[...].astype(F32)
    pair_ref[...] = pair
    low_ref[...] = pair.astype(BF16)


def finish_pair(mine, theirs, after=()):
    other = swap_core(theirs)
    outs = [sds(*mine.shape, dtype=F32), sds(*mine.shape)]
    pair, low = call(pair_kernel, outs, mine, other, after=after)
    return pair, swap_x(low)


def layer_forward(
    pieces, residual, first_weight, second_weight, gains, shifts, tables, inner, last, at
):
    chunks = len(residual)
    queries, keys, values, keys_t, values_t = qkv_call(
        pieces, first_weight, tables, inner, ()
    )
    keep(*pieces, queries, keys, values, keys_t, values_t, first_weight)
    context, logsum, first_norm, hidden_pieces, pairs = [], [], [], [], []
    for k in range(chunks):
        args = (queries, keys, values_t, first_weight)
        theirs = attend_call(2 * k + 1, *args, BF16)
        keep(theirs[0])
        mine = attend_call(2 * k, *args, F32)
        keep(mine[0])
        context += [mine[0], theirs[0]]
        logsum += [mine[1], theirs[1]]
        pairs.append(finish_pair(mine[2], theirs[2], at(("pair", k))))
    drop(values_t)
    logsum = jnp.concatenate(logsum, axis=1)
    keep(logsum)
    if callable(second_weight):
        second_weight = second_weight()
    second_norm, result, result_pieces, second_pairs = [], [], [], []
    for k in range(chunks):
        low, *kept = norm_call(
            residual[k], *pairs[k], gains[0:1], shifts[0:1], False, at(("norm_one", k))
        )
        first_norm.append(kept)
        hidden_pieces += [low, swap_core(low)]
        keep(*kept)
        mine = mlp_call(hidden_pieces[2 * k], second_weight, F32)
        keep(hidden_pieces[2 * k], second_weight)
        theirs = mlp_call(hidden_pieces[2 * k + 1], second_weight, BF16)
        keep(hidden_pieces[2 * k + 1])
        second_pairs.append(finish_pair(mine, theirs))
    for k in range(chunks):
        low, *kept = norm_call(
            hidden_pieces[2 * k], *second_pairs[k], gains[1:2], shifts[1:2], last,
            at(("norm_two", k)),
        )
        keep(*kept[:2])
        second_norm.append(kept[:2])
        result += kept[2:]
        result_pieces.append(low)
    saved = (
        pieces, queries, keys, values, keys_t, context, logsum,
        first_norm, hidden_pieces, second_norm, first_weight, second_weight,
    )
    return result, result_pieces, saved


def layer_backward(incoming, saved, gains, tables, parity, count, at):
    (
        pieces, queries, keys, values, keys_t, context, logsum,
        first_norm, hidden_pieces, second_norm, first_weight, second_weight,
    ) = saved
    chunks = len(incoming)
    mixed, active, vectors_two, pair_grads, pairs = [], [], [], [], []
    for k in range(chunks):
        low, vector = norm_back_call(
            incoming[k], *second_norm[k], gains[1:2], at(("norm_two", k))
        )
        drop(*second_norm[k])
        vectors_two.append(vector)
        mixed += [low, swap_core(low)]
        for h, dtype in ((0, F32), (1, BF16)):
            act, grad, out = mlp_back_call(
                hidden_pieces[2 * k + h], mixed[2 * k + h], second_weight, dtype
            )
            keep(act, grad, mixed[2 * k + h])
            active.append(act)
            pair_grads.append(grad)
            if h == 0:
                mine = out
        pairs.append(finish_pair(mine, out))
    drop(second_weight)
    at("sums")
    late = scatter_start(
        weight_call(parity, [(hidden_pieces, pair_grads), (mixed, active)], count)
    )
    at(late)
    drop(*hidden_pieces, *pair_grads, *active, *mixed[1::2])
    attended, vectors_one, carried = [], [], ()
    for k in range(chunks):
        low, vector = norm_back_call(
            (mixed[2 * k], *pairs[k]), *first_norm[k], gains[0:1], at(("norm_one", k))
        )
        drop(*first_norm[k], mixed[2 * k])
        vectors_one.append(vector)
        if k == chunks - 1:
            at(("vectors", vectors_one + vectors_two))
        attended += [low, swap_core(low)]
        context_grad = context_back_call(*attended[2 * k :], first_weight)
        keep(*attended[2 * k :])
        operands = (queries, context_grad, logsum, keys, values, keys_t, *tables[:2])
        out, dk, dv = attend_back_call(
            k * context_grad.shape[0], k == chunks - 1, operands, carried, at(("attend_back", k))
        )
        carried = (dk, dv, out)
        at(("attend", k))
    drop(queries, logsum, keys, values, keys_t)
    return out, (pieces, attended, context), late


def rotary_tables(length):
    half = HD // 2
    angles = np.arange(length, dtype=np.float64)[:, None] * np.exp(
        np.arange(half, dtype=np.float64)[None, :] * (-2.0 * math.log(rotary_base) / HD)
    )
    cosine, sine = np.cos(angles), np.sin(angles)
    return (
        np.concatenate([cosine] * 4, axis=1).astype(np.float32),
        np.concatenate([-sine, sine] * 2, axis=1).astype(np.float32),
    )


def turn_kernel(where_ref, in_ref, *out_refs):
    index = where_ref[3]
    for step in range(4):
        for flip in range(2):
            out_refs[flip][step] = in_ref[index ^ (2 * step + flip)]


def couple_kernel(own_ref, other_ref, *out_refs):
    for step, out_ref in enumerate(out_refs):
        out_ref[0] = own_ref[step]
        out_ref[1] = other_ref[step]


def join_kernel(*refs):
    *in_refs, out_ref = refs
    for step, ref in enumerate(in_refs):
        out_ref[2 * step : 2 * step + 2] = ref[...]


def exchange_start(blocks, where):
    _, rows, width = blocks.shape
    own, sent = call(turn_kernel, [sds(4, rows, width)] * 2, where, blocks, scalars=1)
    return own, swap_dp(sent, 1)


def exchange_middle(own, sent, after=()):
    _, rows, width = own.shape
    pairs = call(couple_kernel, [sds(2, rows, width)] * 4, own, sent, after=after)
    return [pairs[0]] + [swap_dp(pairs[step], 2 * step) for step in (1, 2, 3)]


def exchange_finish(moved, after=()):
    _, rows, width = moved[0].shape
    return call(join_kernel, [sds(8, rows, width)], *moved, after=after)[0]


def deal_kernel(where_ref, *refs):
    *in_refs, out_ref = refs
    core, own, index = where_ref[0], where_ref[2], where_ref[3]
    count, share, _ = in_refs[0].shape
    part = out_ref.shape[0] // count
    for step in range(count):
        source = index ^ step
        quarter = source // 2
        block = 2 * ((quarter // 2) * 2 + ((quarter % 2) ^ core)) + source % 2
        for offset, ref in enumerate(in_refs):
            start = pl.multiple_of(block * part + (own ^ offset) * share, share)
            out_ref[pl.ds(start, share), :] = ref[step]


def deal_steps(tokens, dealing_order, where):
    count, part, width = tokens.shape
    share = part // 4
    mine = lax.dynamic_slice_in_dim(tokens, where[2] * share, share, 1)
    picked = jnp.take(mine, dealing_order, axis=0)
    state = []

    def spread(arrived):
        far = swap_x(arrived)
        state[:] = [arrived, swap_core(arrived), far, swap_core(far)]

    if count != 8 or share % 16:
        spread(lax.all_to_all(picked, "dp", split_axis=0, concat_axis=0, tiled=True))
        return [], state
    state[:] = exchange_start(picked, where)

    def middle():
        state[:] = exchange_middle(*state)

    def finish():
        spread(exchange_finish(state))

    return [middle, finish], state


def deal_finish(pieces, where, local_order):
    count, share, width = pieces[0].shape
    length = 4 * count * share
    if count == 8 and share % 16 == 0:
        return call(deal_kernel, [sds(length, width)], where, *pieces, scalars=1)[0]
    stacked = jnp.stack(pieces)
    blocks = [
        lax.dynamic_index_in_dim(stacked, where[2] ^ slot, 0, keepdims=False) for slot in range(4)
    ]
    whole = jnp.stack(blocks, axis=1).reshape(length, width)
    return local_order(whole).reshape(length, width)


def pack_kernel(project_ref, gate_up_ref, output_ref, down_ref, *out_refs):
    inner, hidden = output_ref.shape[1], down_ref.shape[2]
    columns = [project_ref[0, part] for part in range(3)] + [output_ref[0].T]
    columns += [gate_up_ref[0, :, part] for part in range(2)] + [down_ref[0]]
    start = 0
    for column in columns:
        low, size = column.astype(BF16), column.shape[1]
        first = 0
        for ref in out_refs[1:]:
            last = first + ref.shape[1]
            if first <= start < last:
                ref[:, start - first : start - first + size] = low
            first = last
        out_refs[0][:, start : start + size] = low
        start += size


def pack_call(layer, halves, project, gate_up, output, down, after=()):
    operands = (jnp.swapaxes(project, 1, 2), gate_up, output, jnp.swapaxes(down, 1, 2))
    rows, inner, hidden = project.shape[1], output.shape[1], down.shape[1]
    total, cut = 4 * inner + 3 * hidden, 4 * inner + hidden
    outs = [sds(rows, n) for n in ([total, cut, total - cut] if halves else [total])]
    after = (*after, *Order.last)

    def spec(w):
        return pl.BlockSpec((1, *w.shape[1:]), lambda i: (layer,) + (0,) * (w.ndim - 1))

    def body(*refs):
        pack_kernel(*refs[:4], *refs[4 + len(after) :])

    results = pl.pallas_call(
        body,
        grid=(1,),
        in_specs=[spec(w) for w in operands] + [pl.BlockSpec(memory_space=pl.ANY)] * len(after),
        out_specs=[pl.BlockSpec(out.shape, lambda i: (0, 0)) for out in outs],
        out_shape=outs,
        compiler_params=pltpu.CompilerParams(vmem_limit_bytes=VMEM_LIMIT),
        cost_estimate=pl.CostEstimate(flops=0, bytes_accessed=1000, transcendentals=0),
    )(*operands, *after)
    Order.last = (results[-1],)
    return results


def on_device(
    tokens, dealing_order, lengths, project_weight, gate_up_weight, output_weight, down_weight,
    norm_gains, norm_biases, cotangent,
):
    Order.last, Order.waiting, Order.kept = (), (), []
    dp_index = lax.axis_index("dp")
    tensor_index = lax.axis_index("tensor")
    core, side = tensor_index % 2, tensor_index // 2
    count, part, width = tokens.shape
    dp_count = lax.axis_size("dp")
    length = 4 * cotangent.shape[1]
    quarter = length // 4
    chunks = 2
    inner = output_weight.shape[1]
    hidden = down_weight.shape[1]
    rows_here = project_weight.shape[1]

    sources = (project_weight, gate_up_weight, output_weight, down_weight)
    length_now = jnp.take(lengths, jnp.take(dealing_order, dp_index))
    where = jnp.stack([core, side, tensor_index, dp_index, length_now, dp_index % 2]).astype(jnp.int32)
    own = cotangent[0]
    other = swap_x(own)

    def local_order(rows):
        split = rows.reshape(chunks, 2, quarter, rows.shape[-1])
        return jnp.where(core == 0, split, split[:, ::-1])

    places = jnp.arange(length)[:, None]
    marks = jnp.where(places < length_now, 0.0, -1e30).astype(F32)
    tables = tuple(
        local_order(table).reshape(length, 128)
        for table in (*map(jnp.asarray, rotary_tables(length)), jnp.broadcast_to(marks, (length, 128)))
    )
    shard = pack_call(0, False, *sources)[0]
    meanwhile, moving = deal_steps(tokens, dealing_order, where)
    started = [first_gather(shard, meanwhile)]
    weights, saved_all = [], []
    keep(*tables[:2])
    for layer in range(LAYERS):
        points = {}
        if layer < LAYERS - 1:
            before = [started[layer][key] for key in ((2, 0), (7, 0))] if len(started[layer]) > 1 else ()
            packed = pack_call(layer + 1, True, *sources, after=before)
            started.append(gather_start(packed[0], packed[1:]))
            if len(started[-1]) > 1:
                cut = packed[1].shape[1]
                points = {
                    "place": ((2, 0),),
                    ("pair", 0): ((4, 0),),
                    ("norm_one", 0): ((4, cut), (3, 0)),
                    ("norm_one", 1): ((6, 0), (1, 0), (5, 0)),
                    ("norm_two", 0): ((6, cut), (5, cut)),
                    ("norm_two", 1): ((7, 0),),
                }

        def at(point, points=points):
            return tuple(started[-1][key] for key in points.get(point, ()))

        weights.append(gather_finish(where, started[layer], 4 * inner, at("place")))
        if layer == 0:
            dealt = deal_finish(moving, where, local_order)
            pieces = [dealt]
            residual = [dealt[2 * k * quarter : (2 * k + 1) * quarter] for k in range(chunks)]
        current, residual, saved = layer_forward(
            pieces, residual, *weights[layer], norm_gains[layer], norm_biases[layer], tables,
            inner, layer == LAYERS - 1, at,
        )
        saved_all.append(saved)
        if layer < LAYERS - 1:
            pieces = [p for piece in residual for p in (piece, swap_core(piece))]
    layer_outputs = call(
        show_kernel, [sds(quarter, width, dtype=F32)], where, *current, scalars=1
    )
    incoming = [
        call(
            functools.partial(seed_kernel, k), [sds(quarter, width)], where, own, other, scalars=1
        )
        for k in range(chunks)
    ]
    received, vectors, steps = [None] * LAYERS, [None] * LAYERS, []
    for step in (1, 2):
        steps.append(lambda v, s=step: lax.ppermute(v, "tensor", [(i, i ^ s) for i in range(4)]))
    step = 1
    while step < dp_count:
        steps.append(functools.partial(swap_dp, step=step))
        step *= 2
    split = where if stepwise(rows_here) else None
    own_sums, above = {}, {}

    def sum_norms(index):
        if index < len(steps):
            own_sums["norms"] = add_call(own_sums["norms"], steps[index](own_sums["norms"]), F32)

    def at(layer, point):
        if isinstance(point, list):
            own_sums["second"] = point
            return ()
        if point[0] == "vectors":
            vectors[layer] = point[1]
            if layer == 0:
                flat = [v for group in vectors for v in group]
                own_sums["norms"] = call(
                    gather_vectors_kernel, [sds(len(flat), width, dtype=F32)], *flat
                )[0]
            return ()
        if split is None:
            return ()
        if layer:
            after = {("norm_one", 0): 1, ("norm_one", 1): 2, ("input", 0): 3}
        else:
            after = {("attend_back", 0): 1, ("attend_back", 1): 2, "input": 3}
        if point in after:
            return (own_sums["second"][after[point]],)
        if layer == LAYERS - 1:
            return ()
        if point == "sums":
            above["first"] = scatter_finish(where, above["first"])
        after = {
            ("norm_two", 0): ("second", 1), ("norm_two", 1): ("second", 2),
            ("norm_one", 0): ("second", 3), ("norm_one", 1): ("first", 1),
        }
        if point in after:
            name, number = after[point]
            return tuple(above[name][number : number + 3]) if name == "first" else (above[name][number],)
        return ()

    for layer in reversed(range(LAYERS)):
        triple, (rows_in, attended, context), late = layer_backward(
            incoming, saved_all[layer], norm_gains[layer], tables, split, dp_count,
            functools.partial(at, layer),
        )
        first_weight = weights[layer][0]
        if layer:
            incoming = []
            for k in range(chunks):
                theirs = input_back_call(
                    2 * k + 1, triple, first_weight, BF16, at(layer, ("input", k))
                )
                mine = input_back_call(2 * k, triple, first_weight, F32)
                incoming.append((attended[2 * k], *finish_pair(mine, theirs)))
            drop(first_weight)
            above["second"] = scatter_finish(where, late)
            sums = weight_call(split, [(rows_in, [triple]), (attended, context)], dp_count)
            drop(*rows_in, *attended[1::2], *context)
            above["first"] = scatter_start(sums)
            if split is None:
                above["first"] = scatter_finish(where, above["first"])

    kept, sent = input_last_call(where, triple, first_weight, attended[::2], at(0, "input"))
    sent = swap_core(sent)
    drop(first_weight, *tables[:2])
    second_sum = scatter_finish(where, late)
    arriving = [second_sum[step : step + 1] for step in (2, 3, 1)]
    sum_norms(0)
    sums = weight_call(split, [(rows_in, [triple]), (attended, context)], dp_count)
    Order.kept = []
    sums = scatter_start(sums)
    mine, theirs = call(
        side_kernel,
        [sds(count, part // 2, width // 2, dtype=F32), sds(count, part // 2, width // 2)],
        where, kept, sent, scalars=1,
    )
    sum_norms(1)
    total = add_call(mine, swap_x(theirs), BF16, arriving[0])
    if split is None:
        near = lax.all_to_all(total, "dp", split_axis=0, concat_axis=0, tiled=True)
        first_sum = scatter_finish(where, sums)
    else:
        moving = exchange_start(total, where)
        first_sum = scatter_finish(where, sums)
        sum_norms(2)
        moving = exchange_middle(*moving, arriving[1])
        sum_norms(3)
        near = exchange_finish(moving, arriving[2])
    far = swap_x(near)
    for index in range(2 if split is None else 4, len(steps) - 1):
        sum_norms(index)
    norms = own_sums["norms"]
    gains_total, biases_total = call(
        norms_kernel, [sds(LAYERS, 2, width, dtype=F32)] * 2, norms, steps[-1](norms)
    )
    received[1] = [total_call(above["first"]), total_call(above["second"])]
    received[0] = [first_sum, second_sum]
    returned = call(
        functools.partial(last_kernel, split is not None), [sds(count, part, width, dtype=F32)],
        dealing_order, where, near, far, swap_core(near), swap_core(far), scalars=2,
        after=first_sum[1:],
    )[0]

    shapes = (
        jnp.swapaxes(project_weight, 1, 2), gate_up_weight, output_weight,
        jnp.swapaxes(down_weight, 1, 2),
    )
    project_grad, gate_up_grad, output_grad, down_grad = call(
        functools.partial(grads_kernel, tuple(tuple(len(g) for g in r) for r in received)),
        [sds(*w.shape, dtype=F32) for w in shapes],
        *[r for groups in received for group in groups for r in group],
    )
    return (
        layer_outputs[0][None], returned, jnp.swapaxes(project_grad, 1, 2), gate_up_grad, output_grad,
        jnp.swapaxes(down_grad, 1, 2), gains_total, biases_total,
    )


def solution(mesh):
    placed = (
        P(None, "dp", None),
        P(),
        P(),
        P(None, "dp", None, "tensor"),
        P(None, "dp", None, "tensor"),
        P(None, "tensor", "dp"),
        P(None, "tensor", "dp"),
        P(),
        P(),
        P("dp", "tensor", None),
    )
    return jax.shard_map(
        on_device,
        mesh=mesh,
        in_specs=placed,
        out_specs=(
            P("dp", "tensor", None),
            P(None, "dp", None),
            P(None, "dp", None, "tensor"),
            P(None, "dp", None, "tensor"),
            P(None, "tensor", "dp"),
            P(None, "tensor", "dp"),
            P(),
            P(),
        ),
        check_vma=False,
    )
```

time: 603 us -> 521 us (0.86)
  local copies, waits for them, and re-layouts: 64.7 us -> 14.4 us
  other arithmetic: 40 us -> 0.31 us
  between operations: 18 us -> 3.75 us
  Pallas kernels: 118 us -> 129 us
  starting transfers between devices: 87.5 us -> 97.6 us
    ppermute x21 -> x49, starting transfers between devices: 30 us -> 80.4 us  [swap_dp(): lax.ppermute(value, 'dp', [(i, i ^ step) for i in range(lax.axis_size('dp...]
    unnamed x347 -> x72, local copies, waits for them, and re-layouts: 55.5 us -> 10.5 us
    all_to_all x6 -> x0, starting transfers between devices: 30.4 us -> none  [the longest x4 19.5 us: scatter_sum(): lax.all_to_all(pair, 'dp', 0, 0, axis_index_groups=groups, tiled=True)]
    ppermute x18, waiting for transfers between devices: 101 us -> 77.2 us  [swap_x(): lax.ppermute(value, 'tensor', [(i, i ^ 2) for i in range(lax.axis_size('t...]
    ppermute x21 -> x49, waiting for transfers between devices: 144 us -> 167 us  [swap_dp(): lax.ppermute(value, 'dp', [(i, i ^ step) for i in range(lax.axis_size('dp...]
    convert_element_type x20 -> x0, other arithmetic: 14.3 us -> none  [the longest x4 8.15 us: scatter_sum(): pair = (kept.astype(F32) + swap_dp(sent, 1).astype(F32)).astype(BF16)]
    all_to_all x6 -> x0, waiting for transfers between devices: 12.7 us -> none  [the longest x1 10.1 us: deal(): lax.all_to_all(picked, 'dp', split_axis=0, concat_axis=0, tiled=True)]
    ppermute x32 -> x33, waiting for transfers between devices: 2.74 us -> 14.4 us  [swap_core(): lax.ppermute(value, 'tensor', [(i, i ^ 1) for i in range(lax.axis_size('t...]
  transfers between devices with their start and end apart: 81 -> 102, of which waited for: 35 -> 57; matrix products, arithmetic and copies ran while one was open for 7% -> 1% of each run, Pallas kernels for 20% -> 19%
where the time goes in v2:
time: 521 us; the launch traced here: 512 us
  waiting for transfers between devices  267 us (51%)
  Pallas kernels  129 us (25%)
  starting transfers between devices  97.6 us (19%)
  local copies, waits for them, and re-layouts  14.4 us (3%)
    ppermute x49, waiting for transfers between devices, swap_dp(): lax.ppermute(value, 'dp', [(i, i ^ step) for i in range(lax.axis_size('dp...  167 us
    pallas_call x103, Pallas kernels, call(): pl.pallas_call(body, in_specs=[smem] * scalars + [vmem] * (used - scalars...  126 us
    ppermute x49, starting transfers between devices, swap_dp(): lax.ppermute(value, 'dp', [(i, i ^ step) for i in range(lax.axis_size('dp...  80.4 us
    ppermute x18, waiting for transfers between devices, swap_x(): lax.ppermute(value, 'tensor', [(i, i ^ 2) for i in range(lax.axis_size('t...  77.2 us
    ppermute x33, waiting for transfers between devices, swap_core(): lax.ppermute(value, 'tensor', [(i, i ^ 1) for i in range(lax.axis_size('t...  14.4 us
    unnamed x72, local copies, waits for them, and re-layouts  10.5 us
  transfers between devices with their start and end apart: 102, of which 57 were waited for; matrix products, arithmetic and copies ran while one was open for 1% of the time, Pallas kernels for 19%

profile of v2, /device:TPU:0, one launch (start us, length us, event | category | flops | bytes accessed | tf_op | source)
XLA Modules:
  0.0 512.2 jit_solution(8050496561579981186)
XLA Ops:
  6.4 3.0 collective-permute-start.2
  9.4 2.6 collective-permute-start.1
  17.7 5.0 collective-permute-done.2.refs_2_
  22.7 15.0 %collective-permute-done.1.refs_1_.refs_3_ = bf16[96,3072]{1,0:T(8,128)(2,1)S(1)} collective-permute-done((bf16[96,3072]{1,0:T(8,128)(2,1)S(1)}, bf16[96,3072]{1,0:T(8,128)(2,1)S(1)}, u32[]{:S(2)}, u32[]{:S(2)}) %collective-permute-start.1) | collective-permute-done | bytes 589856 | tf_op jit(solution)/shard_map/ppermute | solution.py:84
  37.8 3.6 collective-permute-start.6
  43.4 17.2 %collective-permute-done.refs_1_ = bf16[4,32,768]{2,1,0:T(8,128)(2,1)S(1)} collective-permute-done((bf16[4,32,768]{2,1,0:T(8,128)(2,1)S(1)}, bf16[4,32,768]{2,1,0:T(8,128)(2,1)S(1)}, u32[]{:S(2)}, u32[]{:S(2)}) %collective-permute-start) | collective-permute-done | bytes 196640 | tf_op jit(solution)/shard_map/ppermute | solution.py:84
  62.0 5.9 %collective-permute-start.12 = (bf16[96,3072]{1,0:T(8,128)(2,1)}, bf16[96,3072]{1,0:T(8,128)(2,1)}, u32[]{:S(2)}, u32[]{:S(2)}) collective-permute-start(bf16[96,3072]{1,0:T(8,128)(2,1)} %shard_map.183.refs_4_), channel_id=1, source_target_pairs={{0,8},{4,12},{8,0},{12,4},{16,24},{20,28},{24,16},{28,20},{1,9},{5... | collective-permute-start | bytes 1769480 | tf_op jit(solution)/shard_map/ppermute | solution.py:84
  69.6 2.6 collective-permute-start.5
  72.3 13.0 %collective-permute-done.3.refs_1_ = bf16[2,32,768]{2,1,0:T(8,128)(2,1)S(1)} collective-permute-done((bf16[2,32,768]{2,1,0:T(8,128)(2,1)S(1)}, bf16[2,32,768]{2,1,0:T(8,128)(2,1)S(1)}, u32[]{:S(2)}, u32[]{:S(2)}) %collective-permute-start.3) | collective-permute-done | bytes 98336 | tf_op jit(solution)/shard_map/ppermute | solution.py:84
  85.3 2.7 collective-permute-done.5.refs_3_
  98.7 7.7 %collective-permute-done.13.refs_8_ = bf16[96,3072]{1,0:T(8,128)(2,1)S(1)} collective-permute-done((bf16[96,3072]{1,0:T(8,128)(2,1)}, bf16[96,3072]{1,0:T(8,128)(2,1)S(1)}, u32[]{:S(2)}, u32[]{:S(2)}) %collective-permute-start.13) | collective-permute-done | bytes 589856 | tf_op jit(solution)/shard_map/ppermute | solution.py:84
  106.4 4.6 collective-permute-done.14.refs_11_.refs_3_
  116.2 2.2 shard_map.189
  122.6 2.5 shard_map.192
  127.8 6.6 %collective-permute-done.18.refs_18_.refs_7_ = bf16[96,1536]{1,0:T(8,128)(2,1)S(1)} collective-permute-done((bf16[96,1536]{1,0:T(8,128)(2,1)S(1)}, bf16[96,1536]{1,0:T(8,128)(2,1)S(1)}, u32[]{:S(2)}, u32[]{:S(2)}) %collective-permute-start.18) | collective-permute-done | bytes 294944 | tf_op jit(solution)/shard_map/ppermute | solution.py:84
  141.7 8.5 %collective-permute-done.25.refs_23_.refs_9_ = bf16[96,1536]{1,0:T(8,128)(2,1)S(1)} collective-permute-done((bf16[96,1536]{1,0:T(8,128)(2,1)S(1)}, bf16[96,1536]{1,0:T(8,128)(2,1)S(1)}, u32[]{:S(2)}, u32[]{:S(2)}) %collective-permute-start.25) | collective-permute-done | bytes 294944 | tf_op jit(solution)/shard_map/ppermute | solution.py:84
  150.2 6.6 %collective-permute-done.27.refs_25_.refs_6_ = bf16[96,1536]{1,0:T(8,128)(2,1)S(1)} collective-permute-done((bf16[96,1536]{1,0:T(8,128)(2,1)S(1)}, bf16[96,1536]{1,0:T(8,128)(2,1)S(1)}, u32[]{:S(2)}, u32[]{:S(2)}) %collective-permute-start.27) | collective-permute-done | bytes 294944 | tf_op jit(solution)/shard_map/ppermute | solution.py:84
  166.8 6.6 %collective-permute-done.29.refs_27_.refs_11_ = bf16[96,1536]{1,0:T(8,128)(2,1)S(1)} collective-permute-done((bf16[96,1536]{1,0:T(8,128)(2,1)S(1)}, bf16[96,1536]{1,0:T(8,128)(2,1)S(1)}, u32[]{:S(2)}, u32[]{:S(2)}) %collective-permute-start.29) | collective-permute-done | bytes 294944 | tf_op jit(solution)/shard_map/ppermute | solution.py:84
  175.1 4.4 collective-permute-done.34.refs_29_.refs_10_
  182.3 7.8 %collective-permute-done.36.refs_12_ = bf16[96,1536]{1,0:T(8,128)(2,1)S(1)} collective-permute-done((bf16[96,1536]{1,0:T(8,128)(2,1)S(1)}, bf16[96,1536]{1,0:T(8,128)(2,1)S(1)}, u32[]{:S(2)}, u32[]{:S(2)}) %collective-permute-start.36) | collective-permute-done | bytes 294944 | tf_op jit(solution)/shard_map/ppermute | solution.py:84
  191.1 2.3 shard_map.206
  193.4 2.2 shard_map.207
  195.7 2.2 shard_map.208
  198.9 2.2 shard_map.210
  201.4 2.2 shard_map.211
  203.7 5.9 %collective-permute-done.38.refs_2_ = bf16[256,768]{1,0:T(8,128)(2,1)S(1)} collective-permute-done((bf16[256,768]{1,0:T(8,128)(2,1)S(1)}, bf16[256,768]{1,0:T(8,128)(2,1)S(1)}, u32[]{:S(2)}, u32[]{:S(2)}) %collective-permute-start.38) | collective-permute-done | bytes 393248 | tf_op jit(solution)/shard_map/ppermute | solution.py:80
  214.9 9.7 %collective-permute-done.43.refs_2_ = bf16[256,768]{1,0:T(8,128)(2,1)S(1)} collective-permute-done((bf16[256,768]{1,0:T(8,128)(2,1)S(1)}, bf16[256,768]{1,0:T(8,128)(2,1)S(1)}, u32[]{:S(2)}, u32[]{:S(2)}) %collective-permute-start.43) | collective-permute-done | bytes 393248 | tf_op jit(solution)/shard_map/ppermute | solution.py:80
  232.2 8.1 %collective-permute-done.42.refs_2_ = bf16[256,768]{1,0:T(8,128)(2,1)S(1)} collective-permute-done((bf16[256,768]{1,0:T(8,128)(2,1)S(1)}, bf16[256,768]{1,0:T(8,128)(2,1)S(1)}, u32[]{:S(2)}, u32[]{:S(2)}) %collective-permute-start.42) | collective-permute-done | bytes 393248 | tf_op jit(solution)/shard_map/ppermute | solution.py:80
  241.5 7.3 %collective-permute-done.46.refs_2_ = bf16[256,768]{1,0:T(8,128)(2,1)S(1)} collective-permute-done((bf16[256,768]{1,0:T(8,128)(2,1)S(1)}, bf16[256,768]{1,0:T(8,128)(2,1)S(1)}, u32[]{:S(2)}, u32[]{:S(2)}) %collective-permute-start.46) | collective-permute-done | bytes 393248 | tf_op jit(solution)/shard_map/ppermute | solution.py:80
  251.4 5.2 %collective-permute-done.47.refs_2_ = bf16[256,768]{1,0:T(8,128)(2,1)S(1)} collective-permute-done((bf16[256,768]{1,0:T(8,128)(2,1)S(1)}, bf16[256,768]{1,0:T(8,128)(2,1)S(1)}, u32[]{:S(2)}, u32[]{:S(2)}) %collective-permute-start.47) | collective-permute-done | bytes 393248 | tf_op jit(solution)/shard_map/ppermute | solution.py:80
  262.0 2.2 shard_map.228
  269.3 2.2 shard_map.232
  273.4 5.0 shard_map.234
  281.3 9.6 %collective-permute-done.53.refs_2_ = bf16[256,768]{1,0:T(8,128)(2,1)S(1)} collective-permute-done((bf16[256,768]{1,0:T(8,128)(2,1)S(1)}, bf16[256,768]{1,0:T(8,128)(2,1)S(1)}, u32[]{:S(2)}, u32[]{:S(2)}) %collective-permute-start.53) | collective-permute-done | bytes 393248 | tf_op jit(solution)/shard_map/ppermute | solution.py:80
  290.8 3.8 collective-permute-done.54.refs_50_.refs_2_
  298.1 6.4 %shard_map.237 = (bf16[512,192]{1,0:T(8,128)(2,1)S(1)}, f32[1024,256]{1,0:T(8,128)S(1)}, f32[1024,192]{1,0:T(8,128)S(1)}) custom-call(bf16[1024,256]{1,0:T(8,128)(2,1)S(1)} %get-tuple-element.250.refs_0_.refs_33_.refs_35_.refs_36_.refs_34_.refs_48_.refs_37_, bf16[512,192]{1,0:T(8,128)(2,1)S(1)} %shard_map.236.refs_1_.refs_47_, ...), custom_call_target="tpu_custom_call" | custom-call | flops 4026531 | bytes 5144 | tf_op jit(solution)/shard_map/pallas_call | solution.py:56
  304.5 2.3 collective-permute-done.52.refs_2_
  310.0 7.4 %shard_map.240 = (bf16[1024,576]{1,0:T(8,128)(2,1)S(1)}, f32[1024,256]{1,0:T(8,128)}, f32[1024,192]{1,0:T(8,128)S(1)}) custom-call(bf16[1024,256]{1,0:T(8,128)(2,1)S(1)} %get-tuple-element.250.refs_0_.refs_33_.refs_35_.refs_36_.refs_34_.refs_48_.refs_37_, bf16[512,192]{1,0:T(8,128)(2,1)S(1)} %shard_map.239.refs_1_.refs_49_, ...), custom_call_target="tpu_custom_call" | custom-call | flops 4026531 | bytes 8159 | tf_op jit(solution)/shard_map/pallas_call | solution.py:56
  327.3 2.5 shard_map.248
  329.8 8.1 %collective-permute-done.62.refs_2_ = bf16[256,768]{1,0:T(8,128)(2,1)S(1)} collective-permute-done((bf16[256,768]{1,0:T(8,128)(2,1)S(1)}, bf16[256,768]{1,0:T(8,128)(2,1)S(1)}, u32[]{:S(2)}, u32[]{:S(2)}) %collective-permute-start.62) | collective-permute-done | bytes 393248 | tf_op jit(solution)/shard_map/ppermute | solution.py:80
  346.6 9.7 %collective-permute-done.61.refs_2_ = bf16[256,768]{1,0:T(8,128)(2,1)S(1)} collective-permute-done((bf16[256,768]{1,0:T(8,128)(2,1)S(1)}, bf16[256,768]{1,0:T(8,128)(2,1)S(1)}, u32[]{:S(2)}, u32[]{:S(2)}) %collective-permute-start.61) | collective-permute-done | bytes 393248 | tf_op jit(solution)/shard_map/ppermute | solution.py:80
  356.3 5.2 %collective-permute-done.65.refs_36_.refs_2_ = bf16[96,2304]{1,0:T(8,128)(2,1)S(1)} collective-permute-done((bf16[96,2304]{1,0:T(8,128)(2,1)S(1)}, bf16[96,2304]{1,0:T(8,128)(2,1)S(1)}, u32[]{:S(2)}, u32[]{:S(2)}) %collective-permute-start.65) | collective-permute-done | bytes 442400 | tf_op jit(solution)/shard_map/ppermute | solution.py:84
  363.7 2.3 shard_map.254
  370.8 7.1 %collective-permute-done.72.refs_2_ = bf16[4,96,768]{2,1,0:T(8,128)(2,1)S(1)} collective-permute-done((bf16[4,96,768]{2,1,0:T(8,128)(2,1)S(1)}, bf16[4,96,768]{2,1,0:T(8,128)(2,1)S(1)}, u32[]{:S(2)}, u32[]{:S(2)}) %collective-permute-start.72) | collective-permute-done | bytes 589856 | tf_op jit(solution)/shard_map/ppermute | solution.py:84
  378.6 4.5 shard_map.258
  385.7 4.8 collective-permute-start.74
  390.9 3.7 collective-permute-done.74.refs_23_.refs_1_
  397.2 2.2 collective-permute-done.77.refs_21_.refs_2_
  401.9 6.3 %shard_map.261 = (bf16[512,192]{1,0:T(8,128)(2,1)S(1)}, f32[1024,256]{1,0:T(8,128)S(1)}, f32[1024,192]{1,0:T(8,128)S(1)}) custom-call(bf16[1024,256]{1,0:T(8,128)(2,1)S(1)} %get-tuple-element.210.refs_0_.refs_5_.refs_8_.refs_16_.refs_9_.refs_7_.refs_6_.refs_20_.refs_12_.refs_17_.refs_11_, bf16[512,192]{1,0:T(8,128)(2,1)S(1)} %shard_map.260.refs_1_.refs_22_, ...), custom_call_target="tpu_custom_call" | custom-call | flops 4026531 | bytes 5144 | tf_op jit(solution)/shard_map/pallas_call | solution.py:56
  412.1 7.5 %shard_map.265 = (bf16[1024,576]{1,0:T(8,128)(2,1)S(1)}, f32[1024,256]{1,0:T(8,128)}, f32[1024,192]{1,0:T(8,128)S(1)}) custom-call(bf16[1024,256]{1,0:T(8,128)(2,1)S(1)} %get-tuple-element.210.refs_0_.refs_5_.refs_8_.refs_16_.refs_9_.refs_7_.refs_6_.refs_20_.refs_12_.refs_17_.refs_11_, bf16[512,192]{1,0:T(8,128)(2,1)S(1)} %shard_map.264.refs_1_.refs_24_, ...), custom_call_target="tpu_custom_call" | custom-call | flops 4026531 | bytes 8159 | tf_op jit(solution)/shard_map/pallas_call | solution.py:56
  419.5 3.8 collective-permute-done.80.refs_16_.refs_4_
  427.9 2.5 shard_map.269
  436.8 7.6 %collective-permute-done.85.refs_1_ = f32[8,768]{1,0:T(8,128)S(1)} collective-permute-done((f32[8,768]{1,0:T(8,128)S(1)}, f32[8,768]{1,0:T(8,128)S(1)}, u32[]{:S(2)}, u32[]{:S(2)}) %collective-permute-start.85) | collective-permute-done | bytes 24608 | tf_op jit(solution)/shard_map/ppermute | solution.py:1048
  444.4 2.2 collective-permute-start.93
  446.6 11.8 %collective-permute-done.84.refs_2_.refs_6_ = bf16[96,2304]{1,0:T(8,128)(2,1)S(1)} collective-permute-done((bf16[96,2304]{1,0:T(8,128)(2,1)S(1)}, bf16[96,2304]{1,0:T(8,128)(2,1)S(1)}, u32[]{:S(2)}, u32[]{:S(2)}) %collective-permute-start.84) | collective-permute-done | bytes 442400 | tf_op jit(solution)/shard_map/ppermute | solution.py:84
  461.8 4.6 collective-permute-done.88.refs_1_
  471.9 3.6 collective-permute-done.94.refs_1_
  475.5 3.3 collective-permute-done.91.refs_2_
  479.2 8.4 %collective-permute-done.95.refs_3_ = bf16[8,64,384]{2,1,0:T(8,128)(2,1)S(1)} collective-permute-done((bf16[8,64,384]{2,1,0:T(8,128)(2,1)S(1)}, bf16[8,64,384]{2,1,0:T(8,128)(2,1)S(1)}, u32[]{:S(2)}, u32[]{:S(2)}) %collective-permute-start.95) | collective-permute-done | bytes 393248 | tf_op jit(solution)/shard_map/ppermute | solution.py:80
  487.6 3.8 collective-permute-start.101
  491.4 2.6 collective-permute-start.99
  497.4 2.8 collective-permute-done.98.refs_6_.refs_1_
  500.2 5.2 %collective-permute-done.99.refs_7_.refs_2_ = bf16[96,768]{1,0:T(8,128)(2,1)S(1)} collective-permute-done((bf16[96,768]{1,0:T(8,128)(2,1)S(1)}, bf16[96,768]{1,0:T(8,128)(2,1)S(1)}, u32[]{:S(2)}, u32[]{:S(2)}) %collective-permute-start.99) | collective-permute-done | bytes 147488 | tf_op jit(solution)/shard_map/ppermute | solution.py:84
  505.4 2.4 shard_map.282.refs_10_
  (335 shorter events, 165.9 us)
Async XLA Ops:
  6.4 16.4 %collective-permute-start.2 = (bf16[96,3072]{1,0:T(8,128)(2,1)S(1)}, bf16[96,3072]{1,0:T(8,128)(2,1)S(1)}, u32[]{:S(2)}, u32[]{:S(2)}) collective-permute-start(bf16[96,3072]{1,0:T(8,128)(2,1)S(1)} %shard_map.179.refs_2_.refs_0_.refs_1_), channel_id=1, source_target_pairs={{0,4},{4,0},{8,12},{12,8},{16,20},{20,16},{24,28},{28,24},{1,5},{5... | collective-permute-start | bytes 1769480 | tf_op jit(solution)/shard_map/ppermute | solution.py:84
  9.4 28.3 %collective-permute-start.1 = (bf16[96,3072]{1,0:T(8,128)(2,1)S(1)}, bf16[96,3072]{1,0:T(8,128)(2,1)S(1)}, u32[]{:S(2)}, u32[]{:S(2)}) collective-permute-start(bf16[96,3072]{1,0:T(8,128)(2,1)S(1)} %shard_map.179.refs_2_.refs_0_.refs_1_), channel_id=1, source_target_pairs={{0,16},{4,20},{8,24},{12,28},{16,0},{20,4},{24,8},{28,12},{1,17},{... | collective-permute-start | bytes 1769480 | tf_op jit(solution)/shard_map/ppermute | solution.py:84
  37.8 22.8 %collective-permute-start.6 = (bf16[96,3072]{1,0:T(8,128)(2,1)S(1)}, bf16[96,3072]{1,0:T(8,128)(2,1)}, u32[]{:S(2)}, u32[]{:S(2)}) collective-permute-start(bf16[96,3072]{1,0:T(8,128)(2,1)S(1)} %shard_map.181.refs_2_), channel_id=1, source_target_pairs={{0,24},{4,28},{8,16},{12,20},{16,8},{20,12},{24,0},{28,4},{1,25},{... | collective-permute-start | bytes 1769480 | tf_op jit(solution)/shard_map/ppermute | solution.py:84
  41.3 19.8 %collective-permute-start.7 = (bf16[96,3072]{1,0:T(8,128)(2,1)S(1)}, bf16[96,3072]{1,0:T(8,128)(2,1)S(1)}, u32[]{:S(2)}, u32[]{:S(2)}) collective-permute-start(bf16[96,3072]{1,0:T(8,128)(2,1)S(1)} %collective-permute-done.1.refs_1_.refs_3_), channel_id=1, source_target_pairs={{0,4},{4,0},{8,12},{12,8},{16,20},{20,16},{24,28},{28,24},{1,5},{5... | collective-permute-start | bytes 1769480 | tf_op jit(solution)/shard_map/ppermute | solution.py:84
  41.8 18.7 %collective-permute-start = (bf16[4,32,768]{2,1,0:T(8,128)(2,1)S(1)}, bf16[4,32,768]{2,1,0:T(8,128)(2,1)S(1)}, u32[]{:S(2)}, u32[]{:S(2)}) collective-permute-start(bf16[4,32,768]{2,1,0:T(8,128)(2,1)S(1)} %get-tuple-element.202), channel_id=1, source_target_pairs={{0,4},{4,0},{8,12},{12,8},{16,20},{20,16},{24,28},{28,24},{1,5},{5... | collective-permute-start | bytes 589832 | tf_op jit(solution)/shard_map/ppermute | solution.py:84
  60.6 29.1 %collective-permute-start.11 = (bf16[96,3072]{1,0:T(8,128)(2,1)}, bf16[96,3072]{1,0:T(8,128)(2,1)}, u32[]{:S(2)}, u32[]{:S(2)}) collective-permute-start(bf16[96,3072]{1,0:T(8,128)(2,1)} %collective-permute-done.6.refs_1_.refs_5_), channel_id=1, source_target_pairs={{0,4},{4,0},{8,12},{12,8},{16,20},{20,16},{24,28},{28,24},{1,5},{5... | collective-permute-start | bytes 1769480 | tf_op jit(solution)/shard_map/ppermute | solution.py:84
  62.0 27.6 %collective-permute-start.12 = (bf16[96,3072]{1,0:T(8,128)(2,1)}, bf16[96,3072]{1,0:T(8,128)(2,1)}, u32[]{:S(2)}, u32[]{:S(2)}) collective-permute-start(bf16[96,3072]{1,0:T(8,128)(2,1)} %shard_map.183.refs_4_), channel_id=1, source_target_pairs={{0,8},{4,12},{8,0},{12,4},{16,24},{20,28},{24,16},{28,20},{1,9},{5... | collective-permute-start | bytes 1769480 | tf_op jit(solution)/shard_map/ppermute | solution.py:84
  67.9 17.4 %collective-permute-start.3 = (bf16[2,32,768]{2,1,0:T(8,128)(2,1)S(1)}, bf16[2,32,768]{2,1,0:T(8,128)(2,1)S(1)}, u32[]{:S(2)}, u32[]{:S(2)}) collective-permute-start(bf16[2,32,768]{2,1,0:T(8,128)(2,1)S(1)} %get-tuple-element.204), channel_id=1, source_target_pairs={{0,8},{4,12},{8,0},{12,4},{16,24},{20,28},{24,16},{28,20},{1,9},{5... | collective-permute-start | bytes 294920 | tf_op jit(solution)/shard_map/ppermute | solution.py:84
  67.9 17.4 %collective-permute-start.4 = (bf16[2,32,768]{2,1,0:T(8,128)(2,1)S(1)}, bf16[2,32,768]{2,1,0:T(8,128)(2,1)S(1)}, u32[]{:S(2)}, u32[]{:S(2)}) collective-permute-start(bf16[2,32,768]{2,1,0:T(8,128)(2,1)S(1)} %get-tuple-element.205), channel_id=1, source_target_pairs={{0,16},{4,20},{8,24},{12,28},{16,0},{20,4},{24,8},{28,12},{1,17},{... | collective-permute-start | bytes 294920 | tf_op jit(solution)/shard_map/ppermute | solution.py:84
  69.6 18.4 %collective-permute-start.5 = (bf16[2,32,768]{2,1,0:T(8,128)(2,1)S(1)}, bf16[2,32,768]{2,1,0:T(8,128)(2,1)S(1)}, u32[]{:S(2)}, u32[]{:S(2)}) collective-permute-start(bf16[2,32,768]{2,1,0:T(8,128)(2,1)S(1)} %get-tuple-element.206), channel_id=1, source_target_pairs={{0,24},{4,28},{8,16},{12,20},{16,8},{20,12},{24,0},{28,4},{1,25},{... | collective-permute-start | bytes 294920 | tf_op jit(solution)/shard_map/ppermute | solution.py:84
  93.1 17.9 %collective-permute-start.14 = (bf16[96,3072]{1,0:T(8,128)(2,1)S(1)}, bf16[96,3072]{1,0:T(8,128)(2,1)S(1)}, u32[]{:S(2)}, u32[]{:S(2)}) collective-permute-start(bf16[96,3072]{1,0:T(8,128)(2,1)S(1)} %get-tuple-element.207.refs_1_), channel_id=1, source_target_pairs={{0,8},{4,12},{8,0},{12,4},{16,24},{20,28},{24,16},{28,20},{1,9},{5... | collective-permute-start | bytes 1769480 | tf_op jit(solution)/shard_map/ppermute | solution.py:84
  93.2 13.2 %collective-permute-start.13 = (bf16[96,3072]{1,0:T(8,128)(2,1)}, bf16[96,3072]{1,0:T(8,128)(2,1)S(1)}, u32[]{:S(2)}, u32[]{:S(2)}) collective-permute-start(bf16[96,3072]{1,0:T(8,128)(2,1)} %collective-permute-done.12.refs_4_.refs_7_), channel_id=1, source_target_pairs={{0,4},{4,0},{8,12},{12,8},{16,20},{20,16},{24,28},{28,24},{1,5},{5... | collective-permute-start | bytes 1769480 | tf_op jit(solution)/shard_map/ppermute | solution.py:84
  95.0 17.8 %collective-permute-start.8 = (bf16[8,32,768]{2,1,0:T(8,128)(2,1)S(1)}, bf16[8,32,768]{2,1,0:T(8,128)(2,1)S(1)}, u32[]{:S(2)}, u32[]{:S(2)}) collective-permute-start(bf16[8,32,768]{2,1,0:T(8,128)(2,1)S(1)} %shard_map.184.refs_6_.refs_1_), channel_id=1, source_target_pairs={{0,1},{1,0},{2,3},{3,2},{4,5},{5,4},{6,7},{7,6},{8,9},{9,8},{10,11... | collective-permute-start | bytes 1179656 | tf_op jit(solution)/shard_map/ppermute | solution.py:76
  97.3 15.6 %collective-permute-start.10 = (bf16[8,32,768]{2,1,0:T(8,128)(2,1)}, bf16[8,32,768]{2,1,0:T(8,128)(2,1)S(1)}, u32[]{:S(2)}, u32[]{:S(2)}) collective-permute-start(bf16[8,32,768]{2,1,0:T(8,128)(2,1)} %collective-permute-done.9.refs_3_), channel_id=1, source_target_pairs={{0,1},{1,0},{2,3},{3,2},{4,5},{5,4},{6,7},{7,6},{8,9},{9,8},{10,11... | collective-permute-start | bytes 1179656 | tf_op jit(solution)/shard_map/ppermute | solution.py:76
  97.5 24.9 %collective-permute-start.16 = (bf16[96,1536]{1,0:T(8,128)(2,1)S(1)}, bf16[96,1536]{1,0:T(8,128)(2,1)S(1)}, u32[]{:S(2)}, u32[]{:S(2)}) collective-permute-start(bf16[96,1536]{1,0:T(8,128)(2,1)S(1)} %get-tuple-element.220), channel_id=1, source_target_pairs={{0,16},{4,20},{8,24},{12,28},{16,0},{20,4},{24,8},{28,12},{1,17},{... | collective-permute-start | bytes 884744 | tf_op jit(solution)/shard_map/ppermute | solution.py:84
  118.5 15.9 %collective-permute-start.18 = (bf16[96,1536]{1,0:T(8,128)(2,1)S(1)}, bf16[96,1536]{1,0:T(8,128)(2,1)S(1)}, u32[]{:S(2)}, u32[]{:S(2)}) collective-permute-start(bf16[96,1536]{1,0:T(8,128)(2,1)S(1)} %get-tuple-element.208.refs_12_), channel_id=1, source_target_pairs={{0,16},{4,20},{8,24},{12,28},{16,0},{20,4},{24,8},{28,12},{1,17},{... | collective-permute-start | bytes 884744 | tf_op jit(solution)/shard_map/ppermute | solution.py:84
  118.6 15.8 %collective-permute-start.19 = (bf16[96,3072]{1,0:T(8,128)(2,1)S(1)}, bf16[96,3072]{1,0:T(8,128)(2,1)S(1)}, u32[]{:S(2)}, u32[]{:S(2)}) collective-permute-start(bf16[96,3072]{1,0:T(8,128)(2,1)S(1)} %collective-permute-done.14.refs_11_.refs_3_), channel_id=1, source_target_pairs={{0,4},{4,0},{8,12},{12,8},{16,20},{20,16},{24,28},{28,24},{1,5},{5... | collective-permute-start | bytes 1769480 | tf_op jit(solution)/shard_map/ppermute | solution.py:84
  122.5 11.8 %collective-permute-start.17 = (bf16[256,768]{1,0:T(8,128)(2,1)S(1)}, bf16[256,768]{1,0:T(8,128)(2,1)S(1)}, u32[]{:S(2)}, u32[]{:S(2)}) collective-permute-start(bf16[256,768]{1,0:T(8,128)(2,1)S(1)} %get-tuple-element.223.refs_11_), channel_id=1, source_target_pairs={{0,2},{1,3},{2,0},{3,1},{4,6},{5,7},{6,4},{7,5},{8,10},{9,11},{10,... | collective-permute-start | bytes 1179656 | tf_op jit(solution)/shard_map/ppermute | solution.py:80
  134.9 22.0 %collective-permute-start.26 = (bf16[96,3072]{1,0:T(8,128)(2,1)S(1)}, bf16[96,3072]{1,0:T(8,128)(2,1)S(1)}, u32[]{:S(2)}, u32[]{:S(2)}) collective-permute-start(bf16[96,3072]{1,0:T(8,128)(2,1)S(1)} %get-tuple-element.207.refs_1_), channel_id=1, source_target_pairs={{0,4},{4,0},{8,12},{12,8},{16,20},{20,16},{24,28},{28,24},{1,5},{5... | collective-permute-start | bytes 1769480 | tf_op jit(solution)/shard_map/ppermute | solution.py:84
  139.1 17.8 %collective-permute-start.24 = (bf16[256,768]{1,0:T(8,128)(2,1)S(1)}, bf16[256,768]{1,0:T(8,128)(2,1)S(1)}, u32[]{:S(2)}, u32[]{:S(2)}) collective-permute-start(bf16[256,768]{1,0:T(8,128)(2,1)S(1)} %get-tuple-element.230.refs_20_), channel_id=1, source_target_pairs={{0,2},{1,3},{2,0},{3,1},{4,6},{5,7},{6,4},{7,5},{8,10},{9,11},{10,... | collective-permute-start | bytes 1179656 | tf_op jit(solution)/shard_map/ppermute | solution.py:80
  139.1 11.2 %collective-permute-start.25 = (bf16[96,1536]{1,0:T(8,128)(2,1)S(1)}, bf16[96,1536]{1,0:T(8,128)(2,1)S(1)}, u32[]{:S(2)}, u32[]{:S(2)}) collective-permute-start(bf16[96,1536]{1,0:T(8,128)(2,1)S(1)} %get-tuple-element.220), channel_id=1, source_target_pairs={{0,24},{4,28},{8,16},{12,20},{16,8},{20,12},{24,0},{28,4},{1,25},{... | collective-permute-start | bytes 884744 | tf_op jit(solution)/shard_map/ppermute | solution.py:84
  141.1 15.8 %collective-permute-start.27 = (bf16[96,1536]{1,0:T(8,128)(2,1)S(1)}, bf16[96,1536]{1,0:T(8,128)(2,1)S(1)}, u32[]{:S(2)}, u32[]{:S(2)}) collective-permute-start(bf16[96,1536]{1,0:T(8,128)(2,1)S(1)} %collective-permute-done.16.refs_13_.refs_5_), channel_id=1, source_target_pairs={{0,4},{4,0},{8,12},{12,8},{16,20},{20,16},{24,28},{28,24},{1,5},{5... | collective-permute-start | bytes 884744 | tf_op jit(solution)/shard_map/ppermute | solution.py:84
  160.5 14.2 %collective-permute-start.23 = (bf16[256,768]{1,0:T(8,128)(2,1)S(1)}, bf16[256,768]{1,0:T(8,128)(2,1)S(1)}, u32[]{:S(2)}, u32[]{:S(2)}) collective-permute-start(bf16[256,768]{1,0:T(8,128)(2,1)S(1)} %get-tuple-element.236.refs_26_), channel_id=1, source_target_pairs={{0,2},{1,3},{2,0},{3,1},{4,6},{5,7},{6,4},{7,5},{8,10},{9,11},{10,... | collective-permute-start | bytes 1179656 | tf_op jit(solution)/shard_map/ppermute | solution.py:80
  162.2 18.1 %collective-permute-start.33 = (bf16[256,768]{1,0:T(8,128)(2,1)S(1)}, bf16[256,768]{1,0:T(8,128)(2,1)S(1)}, u32[]{:S(2)}, u32[]{:S(2)}) collective-permute-start(bf16[256,768]{1,0:T(8,128)(2,1)S(1)} %get-tuple-element.241.refs_29_), channel_id=1, source_target_pairs={{0,2},{1,3},{2,0},{3,1},{4,6},{5,7},{6,4},{7,5},{8,10},{9,11},{10,... | collective-permute-start | bytes 1179656 | tf_op jit(solution)/shard_map/ppermute | solution.py:80
  162.7 10.6 %collective-permute-start.29 = (bf16[96,1536]{1,0:T(8,128)(2,1)S(1)}, bf16[96,1536]{1,0:T(8,128)(2,1)S(1)}, u32[]{:S(2)}, u32[]{:S(2)}) collective-permute-start(bf16[96,1536]{1,0:T(8,128)(2,1)S(1)} %get-tuple-element.208.refs_12_), channel_id=1, source_target_pairs={{0,24},{4,28},{8,16},{12,20},{16,8},{20,12},{24,0},{28,4},{1,25},{... | collective-permute-start | bytes 884744 | tf_op jit(solution)/shard_map/ppermute | solution.py:84
  164.7 9.9 %collective-permute-start.30 = (bf16[96,1536]{1,0:T(8,128)(2,1)S(1)}, bf16[96,1536]{1,0:T(8,128)(2,1)S(1)}, u32[]{:S(2)}, u32[]{:S(2)}) collective-permute-start(bf16[96,1536]{1,0:T(8,128)(2,1)S(1)} %collective-permute-done.18.refs_18_.refs_7_), channel_id=1, source_target_pairs={{0,4},{4,0},{8,12},{12,8},{16,20},{20,16},{24,28},{28,24},{1,5},{5... | collective-permute-start | bytes 884744 | tf_op jit(solution)/shard_map/ppermute | solution.py:84
  166.2 13.2 %collective-permute-start.34 = (bf16[96,1536]{1,0:T(8,128)(2,1)S(1)}, bf16[96,1536]{1,0:T(8,128)(2,1)S(1)}, u32[]{:S(2)}, u32[]{:S(2)}) collective-permute-start(bf16[96,1536]{1,0:T(8,128)(2,1)S(1)} %collective-permute-done.25.refs_23_.refs_9_), channel_id=1, source_target_pairs={{0,4},{4,0},{8,12},{12,8},{16,20},{20,16},{24,28},{28,24},{1,5},{5... | collective-permute-start | bytes 884744 | tf_op jit(solution)/shard_map/ppermute | solution.py:84
  175.0 16.0 %collective-permute-start.32 = (bf16[256,768]{1,0:T(8,128)(2,1)S(1)}, bf16[256,768]{1,0:T(8,128)(2,1)S(1)}, u32[]{:S(2)}, u32[]{:S(2)}) collective-permute-start(bf16[256,768]{1,0:T(8,128)(2,1)S(1)} %get-tuple-element.242.refs_0_.refs_31_.refs_29_.refs_32_.refs_30_.refs_44_.refs_33_.refs_36_.refs_1_), channel_id=1, source_target_pairs={{0,1},{1,0},{2,3},{3,2},{4,5},{5,4},{6,7},{7,6},{8,9},{9,8},{10,11... | collective-permute-start | bytes 1179656 | tf_op jit(solution)/shard_map/ppermute | solution.py:76
  180.7 10.4 %collective-permute-start.35 = (bf16[256,768]{1,0:T(8,128)(2,1)S(1)}, bf16[256,768]{1,0:T(8,128)(2,1)S(1)}, u32[]{:S(2)}, u32[]{:S(2)}) collective-permute-start(bf16[256,768]{1,0:T(8,128)(2,1)S(1)} %get-tuple-element.246.refs_2_.refs_33_.refs_31_.refs_0_.refs_34_.refs_32_.refs_46_.refs_35_.refs_38_.refs_3_), channel_id=1, source_target_pairs={{0,1},{1,0},{2,3},{3,2},{4,5},{5,4},{6,7},{7,6},{8,9},{9,8},{10,11... | collective-permute-start | bytes 1179656 | tf_op jit(solution)/shard_map/ppermute | solution.py:76
  180.8 9.4 %collective-permute-start.36 = (bf16[96,1536]{1,0:T(8,128)(2,1)S(1)}, bf16[96,1536]{1,0:T(8,128)(2,1)S(1)}, u32[]{:S(2)}, u32[]{:S(2)}) collective-permute-start(bf16[96,1536]{1,0:T(8,128)(2,1)S(1)} %collective-permute-done.29.refs_27_.refs_11_), channel_id=1, source_target_pairs={{0,4},{4,0},{8,12},{12,8},{16,20},{20,16},{24,28},{28,24},{1,5},{5... | collective-permute-start | bytes 884744 | tf_op jit(solution)/shard_map/ppermute | solution.py:84
  198.1 11.6 %collective-permute-start.38 = (bf16[256,768]{1,0:T(8,128)(2,1)S(1)}, bf16[256,768]{1,0:T(8,128)(2,1)S(1)}, u32[]{:S(2)}, u32[]{:S(2)}) collective-permute-start(bf16[256,768]{1,0:T(8,128)(2,1)S(1)} %get-tuple-element.262.refs_39_), channel_id=1, source_target_pairs={{0,2},{1,3},{2,0},{3,1},{4,6},{5,7},{6,4},{7,5},{8,10},{9,11},{10,... | collective-permute-start | bytes 1179656 | tf_op jit(solution)/shard_map/ppermute | solution.py:80
  213.2 11.4 %collective-permute-start.43 = (bf16[256,768]{1,0:T(8,128)(2,1)S(1)}, bf16[256,768]{1,0:T(8,128)(2,1)S(1)}, u32[]{:S(2)}, u32[]{:S(2)}) collective-permute-start(bf16[256,768]{1,0:T(8,128)(2,1)S(1)} %get-tuple-element.269.refs_45_), channel_id=1, source_target_pairs={{0,2},{1,3},{2,0},{3,1},{4,6},{5,7},{6,4},{7,5},{8,10},{9,11},{10,... | collective-permute-start | bytes 1179656 | tf_op jit(solution)/shard_map/ppermute | solution.py:80
  228.4 11.9 %collective-permute-start.42 = (bf16[256,768]{1,0:T(8,128)(2,1)S(1)}, bf16[256,768]{1,0:T(8,128)(2,1)S(1)}, u32[]{:S(2)}, u32[]{:S(2)}) collective-permute-start(bf16[256,768]{1,0:T(8,128)(2,1)S(1)} %get-tuple-element.275.refs_50_), channel_id=1, source_target_pairs={{0,2},{1,3},{2,0},{3,1},{4,6},{5,7},{6,4},{7,5},{8,10},{9,11},{10,... | collective-permute-start | bytes 1179656 | tf_op jit(solution)/shard_map/ppermute | solution.py:80
  230.1 18.6 %collective-permute-start.46 = (bf16[256,768]{1,0:T(8,128)(2,1)S(1)}, bf16[256,768]{1,0:T(8,128)(2,1)S(1)}, u32[]{:S(2)}, u32[]{:S(2)}) collective-permute-start(bf16[256,768]{1,0:T(8,128)(2,1)S(1)} %get-tuple-element.280.refs_55_), channel_id=1, source_target_pairs={{0,2},{1,3},{2,0},{3,1},{4,6},{5,7},{6,4},{7,5},{8,10},{9,11},{10,... | collective-permute-start | bytes 1179656 | tf_op jit(solution)/shard_map/ppermute | solution.py:80
  231.0 25.7 %collective-permute-start.47 = (bf16[256,768]{1,0:T(8,128)(2,1)S(1)}, bf16[256,768]{1,0:T(8,128)(2,1)S(1)}, u32[]{:S(2)}, u32[]{:S(2)}) collective-permute-start(bf16[256,768]{1,0:T(8,128)(2,1)S(1)} %bitcast.203), channel_id=1, source_target_pairs={{0,2},{1,3},{2,0},{3,1},{4,6},{5,7},{6,4},{7,5},{8,10},{9,11},{10,... | collective-permute-start | bytes 1179656 | tf_op jit(solution)/shard_map/ppermute | solution.py:80
  278.4 16.2 %collective-permute-start.54 = (bf16[4,96,768]{2,1,0:T(8,128)(2,1)S(1)}, bf16[4,96,768]{2,1,0:T(8,128)(2,1)S(1)}, u32[]{:S(2)}, u32[]{:S(2)}) collective-permute-start(bf16[4,96,768]{2,1,0:T(8,128)(2,1)S(1)} %get-tuple-element.308.refs_51_), channel_id=1, source_target_pairs={{0,4},{4,0},{8,12},{12,8},{16,20},{20,16},{24,28},{28,24},{1,5},{5... | collective-permute-start | bytes 1769480 | tf_op jit(solution)/shard_map/ppermute | solution.py:84
  279.9 10.9 %collective-permute-start.53 = (bf16[256,768]{1,0:T(8,128)(2,1)S(1)}, bf16[256,768]{1,0:T(8,128)(2,1)S(1)}, u32[]{:S(2)}, u32[]{:S(2)}) collective-permute-start(bf16[256,768]{1,0:T(8,128)(2,1)S(1)} %get-tuple-element.296.refs_61_), channel_id=1, source_target_pairs={{0,2},{1,3},{2,0},{3,1},{4,6},{5,7},{6,4},{7,5},{8,10},{9,11},{10,... | collective-permute-start | bytes 1179656 | tf_op jit(solution)/shard_map/ppermute | solution.py:80
  280.7 26.5 %collective-permute-start.56 = (bf16[4,96,768]{2,1,0:T(8,128)(2,1)S(1)}, bf16[4,96,768]{2,1,0:T(8,128)(2,1)S(1)}, u32[]{:S(2)}, u32[]{:S(2)}) collective-permute-start(bf16[4,96,768]{2,1,0:T(8,128)(2,1)S(1)} %get-tuple-element.310), channel_id=1, source_target_pairs={{0,4},{4,0},{8,12},{12,8},{16,20},{20,16},{24,28},{28,24},{1,5},{5... | collective-permute-start | bytes 1769480 | tf_op jit(solution)/shard_map/ppermute | solution.py:84
  295.2 11.5 %collective-permute-start.52 = (bf16[256,768]{1,0:T(8,128)(2,1)S(1)}, bf16[256,768]{1,0:T(8,128)(2,1)S(1)}, u32[]{:S(2)}, u32[]{:S(2)}) collective-permute-start(bf16[256,768]{1,0:T(8,128)(2,1)S(1)} %get-tuple-element.306.refs_62_), channel_id=1, source_target_pairs={{0,2},{1,3},{2,0},{3,1},{4,6},{5,7},{6,4},{7,5},{8,10},{9,11},{10,... | collective-permute-start | bytes 1179656 | tf_op jit(solution)/shard_map/ppermute | solution.py:80
  296.1 23.0 %collective-permute-start.58 = (bf16[4,96,768]{2,1,0:T(8,128)(2,1)S(1)}, bf16[4,96,768]{2,1,0:T(8,128)(2,1)S(1)}, u32[]{:S(2)}, u32[]{:S(2)}) collective-permute-start(bf16[4,96,768]{2,1,0:T(8,128)(2,1)S(1)} %get-tuple-element.318), channel_id=1, source_target_pairs={{0,4},{4,0},{8,12},{12,8},{16,20},{20,16},{24,28},{28,24},{1,5},{5... | collective-permute-start | bytes 1769480 | tf_op jit(solution)/shard_map/ppermute | solution.py:84
  324.9 13.0 %collective-permute-start.63 = (bf16[96,2304]{1,0:T(8,128)(2,1)S(1)}, bf16[96,2304]{1,0:T(8,128)(2,1)S(1)}, u32[]{:S(2)}, u32[]{:S(2)}) collective-permute-start(bf16[96,2304]{1,0:T(8,128)(2,1)S(1)} %get-tuple-element.325), channel_id=1, source_target_pairs={{0,8},{4,12},{8,0},{12,4},{16,24},{20,28},{24,16},{28,20},{1,9},{5... | collective-permute-start | bytes 1327112 | tf_op jit(solution)/shard_map/ppermute | solution.py:84
  327.0 10.9 %collective-permute-start.62 = (bf16[256,768]{1,0:T(8,128)(2,1)S(1)}, bf16[256,768]{1,0:T(8,128)(2,1)S(1)}, u32[]{:S(2)}, u32[]{:S(2)}) collective-permute-start(bf16[256,768]{1,0:T(8,128)(2,1)S(1)} %get-tuple-element.320.refs_41_), channel_id=1, source_target_pairs={{0,2},{1,3},{2,0},{3,1},{4,6},{5,7},{6,4},{7,5},{8,10},{9,11},{10,... | collective-permute-start | bytes 1179656 | tf_op jit(solution)/shard_map/ppermute | solution.py:80
  338.5 23.0 %collective-permute-start.65 = (bf16[96,2304]{1,0:T(8,128)(2,1)S(1)}, bf16[96,2304]{1,0:T(8,128)(2,1)S(1)}, u32[]{:S(2)}, u32[]{:S(2)}) collective-permute-start(bf16[96,2304]{1,0:T(8,128)(2,1)S(1)} %get-tuple-element.334), channel_id=1, source_target_pairs={{0,16},{4,20},{8,24},{12,28},{16,0},{20,4},{24,8},{28,12},{1,17},{... | collective-permute-start | bytes 1327112 | tf_op jit(solution)/shard_map/ppermute | solution.py:84
  344.9 11.4 %collective-permute-start.61 = (bf16[256,768]{1,0:T(8,128)(2,1)S(1)}, bf16[256,768]{1,0:T(8,128)(2,1)S(1)}, u32[]{:S(2)}, u32[]{:S(2)}) collective-permute-start(bf16[256,768]{1,0:T(8,128)(2,1)S(1)} %get-tuple-element.322.refs_44_), channel_id=1, source_target_pairs={{0,2},{1,3},{2,0},{3,1},{4,6},{5,7},{6,4},{7,5},{8,10},{9,11},{10,... | collective-permute-start | bytes 1179656 | tf_op jit(solution)/shard_map/ppermute | solution.py:80
  362.1 15.7 %collective-permute-start.72 = (bf16[4,96,768]{2,1,0:T(8,128)(2,1)S(1)}, bf16[4,96,768]{2,1,0:T(8,128)(2,1)S(1)}, u32[]{:S(2)}, u32[]{:S(2)}) collective-permute-start(bf16[4,96,768]{2,1,0:T(8,128)(2,1)S(1)} %get-tuple-element.350), channel_id=1, source_target_pairs={{0,4},{4,0},{8,12},{12,8},{16,20},{20,16},{24,28},{28,24},{1,5},{5... | collective-permute-start | bytes 1769480 | tf_op jit(solution)/shard_map/ppermute | solution.py:84
  368.4 16.3 %collective-permute-start.71 = (bf16[96,2304]{1,0:T(8,128)(2,1)S(1)}, bf16[96,2304]{1,0:T(8,128)(2,1)S(1)}, u32[]{:S(2)}, u32[]{:S(2)}) collective-permute-start(bf16[96,2304]{1,0:T(8,128)(2,1)S(1)} %get-tuple-element.349), channel_id=1, source_target_pairs={{0,24},{4,28},{8,16},{12,20},{16,8},{20,12},{24,0},{28,4},{1,25},{... | collective-permute-start | bytes 1327112 | tf_op jit(solution)/shard_map/ppermute | solution.py:84
  370.4 14.3 %collective-permute-start.70 = (bf16[256,768]{1,0:T(8,128)(2,1)S(1)}, bf16[256,768]{1,0:T(8,128)(2,1)S(1)}, u32[]{:S(2)}, u32[]{:S(2)}) collective-permute-start(bf16[256,768]{1,0:T(8,128)(2,1)S(1)} %get-tuple-element.337.refs_37_), channel_id=1, source_target_pairs={{0,2},{1,3},{2,0},{3,1},{4,6},{5,7},{6,4},{7,5},{8,10},{9,11},{10,... | collective-permute-start | bytes 1179656 | tf_op jit(solution)/shard_map/ppermute | solution.py:80
  383.1 16.3 %collective-permute-start.77 = (bf16[4,96,768]{2,1,0:T(8,128)(2,1)S(1)}, bf16[4,96,768]{2,1,0:T(8,128)(2,1)S(1)}, u32[]{:S(2)}, u32[]{:S(2)}) collective-permute-start(bf16[4,96,768]{2,1,0:T(8,128)(2,1)S(1)} %get-tuple-element.352.refs_25_), channel_id=1, source_target_pairs={{0,4},{4,0},{8,12},{12,8},{16,20},{20,16},{24,28},{28,24},{1,5},{5... | collective-permute-start | bytes 1769480 | tf_op jit(solution)/shard_map/ppermute | solution.py:84
  385.3 9.9 %collective-permute-start.73 = (bf16[256,768]{1,0:T(8,128)(2,1)S(1)}, bf16[256,768]{1,0:T(8,128)(2,1)S(1)}, u32[]{:S(2)}, u32[]{:S(2)}) collective-permute-start(bf16[256,768]{1,0:T(8,128)(2,1)S(1)} %get-tuple-element.353.refs_0_.refs_19_.refs_21_.refs_23_.refs_17_.refs_3_.refs_12_.refs_9_), channel_id=1, source_target_pairs={{0,1},{1,0},{2,3},{3,2},{4,5},{5,4},{6,7},{7,6},{8,9},{9,8},{10,11... | collective-permute-start | bytes 1179656 | tf_op jit(solution)/shard_map/ppermute | solution.py:76
  385.4 23.2 %collective-permute-start.69 = (bf16[256,768]{1,0:T(8,128)(2,1)S(1)}, bf16[256,768]{1,0:T(8,128)(2,1)S(1)}, u32[]{:S(2)}, u32[]{:S(2)}) collective-permute-start(bf16[256,768]{1,0:T(8,128)(2,1)S(1)} %get-tuple-element.347.refs_38_), channel_id=1, source_target_pairs={{0,2},{1,3},{2,0},{3,1},{4,6},{5,7},{6,4},{7,5},{8,10},{9,11},{10,... | collective-permute-start | bytes 1179656 | tf_op jit(solution)/shard_map/ppermute | solution.py:80
  390.5 21.6 %collective-permute-start.79 = (bf16[4,96,768]{2,1,0:T(8,128)(2,1)S(1)}, bf16[4,96,768]{2,1,0:T(8,128)(2,1)S(1)}, u32[]{:S(2)}, u32[]{:S(2)}) collective-permute-start(bf16[4,96,768]{2,1,0:T(8,128)(2,1)S(1)} %get-tuple-element.363), channel_id=1, source_target_pairs={{0,4},{4,0},{8,12},{12,8},{16,20},{20,16},{24,28},{28,24},{1,5},{5... | collective-permute-start | bytes 1769480 | tf_op jit(solution)/shard_map/ppermute | solution.py:84
  394.6 28.7 %collective-permute-start.80 = (bf16[4,96,768]{2,1,0:T(8,128)(2,1)S(1)}, bf16[4,96,768]{2,1,0:T(8,128)(2,1)S(1)}, u32[]{:S(2)}, u32[]{:S(2)}) collective-permute-start(bf16[4,96,768]{2,1,0:T(8,128)(2,1)S(1)} %get-tuple-element.365), channel_id=1, source_target_pairs={{0,4},{4,0},{8,12},{12,8},{16,20},{20,16},{24,28},{28,24},{1,5},{5... | collective-permute-start | bytes 1769480 | tf_op jit(solution)/shard_map/ppermute | solution.py:84
  395.1 13.4 %collective-permute-start.75 = (bf16[96,768]{1,0:T(8,128)(2,1)S(1)}, bf16[96,768]{1,0:T(8,128)(2,1)S(1)}, u32[]{:S(2)}, u32[]{:S(2)}) collective-permute-start(bf16[96,768]{1,0:T(8,128)(2,1)S(1)} %get-tuple-element.355), channel_id=1, source_target_pairs={{0,16},{4,20},{8,24},{12,28},{16,0},{20,4},{24,8},{28,12},{1,17},{... | collective-permute-start | bytes 442376 | tf_op jit(solution)/shard_map/ppermute | solution.py:84
  426.4 31.9 %collective-permute-start.84 = (bf16[96,2304]{1,0:T(8,128)(2,1)S(1)}, bf16[96,2304]{1,0:T(8,128)(2,1)S(1)}, u32[]{:S(2)}, u32[]{:S(2)}) collective-permute-start(bf16[96,2304]{1,0:T(8,128)(2,1)S(1)} %get-tuple-element.374), channel_id=1, source_target_pairs={{0,16},{4,20},{8,24},{12,28},{16,0},{20,4},{24,8},{28,12},{1,17},{... | collective-permute-start | bytes 1327112 | tf_op jit(solution)/shard_map/ppermute | solution.py:84
  430.3 30.8 %collective-permute-start.89 = (bf16[4,96,768]{2,1,0:T(8,128)(2,1)S(1)}, bf16[4,96,768]{2,1,0:T(8,128)(2,1)S(1)}, u32[]{:S(2)}, u32[]{:S(2)}) collective-permute-start(bf16[4,96,768]{2,1,0:T(8,128)(2,1)S(1)} %get-tuple-element.378), channel_id=1, source_target_pairs={{0,4},{4,0},{8,12},{12,8},{16,20},{20,16},{24,28},{28,24},{1,5},{5... | collective-permute-start | bytes 1769480 | tf_op jit(solution)/shard_map/ppermute | solution.py:84
  432.7 25.7 %collective-permute-start.83 = (bf16[8,64,384]{2,1,0:T(8,128)(2,1)S(1)}, bf16[8,64,384]{2,1,0:T(8,128)(2,1)S(1)}, u32[]{:S(2)}, u32[]{:S(2)}) collective-permute-start(bf16[8,64,384]{2,1,0:T(8,128)(2,1)S(1)} %get-tuple-element.373.refs_2_), channel_id=1, source_target_pairs={{0,2},{1,3},{2,0},{3,1},{4,6},{5,7},{6,4},{7,5},{8,10},{9,11},{10,... | collective-permute-start | bytes 1179656 | tf_op jit(solution)/shard_map/ppermute | solution.py:80
  433.0 33.4 %collective-permute-start.87 = (bf16[96,2304]{1,0:T(8,128)(2,1)S(1)}, bf16[96,2304]{1,0:T(8,128)(2,1)S(1)}, u32[]{:S(2)}, u32[]{:S(2)}) collective-permute-start(bf16[96,2304]{1,0:T(8,128)(2,1)S(1)} %get-tuple-element.377), channel_id=1, source_target_pairs={{0,24},{4,28},{8,16},{12,20},{16,8},{20,12},{24,0},{28,4},{1,25},{... | collective-permute-start | bytes 1327112 | tf_op jit(solution)/shard_map/ppermute | solution.py:84
  444.4 31.1 %collective-permute-start.93 = (bf16[96,2304]{1,0:T(8,128)(2,1)S(1)}, bf16[96,2304]{1,0:T(8,128)(2,1)S(1)}, u32[]{:S(2)}, u32[]{:S(2)}) collective-permute-start(bf16[96,2304]{1,0:T(8,128)(2,1)S(1)} %get-tuple-element.384), channel_id=1, source_target_pairs={{0,8},{4,12},{8,0},{12,4},{16,24},{20,28},{24,16},{28,20},{1,9},{5... | collective-permute-start | bytes 1327112 | tf_op jit(solution)/shard_map/ppermute | solution.py:84
  468.4 10.4 %collective-permute-start.91 = (bf16[2,64,384]{2,1,0:T(8,128)(2,1)S(1)}, bf16[2,64,384]{2,1,0:T(8,128)(2,1)S(1)}, u32[]{:S(2)}, u32[]{:S(2)}) collective-permute-start(bf16[2,64,384]{2,1,0:T(8,128)(2,1)S(1)} %get-tuple-element.382), channel_id=1, source_target_pairs={{0,16},{4,20},{8,24},{12,28},{16,0},{20,4},{24,8},{28,12},{1,17},{... | collective-permute-start | bytes 294920 | tf_op jit(solution)/shard_map/ppermute | solution.py:84
  469.0 9.9 %collective-permute-start.92 = (bf16[2,64,384]{2,1,0:T(8,128)(2,1)S(1)}, bf16[2,64,384]{2,1,0:T(8,128)(2,1)S(1)}, u32[]{:S(2)}, u32[]{:S(2)}) collective-permute-start(bf16[2,64,384]{2,1,0:T(8,128)(2,1)S(1)} %get-tuple-element.383), channel_id=1, source_target_pairs={{0,24},{4,28},{8,16},{12,20},{16,8},{20,12},{24,0},{28,4},{1,25},{... | collective-permute-start | bytes 294920 | tf_op jit(solution)/shard_map/ppermute | solution.py:84
  479.2 26.1 %collective-permute-start.96 = (bf16[8,64,384]{2,1,0:T(8,128)(2,1)S(1)}, bf16[8,64,384]{2,1,0:T(8,128)(2,1)S(1)}, u32[]{:S(2)}, u32[]{:S(2)}) collective-permute-start(bf16[8,64,384]{2,1,0:T(8,128)(2,1)S(1)} %shard_map.278.refs_2_), channel_id=1, source_target_pairs={{0,1},{1,0},{2,3},{3,2},{4,5},{5,4},{6,7},{7,6},{8,9},{9,8},{10,11... | collective-permute-start | bytes 1179656 | tf_op jit(solution)/shard_map/ppermute | solution.py:76
  487.6 17.8 %collective-permute-start.97 = (bf16[8,64,384]{2,1,0:T(8,128)(2,1)S(1)}, bf16[8,64,384]{2,1,0:T(8,128)(2,1)S(1)}, u32[]{:S(2)}, u32[]{:S(2)}) collective-permute-start(bf16[8,64,384]{2,1,0:T(8,128)(2,1)S(1)} %collective-permute-done.95.refs_3_), channel_id=1, source_target_pairs={{0,1},{1,0},{2,3},{3,2},{4,5},{5,4},{6,7},{7,6},{8,9},{9,8},{10,11... | collective-permute-start | bytes 1179656 | tf_op jit(solution)/shard_map/ppermute | solution.py:76
  491.4 13.9 %collective-permute-start.99 = (bf16[96,768]{1,0:T(8,128)(2,1)S(1)}, bf16[96,768]{1,0:T(8,128)(2,1)S(1)}, u32[]{:S(2)}, u32[]{:S(2)}) collective-permute-start(bf16[96,768]{1,0:T(8,128)(2,1)S(1)} %get-tuple-element.386), channel_id=1, source_target_pairs={{0,16},{4,20},{8,24},{12,28},{16,0},{20,4},{24,8},{28,12},{1,17},{... | collective-permute-start | bytes 442376 | tf_op jit(solution)/shard_map/ppermute | solution.py:84
  494.0 11.3 %collective-permute-start.100 = (bf16[96,768]{1,0:T(8,128)(2,1)S(1)}, bf16[96,768]{1,0:T(8,128)(2,1)S(1)}, u32[]{:S(2)}, u32[]{:S(2)}) collective-permute-start(bf16[96,768]{1,0:T(8,128)(2,1)S(1)} %get-tuple-element.387), channel_id=1, source_target_pairs={{0,24},{4,28},{8,16},{12,20},{16,8},{20,12},{24,0},{28,4},{1,25},{... | collective-permute-start | bytes 442376 | tf_op jit(solution)/shard_map/ppermute | solution.py:84
  (71 other events, 494.7 us)

commit v3 on v2

--- a/solution.py
+++ b/solution.py
@@ -88,34 +88,29 @@
     return lax.axis_size("dp") == 8 and rows % 16 == 0
 
 
-def place_kernel(spots, split, index_ref, *refs):
-    *pieces, first_ref, second_ref = refs
+def place_kernel(offsets, index_ref, *refs):
+    pieces, out_refs = refs[: len(offsets)], refs[len(offsets) :]
     rows = pieces[0].shape[0]
-    for (offset, column), piece in zip(spots, pieces):
+    for offset, piece in zip(offsets, pieces):
         here = pl.ds(pl.multiple_of((index_ref[3] ^ offset) * rows, rows), rows)
-        width = piece.shape[1]
-        if column < split:
-            first_ref[here, :] = piece[:, :split]
-            second_ref[here, : width - split] = piece[:, split:]
-        else:
-            second_ref[here, column - split : column - split + width] = piece[...]
+        start = 0
+        for out_ref in out_refs:
+            last = start + out_ref.shape[1]
+            out_ref[here, :] = piece[:, start:last]
+            start = last
 
 
 def copy_kernel(in_ref, out_ref):
     out_ref[...] = in_ref[...]
 
 
-def gather_start(shard, halves):
+def gather_start(shard):
     if not stepwise(shard.shape[0]):
-        return {(0, 0): lax.all_gather(shard, "dp", axis=0, tiled=True)}
-    pieces = {(0, 0): shard, (1, 0): swap_dp(shard, 1)}
+        return {0: lax.all_gather(shard, "dp", axis=0, tiled=True)}
+    pieces = {0: shard, 1: swap_dp(shard, 1)}
     for step in (2, 4, 6):
-        column = 0
-        for part in halves if step > 2 else [shard]:
-            along = swap_dp(part, step)
-            pieces[step, column] = along
-            pieces[step + 1, column] = swap_dp(along, 1)
-            column += part.shape[1]
+        pieces[step] = swap_dp(shard, step)
+        pieces[step + 1] = swap_dp(pieces[step], 1)
     return pieces
 
 
@@ -123,29 +118,30 @@
     if not stepwise(shard.shape[0]):
         for step in meanwhile:
             step()
-        return {(0, 0): lax.all_gather(shard, "dp", axis=0, tiled=True)}
-    pieces = {(0, 0): shard, (1, 0): swap_dp(shard, 1)}
-    sent, across = shard, pieces[1, 0]
-    for number, step in enumerate((4, 6, 2)):
-        along = swap_dp(sent, step)
-        pieces[step, 0] = along
-        if step != 2:
-            sent = call(copy_kernel, [sds(*shard.shape)], shard, after=[along, across])[0]
-        across = pieces[step + 1, 0] = swap_dp(along, 1)
-        if number < len(meanwhile):
-            meanwhile[number]()
+        return {0: lax.all_gather(shard, "dp", axis=0, tiled=True)}
+    pieces = {0: shard, 1: swap_dp(shard, 1), 2: swap_dp(shard, 2), 4: swap_dp(shard, 4)}
+    after = [pieces[1], pieces[2], pieces[4]]
+    for step in meanwhile:
+        step()
+    sent = call(copy_kernel, [sds(*shard.shape)], shard, after=after)[0]
+    pieces[6] = swap_dp(sent, 6)
+    for step in (2, 4, 6):
+        pieces[step + 1] = swap_dp(pieces[step], 1)
     return pieces
 
 
-def gather_finish(where, pieces, split, after=()):
+def gather_finish(where, pieces, widths, after=()):
     if len(pieces) == 1:
-        whole = pieces[0, 0]
-        return whole[:, :split], whole[:, split:]
-    rows, width = pieces[0, 0].shape
-    outs = [sds(8 * rows, n) for n in (split, width - split)]
+        whole, parts = pieces[0], []
+        for width in widths:
+            parts.append(whole[:, :width])
+            whole = whole[:, width:]
+        return parts
+    rows = pieces[0].shape[0]
     return call(
-        functools.partial(place_kernel, tuple(pieces), split),
-        outs, where, *pieces.values(), scalars=1, after=after,
+        functools.partial(place_kernel, tuple(pieces)),
+        [sds(8 * rows, width) for width in widths],
+        where, *pieces.values(), scalars=1, after=after,
     )
 
 
@@ -733,13 +729,12 @@
         keep(mine[0])
         context += [mine[0], theirs[0]]
         logsum += [mine[1], theirs[1]]
-        pairs.append(finish_pair(mine[2], theirs[2], at(("pair", k))))
+        pairs.append(finish_pair(mine[2], theirs[2], ()))
     drop(values_t)
     logsum = jnp.concatenate(logsum, axis=1)
     keep(logsum)
-    if callable(second_weight):
-        second_weight = second_weight()
     second_norm, result, result_pieces, second_pairs = [], [], [], []
+    mine, theirs = [], []
     for k in range(chunks):
         low, *kept = norm_call(
             residual[k], *pairs[k], gains[0:1], shifts[0:1], False, at(("norm_one", k))
@@ -747,11 +742,15 @@
         first_norm.append(kept)
         hidden_pieces += [low, swap_core(low)]
         keep(*kept)
-        mine = mlp_call(hidden_pieces[2 * k], second_weight, F32)
-        keep(hidden_pieces[2 * k], second_weight)
-        theirs = mlp_call(hidden_pieces[2 * k + 1], second_weight, BF16)
+        if k == 0:
+            second_weight = second_weight()
+        mine.append(mlp_call(low, second_weight, F32))
+        keep(low, second_weight)
+    for k in range(chunks):
+        theirs.append(mlp_call(hidden_pieces[2 * k + 1], second_weight, BF16))
         keep(hidden_pieces[2 * k + 1])
-        second_pairs.append(finish_pair(mine, theirs))
+    for k in range(chunks):
+        second_pairs.append(finish_pair(mine[k], theirs[k]))
     for k in range(chunks):
         low, *kept = norm_call(
             hidden_pieces[2 * k], *second_pairs[k], gains[1:2], shifts[1:2], last,
@@ -775,6 +774,7 @@
     ) = saved
     chunks = len(incoming)
     mixed, active, vectors_two, pair_grads, pairs = [], [], [], [], []
+    outs = []
     for k in range(chunks):
         low, vector = norm_back_call(
             incoming[k], *second_norm[k], gains[1:2], at(("norm_two", k))
@@ -782,16 +782,16 @@
         drop(*second_norm[k])
         vectors_two.append(vector)
         mixed += [low, swap_core(low)]
-        for h, dtype in ((0, F32), (1, BF16)):
-            act, grad, out = mlp_back_call(
-                hidden_pieces[2 * k + h], mixed[2 * k + h], second_weight, dtype
-            )
-            keep(act, grad, mixed[2 * k + h])
-            active.append(act)
-            pair_grads.append(grad)
-            if h == 0:
-                mine = out
-        pairs.append(finish_pair(mine, out))
+        outs += mlp_back_call(hidden_pieces[2 * k], low, second_weight, F32)
+        keep(*outs[-3:-1], low)
+    for k in range(chunks):
+        outs += mlp_back_call(hidden_pieces[2 * k + 1], mixed[2 * k + 1], second_weight, BF16)
+        keep(*outs[-3:-1], mixed[2 * k + 1])
+    for k in range(chunks):
+        here, there = outs[3 * k : 3 * k + 3], outs[3 * (chunks + k) : 3 * (chunks + k) + 3]
+        active += [here[0], there[0]]
+        pair_grads += [here[1], there[1]]
+        pairs.append(finish_pair(here[2], there[2]))
     drop(second_weight)
     at("sums")
     late = scatter_start(
@@ -925,24 +925,19 @@
     inner, hidden = output_ref.shape[1], down_ref.shape[2]
     columns = [project_ref[0, part] for part in range(3)] + [output_ref[0].T]
     columns += [gate_up_ref[0, :, part] for part in range(2)] + [down_ref[0]]
-    start = 0
-    for column in columns:
-        low, size = column.astype(BF16), column.shape[1]
-        first = 0
-        for ref in out_refs[1:]:
-            last = first + ref.shape[1]
-            if first <= start < last:
-                ref[:, start - first : start - first + size] = low
-            first = last
-        out_refs[0][:, start : start + size] = low
-        start += size
-
-
-def pack_call(layer, halves, project, gate_up, output, down, after=()):
+    for out_ref in out_refs:
+        start = 0
+        while start < out_ref.shape[1]:
+            column = columns.pop(0)
+            out_ref[:, start : start + column.shape[1]] = column.astype(BF16)
+            start += column.shape[1]
+
+
+def pack_call(layer, together, project, gate_up, output, down, after=()):
     operands = (jnp.swapaxes(project, 1, 2), gate_up, output, jnp.swapaxes(down, 1, 2))
     rows, inner, hidden = project.shape[1], output.shape[1], down.shape[1]
-    total, cut = 4 * inner + 3 * hidden, 4 * inner + hidden
-    outs = [sds(rows, n) for n in ([total, cut, total - cut] if halves else [total])]
+    sizes = [4 * inner, 3 * hidden]
+    outs = [sds(rows, n) for n in ([sum(sizes)] if together else sizes)]
     after = (*after, *Order.last)
 
     def spec(w):
@@ -960,7 +955,7 @@
         compiler_params=pltpu.CompilerParams(vmem_limit_bytes=VMEM_LIMIT),
         cost_estimate=pl.CostEstimate(flops=0, bytes_accessed=1000, transcendentals=0),
     )(*operands, *after)
-    Order.last = (results[-1],)
+    Order.last = (results[0],)
     return results
 
 
@@ -997,39 +992,47 @@
         local_order(table).reshape(length, 128)
         for table in (*map(jnp.asarray, rotary_tables(length)), jnp.broadcast_to(marks, (length, 128)))
     )
-    shard = pack_call(0, False, *sources)[0]
+    shard = pack_call(0, True, *sources)[0]
     meanwhile, moving = deal_steps(tokens, dealing_order, where)
-    started = [first_gather(shard, meanwhile)]
-    weights, saved_all = [], []
+    pieces = first_gather(shard, meanwhile)
+    widths = (4 * inner, 3 * hidden)
+    coming = [(pieces, None)]
+    saved_all = []
     keep(*tables[:2])
     for layer in range(LAYERS):
-        points = {}
+        here, points = coming[layer], {}
         if layer < LAYERS - 1:
-            before = [started[layer][key] for key in ((2, 0), (7, 0))] if len(started[layer]) > 1 else ()
-            packed = pack_call(layer + 1, True, *sources, after=before)
-            started.append(gather_start(packed[0], packed[1:]))
-            if len(started[-1]) > 1:
-                cut = packed[1].shape[1]
+            before = [pieces[step] for step in (6, 3, 5)] if layer == 0 and len(pieces) > 1 else ()
+            packed = pack_call(layer + 1, False, *sources, after=before)
+            first, second = (gather_start(part) for part in packed)
+            coming.append((first, second))
+            if len(first) > 1:
                 points = {
-                    "place": ((2, 0),),
-                    ("pair", 0): ((4, 0),),
-                    ("norm_one", 0): ((4, cut), (3, 0)),
-                    ("norm_one", 1): ((6, 0), (1, 0), (5, 0)),
-                    ("norm_two", 0): ((6, cut), (5, cut)),
-                    ("norm_two", 1): ((7, 0),),
+                    "place": (first, (2, 4, 6)),
+                    ("norm_one", 0): (first, (1, 3, 5, 7)),
+                    ("norm_one", 1): (second, (2, 4, 1)),
+                    ("norm_two", 0): (second, (3,)),
+                    ("norm_two", 1): (second, (6, 5)),
                 }
+        if layer and len(here[0]) > 1:
+            points[("norm_one", 0)] = (here[1], (7,))
 
         def at(point, points=points):
-            return tuple(started[-1][key] for key in points.get(point, ()))
-
-        weights.append(gather_finish(where, started[layer], 4 * inner, at("place")))
+            found, steps = points.get(point, ({}, ()))
+            return tuple(found[step] for step in steps)
+
         if layer == 0:
+            first_weight, second_weight = gather_finish(where, here[0], widths, at("place"))
             dealt = deal_finish(moving, where, local_order)
             pieces = [dealt]
             residual = [dealt[2 * k * quarter : (2 * k + 1) * quarter] for k in range(chunks)]
+            late_weight = lambda: second_weight
+        else:
+            (first_weight,) = gather_finish(where, here[0], widths[:1])
+            late_weight = lambda here=here: gather_finish(where, here[1], widths[1:])[0]
         current, residual, saved = layer_forward(
-            pieces, residual, *weights[layer], norm_gains[layer], norm_biases[layer], tables,
-            inner, layer == LAYERS - 1, at,
+            pieces, residual, first_weight, late_weight, norm_gains[layer], norm_biases[layer],
+            tables, inner, layer == LAYERS - 1, at,
         )
         saved_all.append(saved)
         if layer < LAYERS - 1:
@@ -1074,28 +1077,28 @@
         if layer:
             after = {("norm_one", 0): 1, ("norm_one", 1): 2, ("input", 0): 3}
         else:
-            after = {("attend_back", 0): 1, ("attend_back", 1): 2, "input": 3}
+            after = {("norm_one", 1): 1, ("attend_back", 1): 2, "input": 3}
+        found = ()
         if point in after:
-            return (own_sums["second"][after[point]],)
+            found = (own_sums["second"][after[point]],)
         if layer == LAYERS - 1:
-            return ()
-        if point == "sums":
+            return found
+        if point == ("norm_two", 1):
+            return tuple(above["second"][1:3])
+        if point == ("norm_one", 0):
             above["first"] = scatter_finish(where, above["first"])
-        after = {
-            ("norm_two", 0): ("second", 1), ("norm_two", 1): ("second", 2),
-            ("norm_one", 0): ("second", 3), ("norm_one", 1): ("first", 1),
-        }
-        if point in after:
-            name, number = after[point]
-            return tuple(above[name][number : number + 3]) if name == "first" else (above[name][number],)
-        return ()
+        if point == ("norm_one", 1):
+            return found + tuple(above["first"][1:])
+        if point == ("attend_back", 1):
+            return found + tuple(above["second"][3:])
+        return found
 
     for layer in reversed(range(LAYERS)):
         triple, (rows_in, attended, context), late = layer_backward(
             incoming, saved_all[layer], norm_gains[layer], tables, split, dp_count,
             functools.partial(at, layer),
         )
-        first_weight = weights[layer][0]
+        first_weight = saved_all[layer][-2]
         if layer:
             incoming = []
             for k in range(chunks):
@@ -1116,7 +1119,7 @@
     sent = swap_core(sent)
     drop(first_weight, *tables[:2])
     second_sum = scatter_finish(where, late)
-    arriving = [second_sum[step : step + 1] for step in (2, 3, 1)]
+    arriving = [second_sum[1:2], [], second_sum[2:]]
     sum_norms(0)
     sums = weight_call(split, [(rows_in, [triple]), (attended, context)], dp_count)
     Order.kept = []
@@ -1137,7 +1140,7 @@
         sum_norms(2)
         moving = exchange_middle(*moving, arriving[1])
         sum_norms(3)
-        near = exchange_finish(moving, arriving[2])
+        near = exchange_finish(moving, arriving[2] + first_sum[1:])
     far = swap_x(near)
     for index in range(2 if split is None else 4, len(steps) - 1):
         sum_norms(index)
@@ -1150,7 +1153,6 @@
     returned = call(
         functools.partial(last_kernel, split is not None), [sds(count, part, width, dtype=F32)],
         dealing_order, where, near, far, swap_core(near), swap_core(far), scalars=2,
-        after=first_sum[1:],
     )[0]
 
     shapes = (

time: 521 us -> 496 us (0.952)
  waiting for transfers between devices: 267 us -> 222 us
  starting transfers between devices: 97.6 us -> 115 us
    ppermute x49 -> x52, waiting for transfers between devices: 167 us -> 133 us  [swap_dp(): lax.ppermute(value, 'dp', [(i, i ^ step) for i in range(lax.axis_size('dp...]
    ppermute x18, starting transfers between devices: 10.3 us -> 22.4 us  [swap_x(): lax.ppermute(value, 'tensor', [(i, i ^ 2) for i in range(lax.axis_size('t...]
    ppermute x33, waiting for transfers between devices: 14.4 us -> 7.31 us  [swap_core(): lax.ppermute(value, 'tensor', [(i, i ^ 1) for i in range(lax.axis_size('t...]
    ppermute x49 -> x52, starting transfers between devices: 80.4 us -> 85.7 us  [swap_dp(): lax.ppermute(value, 'dp', [(i, i ^ step) for i in range(lax.axis_size('dp...]
    unnamed x72 -> x76, local copies, waits for them, and re-layouts: 10.5 us -> 11.8 us
  transfers between devices with their start and end apart: 102 -> 105, of which waited for: 57 -> 56; matrix products, arithmetic and copies ran while one was open for 1% -> 1% of each run, Pallas kernels for 19% -> 20%
where the time goes in v3:
time: 496 us; the launch traced here: 487 us
  waiting for transfers between devices  222 us (45%)
  Pallas kernels  129 us (26%)
  starting transfers between devices  115 us (23%)
  local copies, waits for them, and re-layouts  15.7 us (3%)
    ppermute x52, waiting for transfers between devices, swap_dp(): lax.ppermute(value, 'dp', [(i, i ^ step) for i in range(lax.axis_size('dp...  133 us
    pallas_call x103, Pallas kernels, call(): pl.pallas_call(body, in_specs=[smem] * scalars + [vmem] * (used - scalars...  127 us
    ppermute x52, starting transfers between devices, swap_dp(): lax.ppermute(value, 'dp', [(i, i ^ step) for i in range(lax.axis_size('dp...  85.7 us
    ppermute x18, waiting for transfers between devices, swap_x(): lax.ppermute(value, 'tensor', [(i, i ^ 2) for i in range(lax.axis_size('t...  72.2 us
    ppermute x18, starting transfers between devices, swap_x(): lax.ppermute(value, 'tensor', [(i, i ^ 2) for i in range(lax.axis_size('t...  22.4 us
    unnamed x76, local copies, waits for them, and re-layouts  11.8 us
  transfers between devices with their start and end apart: 105, of which 56 were waited for; matrix products, arithmetic and copies ran while one was open for 1% of the time, Pallas kernels for 20%

profile of v3, /device:TPU:0, one launch (start us, length us, event | category | flops | bytes accessed | tf_op | source)
XLA Modules:
  0.0 486.6 jit_solution(421908486434890457)
XLA Ops:
  6.4 3.0 collective-permute-start.7
  11.0 2.6 collective-permute-start.9
  19.9 7.1 %collective-permute-done.refs_1_ = bf16[4,32,768]{2,1,0:T(8,128)(2,1)S(1)} collective-permute-done((bf16[4,32,768]{2,1,0:T(8,128)(2,1)S(1)}, bf16[4,32,768]{2,1,0:T(8,128)(2,1)S(1)}, u32[]{:S(2)}, u32[]{:S(2)}) %collective-permute-start) | collective-permute-done | bytes 196640 | tf_op jit(solution)/shard_map/ppermute | solution.py:84
  28.8 2.6 collective-permute-start.2
  31.4 8.4 %collective-permute-done.1.refs_1_ = bf16[2,32,768]{2,1,0:T(8,128)(2,1)S(1)} collective-permute-done((bf16[2,32,768]{2,1,0:T(8,128)(2,1)S(1)}, bf16[2,32,768]{2,1,0:T(8,128)(2,1)S(1)}, u32[]{:S(2)}, u32[]{:S(2)}) %collective-permute-start.1) | collective-permute-done | bytes 98336 | tf_op jit(solution)/shard_map/ppermute | solution.py:84
  39.8 3.1 collective-permute-start.3
  48.3 3.1 collective-permute-start.10
  54.8 6.4 %collective-permute-done.5.refs_3_ = bf16[8,32,768]{2,1,0:T(8,128)(2,1)} collective-permute-done((bf16[8,32,768]{2,1,0:T(8,128)(2,1)S(1)}, bf16[8,32,768]{2,1,0:T(8,128)(2,1)}, u32[]{:S(2)}, u32[]{:S(2)}) %collective-permute-start.5) | collective-permute-done | bytes 393248 | tf_op jit(solution)/shard_map/ppermute | solution.py:80
  61.2 2.4 collective-permute-done.10.refs_4_.refs_5_
  63.7 4.1 collective-permute-done.11.refs_5_.refs_6_
  67.8 8.7 %collective-permute-done.12.refs_6_.refs_7_ = bf16[96,3072]{1,0:T(8,128)(2,1)} collective-permute-done((bf16[96,3072]{1,0:T(8,128)(2,1)}, bf16[96,3072]{1,0:T(8,128)(2,1)}, u32[]{:S(2)}, u32[]{:S(2)}) %collective-permute-start.12) | collective-permute-done | bytes 589856 | tf_op jit(solution)/shard_map/ppermute | solution.py:84
  83.5 2.5 collective-permute-done.14.refs_11_.refs_3_
  86.0 2.4 collective-permute-start.16
  88.6 6.2 %collective-permute-done.15.refs_12_.refs_5_ = bf16[96,768]{1,0:T(8,128)(2,1)S(1)} collective-permute-done((bf16[96,768]{1,0:T(8,128)(2,1)S(1)}, bf16[96,768]{1,0:T(8,128)(2,1)S(1)}, u32[]{:S(2)}, u32[]{:S(2)}) %collective-permute-start.15) | collective-permute-done | bytes 147488 | tf_op jit(solution)/shard_map/ppermute | solution.py:84
  100.3 2.2 shard_map.188
  105.0 2.5 shard_map.191
  112.2 2.2 shard_map.192
  119.0 2.2 collective-permute-done.21.refs_20_.refs_6_
  125.8 7.4 %collective-permute-done.18.refs_2_ = bf16[256,768]{1,0:T(8,128)(2,1)S(1)} collective-permute-done((bf16[256,768]{1,0:T(8,128)(2,1)S(1)}, bf16[256,768]{1,0:T(8,128)(2,1)S(1)}, u32[]{:S(2)}, u32[]{:S(2)}) %collective-permute-start.18) | collective-permute-done | bytes 393248 | tf_op jit(solution)/shard_map/ppermute | solution.py:80
  134.9 2.9 collective-permute-done.27.refs_23_.refs_5_
  144.4 2.5 collective-permute-start.36
  150.4 6.3 %collective-permute-done.32.refs_27_.refs_4_ = bf16[96,2304]{1,0:T(8,128)(2,1)S(1)} collective-permute-done((bf16[96,2304]{1,0:T(8,128)(2,1)S(1)}, bf16[96,2304]{1,0:T(8,128)(2,1)S(1)}, u32[]{:S(2)}, u32[]{:S(2)}) %collective-permute-start.32) | collective-permute-done | bytes 442400 | tf_op jit(solution)/shard_map/ppermute | solution.py:84
  156.7 3.5 collective-permute-done.31.refs_2_
  160.7 5.0 %collective-permute-done.37.refs_30_.refs_6_ = bf16[96,2304]{1,0:T(8,128)(2,1)S(1)} collective-permute-done((bf16[96,2304]{1,0:T(8,128)(2,1)S(1)}, bf16[96,2304]{1,0:T(8,128)(2,1)S(1)}, u32[]{:S(2)}, u32[]{:S(2)}) %collective-permute-start.37) | collective-permute-done | bytes 442400 | tf_op jit(solution)/shard_map/ppermute | solution.py:84
  169.4 2.3 shard_map.205
  171.7 2.2 shard_map.206
  174.1 2.2 shard_map.207
  176.5 2.2 shard_map.209
  181.6 2.2 shard_map.210
  184.6 6.8 %collective-permute-done.41.refs_45_.refs_8_ = bf16[96,2304]{1,0:T(8,128)(2,1)S(1)} collective-permute-done((bf16[96,2304]{1,0:T(8,128)(2,1)S(1)}, bf16[96,2304]{1,0:T(8,128)(2,1)S(1)}, u32[]{:S(2)}, u32[]{:S(2)}) %collective-permute-start.41) | collective-permute-done | bytes 442400 | tf_op jit(solution)/shard_map/ppermute | solution.py:84
  194.6 4.8 collective-permute-done.44.refs_2_
  208.4 8.2 %collective-permute-done.47.refs_2_ = bf16[256,768]{1,0:T(8,128)(2,1)S(1)} collective-permute-done((bf16[256,768]{1,0:T(8,128)(2,1)S(1)}, bf16[256,768]{1,0:T(8,128)(2,1)S(1)}, u32[]{:S(2)}, u32[]{:S(2)}) %collective-permute-start.47) | collective-permute-done | bytes 393248 | tf_op jit(solution)/shard_map/ppermute | solution.py:80
  217.7 7.3 %collective-permute-done.49.refs_2_ = bf16[256,768]{1,0:T(8,128)(2,1)S(1)} collective-permute-done((bf16[256,768]{1,0:T(8,128)(2,1)S(1)}, bf16[256,768]{1,0:T(8,128)(2,1)S(1)}, u32[]{:S(2)}, u32[]{:S(2)}) %collective-permute-start.49) | collective-permute-done | bytes 393248 | tf_op jit(solution)/shard_map/ppermute | solution.py:80
  227.7 5.3 %collective-permute-done.50.refs_2_ = bf16[256,768]{1,0:T(8,128)(2,1)S(1)} collective-permute-done((bf16[256,768]{1,0:T(8,128)(2,1)S(1)}, bf16[256,768]{1,0:T(8,128)(2,1)S(1)}, u32[]{:S(2)}, u32[]{:S(2)}) %collective-permute-start.50) | collective-permute-done | bytes 393248 | tf_op jit(solution)/shard_map/ppermute | solution.py:80
  248.0 5.0 %shard_map.234 = (bf16[4,96,2304]{2,1,0:T(8,128)(2,1)S(1)}, bf16[4,96,768]{2,1,0:T(8,128)(2,1)S(1)}, bf16[4,96,768]{2,1,0:T(8,128)(2,1)S(1)}, bf16[4,96,768]{2,1,0:T(8,128)(2,1)S(1)}) custom-call(s32[6]{0:T(128)S(1)} %stack.27.refs_0_.refs_1_, bf16[256,768]{1,0:T(8,128)(2,1)S(1)} %get-tuple-element.265.refs_0_.refs_47_.refs_45_.refs_48_.refs_46_.refs_1_, ...), custom_call_target="tpu_custom_call" | custom-call | flops 3623878 | bytes 11403 | tf_op jit(solution)/shard_map/pallas_call | solution.py:56
  256.6 8.7 %collective-permute-done.56.refs_2_ = bf16[256,768]{1,0:T(8,128)(2,1)S(1)} collective-permute-done((bf16[256,768]{1,0:T(8,128)(2,1)S(1)}, bf16[256,768]{1,0:T(8,128)(2,1)S(1)}, u32[]{:S(2)}, u32[]{:S(2)}) %collective-permute-start.56) | collective-permute-done | bytes 393248 | tf_op jit(solution)/shard_map/ppermute | solution.py:80
  265.2 4.0 collective-permute-done.57.refs_50_.refs_2_
  272.9 6.4 %shard_map.237 = (bf16[512,192]{1,0:T(8,128)(2,1)S(1)}, f32[1024,256]{1,0:T(8,128)S(1)}, f32[1024,192]{1,0:T(8,128)S(1)}) custom-call(bf16[1024,256]{1,0:T(8,128)(2,1)S(1)} %get-tuple-element.245.refs_0_.refs_33_.refs_35_.refs_40_.refs_36_.refs_34_.refs_48_.refs_37_, bf16[512,192]{1,0:T(8,128)(2,1)S(1)} %shard_map.236.refs_1_.refs_47_, ...), custom_call_target="tpu_custom_call" | custom-call | flops 4026531 | bytes 5144 | tf_op jit(solution)/shard_map/pallas_call | solution.py:56
  284.7 7.5 %shard_map.240 = (bf16[1024,576]{1,0:T(8,128)(2,1)S(1)}, f32[1024,256]{1,0:T(8,128)}, f32[1024,192]{1,0:T(8,128)S(1)}) custom-call(bf16[1024,256]{1,0:T(8,128)(2,1)S(1)} %get-tuple-element.245.refs_0_.refs_33_.refs_35_.refs_40_.refs_36_.refs_34_.refs_48_.refs_37_, bf16[512,192]{1,0:T(8,128)(2,1)S(1)} %shard_map.239.refs_1_.refs_49_, ...), custom_call_target="tpu_custom_call" | custom-call | flops 4026531 | bytes 8159 | tf_op jit(solution)/shard_map/pallas_call | solution.py:56
  303.4 2.5 shard_map.248
  305.9 3.1 collective-permute-done.65.refs_2_
  311.8 5.1 %collective-permute-done.64.refs_2_ = bf16[256,768]{1,0:T(8,128)(2,1)S(1)} collective-permute-done((bf16[256,768]{1,0:T(8,128)(2,1)S(1)}, bf16[256,768]{1,0:T(8,128)(2,1)S(1)}, u32[]{:S(2)}, u32[]{:S(2)}) %collective-permute-start.64) | collective-permute-done | bytes 393248 | tf_op jit(solution)/shard_map/ppermute | solution.py:80
  316.9 4.5 collective-permute-done.66.refs_33_.refs_1_
  321.4 2.7 collective-permute-done.67.refs_34_.refs_2_
  330.4 2.3 shard_map.254
  334.6 4.5 shard_map.257
  340.4 5.3 %collective-permute-done.74.refs_2_ = bf16[4,96,768]{2,1,0:T(8,128)(2,1)S(1)} collective-permute-done((bf16[4,96,768]{2,1,0:T(8,128)(2,1)S(1)}, bf16[4,96,768]{2,1,0:T(8,128)(2,1)S(1)}, u32[]{:S(2)}, u32[]{:S(2)}) %collective-permute-start.74) | collective-permute-done | bytes 589856 | tf_op jit(solution)/shard_map/ppermute | solution.py:84
  348.3 2.6 collective-permute-start.78
  353.6 8.5 %collective-permute-done.78.refs_25_.refs_2_ = bf16[96,768]{1,0:T(8,128)(2,1)S(1)} collective-permute-done((bf16[96,768]{1,0:T(8,128)(2,1)S(1)}, bf16[96,768]{1,0:T(8,128)(2,1)S(1)}, u32[]{:S(2)}, u32[]{:S(2)}) %collective-permute-start.78) | collective-permute-done | bytes 147488 | tf_op jit(solution)/shard_map/ppermute | solution.py:84
  366.7 6.4 %shard_map.261 = (bf16[512,192]{1,0:T(8,128)(2,1)S(1)}, f32[1024,256]{1,0:T(8,128)S(1)}, f32[1024,192]{1,0:T(8,128)S(1)}) custom-call(bf16[1024,256]{1,0:T(8,128)(2,1)S(1)} %get-tuple-element.206.refs_0_.refs_5_.refs_8_.refs_12_.refs_9_.refs_7_.refs_6_.refs_20_.refs_17_.refs_11_, bf16[512,192]{1,0:T(8,128)(2,1)S(1)} %shard_map.260.refs_1_.refs_21_, ...), custom_call_target="tpu_custom_call" | custom-call | flops 4026531 | bytes 5144 | tf_op jit(solution)/shard_map/pallas_call | solution.py:56
  376.2 2.3 collective-permute-done.81.refs_23_.refs_3_
  378.4 7.4 %shard_map.265 = (bf16[1024,576]{1,0:T(8,128)(2,1)S(1)}, f32[1024,256]{1,0:T(8,128)}, f32[1024,192]{1,0:T(8,128)S(1)}) custom-call(bf16[1024,256]{1,0:T(8,128)(2,1)S(1)} %get-tuple-element.206.refs_0_.refs_5_.refs_8_.refs_12_.refs_9_.refs_7_.refs_6_.refs_20_.refs_17_.refs_11_, bf16[512,192]{1,0:T(8,128)(2,1)S(1)} %shard_map.264.refs_1_.refs_25_, ...), custom_call_target="tpu_custom_call" | custom-call | flops 4026531 | bytes 8159 | tf_op jit(solution)/shard_map/pallas_call | solution.py:56
  385.9 2.7 collective-permute-done.83.refs_16_.refs_4_
  393.0 2.5 shard_map.269
  396.8 5.0 %collective-permute-start.87 = (bf16[96,2304]{1,0:T(8,128)(2,1)S(1)}, bf16[96,2304]{1,0:T(8,128)(2,1)S(1)}, u32[]{:S(2)}, u32[]{:S(2)}) collective-permute-start(bf16[96,2304]{1,0:T(8,128)(2,1)S(1)} %get-tuple-element.368), channel_id=1, source_target_pairs={{0,8},{4,12},{8,0},{12,4},{16,24},{20,28},{24,16},{28,20},{1,9},{5... | collective-permute-start | bytes 1327112 | tf_op jit(solution)/shard_map/ppermute | solution.py:84
  405.2 8.5 %collective-permute-done.88.refs_1_ = f32[8,768]{1,0:T(8,128)S(1)} collective-permute-done((f32[8,768]{1,0:T(8,128)S(1)}, f32[8,768]{1,0:T(8,128)S(1)}, u32[]{:S(2)}, u32[]{:S(2)}) %collective-permute-start.88) | collective-permute-done | bytes 24608 | tf_op jit(solution)/shard_map/ppermute | solution.py:1051
  415.8 3.7 collective-permute-done.87.refs_2_.refs_5_
  423.1 16.6 %collective-permute-done.95.refs_4_.refs_6_ = bf16[96,2304]{1,0:T(8,128)(2,1)S(1)} collective-permute-done((bf16[96,2304]{1,0:T(8,128)(2,1)S(1)}, bf16[96,2304]{1,0:T(8,128)(2,1)S(1)}, u32[]{:S(2)}, u32[]{:S(2)}) %collective-permute-start.95) | collective-permute-done | bytes 442400 | tf_op jit(solution)/shard_map/ppermute | solution.py:84
  443.3 9.6 %collective-permute-start.92 = (bf16[2,64,384]{2,1,0:T(8,128)(2,1)S(1)}, bf16[2,64,384]{2,1,0:T(8,128)(2,1)S(1)}, u32[]{:S(2)}, u32[]{:S(2)}) collective-permute-start(bf16[2,64,384]{2,1,0:T(8,128)(2,1)S(1)} %get-tuple-element.374), channel_id=1, source_target_pairs={{0,8},{4,12},{8,0},{12,4},{16,24},{20,28},{24,16},{28,20},{1,9},{5... | collective-permute-start | bytes 294920 | tf_op jit(solution)/shard_map/ppermute | solution.py:84
  455.3 2.4 collective-permute-done.98.refs_7_.refs_2_
  457.7 6.7 %collective-permute-done.93.refs_2_ = bf16[2,64,384]{2,1,0:T(8,128)(2,1)S(1)} collective-permute-done((bf16[2,64,384]{2,1,0:T(8,128)(2,1)S(1)}, bf16[2,64,384]{2,1,0:T(8,128)(2,1)S(1)}, u32[]{:S(2)}, u32[]{:S(2)}) %collective-permute-start.93) | collective-permute-done | bytes 98336 | tf_op jit(solution)/shard_map/ppermute | solution.py:84
  465.6 7.0 %collective-permute-done.101.refs_3_ = bf16[8,64,384]{2,1,0:T(8,128)(2,1)S(1)} collective-permute-done((bf16[8,64,384]{2,1,0:T(8,128)(2,1)S(1)}, bf16[8,64,384]{2,1,0:T(8,128)(2,1)S(1)}, u32[]{:S(2)}, u32[]{:S(2)}) %collective-permute-start.101) | collective-permute-done | bytes 393248 | tf_op jit(solution)/shard_map/ppermute | solution.py:80
  472.6 3.2 collective-permute-start.104
  479.8 2.4 shard_map.282.refs_10_
  (345 shorter events, 181.0 us)
Async XLA Ops:
  6.4 40.0 %collective-permute-start.7 = (bf16[96,3072]{1,0:T(8,128)(2,1)S(1)}, bf16[96,3072]{1,0:T(8,128)(2,1)S(1)}, u32[]{:S(2)}, u32[]{:S(2)}) collective-permute-start(bf16[96,3072]{1,0:T(8,128)(2,1)S(1)} %shard_map.179.refs_2_.refs_0_.refs_1_), channel_id=1, source_target_pairs={{0,4},{4,0},{8,12},{12,8},{16,20},{20,16},{24,28},{28,24},{1,5},{5... | collective-permute-start | bytes 1769480 | tf_op jit(solution)/shard_map/ppermute | solution.py:84
  9.4 37.0 %collective-permute-start.8 = (bf16[96,3072]{1,0:T(8,128)(2,1)S(1)}, bf16[96,3072]{1,0:T(8,128)(2,1)S(1)}, u32[]{:S(2)}, u32[]{:S(2)}) collective-permute-start(bf16[96,3072]{1,0:T(8,128)(2,1)S(1)} %shard_map.179.refs_2_.refs_0_.refs_1_), channel_id=1, source_target_pairs={{0,8},{4,12},{8,0},{12,4},{16,24},{20,28},{24,16},{28,20},{1,9},{5... | collective-permute-start | bytes 1769480 | tf_op jit(solution)/shard_map/ppermute | solution.py:84
  11.0 35.5 %collective-permute-start.9 = (bf16[96,3072]{1,0:T(8,128)(2,1)S(1)}, bf16[96,3072]{1,0:T(8,128)(2,1)}, u32[]{:S(2)}, u32[]{:S(2)}) collective-permute-start(bf16[96,3072]{1,0:T(8,128)(2,1)S(1)} %shard_map.179.refs_2_.refs_0_.refs_1_), channel_id=1, source_target_pairs={{0,16},{4,20},{8,24},{12,28},{16,0},{20,4},{24,8},{28,12},{1,17},{... | collective-permute-start | bytes 1769480 | tf_op jit(solution)/shard_map/ppermute | solution.py:84
  27.0 12.8 %collective-permute-start.1 = (bf16[2,32,768]{2,1,0:T(8,128)(2,1)S(1)}, bf16[2,32,768]{2,1,0:T(8,128)(2,1)S(1)}, u32[]{:S(2)}, u32[]{:S(2)}) collective-permute-start(bf16[2,32,768]{2,1,0:T(8,128)(2,1)S(1)} %get-tuple-element.201), channel_id=1, source_target_pairs={{0,8},{4,12},{8,0},{12,4},{16,24},{20,28},{24,16},{28,20},{1,9},{5... | collective-permute-start | bytes 294920 | tf_op jit(solution)/shard_map/ppermute | solution.py:84
  28.8 15.6 %collective-permute-start.2 = (bf16[2,32,768]{2,1,0:T(8,128)(2,1)S(1)}, bf16[2,32,768]{2,1,0:T(8,128)(2,1)S(1)}, u32[]{:S(2)}, u32[]{:S(2)}) collective-permute-start(bf16[2,32,768]{2,1,0:T(8,128)(2,1)S(1)} %get-tuple-element.202), channel_id=1, source_target_pairs={{0,16},{4,20},{8,24},{12,28},{16,0},{20,4},{24,8},{28,12},{1,17},{... | collective-permute-start | bytes 294920 | tf_op jit(solution)/shard_map/ppermute | solution.py:84
  48.3 15.4 %collective-permute-start.10 = (bf16[96,3072]{1,0:T(8,128)(2,1)}, bf16[96,3072]{1,0:T(8,128)(2,1)S(1)}, u32[]{:S(2)}, u32[]{:S(2)}) collective-permute-start(bf16[96,3072]{1,0:T(8,128)(2,1)} %shard_map.183.refs_7_), channel_id=1, source_target_pairs={{0,24},{4,28},{8,16},{12,20},{16,8},{20,12},{24,0},{28,4},{1,25},{... | collective-permute-start | bytes 1769480 | tf_op jit(solution)/shard_map/ppermute | solution.py:84
  51.3 16.5 %collective-permute-start.11 = (bf16[96,3072]{1,0:T(8,128)(2,1)}, bf16[96,3072]{1,0:T(8,128)(2,1)S(1)}, u32[]{:S(2)}, u32[]{:S(2)}) collective-permute-start(bf16[96,3072]{1,0:T(8,128)(2,1)} %copy-done.8), channel_id=1, source_target_pairs={{0,4},{4,0},{8,12},{12,8},{16,20},{20,16},{24,28},{28,24},{1,5},{5... | collective-permute-start | bytes 1769480 | tf_op jit(solution)/shard_map/ppermute | solution.py:84
  51.8 24.7 %collective-permute-start.12 = (bf16[96,3072]{1,0:T(8,128)(2,1)}, bf16[96,3072]{1,0:T(8,128)(2,1)}, u32[]{:S(2)}, u32[]{:S(2)}) collective-permute-start(bf16[96,3072]{1,0:T(8,128)(2,1)} %collective-permute-done.9.refs_3_.refs_4_), channel_id=1, source_target_pairs={{0,4},{4,0},{8,12},{12,8},{16,20},{20,16},{24,28},{28,24},{1,5},{5... | collective-permute-start | bytes 1769480 | tf_op jit(solution)/shard_map/ppermute | solution.py:84
  54.8 42.1 %collective-permute-start.4 = (bf16[8,32,768]{2,1,0:T(8,128)(2,1)S(1)}, bf16[8,32,768]{2,1,0:T(8,128)(2,1)S(1)}, u32[]{:S(2)}, u32[]{:S(2)}) collective-permute-start(bf16[8,32,768]{2,1,0:T(8,128)(2,1)S(1)} %shard_map.182.refs_4_.refs_1_), channel_id=1, source_target_pairs={{0,1},{1,0},{2,3},{3,2},{4,5},{5,4},{6,7},{7,6},{8,9},{9,8},{10,11... | collective-permute-start | bytes 1179656 | tf_op jit(solution)/shard_map/ppermute | solution.py:76
  61.2 35.7 %collective-permute-start.6 = (bf16[8,32,768]{2,1,0:T(8,128)(2,1)}, bf16[8,32,768]{2,1,0:T(8,128)(2,1)S(1)}, u32[]{:S(2)}, u32[]{:S(2)}) collective-permute-start(bf16[8,32,768]{2,1,0:T(8,128)(2,1)} %collective-permute-done.5.refs_3_), channel_id=1, source_target_pairs={{0,1},{1,0},{2,3},{3,2},{4,5},{5,4},{6,7},{7,6},{8,9},{9,8},{10,11... | collective-permute-start | bytes 1179656 | tf_op jit(solution)/shard_map/ppermute | solution.py:76
  81.4 13.9 %collective-permute-start.13 = (bf16[96,3072]{1,0:T(8,128)(2,1)S(1)}, bf16[96,3072]{1,0:T(8,128)(2,1)S(1)}, u32[]{:S(2)}, u32[]{:S(2)}) collective-permute-start(bf16[96,3072]{1,0:T(8,128)(2,1)S(1)} %collective-permute-done.10.refs_4_.refs_5_), channel_id=1, source_target_pairs={{0,4},{4,0},{8,12},{12,8},{16,20},{20,16},{24,28},{28,24},{1,5},{5... | collective-permute-start | bytes 1769480 | tf_op jit(solution)/shard_map/ppermute | solution.py:84
  82.1 12.7 %collective-permute-start.15 = (bf16[96,768]{1,0:T(8,128)(2,1)S(1)}, bf16[96,768]{1,0:T(8,128)(2,1)S(1)}, u32[]{:S(2)}, u32[]{:S(2)}) collective-permute-start(bf16[96,768]{1,0:T(8,128)(2,1)S(1)} %get-tuple-element.204.refs_14_.refs_1_), channel_id=1, source_target_pairs={{0,16},{4,20},{8,24},{12,28},{16,0},{20,4},{24,8},{28,12},{1,17},{... | collective-permute-start | bytes 442376 | tf_op jit(solution)/shard_map/ppermute | solution.py:84
  110.8 13.5 %collective-permute-start.22 = (bf16[96,768]{1,0:T(8,128)(2,1)S(1)}, bf16[96,768]{1,0:T(8,128)(2,1)S(1)}, u32[]{:S(2)}, u32[]{:S(2)}) collective-permute-start(bf16[96,768]{1,0:T(8,128)(2,1)S(1)} %collective-permute-done.16.refs_13_.refs_7_), channel_id=1, source_target_pairs={{0,4},{4,0},{8,12},{12,8},{16,20},{20,16},{24,28},{28,24},{1,5},{5... | collective-permute-start | bytes 442376 | tf_op jit(solution)/shard_map/ppermute | solution.py:84
  114.4 20.5 %collective-permute-start.26 = (bf16[96,2304]{1,0:T(8,128)(2,1)S(1)}, bf16[96,2304]{1,0:T(8,128)(2,1)S(1)}, u32[]{:S(2)}, u32[]{:S(2)}) collective-permute-start(bf16[96,2304]{1,0:T(8,128)(2,1)S(1)} %get-tuple-element.231.refs_1_), channel_id=1, source_target_pairs={{0,8},{4,12},{8,0},{12,4},{16,24},{20,28},{24,16},{28,20},{1,9},{5... | collective-permute-start | bytes 1327112 | tf_op jit(solution)/shard_map/ppermute | solution.py:84
  116.6 21.2 %collective-permute-start.27 = (bf16[96,2304]{1,0:T(8,128)(2,1)S(1)}, bf16[96,2304]{1,0:T(8,128)(2,1)S(1)}, u32[]{:S(2)}, u32[]{:S(2)}) collective-permute-start(bf16[96,2304]{1,0:T(8,128)(2,1)S(1)} %get-tuple-element.231.refs_1_), channel_id=1, source_target_pairs={{0,16},{4,20},{8,24},{12,28},{16,0},{20,4},{24,8},{28,12},{1,17},{... | collective-permute-start | bytes 1327112 | tf_op jit(solution)/shard_map/ppermute | solution.py:84
  118.0 19.8 %collective-permute-start.28 = (bf16[96,2304]{1,0:T(8,128)(2,1)S(1)}, bf16[96,2304]{1,0:T(8,128)(2,1)S(1)}, u32[]{:S(2)}, u32[]{:S(2)}) collective-permute-start(bf16[96,2304]{1,0:T(8,128)(2,1)S(1)} %get-tuple-element.231.refs_1_), channel_id=1, source_target_pairs={{0,4},{4,0},{8,12},{12,8},{16,20},{20,16},{24,28},{28,24},{1,5},{5... | collective-permute-start | bytes 1327112 | tf_op jit(solution)/shard_map/ppermute | solution.py:84
  121.2 12.1 %collective-permute-start.18 = (bf16[256,768]{1,0:T(8,128)(2,1)S(1)}, bf16[256,768]{1,0:T(8,128)(2,1)S(1)}, u32[]{:S(2)}, u32[]{:S(2)}) collective-permute-start(bf16[256,768]{1,0:T(8,128)(2,1)S(1)} %get-tuple-element.218.refs_11_), channel_id=1, source_target_pairs={{0,2},{1,3},{2,0},{3,1},{4,6},{5,7},{6,4},{7,5},{8,10},{9,11},{10,... | collective-permute-start | bytes 1179656 | tf_op jit(solution)/shard_map/ppermute | solution.py:80
  124.3 14.5 %collective-permute-start.25 = (bf16[256,768]{1,0:T(8,128)(2,1)S(1)}, bf16[256,768]{1,0:T(8,128)(2,1)S(1)}, u32[]{:S(2)}, u32[]{:S(2)}) collective-permute-start(bf16[256,768]{1,0:T(8,128)(2,1)S(1)} %get-tuple-element.225.refs_22_), channel_id=1, source_target_pairs={{0,2},{1,3},{2,0},{3,1},{4,6},{5,7},{6,4},{7,5},{8,10},{9,11},{10,... | collective-permute-start | bytes 1179656 | tf_op jit(solution)/shard_map/ppermute | solution.py:80
  143.6 13.0 %collective-permute-start.32 = (bf16[96,2304]{1,0:T(8,128)(2,1)S(1)}, bf16[96,2304]{1,0:T(8,128)(2,1)S(1)}, u32[]{:S(2)}, u32[]{:S(2)}) collective-permute-start(bf16[96,2304]{1,0:T(8,128)(2,1)S(1)} %collective-permute-done.26.refs_22_.refs_3_), channel_id=1, source_target_pairs={{0,4},{4,0},{8,12},{12,8},{16,20},{20,16},{24,28},{28,24},{1,5},{5... | collective-permute-start | bytes 1327112 | tf_op jit(solution)/shard_map/ppermute | solution.py:84
  144.4 16.3 %collective-permute-start.36 = (bf16[96,2304]{1,0:T(8,128)(2,1)S(1)}, bf16[96,2304]{1,0:T(8,128)(2,1)S(1)}, u32[]{:S(2)}, u32[]{:S(2)}) collective-permute-start(bf16[96,2304]{1,0:T(8,128)(2,1)S(1)} %get-tuple-element.231.refs_1_), channel_id=1, source_target_pairs={{0,24},{4,28},{8,16},{12,20},{16,8},{20,12},{24,0},{28,4},{1,25},{... | collective-permute-start | bytes 1327112 | tf_op jit(solution)/shard_map/ppermute | solution.py:84
  146.9 18.8 %collective-permute-start.37 = (bf16[96,2304]{1,0:T(8,128)(2,1)S(1)}, bf16[96,2304]{1,0:T(8,128)(2,1)S(1)}, u32[]{:S(2)}, u32[]{:S(2)}) collective-permute-start(bf16[96,2304]{1,0:T(8,128)(2,1)S(1)} %collective-permute-done.27.refs_23_.refs_5_), channel_id=1, source_target_pairs={{0,4},{4,0},{8,12},{12,8},{16,20},{20,16},{24,28},{28,24},{1,5},{5... | collective-permute-start | bytes 1327112 | tf_op jit(solution)/shard_map/ppermute | solution.py:84
  148.1 12.1 %collective-permute-start.31 = (bf16[256,768]{1,0:T(8,128)(2,1)S(1)}, bf16[256,768]{1,0:T(8,128)(2,1)S(1)}, u32[]{:S(2)}, u32[]{:S(2)}) collective-permute-start(bf16[256,768]{1,0:T(8,128)(2,1)S(1)} %get-tuple-element.236.refs_25_), channel_id=1, source_target_pairs={{0,2},{1,3},{2,0},{3,1},{4,6},{5,7},{6,4},{7,5},{8,10},{9,11},{10,... | collective-permute-start | bytes 1179656 | tf_op jit(solution)/shard_map/ppermute | solution.py:80
  149.8 17.4 %collective-permute-start.35 = (bf16[256,768]{1,0:T(8,128)(2,1)S(1)}, bf16[256,768]{1,0:T(8,128)(2,1)S(1)}, u32[]{:S(2)}, u32[]{:S(2)}) collective-permute-start(bf16[256,768]{1,0:T(8,128)(2,1)S(1)} %get-tuple-element.237.refs_28_), channel_id=1, source_target_pairs={{0,2},{1,3},{2,0},{3,1},{4,6},{5,7},{6,4},{7,5},{8,10},{9,11},{10,... | collective-permute-start | bytes 1179656 | tf_op jit(solution)/shard_map/ppermute | solution.py:80
  179.2 12.2 %collective-permute-start.41 = (bf16[96,2304]{1,0:T(8,128)(2,1)S(1)}, bf16[96,2304]{1,0:T(8,128)(2,1)S(1)}, u32[]{:S(2)}, u32[]{:S(2)}) collective-permute-start(bf16[96,2304]{1,0:T(8,128)(2,1)S(1)} %collective-permute-done.36.refs_29_.refs_7_), channel_id=1, source_target_pairs={{0,4},{4,0},{8,12},{12,8},{16,20},{20,16},{24,28},{28,24},{1,5},{5... | collective-permute-start | bytes 1327112 | tf_op jit(solution)/shard_map/ppermute | solution.py:84
  180.1 12.0 %collective-permute-start.40 = (bf16[256,768]{1,0:T(8,128)(2,1)S(1)}, bf16[256,768]{1,0:T(8,128)(2,1)S(1)}, u32[]{:S(2)}, u32[]{:S(2)}) collective-permute-start(bf16[256,768]{1,0:T(8,128)(2,1)S(1)} %get-tuple-element.257.refs_39_), channel_id=1, source_target_pairs={{0,2},{1,3},{2,0},{3,1},{4,6},{5,7},{6,4},{7,5},{8,10},{9,11},{10,... | collective-permute-start | bytes 1179656 | tf_op jit(solution)/shard_map/ppermute | solution.py:80
  183.9 15.5 %collective-permute-start.44 = (bf16[256,768]{1,0:T(8,128)(2,1)S(1)}, bf16[256,768]{1,0:T(8,128)(2,1)S(1)}, u32[]{:S(2)}, u32[]{:S(2)}) collective-permute-start(bf16[256,768]{1,0:T(8,128)(2,1)S(1)} %get-tuple-element.264.refs_46_), channel_id=1, source_target_pairs={{0,2},{1,3},{2,0},{3,1},{4,6},{5,7},{6,4},{7,5},{8,10},{9,11},{10,... | collective-permute-start | bytes 1179656 | tf_op jit(solution)/shard_map/ppermute | solution.py:80
  204.6 12.0 %collective-permute-start.47 = (bf16[256,768]{1,0:T(8,128)(2,1)S(1)}, bf16[256,768]{1,0:T(8,128)(2,1)S(1)}, u32[]{:S(2)}, u32[]{:S(2)}) collective-permute-start(bf16[256,768]{1,0:T(8,128)(2,1)S(1)} %get-tuple-element.273.refs_53_), channel_id=1, source_target_pairs={{0,2},{1,3},{2,0},{3,1},{4,6},{5,7},{6,4},{7,5},{8,10},{9,11},{10,... | collective-permute-start | bytes 1179656 | tf_op jit(solution)/shard_map/ppermute | solution.py:80
  206.3 18.7 %collective-permute-start.49 = (bf16[256,768]{1,0:T(8,128)(2,1)S(1)}, bf16[256,768]{1,0:T(8,128)(2,1)S(1)}, u32[]{:S(2)}, u32[]{:S(2)}) collective-permute-start(bf16[256,768]{1,0:T(8,128)(2,1)S(1)} %get-tuple-element.274.refs_55_), channel_id=1, source_target_pairs={{0,2},{1,3},{2,0},{3,1},{4,6},{5,7},{6,4},{7,5},{8,10},{9,11},{10,... | collective-permute-start | bytes 1179656 | tf_op jit(solution)/shard_map/ppermute | solution.py:80
  207.8 25.2 %collective-permute-start.50 = (bf16[256,768]{1,0:T(8,128)(2,1)S(1)}, bf16[256,768]{1,0:T(8,128)(2,1)S(1)}, u32[]{:S(2)}, u32[]{:S(2)}) collective-permute-start(bf16[256,768]{1,0:T(8,128)(2,1)S(1)} %bitcast.205), channel_id=1, source_target_pairs={{0,2},{1,3},{2,0},{3,1},{4,6},{5,7},{6,4},{7,5},{8,10},{9,11},{10,... | collective-permute-start | bytes 1179656 | tf_op jit(solution)/shard_map/ppermute | solution.py:80
  253.0 16.2 %collective-permute-start.57 = (bf16[4,96,768]{2,1,0:T(8,128)(2,1)S(1)}, bf16[4,96,768]{2,1,0:T(8,128)(2,1)S(1)}, u32[]{:S(2)}, u32[]{:S(2)}) collective-permute-start(bf16[4,96,768]{2,1,0:T(8,128)(2,1)S(1)} %get-tuple-element.302.refs_51_), channel_id=1, source_target_pairs={{0,4},{4,0},{8,12},{12,8},{16,20},{20,16},{24,28},{28,24},{1,5},{5... | collective-permute-start | bytes 1769480 | tf_op jit(solution)/shard_map/ppermute | solution.py:84
  254.1 11.1 %collective-permute-start.56 = (bf16[256,768]{1,0:T(8,128)(2,1)S(1)}, bf16[256,768]{1,0:T(8,128)(2,1)S(1)}, u32[]{:S(2)}, u32[]{:S(2)}) collective-permute-start(bf16[256,768]{1,0:T(8,128)(2,1)S(1)} %get-tuple-element.298.refs_65_), channel_id=1, source_target_pairs={{0,2},{1,3},{2,0},{3,1},{4,6},{5,7},{6,4},{7,5},{8,10},{9,11},{10,... | collective-permute-start | bytes 1179656 | tf_op jit(solution)/shard_map/ppermute | solution.py:80
  255.6 26.2 %collective-permute-start.59 = (bf16[4,96,768]{2,1,0:T(8,128)(2,1)S(1)}, bf16[4,96,768]{2,1,0:T(8,128)(2,1)S(1)}, u32[]{:S(2)}, u32[]{:S(2)}) collective-permute-start(bf16[4,96,768]{2,1,0:T(8,128)(2,1)S(1)} %get-tuple-element.304), channel_id=1, source_target_pairs={{0,4},{4,0},{8,12},{12,8},{16,20},{20,16},{24,28},{28,24},{1,5},{5... | collective-permute-start | bytes 1769480 | tf_op jit(solution)/shard_map/ppermute | solution.py:84
  269.8 11.5 %collective-permute-start.55 = (bf16[256,768]{1,0:T(8,128)(2,1)S(1)}, bf16[256,768]{1,0:T(8,128)(2,1)S(1)}, u32[]{:S(2)}, u32[]{:S(2)}) collective-permute-start(bf16[256,768]{1,0:T(8,128)(2,1)S(1)} %get-tuple-element.300.refs_62_), channel_id=1, source_target_pairs={{0,2},{1,3},{2,0},{3,1},{4,6},{5,7},{6,4},{7,5},{8,10},{9,11},{10,... | collective-permute-start | bytes 1179656 | tf_op jit(solution)/shard_map/ppermute | solution.py:80
  271.4 22.5 %collective-permute-start.61 = (bf16[4,96,768]{2,1,0:T(8,128)(2,1)S(1)}, bf16[4,96,768]{2,1,0:T(8,128)(2,1)S(1)}, u32[]{:S(2)}, u32[]{:S(2)}) collective-permute-start(bf16[4,96,768]{2,1,0:T(8,128)(2,1)S(1)} %get-tuple-element.312), channel_id=1, source_target_pairs={{0,4},{4,0},{8,12},{12,8},{16,20},{20,16},{24,28},{28,24},{1,5},{5... | collective-permute-start | bytes 1769480 | tf_op jit(solution)/shard_map/ppermute | solution.py:84
  297.1 11.9 %collective-permute-start.65 = (bf16[256,768]{1,0:T(8,128)(2,1)S(1)}, bf16[256,768]{1,0:T(8,128)(2,1)S(1)}, u32[]{:S(2)}, u32[]{:S(2)}) collective-permute-start(bf16[256,768]{1,0:T(8,128)(2,1)S(1)} %get-tuple-element.314.refs_41_), channel_id=1, source_target_pairs={{0,2},{1,3},{2,0},{3,1},{4,6},{5,7},{6,4},{7,5},{8,10},{9,11},{10,... | collective-permute-start | bytes 1179656 | tf_op jit(solution)/shard_map/ppermute | solution.py:80
  300.2 21.1 %collective-permute-start.66 = (bf16[96,2304]{1,0:T(8,128)(2,1)S(1)}, bf16[96,2304]{1,0:T(8,128)(2,1)S(1)}, u32[]{:S(2)}, u32[]{:S(2)}) collective-permute-start(bf16[96,2304]{1,0:T(8,128)(2,1)S(1)} %get-tuple-element.325), channel_id=1, source_target_pairs={{0,8},{4,12},{8,0},{12,4},{16,24},{20,28},{24,16},{28,20},{1,9},{5... | collective-permute-start | bytes 1327112 | tf_op jit(solution)/shard_map/ppermute | solution.py:84
  301.8 22.3 %collective-permute-start.67 = (bf16[96,2304]{1,0:T(8,128)(2,1)S(1)}, bf16[96,2304]{1,0:T(8,128)(2,1)S(1)}, u32[]{:S(2)}, u32[]{:S(2)}) collective-permute-start(bf16[96,2304]{1,0:T(8,128)(2,1)S(1)} %get-tuple-element.326), channel_id=1, source_target_pairs={{0,16},{4,20},{8,24},{12,28},{16,0},{20,4},{24,8},{28,12},{1,17},{... | collective-permute-start | bytes 1327112 | tf_op jit(solution)/shard_map/ppermute | solution.py:84
  302.4 14.5 %collective-permute-start.64 = (bf16[256,768]{1,0:T(8,128)(2,1)S(1)}, bf16[256,768]{1,0:T(8,128)(2,1)S(1)}, u32[]{:S(2)}, u32[]{:S(2)}) collective-permute-start(bf16[256,768]{1,0:T(8,128)(2,1)S(1)} %get-tuple-element.316.refs_44_), channel_id=1, source_target_pairs={{0,2},{1,3},{2,0},{3,1},{4,6},{5,7},{6,4},{7,5},{8,10},{9,11},{10,... | collective-permute-start | bytes 1179656 | tf_op jit(solution)/shard_map/ppermute | solution.py:80
  309.6 17.3 %collective-permute-start.69 = (bf16[256,768]{1,0:T(8,128)(2,1)S(1)}, bf16[256,768]{1,0:T(8,128)(2,1)S(1)}, u32[]{:S(2)}, u32[]{:S(2)}) collective-permute-start(bf16[256,768]{1,0:T(8,128)(2,1)S(1)} %get-tuple-element.321.refs_1_.refs_32_.refs_27_.refs_29_.refs_9_.refs_22_.refs_0_), channel_id=1, source_target_pairs={{0,1},{1,0},{2,3},{3,2},{4,5},{5,4},{6,7},{7,6},{8,9},{9,8},{10,11... | collective-permute-start | bytes 1179656 | tf_op jit(solution)/shard_map/ppermute | solution.py:76
  329.5 16.2 %collective-permute-start.74 = (bf16[4,96,768]{2,1,0:T(8,128)(2,1)S(1)}, bf16[4,96,768]{2,1,0:T(8,128)(2,1)S(1)}, u32[]{:S(2)}, u32[]{:S(2)}) collective-permute-start(bf16[4,96,768]{2,1,0:T(8,128)(2,1)S(1)} %get-tuple-element.343), channel_id=1, source_target_pairs={{0,4},{4,0},{8,12},{12,8},{16,20},{20,16},{24,28},{28,24},{1,5},{5... | collective-permute-start | bytes 1769480 | tf_op jit(solution)/shard_map/ppermute | solution.py:84
  332.9 13.5 %collective-permute-start.73 = (bf16[256,768]{1,0:T(8,128)(2,1)S(1)}, bf16[256,768]{1,0:T(8,128)(2,1)S(1)}, u32[]{:S(2)}, u32[]{:S(2)}) collective-permute-start(bf16[256,768]{1,0:T(8,128)(2,1)S(1)} %get-tuple-element.339.refs_39_), channel_id=1, source_target_pairs={{0,2},{1,3},{2,0},{3,1},{4,6},{5,7},{6,4},{7,5},{8,10},{9,11},{10,... | collective-permute-start | bytes 1179656 | tf_op jit(solution)/shard_map/ppermute | solution.py:80
  339.2 34.0 %collective-permute-start.76 = (bf16[4,96,768]{2,1,0:T(8,128)(2,1)S(1)}, bf16[4,96,768]{2,1,0:T(8,128)(2,1)S(1)}, u32[]{:S(2)}, u32[]{:S(2)}) collective-permute-start(bf16[4,96,768]{2,1,0:T(8,128)(2,1)S(1)} %get-tuple-element.344.refs_24_), channel_id=1, source_target_pairs={{0,4},{4,0},{8,12},{12,8},{16,20},{20,16},{24,28},{28,24},{1,5},{5... | collective-permute-start | bytes 1769480 | tf_op jit(solution)/shard_map/ppermute | solution.py:84
  347.1 17.2 %collective-permute-start.75 = (bf16[256,768]{1,0:T(8,128)(2,1)S(1)}, bf16[256,768]{1,0:T(8,128)(2,1)S(1)}, u32[]{:S(2)}, u32[]{:S(2)}) collective-permute-start(bf16[256,768]{1,0:T(8,128)(2,1)S(1)} %get-tuple-element.346.refs_0_.refs_19_.refs_21_.refs_23_.refs_17_.refs_3_.refs_12_.refs_9_), channel_id=1, source_target_pairs={{0,1},{1,0},{2,3},{3,2},{4,5},{5,4},{6,7},{7,6},{8,9},{9,8},{10,11... | collective-permute-start | bytes 1179656 | tf_op jit(solution)/shard_map/ppermute | solution.py:76
  347.1 26.0 %collective-permute-start.72 = (bf16[256,768]{1,0:T(8,128)(2,1)S(1)}, bf16[256,768]{1,0:T(8,128)(2,1)S(1)}, u32[]{:S(2)}, u32[]{:S(2)}) collective-permute-start(bf16[256,768]{1,0:T(8,128)(2,1)S(1)} %get-tuple-element.341.refs_36_), channel_id=1, source_target_pairs={{0,2},{1,3},{2,0},{3,1},{4,6},{5,7},{6,4},{7,5},{8,10},{9,11},{10,... | collective-permute-start | bytes 1179656 | tf_op jit(solution)/shard_map/ppermute | solution.py:80
  348.3 13.9 %collective-permute-start.78 = (bf16[96,768]{1,0:T(8,128)(2,1)S(1)}, bf16[96,768]{1,0:T(8,128)(2,1)S(1)}, u32[]{:S(2)}, u32[]{:S(2)}) collective-permute-start(bf16[96,768]{1,0:T(8,128)(2,1)S(1)} %get-tuple-element.348), channel_id=1, source_target_pairs={{0,16},{4,20},{8,24},{12,28},{16,0},{20,4},{24,8},{28,12},{1,17},{... | collective-permute-start | bytes 442376 | tf_op jit(solution)/shard_map/ppermute | solution.py:84
  351.6 11.9 %collective-permute-start.79 = (bf16[96,768]{1,0:T(8,128)(2,1)S(1)}, bf16[96,768]{1,0:T(8,128)(2,1)S(1)}, u32[]{:S(2)}, u32[]{:S(2)}) collective-permute-start(bf16[96,768]{1,0:T(8,128)(2,1)S(1)} %get-tuple-element.349), channel_id=1, source_target_pairs={{0,24},{4,28},{8,16},{12,20},{16,8},{20,12},{24,0},{28,4},{1,25},{... | collective-permute-start | bytes 442376 | tf_op jit(solution)/shard_map/ppermute | solution.py:84
  362.2 16.3 %collective-permute-start.81 = (bf16[4,96,768]{2,1,0:T(8,128)(2,1)S(1)}, bf16[4,96,768]{2,1,0:T(8,128)(2,1)S(1)}, u32[]{:S(2)}, u32[]{:S(2)}) collective-permute-start(bf16[4,96,768]{2,1,0:T(8,128)(2,1)S(1)} %get-tuple-element.356), channel_id=1, source_target_pairs={{0,4},{4,0},{8,12},{12,8},{16,20},{20,16},{24,28},{28,24},{1,5},{5... | collective-permute-start | bytes 1769480 | tf_op jit(solution)/shard_map/ppermute | solution.py:84
  363.5 25.1 %collective-permute-start.83 = (bf16[4,96,768]{2,1,0:T(8,128)(2,1)S(1)}, bf16[4,96,768]{2,1,0:T(8,128)(2,1)S(1)}, u32[]{:S(2)}, u32[]{:S(2)}) collective-permute-start(bf16[4,96,768]{2,1,0:T(8,128)(2,1)S(1)} %get-tuple-element.359), channel_id=1, source_target_pairs={{0,4},{4,0},{8,12},{12,8},{16,20},{20,16},{24,28},{28,24},{1,5},{5... | collective-permute-start | bytes 1769480 | tf_op jit(solution)/shard_map/ppermute | solution.py:84
  364.2 12.0 %collective-permute-start.82 = (bf16[96,2304]{1,0:T(8,128)(2,1)S(1)}, bf16[96,2304]{1,0:T(8,128)(2,1)S(1)}, u32[]{:S(2)}, u32[]{:S(2)}) collective-permute-start(bf16[96,2304]{1,0:T(8,128)(2,1)S(1)} %get-tuple-element.357), channel_id=1, source_target_pairs={{0,24},{4,28},{8,16},{12,20},{16,8},{20,12},{24,0},{28,4},{1,25},{... | collective-permute-start | bytes 1327112 | tf_op jit(solution)/shard_map/ppermute | solution.py:84
  390.6 11.2 %collective-permute-start.84 = (bf16[1024,384]{1,0:T(8,128)(2,1)S(1)}, bf16[1024,384]{1,0:T(8,128)(2,1)S(1)}, u32[]{:S(2)}, u32[]{:S(2)}) collective-permute-start(bf16[1024,384]{1,0:T(8,128)(2,1)S(1)} %get-tuple-element.362.refs_16_), channel_id=1, source_target_pairs={{0,1},{1,0},{2,3},{3,2},{4,5},{5,4},{6,7},{7,6},{8,9},{9,8},{10,11... | collective-permute-start | bytes 2359304 | tf_op jit(solution)/shard_map/ppermute | solution.py:76
  395.4 25.5 %collective-permute-start.91 = (bf16[4,96,768]{2,1,0:T(8,128)(2,1)S(1)}, bf16[4,96,768]{2,1,0:T(8,128)(2,1)S(1)}, u32[]{:S(2)}, u32[]{:S(2)}) collective-permute-start(bf16[4,96,768]{2,1,0:T(8,128)(2,1)S(1)} %get-tuple-element.371), channel_id=1, source_target_pairs={{0,4},{4,0},{8,12},{12,8},{16,20},{20,16},{24,28},{28,24},{1,5},{5... | collective-permute-start | bytes 1769480 | tf_op jit(solution)/shard_map/ppermute | solution.py:84
  396.8 22.6 %collective-permute-start.87 = (bf16[96,2304]{1,0:T(8,128)(2,1)S(1)}, bf16[96,2304]{1,0:T(8,128)(2,1)S(1)}, u32[]{:S(2)}, u32[]{:S(2)}) collective-permute-start(bf16[96,2304]{1,0:T(8,128)(2,1)S(1)} %get-tuple-element.368), channel_id=1, source_target_pairs={{0,8},{4,12},{8,0},{12,4},{16,24},{20,28},{24,16},{28,20},{1,9},{5... | collective-permute-start | bytes 1327112 | tf_op jit(solution)/shard_map/ppermute | solution.py:84
  402.5 17.0 %collective-permute-start.86 = (bf16[8,64,384]{2,1,0:T(8,128)(2,1)S(1)}, bf16[8,64,384]{2,1,0:T(8,128)(2,1)S(1)}, u32[]{:S(2)}, u32[]{:S(2)}) collective-permute-start(bf16[8,64,384]{2,1,0:T(8,128)(2,1)S(1)} %get-tuple-element.367.refs_2_), channel_id=1, source_target_pairs={{0,2},{1,3},{2,0},{3,1},{4,6},{5,7},{6,4},{7,5},{8,10},{9,11},{10,... | collective-permute-start | bytes 1179656 | tf_op jit(solution)/shard_map/ppermute | solution.py:80
  403.5 36.2 %collective-permute-start.95 = (bf16[96,2304]{1,0:T(8,128)(2,1)S(1)}, bf16[96,2304]{1,0:T(8,128)(2,1)S(1)}, u32[]{:S(2)}, u32[]{:S(2)}) collective-permute-start(bf16[96,2304]{1,0:T(8,128)(2,1)S(1)} %get-tuple-element.377), channel_id=1, source_target_pairs={{0,16},{4,20},{8,24},{12,28},{16,0},{20,4},{24,8},{28,12},{1,17},{... | collective-permute-start | bytes 1327112 | tf_op jit(solution)/shard_map/ppermute | solution.py:84
  413.7 29.6 %collective-permute-start.96 = (bf16[96,2304]{1,0:T(8,128)(2,1)S(1)}, bf16[96,2304]{1,0:T(8,128)(2,1)S(1)}, u32[]{:S(2)}, u32[]{:S(2)}) collective-permute-start(bf16[96,2304]{1,0:T(8,128)(2,1)S(1)} %get-tuple-element.378), channel_id=1, source_target_pairs={{0,24},{4,28},{8,16},{12,20},{16,8},{20,12},{24,0},{28,4},{1,25},{... | collective-permute-start | bytes 1327112 | tf_op jit(solution)/shard_map/ppermute | solution.py:84
  420.2 21.6 %collective-permute-start.89 = (bf16[4,64,384]{2,1,0:T(8,128)(2,1)S(1)}, bf16[4,64,384]{2,1,0:T(8,128)(2,1)S(1)}, u32[]{:S(2)}, u32[]{:S(2)}) collective-permute-start(bf16[4,64,384]{2,1,0:T(8,128)(2,1)S(1)} %get-tuple-element.370), channel_id=1, source_target_pairs={{0,4},{4,0},{8,12},{12,8},{16,20},{20,16},{24,28},{28,24},{1,5},{5... | collective-permute-start | bytes 589832 | tf_op jit(solution)/shard_map/ppermute | solution.py:84
  421.6 31.9 %collective-permute-start.97 = (bf16[96,768]{1,0:T(8,128)(2,1)S(1)}, bf16[96,768]{1,0:T(8,128)(2,1)S(1)}, u32[]{:S(2)}, u32[]{:S(2)}) collective-permute-start(bf16[96,768]{1,0:T(8,128)(2,1)S(1)} %get-tuple-element.379), channel_id=1, source_target_pairs={{0,8},{4,12},{8,0},{12,4},{16,24},{20,28},{24,16},{28,20},{1,9},{5... | collective-permute-start | bytes 442376 | tf_op jit(solution)/shard_map/ppermute | solution.py:84
  421.7 18.0 %collective-permute-start.90 = (f32[8,768]{1,0:T(8,128)S(1)}, f32[8,768]{1,0:T(8,128)S(1)}, u32[]{:S(2)}, u32[]{:S(2)}) collective-permute-start(f32[8,768]{1,0:T(8,128)S(1)} %shard_map.271.refs_3_.refs_0_), channel_id=1, source_target_pairs={{0,4},{4,0},{8,12},{12,8},{16,20},{20,16},{24,28},{28,24},{1,5},{5... | collective-permute-start | bytes 73736 | tf_op jit(solution)/shard_map/ppermute | solution.py:84
  439.7 18.0 %collective-permute-start.98 = (bf16[96,768]{1,0:T(8,128)(2,1)S(1)}, bf16[96,768]{1,0:T(8,128)(2,1)S(1)}, u32[]{:S(2)}, u32[]{:S(2)}) collective-permute-start(bf16[96,768]{1,0:T(8,128)(2,1)S(1)} %get-tuple-element.380), channel_id=1, source_target_pairs={{0,16},{4,20},{8,24},{12,28},{16,0},{20,4},{24,8},{28,12},{1,17},{... | collective-permute-start | bytes 442376 | tf_op jit(solution)/shard_map/ppermute | solution.py:84
  439.7 18.0 %collective-permute-start.99 = (bf16[96,768]{1,0:T(8,128)(2,1)S(1)}, bf16[96,768]{1,0:T(8,128)(2,1)S(1)}, u32[]{:S(2)}, u32[]{:S(2)}) collective-permute-start(bf16[96,768]{1,0:T(8,128)(2,1)S(1)} %get-tuple-element.381), channel_id=1, source_target_pairs={{0,24},{4,28},{8,16},{12,20},{16,8},{20,12},{24,0},{28,4},{1,25},{... | collective-permute-start | bytes 442376 | tf_op jit(solution)/shard_map/ppermute | solution.py:84
  441.8 11.1 %collective-permute-start.100 = (f32[8,768]{1,0:T(8,128)S(1)}, f32[8,768]{1,0:T(8,128)S(1)}, u32[]{:S(2)}, u32[]{:S(2)}) collective-permute-start(f32[8,768]{1,0:T(8,128)S(1)} %shard_map.275.refs_2_.refs_0_), channel_id=1, source_target_pairs={{0,8},{4,12},{8,0},{12,4},{16,24},{20,28},{24,16},{28,20},{1,9},{5... | collective-permute-start | bytes 73736 | tf_op jit(solution)/shard_map/ppermute | solution.py:84
  443.3 14.4 %collective-permute-start.92 = (bf16[2,64,384]{2,1,0:T(8,128)(2,1)S(1)}, bf16[2,64,384]{2,1,0:T(8,128)(2,1)S(1)}, u32[]{:S(2)}, u32[]{:S(2)}) collective-permute-start(bf16[2,64,384]{2,1,0:T(8,128)(2,1)S(1)} %get-tuple-element.374), channel_id=1, source_target_pairs={{0,8},{4,12},{8,0},{12,4},{16,24},{20,28},{24,16},{28,20},{1,9},{5... | collective-permute-start | bytes 294920 | tf_op jit(solution)/shard_map/ppermute | solution.py:84
  452.9 11.5 %collective-permute-start.93 = (bf16[2,64,384]{2,1,0:T(8,128)(2,1)S(1)}, bf16[2,64,384]{2,1,0:T(8,128)(2,1)S(1)}, u32[]{:S(2)}, u32[]{:S(2)}) collective-permute-start(bf16[2,64,384]{2,1,0:T(8,128)(2,1)S(1)} %get-tuple-element.375), channel_id=1, source_target_pairs={{0,16},{4,20},{8,24},{12,28},{16,0},{20,4},{24,8},{28,12},{1,17},{... | collective-permute-start | bytes 294920 | tf_op jit(solution)/shard_map/ppermute | solution.py:84
  465.6 13.8 %collective-permute-start.102 = (bf16[8,64,384]{2,1,0:T(8,128)(2,1)S(1)}, bf16[8,64,384]{2,1,0:T(8,128)(2,1)S(1)}, u32[]{:S(2)}, u32[]{:S(2)}) collective-permute-start(bf16[8,64,384]{2,1,0:T(8,128)(2,1)S(1)} %shard_map.278.refs_2_), channel_id=1, source_target_pairs={{0,1},{1,0},{2,3},{3,2},{4,5},{5,4},{6,7},{7,6},{8,9},{9,8},{10,11... | collective-permute-start | bytes 1179656 | tf_op jit(solution)/shard_map/ppermute | solution.py:76
  (76 other events, 492.4 us)

commit v4 on v3

--- a/solution.py
+++ b/solution.py
@@ -1008,8 +1008,8 @@
             coming.append((first, second))
             if len(first) > 1:
                 points = {
-                    "place": (first, (2, 4, 6)),
-                    ("norm_one", 0): (first, (1, 3, 5, 7)),
+                    "place": (first, (2, 4)),
+                    ("norm_one", 0): (first, (6, 1, 3, 5)),
                     ("norm_one", 1): (second, (2, 4, 1)),
                     ("norm_two", 0): (second, (3,)),
                     ("norm_two", 1): (second, (6, 5)),
@@ -1017,11 +1017,21 @@
         if layer and len(here[0]) > 1:
             points[("norm_one", 0)] = (here[1], (7,))
 
-        def at(point, points=points):
+        def at(point, points=points, layer=layer):
+            if layer == 0 and point == ("norm_one", 0):
+                for k in range(chunks):
+                    incoming.append(
+                        call(
+                            functools.partial(seed_kernel, k), [sds(quarter, width)],
+                            where, own, other, scalars=1,
+                        )
+                    )
+                    keep(*incoming[-1])
             found, steps = points.get(point, ({}, ()))
             return tuple(found[step] for step in steps)
 
         if layer == 0:
+            incoming = []
             first_weight, second_weight = gather_finish(where, here[0], widths, at("place"))
             dealt = deal_finish(moving, where, local_order)
             pieces = [dealt]
@@ -1037,15 +1047,8 @@
         saved_all.append(saved)
         if layer < LAYERS - 1:
             pieces = [p for piece in residual for p in (piece, swap_core(piece))]
-    layer_outputs = call(
-        show_kernel, [sds(quarter, width, dtype=F32)], where, *current, scalars=1
-    )
-    incoming = [
-        call(
-            functools.partial(seed_kernel, k), [sds(quarter, width)], where, own, other, scalars=1
-        )
-        for k in range(chunks)
-    ]
+    keep(*current)
+    shown = []
     received, vectors, steps = [None] * LAYERS, [None] * LAYERS, []
     for step in (1, 2):
         steps.append(lambda v, s=step: lax.ppermute(v, "tensor", [(i, i ^ s) for i in range(4)]))
@@ -1063,6 +1066,13 @@
     def at(layer, point):
         if isinstance(point, list):
             own_sums["second"] = point
+            if not shown:
+                shown.extend(
+                    call(
+                        show_kernel, [sds(quarter, width, dtype=F32)], where, *current, scalars=1
+                    )
+                )
+                drop(*current)
             return ()
         if point[0] == "vectors":
             vectors[layer] = point[1]
@@ -1084,13 +1094,14 @@
         if layer == LAYERS - 1:
             return found
         if point == ("norm_two", 1):
-            return tuple(above["second"][1:3])
+            return tuple(above["second"][2:3])
         if point == ("norm_one", 0):
             above["first"] = scatter_finish(where, above["first"])
-        if point == ("norm_one", 1):
-            return found + tuple(above["first"][1:])
+            return tuple(above["second"][1:2])
         if point == ("attend_back", 1):
             return found + tuple(above["second"][3:])
+        if point == "input":
+            return found + tuple(above["first"][1:])
         return found
 
     for layer in reversed(range(LAYERS)):
@@ -1150,22 +1161,22 @@
     )
     received[1] = [total_call(above["first"]), total_call(above["second"])]
     received[0] = [first_sum, second_sum]
+    shapes = (
+        jnp.swapaxes(project_weight, 1, 2), gate_up_weight, output_weight,
+        jnp.swapaxes(down_weight, 1, 2),
+    )
+    project_grad, gate_up_grad, output_grad, down_grad = call(
+        functools.partial(grads_kernel, tuple(tuple(len(g) for g in r) for r in received)),
+        [sds(*w.shape, dtype=F32) for w in shapes],
+        *[r for groups in received for group in groups for r in group],
+    )
     returned = call(
         functools.partial(last_kernel, split is not None), [sds(count, part, width, dtype=F32)],
         dealing_order, where, near, far, swap_core(near), swap_core(far), scalars=2,
     )[0]
 
-    shapes = (
-        jnp.swapaxes(project_weight, 1, 2), gate_up_weight, output_weight,
-        jnp.swapaxes(down_weight, 1, 2),
-    )
-    project_grad, gate_up_grad, output_grad, down_grad = call(
-        functools.partial(grads_kernel, tuple(tuple(len(g) for g in r) for r in received)),
-        [sds(*w.shape, dtype=F32) for w in shapes],
-        *[r for groups in received for group in groups for r in group],
-    )
     return (
-        layer_outputs[0][None], returned, jnp.swapaxes(project_grad, 1, 2), gate_up_grad, output_grad,
+        shown[0][None], returned, jnp.swapaxes(project_grad, 1, 2), gate_up_grad, output_grad,
         jnp.swapaxes(down_grad, 1, 2), gains_total, biases_total,
     )
 

time: 496 us -> 475 us (0.958)
  waiting for transfers between devices: 222 us -> 211 us
  starting transfers between devices: 115 us -> 109 us
    unnamed x76 -> x72, local copies, waits for them, and re-layouts: 11.8 us -> 7.47 us
  transfers between devices with their start and end apart: 105 -> 105, of which waited for: 56 -> 48; matrix products, arithmetic and copies ran while one was open for 1% -> 1% of each run, Pallas kernels for 20% -> 21%
where the time goes in v4:
time: 475 us; the launch traced here: 466 us
  waiting for transfers between devices  211 us (44%)
  Pallas kernels  129 us (27%)
  starting transfers between devices  109 us (23%)
  local copies, waits for them, and re-layouts  11.3 us (2%)
    ppermute x52, waiting for transfers between devices, swap_dp(): lax.ppermute(value, 'dp', [(i, i ^ step) for i in range(lax.axis_size('dp...  129 us
    pallas_call x103, Pallas kernels, call(): pl.pallas_call(body, in_specs=[smem] * scalars + [vmem] * (used - scalars...  127 us
    ppermute x52, starting transfers between devices, swap_dp(): lax.ppermute(value, 'dp', [(i, i ^ step) for i in range(lax.axis_size('dp...  81.2 us
    ppermute x18, waiting for transfers between devices, swap_x(): lax.ppermute(value, 'tensor', [(i, i ^ 2) for i in range(lax.axis_size('t...  68.8 us
    ppermute x18, starting transfers between devices, swap_x(): lax.ppermute(value, 'tensor', [(i, i ^ 2) for i in range(lax.axis_size('t...  21.1 us
  transfers between devices with their start and end apart: 105, of which 48 were waited for; matrix products, arithmetic and copies ran while one was open for 1% of the time, Pallas kernels for 21%

profile of v4, /device:TPU:0, one launch (start us, length us, event | category | flops | bytes accessed | tf_op | source)
XLA Modules:
  0.0 465.9 jit_solution(15387995730437896453)
XLA Ops:
  6.4 3.0 collective-permute-start.7
  11.0 2.6 collective-permute-start.9
  19.9 7.1 %collective-permute-done.refs_1_ = bf16[4,32,768]{2,1,0:T(8,128)(2,1)S(1)} collective-permute-done((bf16[4,32,768]{2,1,0:T(8,128)(2,1)S(1)}, bf16[4,32,768]{2,1,0:T(8,128)(2,1)S(1)}, u32[]{:S(2)}, u32[]{:S(2)}) %collective-permute-start) | collective-permute-done | bytes 196640 | tf_op jit(solution)/shard_map/ppermute | solution.py:84
  28.8 2.6 collective-permute-start.2
  31.4 8.4 %collective-permute-done.1.refs_1_ = bf16[2,32,768]{2,1,0:T(8,128)(2,1)S(1)} collective-permute-done((bf16[2,32,768]{2,1,0:T(8,128)(2,1)S(1)}, bf16[2,32,768]{2,1,0:T(8,128)(2,1)S(1)}, u32[]{:S(2)}, u32[]{:S(2)}) %collective-permute-start.1) | collective-permute-done | bytes 98336 | tf_op jit(solution)/shard_map/ppermute | solution.py:84
  39.8 3.1 collective-permute-start.3
  47.3 3.1 collective-permute-start.10
  54.0 4.5 collective-permute-done.5.refs_3_
  58.5 4.2 collective-permute-done.10.refs_4_.refs_5_
  64.6 3.8 collective-permute-done.11.refs_5_.refs_6_
  68.4 12.6 %collective-permute-done.12.refs_6_.refs_7_ = bf16[96,3072]{1,0:T(8,128)(2,1)S(1)} collective-permute-done((bf16[96,3072]{1,0:T(8,128)(2,1)}, bf16[96,3072]{1,0:T(8,128)(2,1)S(1)}, u32[]{:S(2)}, u32[]{:S(2)}) %collective-permute-start.12) | collective-permute-done | bytes 589856 | tf_op jit(solution)/shard_map/ppermute | solution.py:84
  84.0 5.0 %collective-permute-done.14.refs_11_.refs_3_ = bf16[96,768]{1,0:T(8,128)(2,1)S(1)} collective-permute-done((bf16[96,768]{1,0:T(8,128)(2,1)S(1)}, bf16[96,768]{1,0:T(8,128)(2,1)S(1)}, u32[]{:S(2)}, u32[]{:S(2)}) %collective-permute-start.14) | collective-permute-done | bytes 147488 | tf_op jit(solution)/shard_map/ppermute | solution.py:84
  92.8 2.1 shard_map.187
  94.9 2.2 shard_map.188
  97.2 2.2 shard_map.189
  99.5 2.5 shard_map.191
  108.3 2.2 shard_map.192
  110.6 3.1 collective-permute-done.18.refs_2_
  119.8 8.6 %collective-permute-done.17.refs_2_ = bf16[256,768]{1,0:T(8,128)(2,1)S(1)} collective-permute-done((bf16[256,768]{1,0:T(8,128)(2,1)S(1)}, bf16[256,768]{1,0:T(8,128)(2,1)S(1)}, u32[]{:S(2)}, u32[]{:S(2)}) %collective-permute-start.17) | collective-permute-done | bytes 393248 | tf_op jit(solution)/shard_map/ppermute | solution.py:80
  130.1 4.2 collective-permute-done.26.refs_24_.refs_3_
  141.5 2.3 collective-permute-start.36
  147.8 6.2 %collective-permute-done.32.refs_29_.refs_4_ = bf16[96,2304]{1,0:T(8,128)(2,1)S(1)} collective-permute-done((bf16[96,2304]{1,0:T(8,128)(2,1)S(1)}, bf16[96,2304]{1,0:T(8,128)(2,1)S(1)}, u32[]{:S(2)}, u32[]{:S(2)}) %collective-permute-start.32) | collective-permute-done | bytes 442400 | tf_op jit(solution)/shard_map/ppermute | solution.py:84
  154.0 3.6 collective-permute-done.31.refs_2_
  158.0 5.0 %collective-permute-done.37.refs_32_.refs_6_ = bf16[96,2304]{1,0:T(8,128)(2,1)S(1)} collective-permute-done((bf16[96,2304]{1,0:T(8,128)(2,1)S(1)}, bf16[96,2304]{1,0:T(8,128)(2,1)S(1)}, u32[]{:S(2)}, u32[]{:S(2)}) %collective-permute-start.37) | collective-permute-done | bytes 442400 | tf_op jit(solution)/shard_map/ppermute | solution.py:84
  165.6 5.7 %collective-permute-done.39.refs_8_ = bf16[96,768]{1,0:T(8,128)(2,1)S(1)} collective-permute-done((bf16[96,768]{1,0:T(8,128)(2,1)S(1)}, bf16[96,768]{1,0:T(8,128)(2,1)S(1)}, u32[]{:S(2)}, u32[]{:S(2)}) %collective-permute-start.39) | collective-permute-done | bytes 147488 | tf_op jit(solution)/shard_map/ppermute | solution.py:84
  172.0 2.4 shard_map.207
  174.3 2.2 shard_map.208
  176.6 2.2 shard_map.209
  179.0 2.2 shard_map.211
  183.7 2.2 shard_map.212
  186.7 7.2 %collective-permute-done.42.refs_47_.refs_8_ = bf16[96,2304]{1,0:T(8,128)(2,1)S(1)} collective-permute-done((bf16[96,2304]{1,0:T(8,128)(2,1)S(1)}, bf16[96,2304]{1,0:T(8,128)(2,1)S(1)}, u32[]{:S(2)}, u32[]{:S(2)}) %collective-permute-start.42) | collective-permute-done | bytes 442400 | tf_op jit(solution)/shard_map/ppermute | solution.py:84
  196.8 4.7 %collective-permute-done.45.refs_2_ = bf16[256,768]{1,0:T(8,128)(2,1)S(1)} collective-permute-done((bf16[256,768]{1,0:T(8,128)(2,1)S(1)}, bf16[256,768]{1,0:T(8,128)(2,1)S(1)}, u32[]{:S(2)}, u32[]{:S(2)}) %collective-permute-start.45) | collective-permute-done | bytes 393248 | tf_op jit(solution)/shard_map/ppermute | solution.py:80
  209.9 8.8 %collective-permute-done.48.refs_2_ = bf16[256,768]{1,0:T(8,128)(2,1)S(1)} collective-permute-done((bf16[256,768]{1,0:T(8,128)(2,1)S(1)}, bf16[256,768]{1,0:T(8,128)(2,1)S(1)}, u32[]{:S(2)}, u32[]{:S(2)}) %collective-permute-start.48) | collective-permute-done | bytes 393248 | tf_op jit(solution)/shard_map/ppermute | solution.py:80
  219.8 6.9 %collective-permute-done.50.refs_2_ = bf16[256,768]{1,0:T(8,128)(2,1)S(1)} collective-permute-done((bf16[256,768]{1,0:T(8,128)(2,1)S(1)}, bf16[256,768]{1,0:T(8,128)(2,1)S(1)}, u32[]{:S(2)}, u32[]{:S(2)}) %collective-permute-start.50) | collective-permute-done | bytes 393248 | tf_op jit(solution)/shard_map/ppermute | solution.py:80
  228.4 2.1 shard_map.226
  233.7 2.1 shard_map.229
  240.1 5.0 %shard_map.233 = (bf16[4,96,2304]{2,1,0:T(8,128)(2,1)S(1)}, bf16[4,96,768]{2,1,0:T(8,128)(2,1)S(1)}, bf16[4,96,768]{2,1,0:T(8,128)(2,1)S(1)}, bf16[4,96,768]{2,1,0:T(8,128)(2,1)S(1)}) custom-call(s32[6]{0:T(128)S(1)} %stack.27.refs_0_.refs_1_, bf16[256,768]{1,0:T(8,128)(2,1)S(1)} %get-tuple-element.265.refs_0_.refs_49_.refs_47_.refs_50_.refs_48_.refs_1_, ...), custom_call_target="tpu_custom_call" | custom-call | flops 3623878 | bytes 11403 | tf_op jit(solution)/shard_map/pallas_call | solution.py:56
  250.1 7.6 %collective-permute-done.56.refs_2_ = bf16[256,768]{1,0:T(8,128)(2,1)S(1)} collective-permute-done((bf16[256,768]{1,0:T(8,128)(2,1)S(1)}, bf16[256,768]{1,0:T(8,128)(2,1)S(1)}, u32[]{:S(2)}, u32[]{:S(2)}) %collective-permute-start.56) | collective-permute-done | bytes 393248 | tf_op jit(solution)/shard_map/ppermute | solution.py:80
  257.7 3.5 collective-permute-done.57.refs_52_.refs_2_
  266.5 6.4 %shard_map.237 = (bf16[512,192]{1,0:T(8,128)(2,1)S(1)}, f32[1024,256]{1,0:T(8,128)S(1)}, f32[1024,192]{1,0:T(8,128)S(1)}) custom-call(bf16[1024,256]{1,0:T(8,128)(2,1)S(1)} %get-tuple-element.245.refs_0_.refs_35_.refs_37_.refs_42_.refs_38_.refs_36_.refs_50_.refs_39_, bf16[512,192]{1,0:T(8,128)(2,1)S(1)} %shard_map.236.refs_1_.refs_49_, ...), custom_call_target="tpu_custom_call" | custom-call | flops 4026531 | bytes 5144 | tf_op jit(solution)/shard_map/pallas_call | solution.py:56
  277.4 7.4 %shard_map.240 = (bf16[1024,576]{1,0:T(8,128)(2,1)S(1)}, f32[1024,256]{1,0:T(8,128)}, f32[1024,192]{1,0:T(8,128)S(1)}) custom-call(bf16[1024,256]{1,0:T(8,128)(2,1)S(1)} %get-tuple-element.245.refs_0_.refs_35_.refs_37_.refs_42_.refs_38_.refs_36_.refs_50_.refs_39_, bf16[512,192]{1,0:T(8,128)(2,1)S(1)} %shard_map.239.refs_1_.refs_51_, ...), custom_call_target="tpu_custom_call" | custom-call | flops 4026531 | bytes 8159 | tf_op jit(solution)/shard_map/pallas_call | solution.py:56
  293.5 2.5 shard_map.248
  295.9 5.1 %collective-permute-done.65.refs_2_ = bf16[256,768]{1,0:T(8,128)(2,1)S(1)} collective-permute-done((bf16[256,768]{1,0:T(8,128)(2,1)S(1)}, bf16[256,768]{1,0:T(8,128)(2,1)S(1)}, u32[]{:S(2)}, u32[]{:S(2)}) %collective-permute-start.65) | collective-permute-done | bytes 393248 | tf_op jit(solution)/shard_map/ppermute | solution.py:80
  303.8 5.1 %collective-permute-done.64.refs_2_ = bf16[256,768]{1,0:T(8,128)(2,1)S(1)} collective-permute-done((bf16[256,768]{1,0:T(8,128)(2,1)S(1)}, bf16[256,768]{1,0:T(8,128)(2,1)S(1)}, u32[]{:S(2)}, u32[]{:S(2)}) %collective-permute-start.64) | collective-permute-done | bytes 393248 | tf_op jit(solution)/shard_map/ppermute | solution.py:80
  308.9 5.3 %collective-permute-done.66.refs_35_.refs_2_ = bf16[96,2304]{1,0:T(8,128)(2,1)S(1)} collective-permute-done((bf16[96,2304]{1,0:T(8,128)(2,1)S(1)}, bf16[96,2304]{1,0:T(8,128)(2,1)S(1)}, u32[]{:S(2)}, u32[]{:S(2)}) %collective-permute-start.66) | collective-permute-done | bytes 442400 | tf_op jit(solution)/shard_map/ppermute | solution.py:84
  320.8 2.3 shard_map.254
  325.0 4.5 shard_map.257
  330.6 5.3 %collective-permute-done.74.refs_2_ = bf16[4,96,768]{2,1,0:T(8,128)(2,1)S(1)} collective-permute-done((bf16[4,96,768]{2,1,0:T(8,128)(2,1)S(1)}, bf16[4,96,768]{2,1,0:T(8,128)(2,1)S(1)}, u32[]{:S(2)}, u32[]{:S(2)}) %collective-permute-start.74) | collective-permute-done | bytes 589856 | tf_op jit(solution)/shard_map/ppermute | solution.py:84
  339.5 2.2 collective-permute-start.79
  342.7 6.4 %shard_map.261 = (bf16[512,192]{1,0:T(8,128)(2,1)S(1)}, f32[1024,256]{1,0:T(8,128)S(1)}, f32[1024,192]{1,0:T(8,128)S(1)}) custom-call(bf16[1024,256]{1,0:T(8,128)(2,1)S(1)} %get-tuple-element.206.refs_0_.refs_5_.refs_6_.refs_8_.refs_12_.refs_9_.refs_7_.refs_20_.refs_17_.refs_11_, bf16[512,192]{1,0:T(8,128)(2,1)S(1)} %shard_map.260.refs_1_.refs_23_, ...), custom_call_target="tpu_custom_call" | custom-call | flops 4026531 | bytes 5144 | tf_op jit(solution)/shard_map/pallas_call | solution.py:56
  349.9 3.5 collective-permute-done.79.refs_26_.refs_3_
  353.4 7.7 %collective-permute-start.82 = (bf16[96,768]{1,0:T(8,128)(2,1)S(1)}, bf16[96,768]{1,0:T(8,128)(2,1)S(1)}, u32[]{:S(2)}, u32[]{:S(2)}) collective-permute-start(bf16[96,768]{1,0:T(8,128)(2,1)S(1)} %get-tuple-element.358), channel_id=1, source_target_pairs={{0,16},{4,20},{8,24},{12,28},{16,0},{20,4},{24,8},{28,12},{1,17},{... | collective-permute-start | bytes 442376 | tf_op jit(solution)/shard_map/ppermute | solution.py:84
  363.7 7.5 %shard_map.265 = (bf16[1024,576]{1,0:T(8,128)(2,1)S(1)}, f32[1024,256]{1,0:T(8,128)}, f32[1024,192]{1,0:T(8,128)S(1)}) custom-call(bf16[1024,256]{1,0:T(8,128)(2,1)S(1)} %get-tuple-element.206.refs_0_.refs_5_.refs_6_.refs_8_.refs_12_.refs_9_.refs_7_.refs_20_.refs_17_.refs_11_, bf16[512,192]{1,0:T(8,128)(2,1)S(1)} %shard_map.264.refs_1_.refs_27_, ...), custom_call_target="tpu_custom_call" | custom-call | flops 4026531 | bytes 8159 | tf_op jit(solution)/shard_map/pallas_call | solution.py:56
  377.3 2.5 shard_map.269
  386.5 8.0 %collective-permute-done.88.refs_1_ = f32[8,768]{1,0:T(8,128)S(1)} collective-permute-done((f32[8,768]{1,0:T(8,128)S(1)}, f32[8,768]{1,0:T(8,128)S(1)}, u32[]{:S(2)}, u32[]{:S(2)}) %collective-permute-start.88) | collective-permute-done | bytes 24608 | tf_op jit(solution)/shard_map/ppermute | solution.py:1054
  396.1 3.7 collective-permute-done.87.refs_2_.refs_5_
  403.4 17.2 %collective-permute-done.95.refs_4_.refs_6_ = bf16[96,2304]{1,0:T(8,128)(2,1)S(1)} collective-permute-done((bf16[96,2304]{1,0:T(8,128)(2,1)S(1)}, bf16[96,2304]{1,0:T(8,128)(2,1)S(1)}, u32[]{:S(2)}, u32[]{:S(2)}) %collective-permute-start.95) | collective-permute-done | bytes 442400 | tf_op jit(solution)/shard_map/ppermute | solution.py:84
  424.2 9.6 %collective-permute-start.92 = (bf16[2,64,384]{2,1,0:T(8,128)(2,1)S(1)}, bf16[2,64,384]{2,1,0:T(8,128)(2,1)S(1)}, u32[]{:S(2)}, u32[]{:S(2)}) collective-permute-start(bf16[2,64,384]{2,1,0:T(8,128)(2,1)S(1)} %get-tuple-element.374), channel_id=1, source_target_pairs={{0,8},{4,12},{8,0},{12,4},{16,24},{20,28},{24,16},{28,20},{1,9},{5... | collective-permute-start | bytes 294920 | tf_op jit(solution)/shard_map/ppermute | solution.py:84
  433.9 2.2 collective-permute-start.94
  436.2 4.4 collective-permute-done.98.refs_7_.refs_2_
  440.6 4.6 collective-permute-done.93.refs_2_
  446.4 7.1 %collective-permute-done.101.refs_3_ = bf16[8,64,384]{2,1,0:T(8,128)(2,1)S(1)} collective-permute-done((bf16[8,64,384]{2,1,0:T(8,128)(2,1)S(1)}, bf16[8,64,384]{2,1,0:T(8,128)(2,1)S(1)}, u32[]{:S(2)}, u32[]{:S(2)}) %collective-permute-start.101) | collective-permute-done | bytes 393248 | tf_op jit(solution)/shard_map/ppermute | solution.py:80
  453.4 2.8 collective-permute-start.104
  463.0 2.5 shard_map.283
  (340 shorter events, 157.1 us)
Async XLA Ops:
  6.4 40.0 %collective-permute-start.7 = (bf16[96,3072]{1,0:T(8,128)(2,1)S(1)}, bf16[96,3072]{1,0:T(8,128)(2,1)S(1)}, u32[]{:S(2)}, u32[]{:S(2)}) collective-permute-start(bf16[96,3072]{1,0:T(8,128)(2,1)S(1)} %shard_map.179.refs_2_.refs_0_.refs_1_), channel_id=1, source_target_pairs={{0,4},{4,0},{8,12},{12,8},{16,20},{20,16},{24,28},{28,24},{1,5},{5... | collective-permute-start | bytes 1769480 | tf_op jit(solution)/shard_map/ppermute | solution.py:84
  9.4 37.0 %collective-permute-start.8 = (bf16[96,3072]{1,0:T(8,128)(2,1)S(1)}, bf16[96,3072]{1,0:T(8,128)(2,1)}, u32[]{:S(2)}, u32[]{:S(2)}) collective-permute-start(bf16[96,3072]{1,0:T(8,128)(2,1)S(1)} %shard_map.179.refs_2_.refs_0_.refs_1_), channel_id=1, source_target_pairs={{0,8},{4,12},{8,0},{12,4},{16,24},{20,28},{24,16},{28,20},{1,9},{5... | collective-permute-start | bytes 1769480 | tf_op jit(solution)/shard_map/ppermute | solution.py:84
  11.0 35.4 %collective-permute-start.9 = (bf16[96,3072]{1,0:T(8,128)(2,1)S(1)}, bf16[96,3072]{1,0:T(8,128)(2,1)S(1)}, u32[]{:S(2)}, u32[]{:S(2)}) collective-permute-start(bf16[96,3072]{1,0:T(8,128)(2,1)S(1)} %shard_map.179.refs_2_.refs_0_.refs_1_), channel_id=1, source_target_pairs={{0,16},{4,20},{8,24},{12,28},{16,0},{20,4},{24,8},{28,12},{1,17},{... | collective-permute-start | bytes 1769480 | tf_op jit(solution)/shard_map/ppermute | solution.py:84
  27.0 12.8 %collective-permute-start.1 = (bf16[2,32,768]{2,1,0:T(8,128)(2,1)S(1)}, bf16[2,32,768]{2,1,0:T(8,128)(2,1)S(1)}, u32[]{:S(2)}, u32[]{:S(2)}) collective-permute-start(bf16[2,32,768]{2,1,0:T(8,128)(2,1)S(1)} %get-tuple-element.201), channel_id=1, source_target_pairs={{0,8},{4,12},{8,0},{12,4},{16,24},{20,28},{24,16},{28,20},{1,9},{5... | collective-permute-start | bytes 294920 | tf_op jit(solution)/shard_map/ppermute | solution.py:84
  28.8 15.6 %collective-permute-start.2 = (bf16[2,32,768]{2,1,0:T(8,128)(2,1)S(1)}, bf16[2,32,768]{2,1,0:T(8,128)(2,1)S(1)}, u32[]{:S(2)}, u32[]{:S(2)}) collective-permute-start(bf16[2,32,768]{2,1,0:T(8,128)(2,1)S(1)} %get-tuple-element.202), channel_id=1, source_target_pairs={{0,16},{4,20},{8,24},{12,28},{16,0},{20,4},{24,8},{28,12},{1,17},{... | collective-permute-start | bytes 294920 | tf_op jit(solution)/shard_map/ppermute | solution.py:84
  47.3 15.4 %collective-permute-start.10 = (bf16[96,3072]{1,0:T(8,128)(2,1)}, bf16[96,3072]{1,0:T(8,128)(2,1)S(1)}, u32[]{:S(2)}, u32[]{:S(2)}) collective-permute-start(bf16[96,3072]{1,0:T(8,128)(2,1)} %shard_map.183.refs_7_), channel_id=1, source_target_pairs={{0,24},{4,28},{8,16},{12,20},{16,8},{20,12},{24,0},{28,4},{1,25},{... | collective-permute-start | bytes 1769480 | tf_op jit(solution)/shard_map/ppermute | solution.py:84
  51.9 16.5 %collective-permute-start.11 = (bf16[96,3072]{1,0:T(8,128)(2,1)}, bf16[96,3072]{1,0:T(8,128)(2,1)S(1)}, u32[]{:S(2)}, u32[]{:S(2)}) collective-permute-start(bf16[96,3072]{1,0:T(8,128)(2,1)} %collective-permute-done.8.refs_2_.refs_3_), channel_id=1, source_target_pairs={{0,4},{4,0},{8,12},{12,8},{16,20},{20,16},{24,28},{28,24},{1,5},{5... | collective-permute-start | bytes 1769480 | tf_op jit(solution)/shard_map/ppermute | solution.py:84
  52.4 28.6 %collective-permute-start.12 = (bf16[96,3072]{1,0:T(8,128)(2,1)}, bf16[96,3072]{1,0:T(8,128)(2,1)S(1)}, u32[]{:S(2)}, u32[]{:S(2)}) collective-permute-start(bf16[96,3072]{1,0:T(8,128)(2,1)} %copy-done.5), channel_id=1, source_target_pairs={{0,4},{4,0},{8,12},{12,8},{16,20},{20,16},{24,28},{28,24},{1,5},{5... | collective-permute-start | bytes 1769480 | tf_op jit(solution)/shard_map/ppermute | solution.py:84
  53.9 37.6 %collective-permute-start.4 = (bf16[8,32,768]{2,1,0:T(8,128)(2,1)S(1)}, bf16[8,32,768]{2,1,0:T(8,128)(2,1)S(1)}, u32[]{:S(2)}, u32[]{:S(2)}) collective-permute-start(bf16[8,32,768]{2,1,0:T(8,128)(2,1)S(1)} %shard_map.182.refs_4_.refs_1_), channel_id=1, source_target_pairs={{0,1},{1,0},{2,3},{3,2},{4,5},{5,4},{6,7},{7,6},{8,9},{9,8},{10,11... | collective-permute-start | bytes 1179656 | tf_op jit(solution)/shard_map/ppermute | solution.py:76
  58.5 33.0 %collective-permute-start.6 = (bf16[8,32,768]{2,1,0:T(8,128)(2,1)}, bf16[8,32,768]{2,1,0:T(8,128)(2,1)S(1)}, u32[]{:S(2)}, u32[]{:S(2)}) collective-permute-start(bf16[8,32,768]{2,1,0:T(8,128)(2,1)} %collective-permute-done.5.refs_3_), channel_id=1, source_target_pairs={{0,1},{1,0},{2,3},{3,2},{4,5},{5,4},{6,7},{7,6},{8,9},{9,8},{10,11... | collective-permute-start | bytes 1179656 | tf_op jit(solution)/shard_map/ppermute | solution.py:76
  62.8 27.4 %collective-permute-start.13 = (bf16[96,3072]{1,0:T(8,128)(2,1)S(1)}, bf16[96,3072]{1,0:T(8,128)(2,1)S(1)}, u32[]{:S(2)}, u32[]{:S(2)}) collective-permute-start(bf16[96,3072]{1,0:T(8,128)(2,1)S(1)} %collective-permute-done.10.refs_4_.refs_5_), channel_id=1, source_target_pairs={{0,4},{4,0},{8,12},{12,8},{16,20},{20,16},{24,28},{28,24},{1,5},{5... | collective-permute-start | bytes 1769480 | tf_op jit(solution)/shard_map/ppermute | solution.py:84
  102.6 11.1 %collective-permute-start.18 = (bf16[256,768]{1,0:T(8,128)(2,1)S(1)}, bf16[256,768]{1,0:T(8,128)(2,1)S(1)}, u32[]{:S(2)}, u32[]{:S(2)}) collective-permute-start(bf16[256,768]{1,0:T(8,128)(2,1)S(1)} %bitcast.205), channel_id=1, source_target_pairs={{0,2},{1,3},{2,0},{3,1},{4,6},{5,7},{6,4},{7,5},{8,10},{9,11},{10,... | collective-permute-start | bytes 1179656 | tf_op jit(solution)/shard_map/ppermute | solution.py:80
  103.2 11.5 %collective-permute-start.20 = (bf16[96,768]{1,0:T(8,128)(2,1)S(1)}, bf16[96,768]{1,0:T(8,128)(2,1)S(1)}, u32[]{:S(2)}, u32[]{:S(2)}) collective-permute-start(bf16[96,768]{1,0:T(8,128)(2,1)S(1)} %get-tuple-element.204.refs_13_.refs_1_), channel_id=1, source_target_pairs={{0,24},{4,28},{8,16},{12,20},{16,8},{20,12},{24,0},{28,4},{1,25},{... | collective-permute-start | bytes 442376 | tf_op jit(solution)/shard_map/ppermute | solution.py:84
  113.7 20.5 %collective-permute-start.26 = (bf16[96,2304]{1,0:T(8,128)(2,1)S(1)}, bf16[96,2304]{1,0:T(8,128)(2,1)S(1)}, u32[]{:S(2)}, u32[]{:S(2)}) collective-permute-start(bf16[96,2304]{1,0:T(8,128)(2,1)S(1)} %get-tuple-element.231.refs_1_), channel_id=1, source_target_pairs={{0,8},{4,12},{8,0},{12,4},{16,24},{20,28},{24,16},{28,20},{1,9},{5... | collective-permute-start | bytes 1327112 | tf_op jit(solution)/shard_map/ppermute | solution.py:84
  114.7 21.5 %collective-permute-start.27 = (bf16[96,2304]{1,0:T(8,128)(2,1)S(1)}, bf16[96,2304]{1,0:T(8,128)(2,1)S(1)}, u32[]{:S(2)}, u32[]{:S(2)}) collective-permute-start(bf16[96,2304]{1,0:T(8,128)(2,1)S(1)} %get-tuple-element.231.refs_1_), channel_id=1, source_target_pairs={{0,16},{4,20},{8,24},{12,28},{16,0},{20,4},{24,8},{28,12},{1,17},{... | collective-permute-start | bytes 1327112 | tf_op jit(solution)/shard_map/ppermute | solution.py:84
  115.7 20.5 %collective-permute-start.28 = (bf16[96,2304]{1,0:T(8,128)(2,1)S(1)}, bf16[96,2304]{1,0:T(8,128)(2,1)S(1)}, u32[]{:S(2)}, u32[]{:S(2)}) collective-permute-start(bf16[96,2304]{1,0:T(8,128)(2,1)S(1)} %get-tuple-element.231.refs_1_), channel_id=1, source_target_pairs={{0,4},{4,0},{8,12},{12,8},{16,20},{20,16},{24,28},{28,24},{1,5},{5... | collective-permute-start | bytes 1327112 | tf_op jit(solution)/shard_map/ppermute | solution.py:84
  116.4 12.1 %collective-permute-start.17 = (bf16[256,768]{1,0:T(8,128)(2,1)S(1)}, bf16[256,768]{1,0:T(8,128)(2,1)S(1)}, u32[]{:S(2)}, u32[]{:S(2)}) collective-permute-start(bf16[256,768]{1,0:T(8,128)(2,1)S(1)} %get-tuple-element.218.refs_11_), channel_id=1, source_target_pairs={{0,2},{1,3},{2,0},{3,1},{4,6},{5,7},{6,4},{7,5},{8,10},{9,11},{10,... | collective-permute-start | bytes 1179656 | tf_op jit(solution)/shard_map/ppermute | solution.py:80
  117.8 18.3 %collective-permute-start.25 = (bf16[256,768]{1,0:T(8,128)(2,1)S(1)}, bf16[256,768]{1,0:T(8,128)(2,1)S(1)}, u32[]{:S(2)}, u32[]{:S(2)}) collective-permute-start(bf16[256,768]{1,0:T(8,128)(2,1)S(1)} %get-tuple-element.225.refs_16_), channel_id=1, source_target_pairs={{0,2},{1,3},{2,0},{3,1},{4,6},{5,7},{6,4},{7,5},{8,10},{9,11},{10,... | collective-permute-start | bytes 1179656 | tf_op jit(solution)/shard_map/ppermute | solution.py:80
  141.0 13.0 %collective-permute-start.32 = (bf16[96,2304]{1,0:T(8,128)(2,1)S(1)}, bf16[96,2304]{1,0:T(8,128)(2,1)S(1)}, u32[]{:S(2)}, u32[]{:S(2)}) collective-permute-start(bf16[96,2304]{1,0:T(8,128)(2,1)S(1)} %collective-permute-done.26.refs_24_.refs_3_), channel_id=1, source_target_pairs={{0,4},{4,0},{8,12},{12,8},{16,20},{20,16},{24,28},{28,24},{1,5},{5... | collective-permute-start | bytes 1327112 | tf_op jit(solution)/shard_map/ppermute | solution.py:84
  141.5 16.5 %collective-permute-start.36 = (bf16[96,2304]{1,0:T(8,128)(2,1)S(1)}, bf16[96,2304]{1,0:T(8,128)(2,1)S(1)}, u32[]{:S(2)}, u32[]{:S(2)}) collective-permute-start(bf16[96,2304]{1,0:T(8,128)(2,1)S(1)} %get-tuple-element.231.refs_1_), channel_id=1, source_target_pairs={{0,24},{4,28},{8,16},{12,20},{16,8},{20,12},{24,0},{28,4},{1,25},{... | collective-permute-start | bytes 1327112 | tf_op jit(solution)/shard_map/ppermute | solution.py:84
  143.9 19.2 %collective-permute-start.37 = (bf16[96,2304]{1,0:T(8,128)(2,1)S(1)}, bf16[96,2304]{1,0:T(8,128)(2,1)S(1)}, u32[]{:S(2)}, u32[]{:S(2)}) collective-permute-start(bf16[96,2304]{1,0:T(8,128)(2,1)S(1)} %collective-permute-done.27.refs_25_.refs_5_), channel_id=1, source_target_pairs={{0,4},{4,0},{8,12},{12,8},{16,20},{20,16},{24,28},{28,24},{1,5},{5... | collective-permute-start | bytes 1327112 | tf_op jit(solution)/shard_map/ppermute | solution.py:84
  145.5 12.1 %collective-permute-start.31 = (bf16[256,768]{1,0:T(8,128)(2,1)S(1)}, bf16[256,768]{1,0:T(8,128)(2,1)S(1)}, u32[]{:S(2)}, u32[]{:S(2)}) collective-permute-start(bf16[256,768]{1,0:T(8,128)(2,1)S(1)} %get-tuple-element.236.refs_27_), channel_id=1, source_target_pairs={{0,2},{1,3},{2,0},{3,1},{4,6},{5,7},{6,4},{7,5},{8,10},{9,11},{10,... | collective-permute-start | bytes 1179656 | tf_op jit(solution)/shard_map/ppermute | solution.py:80
  147.1 17.5 %collective-permute-start.35 = (bf16[256,768]{1,0:T(8,128)(2,1)S(1)}, bf16[256,768]{1,0:T(8,128)(2,1)S(1)}, u32[]{:S(2)}, u32[]{:S(2)}) collective-permute-start(bf16[256,768]{1,0:T(8,128)(2,1)S(1)} %get-tuple-element.237.refs_30_), channel_id=1, source_target_pairs={{0,2},{1,3},{2,0},{3,1},{4,6},{5,7},{6,4},{7,5},{8,10},{9,11},{10,... | collective-permute-start | bytes 1179656 | tf_op jit(solution)/shard_map/ppermute | solution.py:80
  157.9 14.0 %collective-permute-start.34 = (bf16[256,768]{1,0:T(8,128)(2,1)S(1)}, bf16[256,768]{1,0:T(8,128)(2,1)S(1)}, u32[]{:S(2)}, u32[]{:S(2)}) collective-permute-start(bf16[256,768]{1,0:T(8,128)(2,1)S(1)} %get-tuple-element.238.refs_0_.refs_33_.refs_31_.refs_38_.refs_34_.refs_32_.refs_46_.refs_35_.refs_1_), channel_id=1, source_target_pairs={{0,1},{1,0},{2,3},{3,2},{4,5},{5,4},{6,7},{7,6},{8,9},{9,8},{10,11... | collective-permute-start | bytes 1179656 | tf_op jit(solution)/shard_map/ppermute | solution.py:76
  181.8 12.2 %collective-permute-start.42 = (bf16[96,2304]{1,0:T(8,128)(2,1)S(1)}, bf16[96,2304]{1,0:T(8,128)(2,1)S(1)}, u32[]{:S(2)}, u32[]{:S(2)}) collective-permute-start(bf16[96,2304]{1,0:T(8,128)(2,1)S(1)} %collective-permute-done.36.refs_31_.refs_7_), channel_id=1, source_target_pairs={{0,4},{4,0},{8,12},{12,8},{16,20},{20,16},{24,28},{28,24},{1,5},{5... | collective-permute-start | bytes 1327112 | tf_op jit(solution)/shard_map/ppermute | solution.py:84
  182.3 12.0 %collective-permute-start.41 = (bf16[256,768]{1,0:T(8,128)(2,1)S(1)}, bf16[256,768]{1,0:T(8,128)(2,1)S(1)}, u32[]{:S(2)}, u32[]{:S(2)}) collective-permute-start(bf16[256,768]{1,0:T(8,128)(2,1)S(1)} %get-tuple-element.257.refs_41_), channel_id=1, source_target_pairs={{0,2},{1,3},{2,0},{3,1},{4,6},{5,7},{6,4},{7,5},{8,10},{9,11},{10,... | collective-permute-start | bytes 1179656 | tf_op jit(solution)/shard_map/ppermute | solution.py:80
  186.0 15.5 %collective-permute-start.45 = (bf16[256,768]{1,0:T(8,128)(2,1)S(1)}, bf16[256,768]{1,0:T(8,128)(2,1)S(1)}, u32[]{:S(2)}, u32[]{:S(2)}) collective-permute-start(bf16[256,768]{1,0:T(8,128)(2,1)S(1)} %get-tuple-element.264.refs_48_), channel_id=1, source_target_pairs={{0,2},{1,3},{2,0},{3,1},{4,6},{5,7},{6,4},{7,5},{8,10},{9,11},{10,... | collective-permute-start | bytes 1179656 | tf_op jit(solution)/shard_map/ppermute | solution.py:80
  206.7 12.0 %collective-permute-start.48 = (bf16[256,768]{1,0:T(8,128)(2,1)S(1)}, bf16[256,768]{1,0:T(8,128)(2,1)S(1)}, u32[]{:S(2)}, u32[]{:S(2)}) collective-permute-start(bf16[256,768]{1,0:T(8,128)(2,1)S(1)} %get-tuple-element.273.refs_55_), channel_id=1, source_target_pairs={{0,2},{1,3},{2,0},{3,1},{4,6},{5,7},{6,4},{7,5},{8,10},{9,11},{10,... | collective-permute-start | bytes 1179656 | tf_op jit(solution)/shard_map/ppermute | solution.py:80
  208.4 18.3 %collective-permute-start.50 = (bf16[256,768]{1,0:T(8,128)(2,1)S(1)}, bf16[256,768]{1,0:T(8,128)(2,1)S(1)}, u32[]{:S(2)}, u32[]{:S(2)}) collective-permute-start(bf16[256,768]{1,0:T(8,128)(2,1)S(1)} %get-tuple-element.274.refs_57_), channel_id=1, source_target_pairs={{0,2},{1,3},{2,0},{3,1},{4,6},{5,7},{6,4},{7,5},{8,10},{9,11},{10,... | collective-permute-start | bytes 1179656 | tf_op jit(solution)/shard_map/ppermute | solution.py:80
  245.0 16.2 %collective-permute-start.57 = (bf16[4,96,768]{2,1,0:T(8,128)(2,1)S(1)}, bf16[4,96,768]{2,1,0:T(8,128)(2,1)S(1)}, u32[]{:S(2)}, u32[]{:S(2)}) collective-permute-start(bf16[4,96,768]{2,1,0:T(8,128)(2,1)S(1)} %get-tuple-element.300.refs_66_), channel_id=1, source_target_pairs={{0,4},{4,0},{8,12},{12,8},{16,20},{20,16},{24,28},{28,24},{1,5},{5... | collective-permute-start | bytes 1769480 | tf_op jit(solution)/shard_map/ppermute | solution.py:84
  246.6 11.1 %collective-permute-start.56 = (bf16[256,768]{1,0:T(8,128)(2,1)S(1)}, bf16[256,768]{1,0:T(8,128)(2,1)S(1)}, u32[]{:S(2)}, u32[]{:S(2)}) collective-permute-start(bf16[256,768]{1,0:T(8,128)(2,1)S(1)} %get-tuple-element.298.refs_69_), channel_id=1, source_target_pairs={{0,2},{1,3},{2,0},{3,1},{4,6},{5,7},{6,4},{7,5},{8,10},{9,11},{10,... | collective-permute-start | bytes 1179656 | tf_op jit(solution)/shard_map/ppermute | solution.py:80
  248.1 26.5 %collective-permute-start.59 = (bf16[4,96,768]{2,1,0:T(8,128)(2,1)S(1)}, bf16[4,96,768]{2,1,0:T(8,128)(2,1)S(1)}, u32[]{:S(2)}, u32[]{:S(2)}) collective-permute-start(bf16[4,96,768]{2,1,0:T(8,128)(2,1)S(1)} %get-tuple-element.304), channel_id=1, source_target_pairs={{0,4},{4,0},{8,12},{12,8},{16,20},{20,16},{24,28},{28,24},{1,5},{5... | collective-permute-start | bytes 1769480 | tf_op jit(solution)/shard_map/ppermute | solution.py:84
  263.0 11.5 %collective-permute-start.55 = (bf16[256,768]{1,0:T(8,128)(2,1)S(1)}, bf16[256,768]{1,0:T(8,128)(2,1)S(1)}, u32[]{:S(2)}, u32[]{:S(2)}) collective-permute-start(bf16[256,768]{1,0:T(8,128)(2,1)S(1)} %get-tuple-element.299.refs_66_), channel_id=1, source_target_pairs={{0,2},{1,3},{2,0},{3,1},{4,6},{5,7},{6,4},{7,5},{8,10},{9,11},{10,... | collective-permute-start | bytes 1179656 | tf_op jit(solution)/shard_map/ppermute | solution.py:80
  264.5 21.4 %collective-permute-start.61 = (bf16[4,96,768]{2,1,0:T(8,128)(2,1)S(1)}, bf16[4,96,768]{2,1,0:T(8,128)(2,1)S(1)}, u32[]{:S(2)}, u32[]{:S(2)}) collective-permute-start(bf16[4,96,768]{2,1,0:T(8,128)(2,1)S(1)} %get-tuple-element.312), channel_id=1, source_target_pairs={{0,4},{4,0},{8,12},{12,8},{16,20},{20,16},{24,28},{28,24},{1,5},{5... | collective-permute-start | bytes 1769480 | tf_op jit(solution)/shard_map/ppermute | solution.py:84
  289.1 11.9 %collective-permute-start.65 = (bf16[256,768]{1,0:T(8,128)(2,1)S(1)}, bf16[256,768]{1,0:T(8,128)(2,1)S(1)}, u32[]{:S(2)}, u32[]{:S(2)}) collective-permute-start(bf16[256,768]{1,0:T(8,128)(2,1)S(1)} %get-tuple-element.314.refs_43_), channel_id=1, source_target_pairs={{0,2},{1,3},{2,0},{3,1},{4,6},{5,7},{6,4},{7,5},{8,10},{9,11},{10,... | collective-permute-start | bytes 1179656 | tf_op jit(solution)/shard_map/ppermute | solution.py:80
  292.3 22.0 %collective-permute-start.66 = (bf16[96,2304]{1,0:T(8,128)(2,1)S(1)}, bf16[96,2304]{1,0:T(8,128)(2,1)S(1)}, u32[]{:S(2)}, u32[]{:S(2)}) collective-permute-start(bf16[96,2304]{1,0:T(8,128)(2,1)S(1)} %get-tuple-element.325), channel_id=1, source_target_pairs={{0,16},{4,20},{8,24},{12,28},{16,0},{20,4},{24,8},{28,12},{1,17},{... | collective-permute-start | bytes 1327112 | tf_op jit(solution)/shard_map/ppermute | solution.py:84
  292.4 16.5 %collective-permute-start.64 = (bf16[256,768]{1,0:T(8,128)(2,1)S(1)}, bf16[256,768]{1,0:T(8,128)(2,1)S(1)}, u32[]{:S(2)}, u32[]{:S(2)}) collective-permute-start(bf16[256,768]{1,0:T(8,128)(2,1)S(1)} %get-tuple-element.316.refs_46_), channel_id=1, source_target_pairs={{0,2},{1,3},{2,0},{3,1},{4,6},{5,7},{6,4},{7,5},{8,10},{9,11},{10,... | collective-permute-start | bytes 1179656 | tf_op jit(solution)/shard_map/ppermute | solution.py:80
  301.6 15.4 %collective-permute-start.68 = (bf16[256,768]{1,0:T(8,128)(2,1)S(1)}, bf16[256,768]{1,0:T(8,128)(2,1)S(1)}, u32[]{:S(2)}, u32[]{:S(2)}) collective-permute-start(bf16[256,768]{1,0:T(8,128)(2,1)S(1)} %get-tuple-element.321.refs_1_.refs_34_.refs_29_.refs_31_.refs_9_.refs_24_.refs_0_), channel_id=1, source_target_pairs={{0,1},{1,0},{2,3},{3,2},{4,5},{5,4},{6,7},{7,6},{8,9},{9,8},{10,11... | collective-permute-start | bytes 1179656 | tf_op jit(solution)/shard_map/ppermute | solution.py:76
  319.7 16.2 %collective-permute-start.74 = (bf16[4,96,768]{2,1,0:T(8,128)(2,1)S(1)}, bf16[4,96,768]{2,1,0:T(8,128)(2,1)S(1)}, u32[]{:S(2)}, u32[]{:S(2)}) collective-permute-start(bf16[4,96,768]{2,1,0:T(8,128)(2,1)S(1)} %get-tuple-element.343), channel_id=1, source_target_pairs={{0,4},{4,0},{8,12},{12,8},{16,20},{20,16},{24,28},{28,24},{1,5},{5... | collective-permute-start | bytes 1769480 | tf_op jit(solution)/shard_map/ppermute | solution.py:84
  323.2 13.5 %collective-permute-start.73 = (bf16[96,2304]{1,0:T(8,128)(2,1)S(1)}, bf16[96,2304]{1,0:T(8,128)(2,1)S(1)}, u32[]{:S(2)}, u32[]{:S(2)}) collective-permute-start(bf16[96,2304]{1,0:T(8,128)(2,1)S(1)} %get-tuple-element.342), channel_id=1, source_target_pairs={{0,8},{4,12},{8,0},{12,4},{16,24},{20,28},{24,16},{28,20},{1,9},{5... | collective-permute-start | bytes 1327112 | tf_op jit(solution)/shard_map/ppermute | solution.py:84
  323.4 13.2 %collective-permute-start.72 = (bf16[256,768]{1,0:T(8,128)(2,1)S(1)}, bf16[256,768]{1,0:T(8,128)(2,1)S(1)}, u32[]{:S(2)}, u32[]{:S(2)}) collective-permute-start(bf16[256,768]{1,0:T(8,128)(2,1)S(1)} %get-tuple-element.338.refs_41_), channel_id=1, source_target_pairs={{0,2},{1,3},{2,0},{3,1},{4,6},{5,7},{6,4},{7,5},{8,10},{9,11},{10,... | collective-permute-start | bytes 1179656 | tf_op jit(solution)/shard_map/ppermute | solution.py:80
  329.5 19.6 %collective-permute-start.76 = (bf16[4,96,768]{2,1,0:T(8,128)(2,1)S(1)}, bf16[4,96,768]{2,1,0:T(8,128)(2,1)S(1)}, u32[]{:S(2)}, u32[]{:S(2)}) collective-permute-start(bf16[4,96,768]{2,1,0:T(8,128)(2,1)S(1)} %get-tuple-element.344.refs_26_), channel_id=1, source_target_pairs={{0,4},{4,0},{8,12},{12,8},{16,20},{20,16},{24,28},{28,24},{1,5},{5... | collective-permute-start | bytes 1769480 | tf_op jit(solution)/shard_map/ppermute | solution.py:84
  337.3 11.8 %collective-permute-start.71 = (bf16[256,768]{1,0:T(8,128)(2,1)S(1)}, bf16[256,768]{1,0:T(8,128)(2,1)S(1)}, u32[]{:S(2)}, u32[]{:S(2)}) collective-permute-start(bf16[256,768]{1,0:T(8,128)(2,1)S(1)} %get-tuple-element.340.refs_38_), channel_id=1, source_target_pairs={{0,2},{1,3},{2,0},{3,1},{4,6},{5,7},{6,4},{7,5},{8,10},{9,11},{10,... | collective-permute-start | bytes 1179656 | tf_op jit(solution)/shard_map/ppermute | solution.py:80
  338.4 25.2 %collective-permute-start.78 = (bf16[4,96,768]{2,1,0:T(8,128)(2,1)S(1)}, bf16[4,96,768]{2,1,0:T(8,128)(2,1)S(1)}, u32[]{:S(2)}, u32[]{:S(2)}) collective-permute-start(bf16[4,96,768]{2,1,0:T(8,128)(2,1)S(1)} %get-tuple-element.353), channel_id=1, source_target_pairs={{0,4},{4,0},{8,12},{12,8},{16,20},{20,16},{24,28},{28,24},{1,5},{5... | collective-permute-start | bytes 1769480 | tf_op jit(solution)/shard_map/ppermute | solution.py:84
  339.5 13.9 %collective-permute-start.79 = (bf16[96,2304]{1,0:T(8,128)(2,1)S(1)}, bf16[96,2304]{1,0:T(8,128)(2,1)S(1)}, u32[]{:S(2)}, u32[]{:S(2)}) collective-permute-start(bf16[96,2304]{1,0:T(8,128)(2,1)S(1)} %get-tuple-element.354), channel_id=1, source_target_pairs={{0,24},{4,28},{8,16},{12,20},{16,8},{20,12},{24,0},{28,4},{1,25},{... | collective-permute-start | bytes 1327112 | tf_op jit(solution)/shard_map/ppermute | solution.py:84
  341.7 31.2 %collective-permute-start.80 = (bf16[4,96,768]{2,1,0:T(8,128)(2,1)S(1)}, bf16[4,96,768]{2,1,0:T(8,128)(2,1)S(1)}, u32[]{:S(2)}, u32[]{:S(2)}) collective-permute-start(bf16[4,96,768]{2,1,0:T(8,128)(2,1)S(1)} %get-tuple-element.356), channel_id=1, source_target_pairs={{0,4},{4,0},{8,12},{12,8},{16,20},{20,16},{24,28},{28,24},{1,5},{5... | collective-permute-start | bytes 1769480 | tf_op jit(solution)/shard_map/ppermute | solution.py:84
  349.7 11.4 %collective-permute-start.77 = (bf16[256,768]{1,0:T(8,128)(2,1)S(1)}, bf16[256,768]{1,0:T(8,128)(2,1)S(1)}, u32[]{:S(2)}, u32[]{:S(2)}) collective-permute-start(bf16[256,768]{1,0:T(8,128)(2,1)S(1)} %get-tuple-element.349.refs_0_.refs_23_.refs_4_.refs_16_.refs_13_.refs_5_), channel_id=1, source_target_pairs={{0,1},{1,0},{2,3},{3,2},{4,5},{5,4},{6,7},{7,6},{8,9},{9,8},{10,11... | collective-permute-start | bytes 1179656 | tf_op jit(solution)/shard_map/ppermute | solution.py:76
  349.8 21.4 %collective-permute-start.81 = (bf16[96,768]{1,0:T(8,128)(2,1)S(1)}, bf16[96,768]{1,0:T(8,128)(2,1)S(1)}, u32[]{:S(2)}, u32[]{:S(2)}) collective-permute-start(bf16[96,768]{1,0:T(8,128)(2,1)S(1)} %get-tuple-element.357), channel_id=1, source_target_pairs={{0,8},{4,12},{8,0},{12,4},{16,24},{20,28},{24,16},{28,20},{1,9},{5... | collective-permute-start | bytes 442376 | tf_op jit(solution)/shard_map/ppermute | solution.py:84
  353.4 18.7 %collective-permute-start.82 = (bf16[96,768]{1,0:T(8,128)(2,1)S(1)}, bf16[96,768]{1,0:T(8,128)(2,1)S(1)}, u32[]{:S(2)}, u32[]{:S(2)}) collective-permute-start(bf16[96,768]{1,0:T(8,128)(2,1)S(1)} %get-tuple-element.358), channel_id=1, source_target_pairs={{0,16},{4,20},{8,24},{12,28},{16,0},{20,4},{24,8},{28,12},{1,17},{... | collective-permute-start | bytes 442376 | tf_op jit(solution)/shard_map/ppermute | solution.py:84
  379.8 22.3 %collective-permute-start.91 = (bf16[4,96,768]{2,1,0:T(8,128)(2,1)S(1)}, bf16[4,96,768]{2,1,0:T(8,128)(2,1)S(1)}, u32[]{:S(2)}, u32[]{:S(2)}) collective-permute-start(bf16[4,96,768]{2,1,0:T(8,128)(2,1)S(1)} %get-tuple-element.371), channel_id=1, source_target_pairs={{0,4},{4,0},{8,12},{12,8},{16,20},{20,16},{24,28},{28,24},{1,5},{5... | collective-permute-start | bytes 1769480 | tf_op jit(solution)/shard_map/ppermute | solution.py:84
  380.9 18.9 %collective-permute-start.87 = (bf16[96,2304]{1,0:T(8,128)(2,1)S(1)}, bf16[96,2304]{1,0:T(8,128)(2,1)S(1)}, u32[]{:S(2)}, u32[]{:S(2)}) collective-permute-start(bf16[96,2304]{1,0:T(8,128)(2,1)S(1)} %get-tuple-element.368), channel_id=1, source_target_pairs={{0,8},{4,12},{8,0},{12,4},{16,24},{20,28},{24,16},{28,20},{1,9},{5... | collective-permute-start | bytes 1327112 | tf_op jit(solution)/shard_map/ppermute | solution.py:84
  383.4 16.4 %collective-permute-start.86 = (bf16[8,64,384]{2,1,0:T(8,128)(2,1)S(1)}, bf16[8,64,384]{2,1,0:T(8,128)(2,1)S(1)}, u32[]{:S(2)}, u32[]{:S(2)}) collective-permute-start(bf16[8,64,384]{2,1,0:T(8,128)(2,1)S(1)} %get-tuple-element.367.refs_2_), channel_id=1, source_target_pairs={{0,2},{1,3},{2,0},{3,1},{4,6},{5,7},{6,4},{7,5},{8,10},{9,11},{10,... | collective-permute-start | bytes 1179656 | tf_op jit(solution)/shard_map/ppermute | solution.py:80
  384.4 36.2 %collective-permute-start.95 = (bf16[96,2304]{1,0:T(8,128)(2,1)S(1)}, bf16[96,2304]{1,0:T(8,128)(2,1)S(1)}, u32[]{:S(2)}, u32[]{:S(2)}) collective-permute-start(bf16[96,2304]{1,0:T(8,128)(2,1)S(1)} %get-tuple-element.377), channel_id=1, source_target_pairs={{0,16},{4,20},{8,24},{12,28},{16,0},{20,4},{24,8},{28,12},{1,17},{... | collective-permute-start | bytes 1327112 | tf_op jit(solution)/shard_map/ppermute | solution.py:84
  394.5 29.6 %collective-permute-start.96 = (bf16[96,2304]{1,0:T(8,128)(2,1)S(1)}, bf16[96,2304]{1,0:T(8,128)(2,1)S(1)}, u32[]{:S(2)}, u32[]{:S(2)}) collective-permute-start(bf16[96,2304]{1,0:T(8,128)(2,1)S(1)} %get-tuple-element.378), channel_id=1, source_target_pairs={{0,24},{4,28},{8,16},{12,20},{16,8},{20,12},{24,0},{28,4},{1,25},{... | collective-permute-start | bytes 1327112 | tf_op jit(solution)/shard_map/ppermute | solution.py:84
  400.5 21.7 %collective-permute-start.89 = (bf16[4,64,384]{2,1,0:T(8,128)(2,1)S(1)}, bf16[4,64,384]{2,1,0:T(8,128)(2,1)S(1)}, u32[]{:S(2)}, u32[]{:S(2)}) collective-permute-start(bf16[4,64,384]{2,1,0:T(8,128)(2,1)S(1)} %get-tuple-element.370), channel_id=1, source_target_pairs={{0,4},{4,0},{8,12},{12,8},{16,20},{20,16},{24,28},{28,24},{1,5},{5... | collective-permute-start | bytes 589832 | tf_op jit(solution)/shard_map/ppermute | solution.py:84
  402.7 31.2 %collective-permute-start.97 = (bf16[96,768]{1,0:T(8,128)(2,1)S(1)}, bf16[96,768]{1,0:T(8,128)(2,1)S(1)}, u32[]{:S(2)}, u32[]{:S(2)}) collective-permute-start(bf16[96,768]{1,0:T(8,128)(2,1)S(1)} %get-tuple-element.379), channel_id=1, source_target_pairs={{0,8},{4,12},{8,0},{12,4},{16,24},{20,28},{24,16},{28,20},{1,9},{5... | collective-permute-start | bytes 442376 | tf_op jit(solution)/shard_map/ppermute | solution.py:84
  402.8 17.8 %collective-permute-start.90 = (f32[8,768]{1,0:T(8,128)S(1)}, f32[8,768]{1,0:T(8,128)S(1)}, u32[]{:S(2)}, u32[]{:S(2)}) collective-permute-start(f32[8,768]{1,0:T(8,128)S(1)} %shard_map.271.refs_3_.refs_0_), channel_id=1, source_target_pairs={{0,4},{4,0},{8,12},{12,8},{16,20},{20,16},{24,28},{28,24},{1,5},{5... | collective-permute-start | bytes 73736 | tf_op jit(solution)/shard_map/ppermute | solution.py:84
  420.6 20.0 %collective-permute-start.98 = (bf16[96,768]{1,0:T(8,128)(2,1)S(1)}, bf16[96,768]{1,0:T(8,128)(2,1)S(1)}, u32[]{:S(2)}, u32[]{:S(2)}) collective-permute-start(bf16[96,768]{1,0:T(8,128)(2,1)S(1)} %get-tuple-element.380), channel_id=1, source_target_pairs={{0,16},{4,20},{8,24},{12,28},{16,0},{20,4},{24,8},{28,12},{1,17},{... | collective-permute-start | bytes 442376 | tf_op jit(solution)/shard_map/ppermute | solution.py:84
  420.6 20.0 %collective-permute-start.99 = (bf16[96,768]{1,0:T(8,128)(2,1)S(1)}, bf16[96,768]{1,0:T(8,128)(2,1)S(1)}, u32[]{:S(2)}, u32[]{:S(2)}) collective-permute-start(bf16[96,768]{1,0:T(8,128)(2,1)S(1)} %get-tuple-element.381), channel_id=1, source_target_pairs={{0,24},{4,28},{8,16},{12,20},{16,8},{20,12},{24,0},{28,4},{1,25},{... | collective-permute-start | bytes 442376 | tf_op jit(solution)/shard_map/ppermute | solution.py:84
  422.2 11.6 %collective-permute-start.100 = (f32[8,768]{1,0:T(8,128)S(1)}, f32[8,768]{1,0:T(8,128)S(1)}, u32[]{:S(2)}, u32[]{:S(2)}) collective-permute-start(f32[8,768]{1,0:T(8,128)S(1)} %shard_map.275.refs_2_.refs_0_), channel_id=1, source_target_pairs={{0,8},{4,12},{8,0},{12,4},{16,24},{20,28},{24,16},{28,20},{1,9},{5... | collective-permute-start | bytes 73736 | tf_op jit(solution)/shard_map/ppermute | solution.py:84
  424.2 16.4 %collective-permute-start.92 = (bf16[2,64,384]{2,1,0:T(8,128)(2,1)S(1)}, bf16[2,64,384]{2,1,0:T(8,128)(2,1)S(1)}, u32[]{:S(2)}, u32[]{:S(2)}) collective-permute-start(bf16[2,64,384]{2,1,0:T(8,128)(2,1)S(1)} %get-tuple-element.374), channel_id=1, source_target_pairs={{0,8},{4,12},{8,0},{12,4},{16,24},{20,28},{24,16},{28,20},{1,9},{5... | collective-permute-start | bytes 294920 | tf_op jit(solution)/shard_map/ppermute | solution.py:84
  433.8 11.4 %collective-permute-start.93 = (bf16[2,64,384]{2,1,0:T(8,128)(2,1)S(1)}, bf16[2,64,384]{2,1,0:T(8,128)(2,1)S(1)}, u32[]{:S(2)}, u32[]{:S(2)}) collective-permute-start(bf16[2,64,384]{2,1,0:T(8,128)(2,1)S(1)} %get-tuple-element.375), channel_id=1, source_target_pairs={{0,16},{4,20},{8,24},{12,28},{16,0},{20,4},{24,8},{28,12},{1,17},{... | collective-permute-start | bytes 294920 | tf_op jit(solution)/shard_map/ppermute | solution.py:84
  433.9 11.3 %collective-permute-start.94 = (bf16[2,64,384]{2,1,0:T(8,128)(2,1)S(1)}, bf16[2,64,384]{2,1,0:T(8,128)(2,1)S(1)}, u32[]{:S(2)}, u32[]{:S(2)}) collective-permute-start(bf16[2,64,384]{2,1,0:T(8,128)(2,1)S(1)} %get-tuple-element.376), channel_id=1, source_target_pairs={{0,24},{4,28},{8,16},{12,20},{16,8},{20,12},{24,0},{28,4},{1,25},{... | collective-permute-start | bytes 294920 | tf_op jit(solution)/shard_map/ppermute | solution.py:84
  446.4 15.5 %collective-permute-start.102 = (bf16[8,64,384]{2,1,0:T(8,128)(2,1)S(1)}, bf16[8,64,384]{2,1,0:T(8,128)(2,1)S(1)}, u32[]{:S(2)}, u32[]{:S(2)}) collective-permute-start(bf16[8,64,384]{2,1,0:T(8,128)(2,1)S(1)} %shard_map.278.refs_2_), channel_id=1, source_target_pairs={{0,1},{1,0},{2,3},{3,2},{4,5},{5,4},{6,7},{7,6},{8,9},{9,8},{10,11... | collective-permute-start | bytes 1179656 | tf_op jit(solution)/shard_map/ppermute | solution.py:76
  (74 other events, 677.5 us)

commit v5 on v4

--- a/solution.py
+++ b/solution.py
@@ -356,8 +356,8 @@
 
 def show_kernel(where_ref, first_ref, second_ref, out_ref):
     rows = out_ref.shape[0]
-    first = first_ref[...] * mask_of(where_ref, 0, rows)
-    second = second_ref[...] * mask_of(where_ref, 1, rows)
+    first = first_ref[...].astype(F32) * mask_of(where_ref, 0, rows)
+    second = second_ref[...].astype(F32) * mask_of(where_ref, 1, rows)
     out_ref[...] = jnp.where(where_ref[1] == 0, first, second)
 
 
@@ -484,7 +484,7 @@
         there = pl.ds(pl.multiple_of(first + step * block, block), block)
         queries = q_ref[there, :]
         context_grad = dc_ref[here, :]
-        columns = []
+        columns, score_grads, all_weights, all_masked, all_grads = [], [], [], [], []
         for head in range(inner // HD):
             masked = jnp.where(head_mask(queries.shape, head, inner), queries, 0)
             masked_grad = jnp.where(head_mask(context_grad.shape, head, inner), context_grad, 0)
@@ -493,9 +493,14 @@
             weight_grad = dot_nt(v_ref[...], masked_grad)
             inner_sum = jnp.sum(weights * weight_grad, axis=0, keepdims=True)
             score_grad = (weights * (weight_grad - inner_sum)).astype(BF16)
-            dk_ref[...] += dot_nn(score_grad, masked)
-            dv_ref[...] += dot_nn(weights.astype(BF16), masked_grad)
             columns.append(dot_nn(kt_ref[head * HD : (head + 1) * HD, :], score_grad))
+            score_grads.append(score_grad)
+            all_weights.append(weights.astype(BF16))
+            all_masked.append(masked)
+            all_grads.append(masked_grad)
+        join = jnp.concatenate
+        dk_ref[...] += dot_nn(join(score_grads, axis=1), join(all_masked, axis=0))
+        dv_ref[...] += dot_nn(join(all_weights, axis=1), join(all_grads, axis=0))
         columns.append(jnp.zeros((padded - inner, block), F32))
         query_grad = jnp.concatenate(columns, axis=0).T * (1.0 / math.sqrt(HD))
         turned = turn_back(query_grad, cos_ref[there, :], sin_ref[there, :]).astype(BF16)
@@ -1042,11 +1047,12 @@
             late_weight = lambda here=here: gather_finish(where, here[1], widths[1:])[0]
         current, residual, saved = layer_forward(
             pieces, residual, first_weight, late_weight, norm_gains[layer], norm_biases[layer],
-            tables, inner, layer == LAYERS - 1, at,
+            tables, inner, False, at,
         )
         saved_all.append(saved)
         if layer < LAYERS - 1:
             pieces = [p for piece in residual for p in (piece, swap_core(piece))]
+    current = residual
     keep(*current)
     shown = []
     received, vectors, steps = [None] * LAYERS, [None] * LAYERS, []
@@ -1085,7 +1091,7 @@
         if split is None:
             return ()
         if layer:
-            after = {("norm_one", 0): 1, ("norm_one", 1): 2, ("input", 0): 3}
+            after = {("norm_one", 1): 1, ("attend_back", 1): 2, ("input", 0): 3}
         else:
             after = {("norm_one", 1): 1, ("attend_back", 1): 2, "input": 3}
         found = ()

time: 475 us -> 474 us (level)
    ppermute x52, waiting for transfers between devices: 129 us -> 136 us  [swap_dp(): lax.ppermute(value, 'dp', [(i, i ^ step) for i in range(lax.axis_size('dp...]
    ppermute x18, waiting for transfers between devices: 68.8 us -> 62.7 us  [swap_x(): lax.ppermute(value, 'tensor', [(i, i ^ 2) for i in range(lax.axis_size('t...]
  transfers between devices with their start and end apart: 105 -> 105, of which waited for: 48 -> 47; matrix products, arithmetic and copies ran while one was open for 1% -> 1% of each run, Pallas kernels for 21% -> 22%
where the time goes in v5:
time: 474 us; the launch traced here: 465 us
  waiting for transfers between devices  211 us (45%)
  Pallas kernels  128 us (27%)
  starting transfers between devices  110 us (23%)
  local copies, waits for them, and re-layouts  11.3 us (2%)
    ppermute x52, waiting for transfers between devices, swap_dp(): lax.ppermute(value, 'dp', [(i, i ^ step) for i in range(lax.axis_size('dp...  136 us
    pallas_call x103, Pallas kernels, call(): pl.pallas_call(body, in_specs=[smem] * scalars + [vmem] * (used - scalars...  125 us
    ppermute x52, starting transfers between devices, swap_dp(): lax.ppermute(value, 'dp', [(i, i ^ step) for i in range(lax.axis_size('dp...  81.2 us
    ppermute x18, waiting for transfers between devices, swap_x(): lax.ppermute(value, 'tensor', [(i, i ^ 2) for i in range(lax.axis_size('t...  62.7 us
    ppermute x18, starting transfers between devices, swap_x(): lax.ppermute(value, 'tensor', [(i, i ^ 2) for i in range(lax.axis_size('t...  21.2 us
  transfers between devices with their start and end apart: 105, of which 47 were waited for; matrix products, arithmetic and copies ran while one was open for 1% of the time, Pallas kernels for 22%

profile of v5, /device:TPU:0, one launch (start us, length us, event | category | flops | bytes accessed | tf_op | source)
XLA Modules:
  0.0 465.1 jit_solution(16712987679550112462)
XLA Ops:
  6.4 3.0 collective-permute-start.7
  11.0 2.6 collective-permute-start.9
  19.9 7.1 %collective-permute-done.refs_1_ = bf16[4,32,768]{2,1,0:T(8,128)(2,1)S(1)} collective-permute-done((bf16[4,32,768]{2,1,0:T(8,128)(2,1)S(1)}, bf16[4,32,768]{2,1,0:T(8,128)(2,1)S(1)}, u32[]{:S(2)}, u32[]{:S(2)}) %collective-permute-start) | collective-permute-done | bytes 196640 | tf_op jit(solution)/shard_map/ppermute | solution.py:84
  28.8 2.6 collective-permute-start.2
  31.4 8.4 %collective-permute-done.1.refs_1_ = bf16[2,32,768]{2,1,0:T(8,128)(2,1)S(1)} collective-permute-done((bf16[2,32,768]{2,1,0:T(8,128)(2,1)S(1)}, bf16[2,32,768]{2,1,0:T(8,128)(2,1)S(1)}, u32[]{:S(2)}, u32[]{:S(2)}) %collective-permute-start.1) | collective-permute-done | bytes 98336 | tf_op jit(solution)/shard_map/ppermute | solution.py:84
  39.8 3.1 collective-permute-start.3
  47.3 3.1 collective-permute-start.10
  54.0 4.5 collective-permute-done.5.refs_3_
  58.5 4.2 collective-permute-done.10.refs_4_.refs_5_
  64.6 3.8 collective-permute-done.11.refs_5_.refs_6_
  68.4 12.6 %collective-permute-done.12.refs_6_.refs_7_ = bf16[96,3072]{1,0:T(8,128)(2,1)S(1)} collective-permute-done((bf16[96,3072]{1,0:T(8,128)(2,1)}, bf16[96,3072]{1,0:T(8,128)(2,1)S(1)}, u32[]{:S(2)}, u32[]{:S(2)}) %collective-permute-start.12) | collective-permute-done | bytes 589856 | tf_op jit(solution)/shard_map/ppermute | solution.py:84
  84.0 5.0 %collective-permute-done.14.refs_11_.refs_3_ = bf16[96,768]{1,0:T(8,128)(2,1)S(1)} collective-permute-done((bf16[96,768]{1,0:T(8,128)(2,1)S(1)}, bf16[96,768]{1,0:T(8,128)(2,1)S(1)}, u32[]{:S(2)}, u32[]{:S(2)}) %collective-permute-start.14) | collective-permute-done | bytes 147488 | tf_op jit(solution)/shard_map/ppermute | solution.py:84
  92.8 2.1 shard_map.187
  94.9 2.2 shard_map.188
  97.2 2.2 shard_map.189
  99.5 2.5 shard_map.191
  108.3 2.2 shard_map.192
  110.6 3.1 collective-permute-done.18.refs_2_
  119.8 8.6 %collective-permute-done.17.refs_2_ = bf16[256,768]{1,0:T(8,128)(2,1)S(1)} collective-permute-done((bf16[256,768]{1,0:T(8,128)(2,1)S(1)}, bf16[256,768]{1,0:T(8,128)(2,1)S(1)}, u32[]{:S(2)}, u32[]{:S(2)}) %collective-permute-start.17) | collective-permute-done | bytes 393248 | tf_op jit(solution)/shard_map/ppermute | solution.py:80
  130.1 4.2 collective-permute-done.26.refs_24_.refs_3_
  141.5 2.3 collective-permute-start.36
  147.8 6.2 %collective-permute-done.32.refs_29_.refs_4_ = bf16[96,2304]{1,0:T(8,128)(2,1)S(1)} collective-permute-done((bf16[96,2304]{1,0:T(8,128)(2,1)S(1)}, bf16[96,2304]{1,0:T(8,128)(2,1)S(1)}, u32[]{:S(2)}, u32[]{:S(2)}) %collective-permute-start.32) | collective-permute-done | bytes 442400 | tf_op jit(solution)/shard_map/ppermute | solution.py:84
  154.0 3.6 collective-permute-done.31.refs_2_
  158.0 5.0 %collective-permute-done.37.refs_32_.refs_6_ = bf16[96,2304]{1,0:T(8,128)(2,1)S(1)} collective-permute-done((bf16[96,2304]{1,0:T(8,128)(2,1)S(1)}, bf16[96,2304]{1,0:T(8,128)(2,1)S(1)}, u32[]{:S(2)}, u32[]{:S(2)}) %collective-permute-start.37) | collective-permute-done | bytes 442400 | tf_op jit(solution)/shard_map/ppermute | solution.py:84
  165.6 5.7 %collective-permute-done.39.refs_8_ = bf16[96,768]{1,0:T(8,128)(2,1)S(1)} collective-permute-done((bf16[96,768]{1,0:T(8,128)(2,1)S(1)}, bf16[96,768]{1,0:T(8,128)(2,1)S(1)}, u32[]{:S(2)}, u32[]{:S(2)}) %collective-permute-start.39) | collective-permute-done | bytes 147488 | tf_op jit(solution)/shard_map/ppermute | solution.py:84
  172.0 2.4 shard_map.207
  174.3 2.2 shard_map.208
  176.6 2.2 shard_map.209
  179.0 2.2 shard_map.211
  183.7 2.2 shard_map.212
  186.7 7.2 %collective-permute-done.42.refs_47_.refs_8_ = bf16[96,2304]{1,0:T(8,128)(2,1)S(1)} collective-permute-done((bf16[96,2304]{1,0:T(8,128)(2,1)S(1)}, bf16[96,2304]{1,0:T(8,128)(2,1)S(1)}, u32[]{:S(2)}, u32[]{:S(2)}) %collective-permute-start.42) | collective-permute-done | bytes 442400 | tf_op jit(solution)/shard_map/ppermute | solution.py:84
  196.8 4.7 %collective-permute-done.45.refs_2_ = bf16[256,768]{1,0:T(8,128)(2,1)S(1)} collective-permute-done((bf16[256,768]{1,0:T(8,128)(2,1)S(1)}, bf16[256,768]{1,0:T(8,128)(2,1)S(1)}, u32[]{:S(2)}, u32[]{:S(2)}) %collective-permute-start.45) | collective-permute-done | bytes 393248 | tf_op jit(solution)/shard_map/ppermute | solution.py:80
  209.9 8.8 %collective-permute-done.48.refs_2_ = bf16[256,768]{1,0:T(8,128)(2,1)S(1)} collective-permute-done((bf16[256,768]{1,0:T(8,128)(2,1)S(1)}, bf16[256,768]{1,0:T(8,128)(2,1)S(1)}, u32[]{:S(2)}, u32[]{:S(2)}) %collective-permute-start.48) | collective-permute-done | bytes 393248 | tf_op jit(solution)/shard_map/ppermute | solution.py:80
  219.0 7.6 %collective-permute-done.50.refs_2_ = bf16[256,768]{1,0:T(8,128)(2,1)S(1)} collective-permute-done((bf16[256,768]{1,0:T(8,128)(2,1)S(1)}, bf16[256,768]{1,0:T(8,128)(2,1)S(1)}, u32[]{:S(2)}, u32[]{:S(2)}) %collective-permute-start.50) | collective-permute-done | bytes 393248 | tf_op jit(solution)/shard_map/ppermute | solution.py:80
  227.6 2.1 shard_map.226
  232.9 2.1 shard_map.229
  239.6 5.0 %shard_map.233 = (bf16[4,96,2304]{2,1,0:T(8,128)(2,1)S(1)}, bf16[4,96,768]{2,1,0:T(8,128)(2,1)S(1)}, bf16[4,96,768]{2,1,0:T(8,128)(2,1)S(1)}, bf16[4,96,768]{2,1,0:T(8,128)(2,1)S(1)}) custom-call(s32[6]{0:T(128)S(1)} %stack.27.refs_0_.refs_1_, bf16[256,768]{1,0:T(8,128)(2,1)S(1)} %get-tuple-element.265.refs_0_.refs_49_.refs_47_.refs_50_.refs_48_.refs_1_, ...), custom_call_target="tpu_custom_call" | custom-call | flops 3623878 | bytes 11403 | tf_op jit(solution)/shard_map/pallas_call | solution.py:56
  254.9 6.5 %shard_map.237 = (bf16[512,192]{1,0:T(8,128)(2,1)S(1)}, f32[1024,256]{1,0:T(8,128)S(1)}, f32[1024,192]{1,0:T(8,128)S(1)}) custom-call(bf16[1024,256]{1,0:T(8,128)(2,1)S(1)} %get-tuple-element.245.refs_0_.refs_35_.refs_37_.refs_42_.refs_38_.refs_36_.refs_50_.refs_39_, bf16[512,192]{1,0:T(8,128)(2,1)S(1)} %shard_map.236.refs_1_.refs_49_, ...), custom_call_target="tpu_custom_call" | custom-call | flops 4026531 | bytes 5144 | tf_op jit(solution)/shard_map/pallas_call | solution.py:56
  265.2 8.2 %collective-permute-done.60.refs_51_.refs_3_ = bf16[4,96,768]{2,1,0:T(8,128)(2,1)S(1)} collective-permute-done((bf16[4,96,768]{2,1,0:T(8,128)(2,1)S(1)}, bf16[4,96,768]{2,1,0:T(8,128)(2,1)S(1)}, u32[]{:S(2)}, u32[]{:S(2)}) %collective-permute-start.60) | collective-permute-done | bytes 589856 | tf_op jit(solution)/shard_map/ppermute | solution.py:84
  273.4 7.4 %shard_map.240 = (bf16[1024,576]{1,0:T(8,128)(2,1)S(1)}, f32[1024,256]{1,0:T(8,128)}, f32[1024,192]{1,0:T(8,128)S(1)}) custom-call(bf16[1024,256]{1,0:T(8,128)(2,1)S(1)} %get-tuple-element.245.refs_0_.refs_35_.refs_37_.refs_42_.refs_38_.refs_36_.refs_50_.refs_39_, bf16[512,192]{1,0:T(8,128)(2,1)S(1)} %shard_map.239.refs_1_.refs_52_, ...), custom_call_target="tpu_custom_call" | custom-call | flops 4026531 | bytes 8159 | tf_op jit(solution)/shard_map/pallas_call | solution.py:56
  280.9 4.4 collective-permute-done.61.refs_43_.refs_4_
  292.7 2.5 shard_map.248
  295.2 5.2 %collective-permute-done.65.refs_2_ = bf16[256,768]{1,0:T(8,128)(2,1)S(1)} collective-permute-done((bf16[256,768]{1,0:T(8,128)(2,1)S(1)}, bf16[256,768]{1,0:T(8,128)(2,1)S(1)}, u32[]{:S(2)}, u32[]{:S(2)}) %collective-permute-start.65) | collective-permute-done | bytes 393248 | tf_op jit(solution)/shard_map/ppermute | solution.py:80
  303.1 5.1 %collective-permute-done.64.refs_2_ = bf16[256,768]{1,0:T(8,128)(2,1)S(1)} collective-permute-done((bf16[256,768]{1,0:T(8,128)(2,1)S(1)}, bf16[256,768]{1,0:T(8,128)(2,1)S(1)}, u32[]{:S(2)}, u32[]{:S(2)}) %collective-permute-start.64) | collective-permute-done | bytes 393248 | tf_op jit(solution)/shard_map/ppermute | solution.py:80
  308.2 5.3 %collective-permute-done.66.refs_35_.refs_2_ = bf16[96,2304]{1,0:T(8,128)(2,1)S(1)} collective-permute-done((bf16[96,2304]{1,0:T(8,128)(2,1)S(1)}, bf16[96,2304]{1,0:T(8,128)(2,1)S(1)}, u32[]{:S(2)}, u32[]{:S(2)}) %collective-permute-start.66) | collective-permute-done | bytes 442400 | tf_op jit(solution)/shard_map/ppermute | solution.py:84
  320.0 2.3 shard_map.254
  324.2 4.5 shard_map.257
  329.8 5.4 %collective-permute-done.74.refs_2_ = bf16[4,96,768]{2,1,0:T(8,128)(2,1)S(1)} collective-permute-done((bf16[4,96,768]{2,1,0:T(8,128)(2,1)S(1)}, bf16[4,96,768]{2,1,0:T(8,128)(2,1)S(1)}, u32[]{:S(2)}, u32[]{:S(2)}) %collective-permute-start.74) | collective-permute-done | bytes 589856 | tf_op jit(solution)/shard_map/ppermute | solution.py:84
  338.7 2.2 collective-permute-start.79
  341.9 6.4 %shard_map.261 = (bf16[512,192]{1,0:T(8,128)(2,1)S(1)}, f32[1024,256]{1,0:T(8,128)S(1)}, f32[1024,192]{1,0:T(8,128)S(1)}) custom-call(bf16[1024,256]{1,0:T(8,128)(2,1)S(1)} %get-tuple-element.206.refs_0_.refs_5_.refs_6_.refs_8_.refs_12_.refs_9_.refs_7_.refs_20_.refs_17_.refs_11_, bf16[512,192]{1,0:T(8,128)(2,1)S(1)} %shard_map.260.refs_1_.refs_23_, ...), custom_call_target="tpu_custom_call" | custom-call | flops 4026531 | bytes 5144 | tf_op jit(solution)/shard_map/pallas_call | solution.py:56
  349.1 3.5 collective-permute-done.79.refs_26_.refs_3_
  352.6 7.8 %collective-permute-start.82 = (bf16[96,768]{1,0:T(8,128)(2,1)S(1)}, bf16[96,768]{1,0:T(8,128)(2,1)S(1)}, u32[]{:S(2)}, u32[]{:S(2)}) collective-permute-start(bf16[96,768]{1,0:T(8,128)(2,1)S(1)} %get-tuple-element.358), channel_id=1, source_target_pairs={{0,16},{4,20},{8,24},{12,28},{16,0},{20,4},{24,8},{28,12},{1,17},{... | collective-permute-start | bytes 442376 | tf_op jit(solution)/shard_map/ppermute | solution.py:84
  363.0 7.6 %shard_map.265 = (bf16[1024,576]{1,0:T(8,128)(2,1)S(1)}, f32[1024,256]{1,0:T(8,128)}, f32[1024,192]{1,0:T(8,128)S(1)}) custom-call(bf16[1024,256]{1,0:T(8,128)(2,1)S(1)} %get-tuple-element.206.refs_0_.refs_5_.refs_6_.refs_8_.refs_12_.refs_9_.refs_7_.refs_20_.refs_17_.refs_11_, bf16[512,192]{1,0:T(8,128)(2,1)S(1)} %shard_map.264.refs_1_.refs_27_, ...), custom_call_target="tpu_custom_call" | custom-call | flops 4026531 | bytes 8159 | tf_op jit(solution)/shard_map/pallas_call | solution.py:56
  376.5 2.5 shard_map.269
  385.8 8.1 %collective-permute-done.88.refs_1_ = f32[8,768]{1,0:T(8,128)S(1)} collective-permute-done((f32[8,768]{1,0:T(8,128)S(1)}, f32[8,768]{1,0:T(8,128)S(1)}, u32[]{:S(2)}, u32[]{:S(2)}) %collective-permute-start.88) | collective-permute-done | bytes 24608 | tf_op jit(solution)/shard_map/ppermute | solution.py:1060
  395.4 3.6 collective-permute-done.87.refs_2_.refs_5_
  402.7 17.2 %collective-permute-done.95.refs_4_.refs_6_ = bf16[96,2304]{1,0:T(8,128)(2,1)S(1)} collective-permute-done((bf16[96,2304]{1,0:T(8,128)(2,1)S(1)}, bf16[96,2304]{1,0:T(8,128)(2,1)S(1)}, u32[]{:S(2)}, u32[]{:S(2)}) %collective-permute-start.95) | collective-permute-done | bytes 442400 | tf_op jit(solution)/shard_map/ppermute | solution.py:84
  423.5 9.6 %collective-permute-start.92 = (bf16[2,64,384]{2,1,0:T(8,128)(2,1)S(1)}, bf16[2,64,384]{2,1,0:T(8,128)(2,1)S(1)}, u32[]{:S(2)}, u32[]{:S(2)}) collective-permute-start(bf16[2,64,384]{2,1,0:T(8,128)(2,1)S(1)} %get-tuple-element.374), channel_id=1, source_target_pairs={{0,8},{4,12},{8,0},{12,4},{16,24},{20,28},{24,16},{28,20},{1,9},{5... | collective-permute-start | bytes 294920 | tf_op jit(solution)/shard_map/ppermute | solution.py:84
  433.2 2.2 collective-permute-start.94
  435.5 4.4 collective-permute-done.98.refs_7_.refs_2_
  439.9 4.6 collective-permute-done.93.refs_2_
  445.7 7.0 %collective-permute-done.101.refs_3_ = bf16[8,64,384]{2,1,0:T(8,128)(2,1)S(1)} collective-permute-done((bf16[8,64,384]{2,1,0:T(8,128)(2,1)S(1)}, bf16[8,64,384]{2,1,0:T(8,128)(2,1)S(1)}, u32[]{:S(2)}, u32[]{:S(2)}) %collective-permute-start.101) | collective-permute-done | bytes 393248 | tf_op jit(solution)/shard_map/ppermute | solution.py:80
  452.7 2.8 collective-permute-start.104
  462.2 2.5 shard_map.283
  (340 shorter events, 153.8 us)
Async XLA Ops:
  6.4 40.0 %collective-permute-start.7 = (bf16[96,3072]{1,0:T(8,128)(2,1)S(1)}, bf16[96,3072]{1,0:T(8,128)(2,1)S(1)}, u32[]{:S(2)}, u32[]{:S(2)}) collective-permute-start(bf16[96,3072]{1,0:T(8,128)(2,1)S(1)} %shard_map.179.refs_2_.refs_0_.refs_1_), channel_id=1, source_target_pairs={{0,4},{4,0},{8,12},{12,8},{16,20},{20,16},{24,28},{28,24},{1,5},{5... | collective-permute-start | bytes 1769480 | tf_op jit(solution)/shard_map/ppermute | solution.py:84
  9.4 37.0 %collective-permute-start.8 = (bf16[96,3072]{1,0:T(8,128)(2,1)S(1)}, bf16[96,3072]{1,0:T(8,128)(2,1)}, u32[]{:S(2)}, u32[]{:S(2)}) collective-permute-start(bf16[96,3072]{1,0:T(8,128)(2,1)S(1)} %shard_map.179.refs_2_.refs_0_.refs_1_), channel_id=1, source_target_pairs={{0,8},{4,12},{8,0},{12,4},{16,24},{20,28},{24,16},{28,20},{1,9},{5... | collective-permute-start | bytes 1769480 | tf_op jit(solution)/shard_map/ppermute | solution.py:84
  11.0 35.4 %collective-permute-start.9 = (bf16[96,3072]{1,0:T(8,128)(2,1)S(1)}, bf16[96,3072]{1,0:T(8,128)(2,1)S(1)}, u32[]{:S(2)}, u32[]{:S(2)}) collective-permute-start(bf16[96,3072]{1,0:T(8,128)(2,1)S(1)} %shard_map.179.refs_2_.refs_0_.refs_1_), channel_id=1, source_target_pairs={{0,16},{4,20},{8,24},{12,28},{16,0},{20,4},{24,8},{28,12},{1,17},{... | collective-permute-start | bytes 1769480 | tf_op jit(solution)/shard_map/ppermute | solution.py:84
  27.0 12.8 %collective-permute-start.1 = (bf16[2,32,768]{2,1,0:T(8,128)(2,1)S(1)}, bf16[2,32,768]{2,1,0:T(8,128)(2,1)S(1)}, u32[]{:S(2)}, u32[]{:S(2)}) collective-permute-start(bf16[2,32,768]{2,1,0:T(8,128)(2,1)S(1)} %get-tuple-element.201), channel_id=1, source_target_pairs={{0,8},{4,12},{8,0},{12,4},{16,24},{20,28},{24,16},{28,20},{1,9},{5... | collective-permute-start | bytes 294920 | tf_op jit(solution)/shard_map/ppermute | solution.py:84
  28.8 15.6 %collective-permute-start.2 = (bf16[2,32,768]{2,1,0:T(8,128)(2,1)S(1)}, bf16[2,32,768]{2,1,0:T(8,128)(2,1)S(1)}, u32[]{:S(2)}, u32[]{:S(2)}) collective-permute-start(bf16[2,32,768]{2,1,0:T(8,128)(2,1)S(1)} %get-tuple-element.202), channel_id=1, source_target_pairs={{0,16},{4,20},{8,24},{12,28},{16,0},{20,4},{24,8},{28,12},{1,17},{... | collective-permute-start | bytes 294920 | tf_op jit(solution)/shard_map/ppermute | solution.py:84
  47.3 15.4 %collective-permute-start.10 = (bf16[96,3072]{1,0:T(8,128)(2,1)}, bf16[96,3072]{1,0:T(8,128)(2,1)S(1)}, u32[]{:S(2)}, u32[]{:S(2)}) collective-permute-start(bf16[96,3072]{1,0:T(8,128)(2,1)} %shard_map.183.refs_7_), channel_id=1, source_target_pairs={{0,24},{4,28},{8,16},{12,20},{16,8},{20,12},{24,0},{28,4},{1,25},{... | collective-permute-start | bytes 1769480 | tf_op jit(solution)/shard_map/ppermute | solution.py:84
  51.9 16.5 %collective-permute-start.11 = (bf16[96,3072]{1,0:T(8,128)(2,1)}, bf16[96,3072]{1,0:T(8,128)(2,1)S(1)}, u32[]{:S(2)}, u32[]{:S(2)}) collective-permute-start(bf16[96,3072]{1,0:T(8,128)(2,1)} %collective-permute-done.8.refs_2_.refs_3_), channel_id=1, source_target_pairs={{0,4},{4,0},{8,12},{12,8},{16,20},{20,16},{24,28},{28,24},{1,5},{5... | collective-permute-start | bytes 1769480 | tf_op jit(solution)/shard_map/ppermute | solution.py:84
  52.4 28.6 %collective-permute-start.12 = (bf16[96,3072]{1,0:T(8,128)(2,1)}, bf16[96,3072]{1,0:T(8,128)(2,1)S(1)}, u32[]{:S(2)}, u32[]{:S(2)}) collective-permute-start(bf16[96,3072]{1,0:T(8,128)(2,1)} %copy-done.5), channel_id=1, source_target_pairs={{0,4},{4,0},{8,12},{12,8},{16,20},{20,16},{24,28},{28,24},{1,5},{5... | collective-permute-start | bytes 1769480 | tf_op jit(solution)/shard_map/ppermute | solution.py:84
  53.9 37.6 %collective-permute-start.4 = (bf16[8,32,768]{2,1,0:T(8,128)(2,1)S(1)}, bf16[8,32,768]{2,1,0:T(8,128)(2,1)S(1)}, u32[]{:S(2)}, u32[]{:S(2)}) collective-permute-start(bf16[8,32,768]{2,1,0:T(8,128)(2,1)S(1)} %shard_map.182.refs_4_.refs_1_), channel_id=1, source_target_pairs={{0,1},{1,0},{2,3},{3,2},{4,5},{5,4},{6,7},{7,6},{8,9},{9,8},{10,11... | collective-permute-start | bytes 1179656 | tf_op jit(solution)/shard_map/ppermute | solution.py:76
  58.5 33.0 %collective-permute-start.6 = (bf16[8,32,768]{2,1,0:T(8,128)(2,1)}, bf16[8,32,768]{2,1,0:T(8,128)(2,1)S(1)}, u32[]{:S(2)}, u32[]{:S(2)}) collective-permute-start(bf16[8,32,768]{2,1,0:T(8,128)(2,1)} %collective-permute-done.5.refs_3_), channel_id=1, source_target_pairs={{0,1},{1,0},{2,3},{3,2},{4,5},{5,4},{6,7},{7,6},{8,9},{9,8},{10,11... | collective-permute-start | bytes 1179656 | tf_op jit(solution)/shard_map/ppermute | solution.py:76
  62.8 27.4 %collective-permute-start.13 = (bf16[96,3072]{1,0:T(8,128)(2,1)S(1)}, bf16[96,3072]{1,0:T(8,128)(2,1)S(1)}, u32[]{:S(2)}, u32[]{:S(2)}) collective-permute-start(bf16[96,3072]{1,0:T(8,128)(2,1)S(1)} %collective-permute-done.10.refs_4_.refs_5_), channel_id=1, source_target_pairs={{0,4},{4,0},{8,12},{12,8},{16,20},{20,16},{24,28},{28,24},{1,5},{5... | collective-permute-start | bytes 1769480 | tf_op jit(solution)/shard_map/ppermute | solution.py:84
  102.6 11.1 %collective-permute-start.18 = (bf16[256,768]{1,0:T(8,128)(2,1)S(1)}, bf16[256,768]{1,0:T(8,128)(2,1)S(1)}, u32[]{:S(2)}, u32[]{:S(2)}) collective-permute-start(bf16[256,768]{1,0:T(8,128)(2,1)S(1)} %bitcast.205), channel_id=1, source_target_pairs={{0,2},{1,3},{2,0},{3,1},{4,6},{5,7},{6,4},{7,5},{8,10},{9,11},{10,... | collective-permute-start | bytes 1179656 | tf_op jit(solution)/shard_map/ppermute | solution.py:80
  103.2 11.5 %collective-permute-start.20 = (bf16[96,768]{1,0:T(8,128)(2,1)S(1)}, bf16[96,768]{1,0:T(8,128)(2,1)S(1)}, u32[]{:S(2)}, u32[]{:S(2)}) collective-permute-start(bf16[96,768]{1,0:T(8,128)(2,1)S(1)} %get-tuple-element.204.refs_13_.refs_1_), channel_id=1, source_target_pairs={{0,24},{4,28},{8,16},{12,20},{16,8},{20,12},{24,0},{28,4},{1,25},{... | collective-permute-start | bytes 442376 | tf_op jit(solution)/shard_map/ppermute | solution.py:84
  113.7 20.5 %collective-permute-start.26 = (bf16[96,2304]{1,0:T(8,128)(2,1)S(1)}, bf16[96,2304]{1,0:T(8,128)(2,1)S(1)}, u32[]{:S(2)}, u32[]{:S(2)}) collective-permute-start(bf16[96,2304]{1,0:T(8,128)(2,1)S(1)} %get-tuple-element.231.refs_1_), channel_id=1, source_target_pairs={{0,8},{4,12},{8,0},{12,4},{16,24},{20,28},{24,16},{28,20},{1,9},{5... | collective-permute-start | bytes 1327112 | tf_op jit(solution)/shard_map/ppermute | solution.py:84
  114.7 21.5 %collective-permute-start.27 = (bf16[96,2304]{1,0:T(8,128)(2,1)S(1)}, bf16[96,2304]{1,0:T(8,128)(2,1)S(1)}, u32[]{:S(2)}, u32[]{:S(2)}) collective-permute-start(bf16[96,2304]{1,0:T(8,128)(2,1)S(1)} %get-tuple-element.231.refs_1_), channel_id=1, source_target_pairs={{0,16},{4,20},{8,24},{12,28},{16,0},{20,4},{24,8},{28,12},{1,17},{... | collective-permute-start | bytes 1327112 | tf_op jit(solution)/shard_map/ppermute | solution.py:84
  115.7 20.5 %collective-permute-start.28 = (bf16[96,2304]{1,0:T(8,128)(2,1)S(1)}, bf16[96,2304]{1,0:T(8,128)(2,1)S(1)}, u32[]{:S(2)}, u32[]{:S(2)}) collective-permute-start(bf16[96,2304]{1,0:T(8,128)(2,1)S(1)} %get-tuple-element.231.refs_1_), channel_id=1, source_target_pairs={{0,4},{4,0},{8,12},{12,8},{16,20},{20,16},{24,28},{28,24},{1,5},{5... | collective-permute-start | bytes 1327112 | tf_op jit(solution)/shard_map/ppermute | solution.py:84
  116.4 12.1 %collective-permute-start.17 = (bf16[256,768]{1,0:T(8,128)(2,1)S(1)}, bf16[256,768]{1,0:T(8,128)(2,1)S(1)}, u32[]{:S(2)}, u32[]{:S(2)}) collective-permute-start(bf16[256,768]{1,0:T(8,128)(2,1)S(1)} %get-tuple-element.218.refs_11_), channel_id=1, source_target_pairs={{0,2},{1,3},{2,0},{3,1},{4,6},{5,7},{6,4},{7,5},{8,10},{9,11},{10,... | collective-permute-start | bytes 1179656 | tf_op jit(solution)/shard_map/ppermute | solution.py:80
  117.8 18.3 %collective-permute-start.25 = (bf16[256,768]{1,0:T(8,128)(2,1)S(1)}, bf16[256,768]{1,0:T(8,128)(2,1)S(1)}, u32[]{:S(2)}, u32[]{:S(2)}) collective-permute-start(bf16[256,768]{1,0:T(8,128)(2,1)S(1)} %get-tuple-element.225.refs_16_), channel_id=1, source_target_pairs={{0,2},{1,3},{2,0},{3,1},{4,6},{5,7},{6,4},{7,5},{8,10},{9,11},{10,... | collective-permute-start | bytes 1179656 | tf_op jit(solution)/shard_map/ppermute | solution.py:80
  141.0 13.0 %collective-permute-start.32 = (bf16[96,2304]{1,0:T(8,128)(2,1)S(1)}, bf16[96,2304]{1,0:T(8,128)(2,1)S(1)}, u32[]{:S(2)}, u32[]{:S(2)}) collective-permute-start(bf16[96,2304]{1,0:T(8,128)(2,1)S(1)} %collective-permute-done.26.refs_24_.refs_3_), channel_id=1, source_target_pairs={{0,4},{4,0},{8,12},{12,8},{16,20},{20,16},{24,28},{28,24},{1,5},{5... | collective-permute-start | bytes 1327112 | tf_op jit(solution)/shard_map/ppermute | solution.py:84
  141.5 16.5 %collective-permute-start.36 = (bf16[96,2304]{1,0:T(8,128)(2,1)S(1)}, bf16[96,2304]{1,0:T(8,128)(2,1)S(1)}, u32[]{:S(2)}, u32[]{:S(2)}) collective-permute-start(bf16[96,2304]{1,0:T(8,128)(2,1)S(1)} %get-tuple-element.231.refs_1_), channel_id=1, source_target_pairs={{0,24},{4,28},{8,16},{12,20},{16,8},{20,12},{24,0},{28,4},{1,25},{... | collective-permute-start | bytes 1327112 | tf_op jit(solution)/shard_map/ppermute | solution.py:84
  143.9 19.2 %collective-permute-start.37 = (bf16[96,2304]{1,0:T(8,128)(2,1)S(1)}, bf16[96,2304]{1,0:T(8,128)(2,1)S(1)}, u32[]{:S(2)}, u32[]{:S(2)}) collective-permute-start(bf16[96,2304]{1,0:T(8,128)(2,1)S(1)} %collective-permute-done.27.refs_25_.refs_5_), channel_id=1, source_target_pairs={{0,4},{4,0},{8,12},{12,8},{16,20},{20,16},{24,28},{28,24},{1,5},{5... | collective-permute-start | bytes 1327112 | tf_op jit(solution)/shard_map/ppermute | solution.py:84
  145.5 12.1 %collective-permute-start.31 = (bf16[256,768]{1,0:T(8,128)(2,1)S(1)}, bf16[256,768]{1,0:T(8,128)(2,1)S(1)}, u32[]{:S(2)}, u32[]{:S(2)}) collective-permute-start(bf16[256,768]{1,0:T(8,128)(2,1)S(1)} %get-tuple-element.236.refs_27_), channel_id=1, source_target_pairs={{0,2},{1,3},{2,0},{3,1},{4,6},{5,7},{6,4},{7,5},{8,10},{9,11},{10,... | collective-permute-start | bytes 1179656 | tf_op jit(solution)/shard_map/ppermute | solution.py:80
  147.1 17.5 %collective-permute-start.35 = (bf16[256,768]{1,0:T(8,128)(2,1)S(1)}, bf16[256,768]{1,0:T(8,128)(2,1)S(1)}, u32[]{:S(2)}, u32[]{:S(2)}) collective-permute-start(bf16[256,768]{1,0:T(8,128)(2,1)S(1)} %get-tuple-element.237.refs_30_), channel_id=1, source_target_pairs={{0,2},{1,3},{2,0},{3,1},{4,6},{5,7},{6,4},{7,5},{8,10},{9,11},{10,... | collective-permute-start | bytes 1179656 | tf_op jit(solution)/shard_map/ppermute | solution.py:80
  157.9 14.0 %collective-permute-start.34 = (bf16[256,768]{1,0:T(8,128)(2,1)S(1)}, bf16[256,768]{1,0:T(8,128)(2,1)S(1)}, u32[]{:S(2)}, u32[]{:S(2)}) collective-permute-start(bf16[256,768]{1,0:T(8,128)(2,1)S(1)} %get-tuple-element.238.refs_0_.refs_33_.refs_31_.refs_38_.refs_34_.refs_32_.refs_46_.refs_35_.refs_1_), channel_id=1, source_target_pairs={{0,1},{1,0},{2,3},{3,2},{4,5},{5,4},{6,7},{7,6},{8,9},{9,8},{10,11... | collective-permute-start | bytes 1179656 | tf_op jit(solution)/shard_map/ppermute | solution.py:76
  181.8 12.2 %collective-permute-start.42 = (bf16[96,2304]{1,0:T(8,128)(2,1)S(1)}, bf16[96,2304]{1,0:T(8,128)(2,1)S(1)}, u32[]{:S(2)}, u32[]{:S(2)}) collective-permute-start(bf16[96,2304]{1,0:T(8,128)(2,1)S(1)} %collective-permute-done.36.refs_31_.refs_7_), channel_id=1, source_target_pairs={{0,4},{4,0},{8,12},{12,8},{16,20},{20,16},{24,28},{28,24},{1,5},{5... | collective-permute-start | bytes 1327112 | tf_op jit(solution)/shard_map/ppermute | solution.py:84
  182.3 12.0 %collective-permute-start.41 = (bf16[256,768]{1,0:T(8,128)(2,1)S(1)}, bf16[256,768]{1,0:T(8,128)(2,1)S(1)}, u32[]{:S(2)}, u32[]{:S(2)}) collective-permute-start(bf16[256,768]{1,0:T(8,128)(2,1)S(1)} %get-tuple-element.257.refs_41_), channel_id=1, source_target_pairs={{0,2},{1,3},{2,0},{3,1},{4,6},{5,7},{6,4},{7,5},{8,10},{9,11},{10,... | collective-permute-start | bytes 1179656 | tf_op jit(solution)/shard_map/ppermute | solution.py:80
  186.0 15.5 %collective-permute-start.45 = (bf16[256,768]{1,0:T(8,128)(2,1)S(1)}, bf16[256,768]{1,0:T(8,128)(2,1)S(1)}, u32[]{:S(2)}, u32[]{:S(2)}) collective-permute-start(bf16[256,768]{1,0:T(8,128)(2,1)S(1)} %get-tuple-element.264.refs_48_), channel_id=1, source_target_pairs={{0,2},{1,3},{2,0},{3,1},{4,6},{5,7},{6,4},{7,5},{8,10},{9,11},{10,... | collective-permute-start | bytes 1179656 | tf_op jit(solution)/shard_map/ppermute | solution.py:80
  206.7 12.0 %collective-permute-start.48 = (bf16[256,768]{1,0:T(8,128)(2,1)S(1)}, bf16[256,768]{1,0:T(8,128)(2,1)S(1)}, u32[]{:S(2)}, u32[]{:S(2)}) collective-permute-start(bf16[256,768]{1,0:T(8,128)(2,1)S(1)} %get-tuple-element.273.refs_55_), channel_id=1, source_target_pairs={{0,2},{1,3},{2,0},{3,1},{4,6},{5,7},{6,4},{7,5},{8,10},{9,11},{10,... | collective-permute-start | bytes 1179656 | tf_op jit(solution)/shard_map/ppermute | solution.py:80
  208.4 18.3 %collective-permute-start.50 = (bf16[256,768]{1,0:T(8,128)(2,1)S(1)}, bf16[256,768]{1,0:T(8,128)(2,1)S(1)}, u32[]{:S(2)}, u32[]{:S(2)}) collective-permute-start(bf16[256,768]{1,0:T(8,128)(2,1)S(1)} %get-tuple-element.274.refs_57_), channel_id=1, source_target_pairs={{0,2},{1,3},{2,0},{3,1},{4,6},{5,7},{6,4},{7,5},{8,10},{9,11},{10,... | collective-permute-start | bytes 1179656 | tf_op jit(solution)/shard_map/ppermute | solution.py:80
  238.0 11.2 %collective-permute-start.56 = (bf16[256,768]{1,0:T(8,128)(2,1)S(1)}, bf16[256,768]{1,0:T(8,128)(2,1)S(1)}, u32[]{:S(2)}, u32[]{:S(2)}) collective-permute-start(bf16[256,768]{1,0:T(8,128)(2,1)S(1)} %get-tuple-element.298.refs_69_), channel_id=1, source_target_pairs={{0,2},{1,3},{2,0},{3,1},{4,6},{5,7},{6,4},{7,5},{8,10},{9,11},{10,... | collective-permute-start | bytes 1179656 | tf_op jit(solution)/shard_map/ppermute | solution.py:80
  244.5 17.9 %collective-permute-start.58 = (bf16[4,96,768]{2,1,0:T(8,128)(2,1)S(1)}, bf16[4,96,768]{2,1,0:T(8,128)(2,1)S(1)}, u32[]{:S(2)}, u32[]{:S(2)}) collective-permute-start(bf16[4,96,768]{2,1,0:T(8,128)(2,1)S(1)} %get-tuple-element.300.refs_66_), channel_id=1, source_target_pairs={{0,4},{4,0},{8,12},{12,8},{16,20},{20,16},{24,28},{28,24},{1,5},{5... | collective-permute-start | bytes 1769480 | tf_op jit(solution)/shard_map/ppermute | solution.py:84
  250.9 11.5 %collective-permute-start.55 = (bf16[256,768]{1,0:T(8,128)(2,1)S(1)}, bf16[256,768]{1,0:T(8,128)(2,1)S(1)}, u32[]{:S(2)}, u32[]{:S(2)}) collective-permute-start(bf16[256,768]{1,0:T(8,128)(2,1)S(1)} %get-tuple-element.299.refs_66_), channel_id=1, source_target_pairs={{0,2},{1,3},{2,0},{3,1},{4,6},{5,7},{6,4},{7,5},{8,10},{9,11},{10,... | collective-permute-start | bytes 1179656 | tf_op jit(solution)/shard_map/ppermute | solution.py:80
  252.4 21.0 %collective-permute-start.60 = (bf16[4,96,768]{2,1,0:T(8,128)(2,1)S(1)}, bf16[4,96,768]{2,1,0:T(8,128)(2,1)S(1)}, u32[]{:S(2)}, u32[]{:S(2)}) collective-permute-start(bf16[4,96,768]{2,1,0:T(8,128)(2,1)S(1)} %get-tuple-element.310), channel_id=1, source_target_pairs={{0,4},{4,0},{8,12},{12,8},{16,20},{20,16},{24,28},{28,24},{1,5},{5... | collective-permute-start | bytes 1769480 | tf_op jit(solution)/shard_map/ppermute | solution.py:84
  253.9 31.3 %collective-permute-start.61 = (bf16[4,96,768]{2,1,0:T(8,128)(2,1)S(1)}, bf16[4,96,768]{2,1,0:T(8,128)(2,1)S(1)}, u32[]{:S(2)}, u32[]{:S(2)}) collective-permute-start(bf16[4,96,768]{2,1,0:T(8,128)(2,1)S(1)} %get-tuple-element.312), channel_id=1, source_target_pairs={{0,4},{4,0},{8,12},{12,8},{16,20},{20,16},{24,28},{28,24},{1,5},{5... | collective-permute-start | bytes 1769480 | tf_op jit(solution)/shard_map/ppermute | solution.py:84
  288.4 11.9 %collective-permute-start.65 = (bf16[256,768]{1,0:T(8,128)(2,1)S(1)}, bf16[256,768]{1,0:T(8,128)(2,1)S(1)}, u32[]{:S(2)}, u32[]{:S(2)}) collective-permute-start(bf16[256,768]{1,0:T(8,128)(2,1)S(1)} %get-tuple-element.314.refs_43_), channel_id=1, source_target_pairs={{0,2},{1,3},{2,0},{3,1},{4,6},{5,7},{6,4},{7,5},{8,10},{9,11},{10,... | collective-permute-start | bytes 1179656 | tf_op jit(solution)/shard_map/ppermute | solution.py:80
  291.5 22.0 %collective-permute-start.66 = (bf16[96,2304]{1,0:T(8,128)(2,1)S(1)}, bf16[96,2304]{1,0:T(8,128)(2,1)S(1)}, u32[]{:S(2)}, u32[]{:S(2)}) collective-permute-start(bf16[96,2304]{1,0:T(8,128)(2,1)S(1)} %get-tuple-element.325), channel_id=1, source_target_pairs={{0,16},{4,20},{8,24},{12,28},{16,0},{20,4},{24,8},{28,12},{1,17},{... | collective-permute-start | bytes 1327112 | tf_op jit(solution)/shard_map/ppermute | solution.py:84
  291.7 16.5 %collective-permute-start.64 = (bf16[256,768]{1,0:T(8,128)(2,1)S(1)}, bf16[256,768]{1,0:T(8,128)(2,1)S(1)}, u32[]{:S(2)}, u32[]{:S(2)}) collective-permute-start(bf16[256,768]{1,0:T(8,128)(2,1)S(1)} %get-tuple-element.316.refs_46_), channel_id=1, source_target_pairs={{0,2},{1,3},{2,0},{3,1},{4,6},{5,7},{6,4},{7,5},{8,10},{9,11},{10,... | collective-permute-start | bytes 1179656 | tf_op jit(solution)/shard_map/ppermute | solution.py:80
  300.9 15.4 %collective-permute-start.68 = (bf16[256,768]{1,0:T(8,128)(2,1)S(1)}, bf16[256,768]{1,0:T(8,128)(2,1)S(1)}, u32[]{:S(2)}, u32[]{:S(2)}) collective-permute-start(bf16[256,768]{1,0:T(8,128)(2,1)S(1)} %get-tuple-element.321.refs_1_.refs_34_.refs_29_.refs_31_.refs_9_.refs_24_.refs_0_), channel_id=1, source_target_pairs={{0,1},{1,0},{2,3},{3,2},{4,5},{5,4},{6,7},{7,6},{8,9},{9,8},{10,11... | collective-permute-start | bytes 1179656 | tf_op jit(solution)/shard_map/ppermute | solution.py:76
  319.0 16.2 %collective-permute-start.74 = (bf16[4,96,768]{2,1,0:T(8,128)(2,1)S(1)}, bf16[4,96,768]{2,1,0:T(8,128)(2,1)S(1)}, u32[]{:S(2)}, u32[]{:S(2)}) collective-permute-start(bf16[4,96,768]{2,1,0:T(8,128)(2,1)S(1)} %get-tuple-element.343), channel_id=1, source_target_pairs={{0,4},{4,0},{8,12},{12,8},{16,20},{20,16},{24,28},{28,24},{1,5},{5... | collective-permute-start | bytes 1769480 | tf_op jit(solution)/shard_map/ppermute | solution.py:84
  322.4 13.4 %collective-permute-start.73 = (bf16[96,2304]{1,0:T(8,128)(2,1)S(1)}, bf16[96,2304]{1,0:T(8,128)(2,1)S(1)}, u32[]{:S(2)}, u32[]{:S(2)}) collective-permute-start(bf16[96,2304]{1,0:T(8,128)(2,1)S(1)} %get-tuple-element.342), channel_id=1, source_target_pairs={{0,8},{4,12},{8,0},{12,4},{16,24},{20,28},{24,16},{28,20},{1,9},{5... | collective-permute-start | bytes 1327112 | tf_op jit(solution)/shard_map/ppermute | solution.py:84
  322.7 13.2 %collective-permute-start.72 = (bf16[256,768]{1,0:T(8,128)(2,1)S(1)}, bf16[256,768]{1,0:T(8,128)(2,1)S(1)}, u32[]{:S(2)}, u32[]{:S(2)}) collective-permute-start(bf16[256,768]{1,0:T(8,128)(2,1)S(1)} %get-tuple-element.338.refs_41_), channel_id=1, source_target_pairs={{0,2},{1,3},{2,0},{3,1},{4,6},{5,7},{6,4},{7,5},{8,10},{9,11},{10,... | collective-permute-start | bytes 1179656 | tf_op jit(solution)/shard_map/ppermute | solution.py:80
  328.7 19.6 %collective-permute-start.76 = (bf16[4,96,768]{2,1,0:T(8,128)(2,1)S(1)}, bf16[4,96,768]{2,1,0:T(8,128)(2,1)S(1)}, u32[]{:S(2)}, u32[]{:S(2)}) collective-permute-start(bf16[4,96,768]{2,1,0:T(8,128)(2,1)S(1)} %get-tuple-element.344.refs_26_), channel_id=1, source_target_pairs={{0,4},{4,0},{8,12},{12,8},{16,20},{20,16},{24,28},{28,24},{1,5},{5... | collective-permute-start | bytes 1769480 | tf_op jit(solution)/shard_map/ppermute | solution.py:84
  336.5 11.8 %collective-permute-start.71 = (bf16[256,768]{1,0:T(8,128)(2,1)S(1)}, bf16[256,768]{1,0:T(8,128)(2,1)S(1)}, u32[]{:S(2)}, u32[]{:S(2)}) collective-permute-start(bf16[256,768]{1,0:T(8,128)(2,1)S(1)} %get-tuple-element.340.refs_38_), channel_id=1, source_target_pairs={{0,2},{1,3},{2,0},{3,1},{4,6},{5,7},{6,4},{7,5},{8,10},{9,11},{10,... | collective-permute-start | bytes 1179656 | tf_op jit(solution)/shard_map/ppermute | solution.py:80
  337.7 25.3 %collective-permute-start.78 = (bf16[4,96,768]{2,1,0:T(8,128)(2,1)S(1)}, bf16[4,96,768]{2,1,0:T(8,128)(2,1)S(1)}, u32[]{:S(2)}, u32[]{:S(2)}) collective-permute-start(bf16[4,96,768]{2,1,0:T(8,128)(2,1)S(1)} %get-tuple-element.353), channel_id=1, source_target_pairs={{0,4},{4,0},{8,12},{12,8},{16,20},{20,16},{24,28},{28,24},{1,5},{5... | collective-permute-start | bytes 1769480 | tf_op jit(solution)/shard_map/ppermute | solution.py:84
  338.7 13.9 %collective-permute-start.79 = (bf16[96,2304]{1,0:T(8,128)(2,1)S(1)}, bf16[96,2304]{1,0:T(8,128)(2,1)S(1)}, u32[]{:S(2)}, u32[]{:S(2)}) collective-permute-start(bf16[96,2304]{1,0:T(8,128)(2,1)S(1)} %get-tuple-element.354), channel_id=1, source_target_pairs={{0,24},{4,28},{8,16},{12,20},{16,8},{20,12},{24,0},{28,4},{1,25},{... | collective-permute-start | bytes 1327112 | tf_op jit(solution)/shard_map/ppermute | solution.py:84
  341.0 31.2 %collective-permute-start.80 = (bf16[4,96,768]{2,1,0:T(8,128)(2,1)S(1)}, bf16[4,96,768]{2,1,0:T(8,128)(2,1)S(1)}, u32[]{:S(2)}, u32[]{:S(2)}) collective-permute-start(bf16[4,96,768]{2,1,0:T(8,128)(2,1)S(1)} %get-tuple-element.356), channel_id=1, source_target_pairs={{0,4},{4,0},{8,12},{12,8},{16,20},{20,16},{24,28},{28,24},{1,5},{5... | collective-permute-start | bytes 1769480 | tf_op jit(solution)/shard_map/ppermute | solution.py:84
  349.0 11.4 %collective-permute-start.77 = (bf16[256,768]{1,0:T(8,128)(2,1)S(1)}, bf16[256,768]{1,0:T(8,128)(2,1)S(1)}, u32[]{:S(2)}, u32[]{:S(2)}) collective-permute-start(bf16[256,768]{1,0:T(8,128)(2,1)S(1)} %get-tuple-element.349.refs_0_.refs_23_.refs_4_.refs_16_.refs_13_.refs_5_), channel_id=1, source_target_pairs={{0,1},{1,0},{2,3},{3,2},{4,5},{5,4},{6,7},{7,6},{8,9},{9,8},{10,11... | collective-permute-start | bytes 1179656 | tf_op jit(solution)/shard_map/ppermute | solution.py:76
  349.0 21.6 %collective-permute-start.81 = (bf16[96,768]{1,0:T(8,128)(2,1)S(1)}, bf16[96,768]{1,0:T(8,128)(2,1)S(1)}, u32[]{:S(2)}, u32[]{:S(2)}) collective-permute-start(bf16[96,768]{1,0:T(8,128)(2,1)S(1)} %get-tuple-element.357), channel_id=1, source_target_pairs={{0,8},{4,12},{8,0},{12,4},{16,24},{20,28},{24,16},{28,20},{1,9},{5... | collective-permute-start | bytes 442376 | tf_op jit(solution)/shard_map/ppermute | solution.py:84
  352.6 18.7 %collective-permute-start.82 = (bf16[96,768]{1,0:T(8,128)(2,1)S(1)}, bf16[96,768]{1,0:T(8,128)(2,1)S(1)}, u32[]{:S(2)}, u32[]{:S(2)}) collective-permute-start(bf16[96,768]{1,0:T(8,128)(2,1)S(1)} %get-tuple-element.358), channel_id=1, source_target_pairs={{0,16},{4,20},{8,24},{12,28},{16,0},{20,4},{24,8},{28,12},{1,17},{... | collective-permute-start | bytes 442376 | tf_op jit(solution)/shard_map/ppermute | solution.py:84
  379.0 22.2 %collective-permute-start.91 = (bf16[4,96,768]{2,1,0:T(8,128)(2,1)S(1)}, bf16[4,96,768]{2,1,0:T(8,128)(2,1)S(1)}, u32[]{:S(2)}, u32[]{:S(2)}) collective-permute-start(bf16[4,96,768]{2,1,0:T(8,128)(2,1)S(1)} %get-tuple-element.371), channel_id=1, source_target_pairs={{0,4},{4,0},{8,12},{12,8},{16,20},{20,16},{24,28},{28,24},{1,5},{5... | collective-permute-start | bytes 1769480 | tf_op jit(solution)/shard_map/ppermute | solution.py:84
  380.1 18.9 %collective-permute-start.87 = (bf16[96,2304]{1,0:T(8,128)(2,1)S(1)}, bf16[96,2304]{1,0:T(8,128)(2,1)S(1)}, u32[]{:S(2)}, u32[]{:S(2)}) collective-permute-start(bf16[96,2304]{1,0:T(8,128)(2,1)S(1)} %get-tuple-element.368), channel_id=1, source_target_pairs={{0,8},{4,12},{8,0},{12,4},{16,24},{20,28},{24,16},{28,20},{1,9},{5... | collective-permute-start | bytes 1327112 | tf_op jit(solution)/shard_map/ppermute | solution.py:84
  382.7 16.4 %collective-permute-start.86 = (bf16[8,64,384]{2,1,0:T(8,128)(2,1)S(1)}, bf16[8,64,384]{2,1,0:T(8,128)(2,1)S(1)}, u32[]{:S(2)}, u32[]{:S(2)}) collective-permute-start(bf16[8,64,384]{2,1,0:T(8,128)(2,1)S(1)} %get-tuple-element.367.refs_2_), channel_id=1, source_target_pairs={{0,2},{1,3},{2,0},{3,1},{4,6},{5,7},{6,4},{7,5},{8,10},{9,11},{10,... | collective-permute-start | bytes 1179656 | tf_op jit(solution)/shard_map/ppermute | solution.py:80
  383.7 36.2 %collective-permute-start.95 = (bf16[96,2304]{1,0:T(8,128)(2,1)S(1)}, bf16[96,2304]{1,0:T(8,128)(2,1)S(1)}, u32[]{:S(2)}, u32[]{:S(2)}) collective-permute-start(bf16[96,2304]{1,0:T(8,128)(2,1)S(1)} %get-tuple-element.377), channel_id=1, source_target_pairs={{0,16},{4,20},{8,24},{12,28},{16,0},{20,4},{24,8},{28,12},{1,17},{... | collective-permute-start | bytes 1327112 | tf_op jit(solution)/shard_map/ppermute | solution.py:84
  393.9 29.6 %collective-permute-start.96 = (bf16[96,2304]{1,0:T(8,128)(2,1)S(1)}, bf16[96,2304]{1,0:T(8,128)(2,1)S(1)}, u32[]{:S(2)}, u32[]{:S(2)}) collective-permute-start(bf16[96,2304]{1,0:T(8,128)(2,1)S(1)} %get-tuple-element.378), channel_id=1, source_target_pairs={{0,24},{4,28},{8,16},{12,20},{16,8},{20,12},{24,0},{28,4},{1,25},{... | collective-permute-start | bytes 1327112 | tf_op jit(solution)/shard_map/ppermute | solution.py:84
  399.7 21.7 %collective-permute-start.89 = (bf16[4,64,384]{2,1,0:T(8,128)(2,1)S(1)}, bf16[4,64,384]{2,1,0:T(8,128)(2,1)S(1)}, u32[]{:S(2)}, u32[]{:S(2)}) collective-permute-start(bf16[4,64,384]{2,1,0:T(8,128)(2,1)S(1)} %get-tuple-element.370), channel_id=1, source_target_pairs={{0,4},{4,0},{8,12},{12,8},{16,20},{20,16},{24,28},{28,24},{1,5},{5... | collective-permute-start | bytes 589832 | tf_op jit(solution)/shard_map/ppermute | solution.py:84
  402.0 31.3 %collective-permute-start.97 = (bf16[96,768]{1,0:T(8,128)(2,1)S(1)}, bf16[96,768]{1,0:T(8,128)(2,1)S(1)}, u32[]{:S(2)}, u32[]{:S(2)}) collective-permute-start(bf16[96,768]{1,0:T(8,128)(2,1)S(1)} %get-tuple-element.379), channel_id=1, source_target_pairs={{0,8},{4,12},{8,0},{12,4},{16,24},{20,28},{24,16},{28,20},{1,9},{5... | collective-permute-start | bytes 442376 | tf_op jit(solution)/shard_map/ppermute | solution.py:84
  402.0 17.8 %collective-permute-start.90 = (f32[8,768]{1,0:T(8,128)S(1)}, f32[8,768]{1,0:T(8,128)S(1)}, u32[]{:S(2)}, u32[]{:S(2)}) collective-permute-start(f32[8,768]{1,0:T(8,128)S(1)} %shard_map.271.refs_3_.refs_0_), channel_id=1, source_target_pairs={{0,4},{4,0},{8,12},{12,8},{16,20},{20,16},{24,28},{28,24},{1,5},{5... | collective-permute-start | bytes 73736 | tf_op jit(solution)/shard_map/ppermute | solution.py:84
  419.9 20.0 %collective-permute-start.98 = (bf16[96,768]{1,0:T(8,128)(2,1)S(1)}, bf16[96,768]{1,0:T(8,128)(2,1)S(1)}, u32[]{:S(2)}, u32[]{:S(2)}) collective-permute-start(bf16[96,768]{1,0:T(8,128)(2,1)S(1)} %get-tuple-element.380), channel_id=1, source_target_pairs={{0,16},{4,20},{8,24},{12,28},{16,0},{20,4},{24,8},{28,12},{1,17},{... | collective-permute-start | bytes 442376 | tf_op jit(solution)/shard_map/ppermute | solution.py:84
  419.9 20.0 %collective-permute-start.99 = (bf16[96,768]{1,0:T(8,128)(2,1)S(1)}, bf16[96,768]{1,0:T(8,128)(2,1)S(1)}, u32[]{:S(2)}, u32[]{:S(2)}) collective-permute-start(bf16[96,768]{1,0:T(8,128)(2,1)S(1)} %get-tuple-element.381), channel_id=1, source_target_pairs={{0,24},{4,28},{8,16},{12,20},{16,8},{20,12},{24,0},{28,4},{1,25},{... | collective-permute-start | bytes 442376 | tf_op jit(solution)/shard_map/ppermute | solution.py:84
  421.5 11.6 %collective-permute-start.100 = (f32[8,768]{1,0:T(8,128)S(1)}, f32[8,768]{1,0:T(8,128)S(1)}, u32[]{:S(2)}, u32[]{:S(2)}) collective-permute-start(f32[8,768]{1,0:T(8,128)S(1)} %shard_map.275.refs_2_.refs_0_), channel_id=1, source_target_pairs={{0,8},{4,12},{8,0},{12,4},{16,24},{20,28},{24,16},{28,20},{1,9},{5... | collective-permute-start | bytes 73736 | tf_op jit(solution)/shard_map/ppermute | solution.py:84
  423.5 16.4 %collective-permute-start.92 = (bf16[2,64,384]{2,1,0:T(8,128)(2,1)S(1)}, bf16[2,64,384]{2,1,0:T(8,128)(2,1)S(1)}, u32[]{:S(2)}, u32[]{:S(2)}) collective-permute-start(bf16[2,64,384]{2,1,0:T(8,128)(2,1)S(1)} %get-tuple-element.374), channel_id=1, source_target_pairs={{0,8},{4,12},{8,0},{12,4},{16,24},{20,28},{24,16},{28,20},{1,9},{5... | collective-permute-start | bytes 294920 | tf_op jit(solution)/shard_map/ppermute | solution.py:84
  433.1 11.4 %collective-permute-start.93 = (bf16[2,64,384]{2,1,0:T(8,128)(2,1)S(1)}, bf16[2,64,384]{2,1,0:T(8,128)(2,1)S(1)}, u32[]{:S(2)}, u32[]{:S(2)}) collective-permute-start(bf16[2,64,384]{2,1,0:T(8,128)(2,1)S(1)} %get-tuple-element.375), channel_id=1, source_target_pairs={{0,16},{4,20},{8,24},{12,28},{16,0},{20,4},{24,8},{28,12},{1,17},{... | collective-permute-start | bytes 294920 | tf_op jit(solution)/shard_map/ppermute | solution.py:84
  433.2 11.3 %collective-permute-start.94 = (bf16[2,64,384]{2,1,0:T(8,128)(2,1)S(1)}, bf16[2,64,384]{2,1,0:T(8,128)(2,1)S(1)}, u32[]{:S(2)}, u32[]{:S(2)}) collective-permute-start(bf16[2,64,384]{2,1,0:T(8,128)(2,1)S(1)} %get-tuple-element.376), channel_id=1, source_target_pairs={{0,24},{4,28},{8,16},{12,20},{16,8},{20,12},{24,0},{28,4},{1,25},{... | collective-permute-start | bytes 294920 | tf_op jit(solution)/shard_map/ppermute | solution.py:84
  445.7 15.5 %collective-permute-start.102 = (bf16[8,64,384]{2,1,0:T(8,128)(2,1)S(1)}, bf16[8,64,384]{2,1,0:T(8,128)(2,1)S(1)}, u32[]{:S(2)}, u32[]{:S(2)}) collective-permute-start(bf16[8,64,384]{2,1,0:T(8,128)(2,1)S(1)} %shard_map.278.refs_2_), channel_id=1, source_target_pairs={{0,1},{1,0},{2,3},{3,2},{4,5},{5,4},{6,7},{7,6},{8,9},{9,8},{10,11... | collective-permute-start | bytes 1179656 | tf_op jit(solution)/shard_map/ppermute | solution.py:76
  (74 other events, 670.3 us)
